TPU v7x, 32 devices: a whole 2x2x4 slice. The times are simulated.
32 devices in a mesh: rep: 2 (over x), pool: 2 (over core), tp: 8 (over z, y).
Axes of the slice: x: 2, y: 2, z: 4, core: 2. Of those that a mesh axis runs over, the one named last changes fastest.
Arguments:
- prompt_x: bfloat16 [8192, 5120], P(('rep', 'pool')), parts along dimension 0, may hold values from -40 to 40
- q_weight: bfloat16 [5120, 4096], P(None, 'tp'), may hold values from -0.078125 to 0.078125
- kv_weight: bfloat16 [5120, 2048], P(None, 'tp'), may hold values from -0.078125 to 0.078125
- prompt_blocks: int32 [4, 3], P('rep'), parts along dimension 0, may hold values from 1 to 8, as said below
- finished: int32 [4, 3], P('rep'), parts along dimension 0, may hold values from 0 to 1, as said below
- placement: int32 [4, 16, 2], P('rep'), parts along dimension 0, may hold values from 0 to 7, as said below
- page_table: int32 [96, 2], P(('rep', 'pool', 'tp')), parts along dimension 0, may hold values from 0 to 5, as said below
- row_lens: int32 [96], P(('rep', 'pool', 'tp')), parts along dimension 0, may hold values from 128 to 256, as said below
- kv_cache: bfloat16 [192, 128, 2048], P(('rep', 'pool', 'tp')), parts along dimension 0, may hold values from -40 to 40
- decode_x: bfloat16 [2, 96, 5120], P(None, ('rep', 'pool')), parts along dimension 1, may hold values from -40 to 40
Outputs:
- prompt_attn: bfloat16 [8192, 4096], P(('rep', 'pool'), 'tp'), parts along dimension 0
- decode_attn: bfloat16 [2, 96, 4096], P(None, ('rep', 'pool', 'tp')), parts along dimension 1
There are 2 independent parts, one for each index of `rep`. A program takes and returns all parts, laid end to end along the dimension named above; an argument that names none is the same for every part. Nothing has to cross between parts.
Inputs may be any that keep to these rules, and one draw needn't show every extreme that they name: `prompt_blocks`: the counts of each group sum to 16; in each group one prompt holds exactly 8 blocks. Every group has at least one finished prompt. placement[g, b, 0] is a device index on tp of group 1 - g and placement[g, b, 1] a slot there; no two blocks of a group share a device and slot; a device receives at most 3 blocks of a group, and one device receives exactly 3; each named slot is a page of some row owned by that device. `page_table`: the rows of one device name each of its 6 slots exactly once. `row_lens`: both bounds are reached in every draw.
All inputs are finite; a program needn't handle non-finite values.
Results may differ from a plain program's by a relative error of at most 0.006.
The roundings to bfloat16 on the way count: a program that leaves them out, or rounds other values in their place, can miss the bound.
Values may be sent and summed in bfloat16 or wider, within the bound.
No kernel may reach another device: no remote copies, remote signals or barrier semaphores. Data moves between devices by JAX's collectives and lax.ppermute only.
A program may use at most 256 MiB of HBM per device.

v0:
```python
import jax
import jax.numpy as jnp
from jax import lax
from jax.sharding import PartitionSpec as P

QH = 32
KVH = 8
HD = 128
BLOCK_TOKENS = 128
PTOK = 2048
PAGES = 2
STEPS = 2
NBLK = 16
DEVICE_SLOTS = 6
KEY_VALUE_COLUMNS = 2048


def from_partner(block, axis, distance):
    count = lax.axis_size(axis)
    route = []
    for low in range(count):
        high = low | 1 << distance
        if high != low and high < count:
            route += [(low, high), (high, low)]
    return lax.ppermute(block, axis, route)


def block_table(prompt_blocks, finished, placement, sender_rows):
    counts = lax.dynamic_index_in_dim(prompt_blocks, sender_rows, 0, keepdims=False)
    done_flags = lax.dynamic_index_in_dim(finished, sender_rows, 0, keepdims=False)
    placed = lax.dynamic_index_in_dim(placement, sender_rows, 0, keepdims=False)
    prompt_end = jnp.cumsum(counts)
    blocks_idx = jnp.arange(placed.shape[0])
    owner_of = jnp.sum((blocks_idx[:, None] >= prompt_end[None, :]).astype(jnp.int32), axis=1)
    prompt_idx = jnp.arange(counts.shape[0])
    is_live = jnp.sum(
        jnp.where(owner_of[:, None] == prompt_idx[None, :], done_flags[None, :], 0), axis=1
    )
    return (placed[:, 0], placed[:, 1], is_live)


def arrival_pick(receiver_rows, tp_count, most):
    blocks_idx = jnp.arange(receiver_rows.shape[0])
    earlier = (receiver_rows[None, :] == receiver_rows[:, None]) & (
        blocks_idx[None, :] < blocks_idx[:, None]
    )
    arrival = jnp.sum(earlier.astype(jnp.int32), axis=1)
    to_rank = receiver_rows[None, None, :] == jnp.arange(tp_count)[:, None, None]
    in_turn = arrival[None, None, :] == jnp.arange(most)[None, :, None]
    return (to_rank & in_turn).astype(jnp.int32)


def local(
    prompt_x,
    q_weight,
    kv_weight,
    prompt_blocks,
    finished,
    placement,
    page_table,
    row_lens,
    kv_cache,
    decode_x,
):
    my_group = lax.axis_index("pool")
    my_rank = lax.axis_index("tp")
    tp_count = lax.axis_size("tp")
    other_group = 1 - my_group
    score_scale = HD ** (-0.5)
    q_per_kv = QH // KVH
    local_q = q_weight.shape[1] // HD
    slice_len = BLOCK_TOKENS // tp_count
    most = 2 + (NBLK - 2) // tp_count
    queries = jnp.dot(prompt_x, q_weight, preferred_element_type=jnp.float32).astype(jnp.bfloat16)
    kv_local = jnp.dot(prompt_x, kv_weight, preferred_element_type=jnp.float32).astype(jnp.bfloat16)
    kv_whole = lax.all_gather(kv_local, "tp", axis=1, tiled=True)
    kv_split = kv_whole.reshape(PTOK, KVH, 2, HD)
    head_kv = lax.dynamic_index_in_dim(kv_split, my_rank * local_q // q_per_kv, 1, keepdims=False)
    blocks = kv_whole.reshape(NBLK, BLOCK_TOKENS, KEY_VALUE_COLUMNS)
    my_slices = lax.dynamic_slice_in_dim(blocks, my_rank * slice_len, slice_len, 1)
    head_q = queries.reshape(PTOK, local_q, HD)
    position = jnp.arange(PTOK)
    counts = lax.dynamic_index_in_dim(prompt_blocks, my_group, 0, keepdims=False)
    prompt_end = jnp.cumsum(counts) * BLOCK_TOKENS
    segment = jnp.sum((position[:, None] >= prompt_end[None, :]).astype(jnp.int32), axis=1)
    allowed = (segment[:, None] == segment[None, :]) & (position[:, None] >= position[None, :])
    scores = (
        jnp.einsum("ihd,jd->hij", head_q, head_kv[:, 0], preferred_element_type=jnp.float32)
        * score_scale
    )
    scores = jnp.where(allowed[None], scores, -jnp.inf)
    row_peak = jnp.max(scores, axis=-1, keepdims=True)
    raised = jnp.exp(scores - row_peak)
    weights = (raised / jnp.sum(raised, axis=-1, keepdims=True)).astype(jnp.bfloat16)
    blended = jnp.einsum("hij,jd->ihd", weights, head_kv[:, 1], preferred_element_type=jnp.float32)
    prompt_attn = blended.astype(jnp.bfloat16).reshape(PTOK, local_q * HD)
    receiver_rows, slot_numbers, is_live = block_table(
        prompt_blocks, finished, placement, other_group
    )
    own_target = lax.dynamic_index_in_dim(placement, my_group, 0, keepdims=False)[:, 0]
    send_pick = arrival_pick(own_target, tp_count, most).astype(jnp.bfloat16)
    outgoing = jnp.einsum(
        "tmb,bsc->tmsc", send_pick, my_slices, preferred_element_type=jnp.float32
    ).astype(jnp.bfloat16)
    assembled = lax.all_to_all(outgoing, "tp", split_axis=0, concat_axis=2, tiled=True).reshape(
        most, BLOCK_TOKENS, KEY_VALUE_COLUMNS
    )
    incoming = from_partner(assembled, "pool", 0)
    in_pick = lax.dynamic_index_in_dim(
        arrival_pick(receiver_rows, tp_count, most), my_rank, 0, keepdims=False
    )
    slot_round = jnp.sum(in_pick * slot_numbers[None, :], axis=1)
    active_round = jnp.sum(in_pick * is_live[None, :], axis=1)
    select_slot = (jnp.arange(DEVICE_SLOTS)[:, None] == slot_round[None, :]) & (
        active_round[None, :] > 0
    )
    written = jnp.sum(select_slot.astype(jnp.int32), axis=1) > 0
    overwritten_cache = jnp.dot(
        select_slot.astype(jnp.bfloat16),
        incoming.reshape(most, BLOCK_TOKENS * KEY_VALUE_COLUMNS),
        preferred_element_type=jnp.float32,
    )
    overwritten_cache = overwritten_cache.astype(jnp.bfloat16).reshape(
        DEVICE_SLOTS, BLOCK_TOKENS, KEY_VALUE_COLUMNS
    )
    cache_now = jnp.where(written[:, None, None], overwritten_cache, kv_cache)
    rows_dev = page_table.shape[0]
    rows_in = decode_x.reshape(-1, decode_x.shape[2])
    decode_q = jnp.dot(rows_in, q_weight, preferred_element_type=jnp.float32).astype(jnp.bfloat16)
    decode_kv = jnp.dot(rows_in, kv_weight, preferred_element_type=jnp.float32).astype(jnp.bfloat16)
    decode_q = decode_q.reshape(STEPS, tp_count, rows_dev, local_q * HD)
    decode_kv = decode_kv.reshape(STEPS, tp_count, rows_dev, kv_weight.shape[1])
    own_q, own_kv = (
        lax.all_to_all(decode_q, "tp", split_axis=1, concat_axis=3, tiled=True),
        lax.all_to_all(decode_kv, "tp", split_axis=1, concat_axis=3, tiled=True),
    )
    own_q = own_q.reshape(STEPS, rows_dev, KVH, q_per_kv, HD)
    own_kv = own_kv.reshape(STEPS, rows_dev, KVH, 2, HD)
    context_len = PAGES * BLOCK_TOKENS
    context = cache_now[page_table.reshape(-1)].reshape(rows_dev, context_len, KVH, 2, HD)
    old_scores = (
        jnp.einsum(
            "srhgd,rthd->srhgt", own_q, context[:, :, :, 0], preferred_element_type=jnp.float32
        )
        * score_scale
    )
    usable = jnp.arange(context_len)[None, :] < row_lens[:, None]
    old_scores = jnp.where(usable[None, :, None, None, :], old_scores, -jnp.inf)
    new_scores = (
        jnp.einsum(
            "srhgd,urhd->srhgu", own_q, own_kv[:, :, :, 0], preferred_element_type=jnp.float32
        )
        * score_scale
    )
    visible = jnp.arange(STEPS)[None, :] <= jnp.arange(STEPS)[:, None]
    new_scores = jnp.where(visible[:, None, None, None, :], new_scores, -jnp.inf)
    top_score = jnp.maximum(jnp.max(old_scores, axis=-1), jnp.max(new_scores, axis=-1))[..., None]
    old_raised = jnp.exp(old_scores - top_score)
    new_raised = jnp.exp(new_scores - top_score)
    totals = jnp.sum(old_raised, axis=-1, keepdims=True) + jnp.sum(
        new_raised, axis=-1, keepdims=True
    )
    old_weights = (old_raised / totals).astype(jnp.bfloat16)
    new_weights = (new_raised / totals).astype(jnp.bfloat16)
    mixed_rows = jnp.einsum(
        "srhgt,rthd->srhgd", old_weights, context[:, :, :, 1], preferred_element_type=jnp.float32
    )
    mixed_rows = mixed_rows + jnp.einsum(
        "srhgu,urhd->srhgd", new_weights, own_kv[:, :, :, 1], preferred_element_type=jnp.float32
    )
    decode_attn = mixed_rows.astype(jnp.bfloat16).reshape(STEPS, rows_dev, QH * HD)
    return (prompt_attn, decode_attn)


def solution(mesh):
    return jax.shard_map(
        local,
        mesh=mesh,
        in_specs=(
            P(("rep", "pool"), None),
            P(None, "tp"),
            P(None, "tp"),
            P("rep", None),
            P("rep", None),
            P("rep", None, None),
            P(("rep", "pool", "tp"), None),
            P(("rep", "pool", "tp")),
            P(("rep", "pool", "tp"), None, None),
            P(None, ("rep", "pool"), None),
        ),
        out_specs=(P(("rep", "pool"), "tp"), P(None, ("rep", "pool", "tp"), None)),
        check_vma=False,
    )
```

profile of v0, /device:TPU:0, one launch (start us, length us, event | category | flops | bytes accessed | tf_op | source)
XLA Modules:
  0.0 260.9 jit_solution(14698172717660703039)
XLA Ops:
  7.2 0.0 copy-start
  7.2 0.0 copy-start.3
  7.2 0.0 all-gather.2.cloned.1.call-start
  7.2 1.7 copy-done
  8.9 11.0 %convolution_convert_fusion.3 = bf16[2048,256]{1,0:T(8,128)(2,1)} fusion(bf16[2048,5120]{1,0:T(8,128)(2,1)} %param.10, bf16[5120,256]{1,0:T(8,128)(2,1)S(1)} %copy-done), kind=kOutput, calls=%fused_computation.18 | convolution fusion | flops 5369233408 | bytes 24641536 | tf_op jit(solution)/shard_map/dot_general | solution.py:75
  19.9 0.0 copy-start.8
  20.0 0.0 all-gather.2.cloned.1.call-update
  20.0 0.6 convolution_convert_fusion.5
  20.6 0.6 copy.65
  21.2 7.3 %all-to-all-start.2 = ((bf16[2,8,3,256]{3,0,2,1:T(2,128)(2,1)}), bf16[2,8,3,256]{3,0,2,1:T(2,128)(2,1)S(1)}, u32[]{:S(2)}, u32[]{:S(2)}) async-start(bf16[2,8,3,256]{3,0,2,1:T(2,128)(2,1)} %copy.65), calls=%async_computation.2 | async-start | bytes 49152 | tf_op jit(solution)/shard_map/all_to_all | solution.py:135
  28.5 0.0 copy-done.5
  28.5 0.2 reduce-window.17
  28.7 0.2 reduce-window.16
  28.9 0.1 copy.60
  29.0 0.1 reshape.334
  29.1 0.0 copy-done.4
  29.2 0.1 convert_reduce_fusion.4
  29.2 0.2 convert_reduce_fusion.2
  29.4 0.1 select_reduce_fusion
  29.5 0.1 fusion.35
  29.7 0.1 convert_reduce_fusion
  29.8 0.2 convert_reduce_fusion.1
  30.0 0.1 convert_reduce_fusion.3
  30.1 0.0 copy-done.8
  30.1 0.6 iota_compare_fusion.3
  30.8 3.8 %convolution_convert_fusion.4 = bf16[48,512]{1,0:T(8,128)(2,1)S(1)} fusion(bf16[48,5120]{1,0:T(8,128)(2,1)S(1)} %bitcast.162, bf16[5120,512]{1,0:T(8,128)(2,1)} %param.11), kind=kOutput, calls=%fused_computation.28 | convolution fusion | flops 251682816 | bytes 5783552 | tf_op jit(solution)/shard_map/dot_general | solution.py:129
  34.5 5.4 %fusion.6 = pred[2048,2048]{0,1:T(8,128)(4,1)} fusion(s32[2048]{0:T(1024)S(1)} %convert_reduce_fusion), kind=kLoop, calls=%fused_computation.12 | loop fusion | flops 12582912 | bytes 4202496 | tf_op jit(solution)/shard_map/and | solution.py:86
  40.0 17.7 %convolution_convert_fusion.1 = bf16[2048,512]{0,1:T(8,128)(2,1)} fusion(bf16[2048,5120]{1,0:T(8,128)(2,1)} %param.10, bf16[5120,512]{1,0:T(8,128)(2,1)} %param.11), kind=kOutput, calls=%fused_computation.15 | convolution fusion | flops 10738466816 | bytes 28311552 | tf_op jit(solution)/shard_map/dot_general | solution.py:74
  57.7 0.7 copy.63
  58.4 0.0 all-to-all-done.2
  58.4 6.0 %all-to-all-start.1 = ((bf16[2,8,3,512]{3,0,2,1:T(2,128)(2,1)}), bf16[2,8,3,512]{3,0,2,1:T(2,128)(2,1)S(1)}, u32[]{:S(2)}, u32[]{:S(2)}) async-start(bf16[2,8,3,512]{3,0,2,1:T(2,128)(2,1)} %copy.63), calls=%async_computation.1 | async-start | bytes 98304 | tf_op jit(solution)/shard_map/all_to_all | solution.py:134
  64.4 7.4 %all-to-all-done.1 = bf16[2,8,3,512]{3,0,2,1:T(2,128)(2,1)S(1)} async-done(((bf16[2,8,3,512]{3,0,2,1:T(2,128)(2,1)}), bf16[2,8,3,512]{3,0,2,1:T(2,128)(2,1)S(1)}, u32[]{:S(2)}, u32[]{:S(2)}) %all-to-all-start.1) | async-done | bytes 49184 | tf_op jit(solution)/shard_map/all_to_all | solution.py:134
  71.8 0.6 fusion.52
  72.4 77.2 %all-gather.2.cloned.1.call-done = bf16[2048,2048]{1,0:T(8,128)(2,1)} async-done(((bf16[2048,256]{1,0:T(8,128)(2,1)}), bf16[2048,2048]{1,0:T(8,128)(2,1)}) %all-gather.2.cloned.1.call-update) | async-done | bytes 8388624 | tf_op jit(solution)/shard_map/all_gather | solution.py:76
  149.6 1.3 constant_dynamic-slice_fusion
  150.9 1.3 convolution_convert_fusion.2
  152.2 2.0 copy.58
  154.3 3.6 %all-to-all-start = ((bf16[8,3,16,2048]{3,2,1,0:T(8,128)(2,1)}), bf16[8,3,16,2048]{3,2,1,0:T(8,128)(2,1)S(1)}, u32[]{:S(2)}, u32[]{:S(2)}) async-start(bf16[8,3,16,2048]{3,2,1,0:T(8,128)(2,1)} %copy.58), calls=%async_computation | async-start | bytes 3145728 | tf_op jit(solution)/shard_map/all_to_all | solution.py:105
  157.8 14.3 %reshape.324 = bf16[2048,8,2,128]{3,2,1,0:T(2,128)(2,1)} reshape(bf16[2048,2048]{1,0:T(8,128)(2,1)} %all-gather.2.cloned.1.call-done) | data formatting | bytes 16777216 | tf_op jit(solution)/shard_map/reshape | solution.py:77
  172.2 1.8 constant_dynamic-slice_fusion.7
  174.0 0.1 copy.125
  174.1 31.3 %fusion.50 = (f32[4,2048]{1,0:T(4,128)S(1)}, f32[4,2048,2048]{1,2,0:T(8,128)}) fusion(pred[2048,2048]{0,1:T(8,128)(4,1)} %fusion.6, bf16[2048,4,128]{0,2,1:T(8,128)(2,1)} %bitcast.167, bf16[2048,2,128]{2,0,1:T(8,128)(2,1)S(1)} %bitcast.163), kind=kOutput, calls=%fused_computation.109 | convolution fusion | flops 4362078208 | bytes 73957376 | tf_op jit(solution)/shard_map/sub | solution.py:93
  205.4 0.0 all-to-all-done
  205.4 1.3 copy.59
  206.7 0.0 collective-permute-start
  206.7 22.3 %fusion.9 = bf16[128,4,2048]{2,0,1:T(8,128)(2,1)S(1)} fusion(f32[4,2048,2048]{1,2,0:T(8,128)} %get-tuple-element.23, f32[4,2048]{1,0:T(4,128)S(1)} %get-tuple-element.22, bf16[2048,2,128]{2,0,1:T(8,128)(2,1)S(1)} %bitcast.164), kind=kOutput, calls=%fused_computation.16 | convolution fusion | flops 4329570304 | bytes 69763072 | tf_op jit(solution)/shard_map/hij,jd->ihd/dot_general | solution.py:95
  228.9 2.5 copy.70
  231.4 0.0 collective-permute-done
  231.4 2.8 %copy.86 = bf16[1,3,128,2048]{3,1,2,0:T(4,128)(2,1)S(1)} copy(bf16[1,3,128,2048]{3,2,1,0:T(8,128)(2,1)} %bitcast.61) | data formatting | bytes 3145728
  234.2 0.0 copy-start.2
  234.2 2.1 convolution_convert_fusion
  236.3 3.5 %bitcast_select_fusion.4 = bf16[6,128,2048]{2,1,0:T(8,128)(2,1)S(1)} fusion(bf16[6,128,2048]{2,1,0:T(8,128)(2,1)S(1)} %copy-done.2, bf16[1,6,128,2048]{3,1,2,0:T(8,128)(2,1)S(1)} %bitcast.157, pred[6]{0:T(512)(128)(4,1)S(1)} %broadcast_compare_fusion), kind=kLoop, calls=%fused_computation.14 | loop fusion | flops 1572864 | bytes 9437190 | tf_op jit(solution)/shard_map/jit(_where)/select_n | solution.py:126
  239.8 2.5 gather_fusion
  242.3 4.7 %reshape.335 = bf16[3,256,8,2,128]{4,3,2,1,0:T(2,128)(2,1)S(1)} reshape(bf16[6,128,2048]{2,1,0:T(8,128)(2,1)} %gather_fusion) | data formatting | bytes 6291456 | tf_op jit(solution)/shard_map/reshape | solution.py:140
  247.0 0.0 copy-start.9
  247.0 4.5 %fusion.48 = (bf16[3,256,8,1,128]{4,3,2,1,0:T(2,128)(2,1)S(1)}, bf16[3,256,8,1,128]{4,3,2,1,0:T(2,128)(2,1)S(1)}) fusion(bf16[3,256,8,2,128]{4,3,2,1,0:T(2,128)(2,1)S(1)} %reshape.335), kind=kLoop, calls=%fused_computation.107 | loop fusion | bytes 6291456 | tf_op jit(solution)/shard_map/slice | solution.py:166
  251.4 0.0 copy-done.9
  251.5 0.0 copy-start.1
  251.5 0.7 fusion.51
  252.2 0.1 fusion.26
  252.3 0.3 fusion.21
  252.6 0.2 fusion.27
  252.8 0.6 fusion.17
  253.5 0.6 reshape.341
  (33 shorter events, 0.3 us)
Async XLA Ops:
  7.2 1.7 copy-start
  7.2 12.8 %copy-start.3 = (bf16[2,24,5120]{2,1,0:T(8,128)(2,1)S(1)}, bf16[2,24,5120]{2,1,0:T(8,128)(2,1)}, u32[]{:S(2)}) copy-start(bf16[2,24,5120]{2,1,0:T(8,128)(2,1)} %param.19) | copy-start | bytes 1474564
  7.2 142.4 %all-gather.2.cloned.1.call-start = ((), (), s32[]{:S(2)}) async-start(), calls=%async_computation.3 | async-start | bytes 9437184 | tf_op jit(solution)/shard_map/all_gather | solution.py:76
  19.9 8.6 %copy-start.5 = (s32[2,3]{1,0:T(2,128)S(1)}, s32[2,3]{1,0:T(2,128)}, u32[]{:S(2)}) copy-start(s32[2,3]{1,0:T(2,128)} %param.13) | copy-start | bytes 76
  19.9 8.9 %copy-start.6 = (s32[3,2]{0,1:T(2,128)S(1)}, s32[3,2]{0,1:T(2,128)}, u32[]{:S(2)}) copy-start(s32[3,2]{0,1:T(2,128)} %param.16) | copy-start | bytes 76
  19.9 9.1 %copy-start.7 = (s32[2,3]{1,0:T(2,128)S(1)}, s32[2,3]{1,0:T(2,128)}, u32[]{:S(2)}) copy-start(s32[2,3]{1,0:T(2,128)} %param.14) | copy-start | bytes 76
  19.9 9.1 %copy-start.4 = (s32[2,16,2]{1,2,0:T(2,128)S(1)}, s32[2,16,2]{1,2,0:T(2,128)}, u32[]{:S(2)}) copy-start(s32[2,16,2]{1,2,0:T(2,128)} %param.15) | copy-start | bytes 772
  19.9 10.2 %copy-start.8 = (s32[3]{0:T(128)S(1)}, s32[3]{0:T(128)}, u32[]{:S(2)}) copy-start(s32[3]{0:T(128)} %param.17) | copy-start | bytes 40
  21.2 37.1 %all-to-all-start.2 = ((bf16[2,8,3,256]{3,0,2,1:T(2,128)(2,1)}), bf16[2,8,3,256]{3,0,2,1:T(2,128)(2,1)S(1)}, u32[]{:S(2)}, u32[]{:S(2)}) async-start(bf16[2,8,3,256]{3,0,2,1:T(2,128)(2,1)} %copy.65), calls=%async_computation.2 | async-start | bytes 49152 | tf_op jit(solution)/shard_map/all_to_all | solution.py:135
  58.4 13.4 %all-to-all-start.1 = ((bf16[2,8,3,512]{3,0,2,1:T(2,128)(2,1)}), bf16[2,8,3,512]{3,0,2,1:T(2,128)(2,1)S(1)}, u32[]{:S(2)}, u32[]{:S(2)}) async-start(bf16[2,8,3,512]{3,0,2,1:T(2,128)(2,1)} %copy.63), calls=%async_computation.1 | async-start | bytes 98304 | tf_op jit(solution)/shard_map/all_to_all | solution.py:134
  154.3 51.1 %all-to-all-start = ((bf16[8,3,16,2048]{3,2,1,0:T(8,128)(2,1)}), bf16[8,3,16,2048]{3,2,1,0:T(8,128)(2,1)S(1)}, u32[]{:S(2)}, u32[]{:S(2)}) async-start(bf16[8,3,16,2048]{3,2,1,0:T(8,128)(2,1)} %copy.58), calls=%async_computation | async-start | bytes 3145728 | tf_op jit(solution)/shard_map/all_to_all | solution.py:105
  206.7 24.8 %collective-permute-start = (bf16[3,128,2048]{2,1,0:T(8,128)(2,1)}, bf16[3,128,2048]{2,1,0:T(8,128)(2,1)}, u32[]{:S(2)}, u32[]{:S(2)}) collective-permute-start(bf16[3,128,2048]{2,1,0:T(8,128)(2,1)} %bitcast.26), channel_id=1, source_target_pairs={{0,8},{8,0},{1,9},{9,1},{2,10},{10,2},{3,11},{11,3},{4,12},{12,4},... | collective-permute-start | bytes 4718600 | tf_op jit(solution)/shard_map/ppermute | solution.py:25
  234.2 2.1 copy-start.2
  247.0 4.5 %copy-start.9 = (pred[3,256]{1,0:T(4,128)(4,1)S(1)}, pred[3,256]{1,0:T(4,128)(4,1)}, u32[]{:S(2)}) copy-start(pred[3,256]{1,0:T(4,128)(4,1)} %iota_compare_fusion.3) | copy-start | bytes 2308
  251.5 2.6 %copy-start.1 = (bf16[5120,256]{1,0:T(8,128)(2,1)S(1)}, bf16[5120,256]{1,0:T(8,128)(2,1)}, u32[]{:S(2)}) copy-start(bf16[5120,256]{1,0:T(8,128)(2,1)} %param.12) | copy-start | bytes 7864324
Sparse Core Ops, SparseCore 0:
  20.1 129.4 all-gather.1
where the time goes:
time: 262 us; the launch traced here: 261 us
  matrix products  92 us (35%)
  waiting for transfers between devices  84.6 us (32%)
  local copies, waits for them, and re-layouts  41.8 us (16%)
  starting transfers between devices  16.9 us (6%)
  between operations  14.4 us (5%)
  other arithmetic  11.2 us (4%)
    all_gather x1, waiting for transfers between devices, local(): kv_whole = lax.all_gather(kv_local, 'tp', axis=1, tiled=True)  77.2 us
    sub x1, matrix products, local(): raised = jnp.exp(scores - row_peak)  31.3 us
    dot_general x1, matrix products, local(): jnp.einsum('hij,jd->ihd', weights, head_kv[:, 1], preferred_element_type=...  22.3 us
    dot_general x1, matrix products, local(): jnp.dot(prompt_x, q_weight, preferred_element_type=jnp.float32)  17.7 us
    reshape x1, local copies, waits for them, and re-layouts, local(): kv_split = kv_whole.reshape(PTOK, KVH, 2, HD)  14.3 us
    dot_general x1, matrix products, local(): jnp.dot(prompt_x, kv_weight, preferred_element_type=jnp.float32)  11 us
    all_to_all x1, waiting for transfers between devices, local(): lax.all_to_all(decode_q, 'tp', split_axis=1, concat_axis=3, tiled=True)  7.4 us
    all_to_all x1, starting transfers between devices, local(): lax.all_to_all(decode_kv, 'tp', split_axis=1, concat_axis=3, tiled=True)  7.28 us
  transfers between devices with their start and end apart: 5, of which 2 were waited for; matrix products, arithmetic and copies ran while one was open for 40% of the time, Pallas kernels for 0%

commit v1 on v0

v1 whole, which is shorter than its diff:
```python
import functools

import jax
import jax.numpy as jnp
from jax import lax
from jax.experimental import pallas as pl
from jax.experimental.pallas import tpu as pltpu
from jax.sharding import PartitionSpec as P

QH = 32
KVH = 8
GQ = QH // KVH
HD = 128
BLOCK_TOKENS = 128
PTOK = 2048
NPROMPT = 3
MOST_BLOCKS = 8
PAGES = 2
STEPS = 2
NBLK = 16
DEVICE_SLOTS = 6
ROWS_DEV = 3
GROUP_ROWS = 8
KEY_VALUE_COLUMNS = 2048
SCALE = HD ** (-0.5)
MASKED = -1e30
PIECES = 5
MIB = 1 << 20
VMEM = pltpu.VMEM
SMEM = pltpu.SMEM


def dot(a, b):
    return jnp.dot(a, b, preferred_element_type=jnp.float32)


def dot_t(a, b):
    return lax.dot_general(a, b, (((1,), (1,)), ((), ())), preferred_element_type=jnp.float32)


def iota(shape, axis):
    return lax.broadcasted_iota(jnp.int32, shape, axis)


def row_of(rs):
    return jnp.where(rs >= 2 * ROWS_DEV, ROWS_DEV, jnp.where(rs >= ROWS_DEV, rs - ROWS_DEV, rs))


def project(first, n, lq, *refs):
    if first:
        dx_ref, x_ref, wq_hbm, wkv_hbm, q_ref, kv_ref, qh_ref = refs[:7]
        out_msgs = refs[7 : 7 + n]
        wq, wkv, sems, held = refs[7 + n :]
    else:
        x_ref, wq_hbm, wkv_hbm, _, _, q_ref, kv_ref, wq, wkv, sems = refs
    piece = wq.shape[0] // PIECES

    def copies(c):
        part = pl.ds(c * piece, piece)
        return (
            pltpu.make_async_copy(wq_hbm.at[part], wq.at[part], sems.at[0, c]),
            pltpu.make_async_copy(wkv_hbm.at[part], wkv.at[part], sems.at[1, c]),
        )

    @pl.when(pl.program_id(0) == 0)
    def _():
        for c in range(PIECES):
            for copy in copies(c):
                copy.start()
        totals = [0.0] * 4
        for c in range(PIECES):
            for copy in copies(c):
                copy.wait()
            part = slice(c * piece, (c + 1) * piece)
            x = x_ref[:, part]
            totals[0] += dot(x, wq[part, :])
            totals[1] += dot(x, wkv[part, :])
            if first:
                dx = dx_ref[:, part]
                totals[2] += dot(dx, wq[part, :])
                totals[3] += dot(dx, wkv[part, :])
        q_ref[...] = totals[0].astype(jnp.bfloat16)
        kv_ref[...] = totals[1].astype(jnp.bfloat16)
        if first:
            me = lax.axis_index("tp")
            rows = STEPS * ROWS_DEV * n
            shape = (n * GROUP_ROWS, rows)
            to, fro = iota(shape, 0), iota(shape, 1)
            owner, rs = to // GROUP_ROWS, to % GROUP_ROWS
            late = rs >= ROWS_DEV
            wanted = owner * ROWS_DEV + row_of(rs) + jnp.where(late, ROWS_DEV * n, 0)
            pick = ((fro == wanted) & (rs < STEPS * ROWS_DEV)).astype(jnp.float32).astype(jnp.bfloat16)
            dq = dot(pick, totals[2].astype(jnp.bfloat16))
            dkv = dot(pick, totals[3].astype(jnp.bfloat16))
            cq = lq * HD
            held[:, :cq] = dq
            held[:, cq:] = dkv
            for h in range(lq):
                part = slice(h * n * GROUP_ROWS, (h + 1) * n * GROUP_ROWS)
                qh_ref[part, :] = dq[:, h * HD : (h + 1) * HD].astype(jnp.bfloat16)
            for d in range(n):
                to = lax.rem(me + d, n)
                out_msgs[d][...] = held[pl.ds(pl.multiple_of(to * GROUP_ROWS, GROUP_ROWS), GROUP_ROWS), :]

    @pl.when(pl.program_id(0) > 0)
    def _():
        x = x_ref[...]
        q_ref[...] = dot(x, wq[...]).astype(jnp.bfloat16)
        kv_ref[...] = dot(x, wkv[...]).astype(jnp.bfloat16)


def project_rows(x, wq, wkv, start, count, block, held=None, dx=None, n=None):
    rows, depth = x.shape
    cq, ckv = wq.shape[1], wkv.shape[1]
    lq = cq // HD
    first = held is None
    offset = start // block
    out_shape = [
        jax.ShapeDtypeStruct((rows, cq), jnp.bfloat16),
        jax.ShapeDtypeStruct((rows, ckv), jnp.bfloat16),
    ]
    out_specs = [
        pl.BlockSpec((block, cq), lambda i: (i + offset, 0)),
        pl.BlockSpec((block, ckv), lambda i: (i + offset, 0)),
    ]
    any_spec = pl.BlockSpec(memory_space=pl.ANY)
    x_spec = pl.BlockSpec((block, depth), lambda i: (i + offset, 0))
    scratch = [
        VMEM((depth, cq), jnp.bfloat16),
        VMEM((depth, ckv), jnp.bfloat16),
        pltpu.SemaphoreType.DMA((2, PIECES)),
    ]
    if first:
        whole = pl.BlockSpec(dx.shape, lambda i: (0, 0))
        args = (dx, x, wq, wkv)
        in_specs = [whole, x_spec, any_spec, any_spec]
        out_shape.append(jax.ShapeDtypeStruct((lq * n * GROUP_ROWS, HD), jnp.bfloat16))
        out_specs.append(pl.BlockSpec((lq * n * GROUP_ROWS, HD), lambda i: (0, 0)))
        for _ in range(n):
            out_shape.append(jax.ShapeDtypeStruct((GROUP_ROWS, cq + ckv), jnp.float32))
            out_specs.append(pl.BlockSpec((GROUP_ROWS, cq + ckv), lambda i: (0, 0)))
        scratch.append(VMEM((n * GROUP_ROWS, cq + ckv), jnp.float32))
        aliases = {}
    else:
        args = (x, wq, wkv) + held
        in_specs = [x_spec] + [any_spec] * 4
        aliases = {3: 0, 4: 1}
    return pl.pallas_call(
        functools.partial(project, first, n, lq),
        grid=(count // block,),
        in_specs=in_specs,
        out_specs=out_specs,
        out_shape=out_shape,
        scratch_shapes=scratch,
        input_output_aliases=aliases,
        compiler_params=pltpu.CompilerParams(vmem_limit_bytes=40 * MIB),
        cost_estimate=pl.CostEstimate(
            flops=2 * count * depth * (cq + ckv),
            bytes_accessed=2 * (count + cq + ckv) * depth + 2 * count * (cq + ckv),
            transcendentals=0,
        ),
        name="project_first" if first else "project",
    )(*args)


def attend_prompt(lq, counts, q_ref, kv_ref, o_ref):
    group = lax.axis_index("pool")
    i = pl.program_id(0)
    first_end = counts[group, 0]
    second_end = first_end + counts[group, 1]
    start = jnp.where(i < first_end, 0, jnp.where(i < second_end, first_end, second_end))
    blocks = i - start + 1
    for k in range(1, MOST_BLOCKS + 1):

        @pl.when(blocks == k)
        def _(k=k):
            rows = pl.ds(pl.multiple_of(start * BLOCK_TOKENS, BLOCK_TOKENS), k * BLOCK_TOKENS)
            keys = kv_ref[rows, :HD]
            values = kv_ref[rows, HD:]
            shape = (BLOCK_TOKENS, BLOCK_TOKENS)
            causal = iota(shape, 0) >= iota(shape, 1)
            for h in range(lq):
                cols = slice(h * HD, (h + 1) * HD)
                scores = dot_t(q_ref[:, cols], keys) * SCALE
                last = jnp.where(causal, scores[:, (k - 1) * BLOCK_TOKENS :], MASKED)
                if k > 1:
                    scores = jnp.concatenate([scores[:, : (k - 1) * BLOCK_TOKENS], last], axis=1)
                else:
                    scores = last
                raised = jnp.exp(scores - jnp.max(scores, axis=1, keepdims=True))
                inverse = 1.0 / jnp.sum(raised, axis=1, keepdims=True)
                weights = (raised * inverse).astype(jnp.bfloat16)
                o_ref[:, cols] = dot(weights, values).astype(jnp.bfloat16)


def prompt_attention(counts, q, kv):
    rows, cq = q.shape
    return pl.pallas_call(
        functools.partial(attend_prompt, cq // HD),
        grid=(rows // BLOCK_TOKENS,),
        in_specs=[
            pl.BlockSpec(memory_space=SMEM),
            pl.BlockSpec((BLOCK_TOKENS, cq), lambda i: (i, 0)),
            pl.BlockSpec(kv.shape, lambda i: (0, 0)),
        ],
        out_specs=pl.BlockSpec((BLOCK_TOKENS, cq), lambda i: (i, 0)),
        out_shape=jax.ShapeDtypeStruct((rows, cq), jnp.bfloat16),
        compiler_params=pltpu.CompilerParams(vmem_limit_bytes=32 * MIB),
        cost_estimate=pl.CostEstimate(
            flops=8 * rows * rows // 2 * cq, bytes_accessed=8 * rows * cq, transcendentals=rows * rows
        ),
        name="prompt_attention",
    )(counts, q, kv)


def row_head(n, lq, h, hh):
    at = h * GQ + hh
    return at // lq, at % lq


def owner_scores(n, lq, counts, done, placed, table, lens, cache, *refs):
    msgs = refs[:n]
    scores_ref, fresh_ref = refs[n : n + 2]
    outs = refs[n + 2 : 2 * n + 2]
    slot_row, slot_limit, held, stats = refs[2 * n + 2 :]
    me = lax.axis_index("tp")
    other = 1 - lax.axis_index("pool")
    first_end = counts[other, 0]
    second_end = first_end + counts[other, 1]
    block_of = [[jnp.int32(-1)] * PAGES for _ in range(ROWS_DEV)]
    for b in range(NBLK):
        live = jnp.where(
            b < first_end, done[other, 0], jnp.where(b < second_end, done[other, 1], done[other, 2])
        )
        slot = jnp.where((live > 0) & (placed[other, b, 0] == me), placed[other, b, 1], -1)
        for r in range(ROWS_DEV):
            for p in range(PAGES):
                block_of[r][p] = jnp.where(slot == table[r, p], b, block_of[r][p])
    for r in range(ROWS_DEV):
        for p in range(PAGES):
            slot_row[table[r, p]] = jnp.int32(r)
            slot_limit[table[r, p]] = jnp.where(block_of[r][p] < 0, lens[r] - p * BLOCK_TOKENS, 0)
    for d in range(n):
        source = lax.rem(me + n - d, n)
        held[pl.ds(pl.multiple_of(source * GROUP_ROWS, GROUP_ROWS), GROUP_ROWS), :] = msgs[d][...]

    cq = lq * HD
    queries, keys, scores = [], [], []
    for h in range(KVH):
        own = []
        for hh in range(GQ):
            t, at = row_head(n, lq, h, hh)
            own.append(held[t * GROUP_ROWS : (t + 1) * GROUP_ROWS, at * HD : (at + 1) * HD])
        own = jnp.concatenate(own, axis=0)
        t, _ = row_head(n, lq, h, 0)
        new_key = held[t * GROUP_ROWS : (t + 1) * GROUP_ROWS, cq : cq + HD]
        queries.append(own)
        keys += [new_key] * GQ
        scores.append(dot_t(own.astype(jnp.bfloat16), cache[:, h * 2 * HD : h * 2 * HD + HD]) * SCALE)
    queries = jnp.concatenate(queries, axis=0)
    earlier = jnp.concatenate([pltpu.roll(key, ROWS_DEV, 0) for key in keys], axis=0)
    keys = jnp.concatenate(keys, axis=0)
    scores = jnp.concatenate(scores, axis=0)
    rows = queries.shape[0]
    shape = (rows, HD)
    at_row, lane = iota(shape, 0), iota(shape, 1)
    rs = at_row % GROUP_ROWS
    r = row_of(rs)
    parts = []
    for slot in range(DEVICE_SLOTS):
        usable = (r == slot_row[slot]) & (lane < slot_limit[slot])
        parts.append(jnp.where(usable, scores[:, slot * BLOCK_TOKENS : (slot + 1) * BLOCK_TOKENS], MASKED))
    scores = jnp.concatenate(parts, axis=1)
    now = jnp.sum(queries * keys, axis=1, keepdims=True) * SCALE
    before = jnp.sum(queries * earlier, axis=1, keepdims=True) * SCALE
    rs1 = iota((rows, 1), 0) % GROUP_ROWS
    r1 = row_of(rs1)
    before = jnp.where((rs1 >= ROWS_DEV) & (rs1 < STEPS * ROWS_DEV), before, MASKED)
    peak = jnp.maximum(jnp.max(scores, axis=1, keepdims=True), jnp.maximum(now, before))
    total = jnp.sum(jnp.exp(scores - peak), axis=1, keepdims=True) + jnp.exp(now - peak) + jnp.exp(before - peak)
    scores_ref[...] = scores
    fresh_ref[...] = jnp.where(lane == 0, now, jnp.where(lane == 1, before, 0.0))

    def by_row(values, rest):
        out = jnp.full((rows, 1), rest, jnp.int32)
        for k in range(ROWS_DEV):
            out = jnp.where(r1 == k, values[k], out)
        return out.astype(jnp.float32)

    kinds = [
        peak,
        total,
        by_row([block_of[k][0] for k in range(ROWS_DEV)], -1),
        by_row([block_of[k][1] for k in range(ROWS_DEV)], -1),
        by_row([lens[k] for k in range(ROWS_DEV)], 0),
    ]
    span = lq * GROUP_ROWS
    spread = [jnp.where(lane == at_row % span, kind, 0.0) for kind in kinds]
    for t in range(n):
        lines = [jnp.sum(kind[t * span : (t + 1) * span], axis=0, keepdims=True) for kind in spread]
        lines.append(jnp.zeros((8 - len(lines), HD), jnp.float32))
        stats[t] = jnp.concatenate(lines, axis=0)
    for d in range(n):
        outs[d][...] = stats[lax.rem(me + d, n)]


def decode_scores(counts, done, placed, table, lens, cache, msgs, lq):
    n = len(msgs)
    rows = QH * GROUP_ROWS
    smem, vmem = pl.BlockSpec(memory_space=SMEM), pl.BlockSpec(memory_space=VMEM)
    out = pl.pallas_call(
        functools.partial(owner_scores, n, lq),
        in_specs=[smem] * 5 + [vmem] * (n + 1),
        out_specs=[vmem] * (n + 2),
        out_shape=[
            jax.ShapeDtypeStruct((rows, DEVICE_SLOTS * BLOCK_TOKENS), jnp.float32),
            jax.ShapeDtypeStruct((rows, HD), jnp.float32),
        ]
        + [jax.ShapeDtypeStruct((8, HD), jnp.float32)] * n,
        scratch_shapes=[
            SMEM((DEVICE_SLOTS,), jnp.int32),
            SMEM((DEVICE_SLOTS,), jnp.int32),
            VMEM((n * GROUP_ROWS, msgs[0].shape[1]), jnp.float32),
            VMEM((n, 8, HD), jnp.float32),
        ],
        compiler_params=pltpu.CompilerParams(vmem_limit_bytes=32 * MIB),
        cost_estimate=pl.CostEstimate(flops=2 * rows * HD * 768, bytes_accessed=4 * MIB, transcendentals=rows * 768),
        name="decode_scores",
    )(counts, done, placed, table, lens, cache, *msgs)
    return out[0], out[1], out[2:]


def handed_part(n, lq, kv_ref, q_ref, *refs):
    msgs = refs[:n]
    outs = refs[n : 2 * n]
    stats, held = refs[2 * n :]
    me = lax.axis_index("tp")
    for d in range(n):
        stats[lax.rem(me + n - d, n)] = msgs[d][...]
    rows = lq * n * GROUP_ROWS
    shape = (rows, HD)
    at_row, lane = iota(shape, 0), iota(shape, 1)
    head, rs = at_row // (n * GROUP_ROWS), at_row % GROUP_ROWS
    mine = lane == head * GROUP_ROWS + rs

    def column(kind):
        lines = [jnp.broadcast_to(stats[u, kind : kind + 1, :], (GROUP_ROWS, HD)) for u in range(n)] * lq
        return jnp.sum(jnp.where(mine, jnp.concatenate(lines, axis=0), 0.0), axis=1, keepdims=True)

    peak, total, first_block, second_block, length = [column(kind) for kind in range(5)]
    scores = dot_t(q_ref[...], kv_ref[:, :HD]) * SCALE
    lane_f = lane.astype(jnp.float32)
    parts = []
    for b in range(NBLK):
        limit = jnp.where(
            first_block == b, length, jnp.where(second_block == b, length - BLOCK_TOKENS, 0.0)
        )
        part = scores[:, b * BLOCK_TOKENS : (b + 1) * BLOCK_TOKENS]
        parts.append(jnp.where(lane_f < limit, part, MASKED))
    scores = jnp.concatenate(parts, axis=1)
    top = jnp.maximum(peak, jnp.max(scores, axis=1, keepdims=True))
    raised = jnp.exp(scores - top)
    total = total * jnp.exp(peak - top) + jnp.sum(raised, axis=1, keepdims=True)
    weights = (raised * (1.0 / total)).astype(jnp.bfloat16)
    mixed = dot(weights, kv_ref[:, HD:]).reshape(lq * n, GROUP_ROWS, HD)

    def line(col):
        spread = jnp.where(lane == rs, col, 0.0).reshape(lq * n, GROUP_ROWS, HD)
        return jnp.sum(spread, axis=1, keepdims=True)

    rs3 = rs.reshape(lq * n, GROUP_ROWS, HD)
    mixed = jnp.where(rs3 == 6, line(top), jnp.where(rs3 == 7, line(total), mixed))
    held[...] = mixed.reshape(lq, n, GROUP_ROWS, HD)
    for d in range(n):
        to = lax.rem(me + d, n)
        for h in range(lq):
            outs[d][h * GROUP_ROWS : (h + 1) * GROUP_ROWS, :] = held[h, to]


def handed_attention(kv, q_other, msgs, lq):
    n = len(msgs)
    rows = lq * n * GROUP_ROWS
    vmem = pl.BlockSpec(memory_space=VMEM)
    return pl.pallas_call(
        functools.partial(handed_part, n, lq),
        in_specs=[vmem] * (n + 2),
        out_specs=[vmem] * n,
        out_shape=[jax.ShapeDtypeStruct((lq * GROUP_ROWS, HD), jnp.float32)] * n,
        scratch_shapes=[VMEM((n, 8, HD), jnp.float32), VMEM((lq, n, GROUP_ROWS, HD), jnp.float32)],
        compiler_params=pltpu.CompilerParams(vmem_limit_bytes=32 * MIB),
        cost_estimate=pl.CostEstimate(flops=4 * rows * HD * PTOK, bytes_accessed=2 * MIB, transcendentals=rows * PTOK),
        name="handed_attention",
    )(kv, q_other, *msgs)


def owner_mix(n, lq, scores_ref, fresh_ref, cache, *refs):
    msgs, parts = refs[:n], refs[n : 2 * n]
    o_ref, held, handed = refs[2 * n :]
    me = lax.axis_index("tp")
    for d in range(n):
        source = lax.rem(me + n - d, n)
        held[pl.ds(pl.multiple_of(source * GROUP_ROWS, GROUP_ROWS), GROUP_ROWS), :] = msgs[d][...]
        handed[source] = parts[d][...]
    groups = QH
    rows = groups * GROUP_ROWS
    mixed = handed[...].reshape(groups, GROUP_ROWS, HD)
    shape = (groups, GROUP_ROWS, HD)
    mine = iota(shape, 1) == iota(shape, 2)

    def column(at):
        line = jnp.broadcast_to(mixed[:, at : at + 1, :], shape)
        return jnp.sum(jnp.where(mine, line, 0.0), axis=2, keepdims=True).reshape(rows, 1)

    peak, inverse = column(6), 1.0 / column(7)
    weights = (jnp.exp(scores_ref[...] - peak) * inverse).astype(jnp.bfloat16)
    fresh = (jnp.exp(fresh_ref[...] - peak) * inverse).astype(jnp.bfloat16).astype(jnp.float32)
    mixed = mixed.reshape(rows, HD)
    span = GQ * GROUP_ROWS
    out = []
    for h in range(KVH):
        part = slice(h * span, (h + 1) * span)
        own = mixed[part] + dot(weights[part], cache[:, (2 * h + 1) * HD : (2 * h + 2) * HD])
        t, _ = row_head(n, lq, h, 0)
        value = held[t * GROUP_ROWS : (t + 1) * GROUP_ROWS, lq * HD + HD : lq * HD + 2 * HD]
        earlier = pltpu.roll(value, ROWS_DEV, 0)
        for hh in range(GQ):
            at = h * span + hh * GROUP_ROWS
            some = slice(at, at + GROUP_ROWS)
            line = own[hh * GROUP_ROWS : (hh + 1) * GROUP_ROWS]
            out.append(line + fresh[some, 0:1] * value + fresh[some, 1:2] * earlier)
    out = jnp.concatenate(out, axis=1)
    for s in range(STEPS):
        o_ref[s] = out[s * ROWS_DEV : (s + 1) * ROWS_DEV].astype(jnp.bfloat16)


def decode_mix(scores, fresh, cache, msgs, parts, lq):
    n = len(msgs)
    vmem = pl.BlockSpec(memory_space=VMEM)
    return pl.pallas_call(
        functools.partial(owner_mix, n, lq),
        in_specs=[vmem] * (2 * n + 3),
        out_specs=vmem,
        out_shape=jax.ShapeDtypeStruct((STEPS, ROWS_DEV, QH * HD), jnp.bfloat16),
        scratch_shapes=[
            VMEM((n * GROUP_ROWS, msgs[0].shape[1]), jnp.float32),
            VMEM((n, lq * GROUP_ROWS, HD), jnp.float32),
        ],
        compiler_params=pltpu.CompilerParams(vmem_limit_bytes=32 * MIB),
        cost_estimate=pl.CostEstimate(flops=2 * 256 * HD * 768, bytes_accessed=4 * MIB, transcendentals=256 * 768),
        name="decode_mix",
    )(scores, fresh, cache, *msgs, *parts)


def along_tp(msgs):
    n = len(msgs)
    return [msgs[0]] + [
        lax.ppermute(msgs[d], "tp", [(i, (i + d) % n) for i in range(n)]) for d in range(1, n)
    ]


def to_other_group(msgs):
    n = len(msgs)
    return [
        lax.ppermute(
            msgs[d],
            ("pool", "tp"),
            [(g * n + i, (1 - g) * n + (i + d) % n) for g in range(2) for i in range(n)],
        )
        for d in range(n)
    ]


def local(
    prompt_x,
    q_weight,
    kv_weight,
    prompt_blocks,
    finished,
    placement,
    page_table,
    row_lens,
    kv_cache,
    decode_x,
):
    n = lax.axis_size("tp")
    lq = q_weight.shape[1] // HD
    share = GQ // lq
    if share > 1:
        sets = [[k * share + i for i in range(share)] for k in range(n // share)]
        kv_weight = lax.all_gather(kv_weight, "tp", axis=1, tiled=True, axis_index_groups=sets)
    cache = kv_cache.reshape(-1, kv_cache.shape[2])
    dx = decode_x.reshape(-1, decode_x.shape[2])
    block = 256
    q, kv, q_own, *msgs = project_rows(prompt_x, q_weight, kv_weight, 0, 2 * block, block, dx=dx, n=n)
    q_other = lax.ppermute(q_own, "pool", [(0, 1), (1, 0)])
    msgs = along_tp(msgs)
    q, kv = project_rows(prompt_x, q_weight, kv_weight, 2 * block, 3 * block, block, held=(q, kv))
    scores, fresh, stats = decode_scores(
        prompt_blocks, finished, placement, page_table, row_lens, cache, msgs, lq
    )
    stats = to_other_group(stats)
    q, kv = project_rows(prompt_x, q_weight, kv_weight, 5 * block, 3 * block, block, held=(q, kv))
    parts = to_other_group(handed_attention(kv, q_other, stats, lq))
    prompt_attn = prompt_attention(prompt_blocks, q, kv)
    decode_attn = decode_mix(scores, fresh, cache, msgs, parts, lq)
    return prompt_attn, decode_attn


def solution(mesh):
    return jax.shard_map(
        local,
        mesh=mesh,
        in_specs=(
            P(("rep", "pool"), None),
            P(None, "tp"),
            P(None, "tp"),
            P("rep", None),
            P("rep", None),
            P("rep", None, None),
            P(("rep", "pool", "tp"), None),
            P(("rep", "pool", "tp")),
            P(("rep", "pool", "tp"), None, None),
            P(None, ("rep", "pool"), None),
        ),
        out_specs=(P(("rep", "pool"), "tp"), P(None, ("rep", "pool", "tp"), None)),
        check_vma=False,
    )
```

time: 262 us -> 114 us (0.44)
  matrix products: 92 us -> 0 us
  waiting for transfers between devices: 84.6 us -> 2.52 us
  Pallas kernels: 0 us -> 59.2 us
  local copies, waits for them, and re-layouts: 41.8 us -> 15.6 us
  starting transfers between devices: 16.9 us -> 34.5 us
  between operations: 14.4 us -> 0.85 us
  other arithmetic: 11.2 us -> 0 us
    all_gather x1 -> x0, waiting for transfers between devices: 77.2 us -> none  [local(): kv_whole = lax.all_gather(kv_local, 'tp', axis=1, tiled=True)]
    dot_general x11 -> x0, matrix products: 60.8 us -> none  [the longest x1 22.3 us: local(): jnp.einsum('hij,jd->ihd', weights, head_kv[:, 1], preferred_element_type=...]
    pallas_call x0 -> x7, Pallas kernels: none -> 59.2 us  [the longest x3 29 us: project_rows(): pl.pallas_call(functools.partial(project, first, n, lq), grid=(count // b...]
    ppermute x1 -> x24, starting transfers between devices: 0.01 us -> 34.5 us  [the longest x16 20.8 us: to_other_group(): lax.ppermute(msgs[d], ('pool', 'tp'), [(g * n + i, (1 - g) * n + (i + d)...]
    sub x1 -> x0, matrix products: 31.3 us -> none  [local(): raised = jnp.exp(scores - row_peak)]
    reshape x9 -> x0, local copies, waits for them, and re-layouts: 21.1 us -> none  [the longest x1 14.3 us: local(): kv_split = kv_whole.reshape(PTOK, KVH, 2, HD)]
    all_to_all x3 -> x0, starting transfers between devices: 16.8 us -> none  [the longest x1 7.28 us: local(): lax.all_to_all(decode_kv, 'tp', split_axis=1, concat_axis=3, tiled=True)]
    unnamed x23 -> x35, local copies, waits for them, and re-layouts: 7.08 us -> 15.6 us
  transfers between devices with their start and end apart: 5 -> 24, of which waited for: 2 -> 3; matrix products, arithmetic and copies ran while one was open for 40% -> 0% of each run, Pallas kernels for 0% -> 43%
where the time goes in v1:
time: 114 us; the launch traced here: 113 us
  Pallas kernels  59.2 us (52%)
  starting transfers between devices  34.5 us (30%)
  local copies, waits for them, and re-layouts  15.6 us (14%)
  waiting for transfers between devices  2.52 us (2%)
    pallas_call x3, Pallas kernels, project_rows(): pl.pallas_call(functools.partial(project, first, n, lq), grid=(count // b...  29 us
    pallas_call x1, Pallas kernels, prompt_attention(): pl.pallas_call(functools.partial(attend_prompt, cq // HD), grid=(rows //...  26 us
    ppermute x16, starting transfers between devices, to_other_group(): lax.ppermute(msgs[d], ('pool', 'tp'), [(g * n + i, (1 - g) * n + (i + d)...  20.8 us
    unnamed x35, local copies, waits for them, and re-layouts  15.6 us
    ppermute x7, starting transfers between devices, along_tp(): lax.ppermute(msgs[d], 'tp', [(i, (i + d) % n) for i in range(n)])  13.7 us
  transfers between devices with their start and end apart: 24, of which 3 were waited for; matrix products, arithmetic and copies ran while one was open for 0% of the time, Pallas kernels for 43%

profile of v1, /device:TPU:0, one launch (start us, length us, event | category | flops | bytes accessed | tf_op | source)
XLA Modules:
  0.0 112.7 jit_solution(3889020456350906242)
XLA Ops:
  0.6 0.0 copy-start
  0.6 2.5 %copy-done = bf16[5120,512]{1,0:T(8,128)(2,1)S(1)} copy-done((bf16[5120,512]{1,0:T(8,128)(2,1)S(1)}, bf16[5120,512]{1,0:T(8,128)(2,1)}, u32[]{:S(2)}) %copy-start) | copy-done | bytes 5242904
  3.1 1.7 %copy-done.2 = bf16[5120,256]{1,0:T(8,128)(2,1)S(1)} copy-done((bf16[5120,256]{1,0:T(8,128)(2,1)S(1)}, bf16[5120,256]{1,0:T(8,128)(2,1)}, u32[]{:S(2)}) %copy-start.2) | copy-done | bytes 2621464
  4.9 1.0 copy-done.10
  5.9 8.7 %project_first.1 = (bf16[2048,512]{1,0:T(8,128)(2,1)S(1)}, bf16[2048,256]{1,0:T(8,128)(2,1)S(1)}, bf16[256,128]{1,0:T(8,128)(2,1)S(1)}, f32[8,768]{1,0:T(8,128)S...) custom-call(bf16[48,5120]{1,0:T(8,128)(2,1)S(1)} %bitcast.4, ...), custom_call_target="tpu_custom_call" | custom-call | flops 4026531840 | bytes 13893632 | tf_op jit(solution)/shard_map/project_first/pallas_call | solution.py:148
  14.6 1.0 copy-done.6
  15.6 1.3 %copy-done.8 = bf16[2048,512]{1,0:T(8,128)(2,1)} copy-done((bf16[2048,512]{1,0:T(8,128)(2,1)}, bf16[2048,512]{1,0:T(8,128)(2,1)S(1)}, u32[]{:S(2)}) %copy-start.8) | copy-done | bytes 2097176
  16.9 3.0 %collective-permute-start = (f32[8,768]{1,0:T(8,128)S(1)}, f32[8,768]{1,0:T(8,128)S(1)}, u32[]{:S(2)}, u32[]{:S(2)}) collective-permute-start(f32[8,768]{1,0:T(8,128)S(1)} %get-tuple-element.42), channel_id=1, source_target_pairs={{0,1},{1,2},{2,3},{3,4},{4,5},{5,6},{6,7},{7,0},{8,9},{9,10},{10,1... | collective-permute-start | bytes 73736 | tf_op jit(solution)/shard_map/ppermute | solution.py:457
  19.9 1.6 %collective-permute-start.1 = (f32[8,768]{1,0:T(8,128)S(1)}, f32[8,768]{1,0:T(8,128)S(1)}, u32[]{:S(2)}, u32[]{:S(2)}) collective-permute-start(f32[8,768]{1,0:T(8,128)S(1)} %get-tuple-element.43), channel_id=1, source_target_pairs={{0,2},{1,3},{2,4},{3,5},{4,6},{5,7},{6,0},{7,1},{8,10},{9,11},{10,... | collective-permute-start | bytes 73736 | tf_op jit(solution)/shard_map/ppermute | solution.py:457
  21.4 2.5 %collective-permute-start.2 = (f32[8,768]{1,0:T(8,128)S(1)}, f32[8,768]{1,0:T(8,128)S(1)}, u32[]{:S(2)}, u32[]{:S(2)}) collective-permute-start(f32[8,768]{1,0:T(8,128)S(1)} %get-tuple-element.44), channel_id=1, source_target_pairs={{0,3},{1,4},{2,5},{3,6},{4,7},{5,0},{6,1},{7,2},{8,11},{9,12},{10,... | collective-permute-start | bytes 73736 | tf_op jit(solution)/shard_map/ppermute | solution.py:457
  24.0 1.2 %collective-permute-start.3 = (f32[8,768]{1,0:T(8,128)S(1)}, f32[8,768]{1,0:T(8,128)S(1)}, u32[]{:S(2)}, u32[]{:S(2)}) collective-permute-start(f32[8,768]{1,0:T(8,128)S(1)} %get-tuple-element.45), channel_id=1, source_target_pairs={{0,4},{1,5},{2,6},{3,7},{4,0},{5,1},{6,2},{7,3},{8,12},{9,13},{10,... | collective-permute-start | bytes 73736 | tf_op jit(solution)/shard_map/ppermute | solution.py:457
  25.2 2.6 %collective-permute-start.4 = (f32[8,768]{1,0:T(8,128)S(1)}, f32[8,768]{1,0:T(8,128)S(1)}, u32[]{:S(2)}, u32[]{:S(2)}) collective-permute-start(f32[8,768]{1,0:T(8,128)S(1)} %get-tuple-element.46), channel_id=1, source_target_pairs={{0,5},{1,6},{2,7},{3,0},{4,1},{5,2},{6,3},{7,4},{8,13},{9,14},{10,... | collective-permute-start | bytes 73736 | tf_op jit(solution)/shard_map/ppermute | solution.py:457
  27.9 0.0 collective-permute-done.refs_1_
  27.9 1.3 %collective-permute-start.5 = (f32[8,768]{1,0:T(8,128)S(1)}, f32[8,768]{1,0:T(8,128)S(1)}, u32[]{:S(2)}, u32[]{:S(2)}) collective-permute-start(f32[8,768]{1,0:T(8,128)S(1)} %get-tuple-element.47), channel_id=1, source_target_pairs={{0,6},{1,7},{2,0},{3,1},{4,2},{5,3},{6,4},{7,5},{8,14},{9,15},{10,... | collective-permute-start | bytes 73736 | tf_op jit(solution)/shard_map/ppermute | solution.py:457
  29.2 0.0 collective-permute-done.1.refs_2_
  29.2 1.4 %collective-permute-start.6 = (f32[8,768]{1,0:T(8,128)S(1)}, f32[8,768]{1,0:T(8,128)S(1)}, u32[]{:S(2)}, u32[]{:S(2)}) collective-permute-start(f32[8,768]{1,0:T(8,128)S(1)} %get-tuple-element.48), channel_id=1, source_target_pairs={{0,7},{1,0},{2,1},{3,2},{4,3},{5,4},{6,5},{7,6},{8,15},{9,8},{10,9... | collective-permute-start | bytes 73736 | tf_op jit(solution)/shard_map/ppermute | solution.py:457
  30.6 0.1 copy.16.placed
  30.7 0.1 copy.17.table
  30.8 0.0 collective-permute-done.2.refs_3_
  30.8 0.0 collective-permute-start.7
  30.8 0.0 collective-permute-done.3.refs_4_
  30.8 0.0 collective-permute-done.4.refs_5_
  30.8 0.9 collective-permute-done.5.refs_6_
  31.7 1.4 %collective-permute-done.6.refs_7_ = f32[8,768]{1,0:T(8,128)S(1)} collective-permute-done((f32[8,768]{1,0:T(8,128)S(1)}, f32[8,768]{1,0:T(8,128)S(1)}, u32[]{:S(2)}, u32[]{:S(2)}) %collective-permute-start.6) | collective-permute-done | bytes 24608 | tf_op jit(solution)/shard_map/ppermute | solution.py:457
  33.1 0.0 copy-start.4
  33.1 1.9 %copy-done.4 = bf16[6,128,2048]{2,1,0:T(8,128)(2,1)S(1)} copy-done((bf16[6,128,2048]{2,1,0:T(8,128)(2,1)S(1)}, bf16[6,128,2048]{2,1,0:T(8,128)(2,1)}, u32[]{:S(2)}) %copy-start.4) | copy-done | bytes 3145752
  35.0 1.9 %decode_scores.1 = (f32[256,768]{1,0:T(8,128)S(1)}, f32[256,128]{1,0:T(8,128)S(1)}, f32[8,128]{1,0:T(8,128)S(1)}, f32[8,128]{1,0:T(8,128)S(1)}, f32[8,128]{1,0:T...) custom-call(s32[2,3]{1,0:T(2,128)S(1)} %copy-done.12, ...), custom_call_target="tpu_custom_call" | custom-call | flops 50331648 | bytes 4194304 | tf_op jit(solution)/shard_map/decode_scores/pallas_call | solution.py:311
  36.8 0.1 collective-permute-start.8
  36.9 1.6 %collective-permute-start.9 = (f32[8,128]{1,0:T(8,128)S(1)}, f32[8,128]{1,0:T(8,128)S(1)}, u32[]{:S(2)}, u32[]{:S(2)}) collective-permute-start(f32[8,128]{1,0:T(8,128)S(1)} %get-tuple-element.53), channel_id=1, source_target_pairs={{0,9},{1,10},{2,11},{3,12},{4,13},{5,14},{6,15},{7,8},{8,1},{9,2},... | collective-permute-start | bytes 12296 | tf_op jit(solution)/shard_map/ppermute | solution.py:464
  38.5 0.0 collective-permute-start.10
  38.5 2.0 %collective-permute-start.11 = (f32[8,128]{1,0:T(8,128)S(1)}, f32[8,128]{1,0:T(8,128)S(1)}, u32[]{:S(2)}, u32[]{:S(2)}) collective-permute-start(f32[8,128]{1,0:T(8,128)S(1)} %get-tuple-element.55), channel_id=1, source_target_pairs={{0,11},{1,12},{2,13},{3,14},{4,15},{5,8},{6,9},{7,10},{8,3},{9,4},... | collective-permute-start | bytes 12296 | tf_op jit(solution)/shard_map/ppermute | solution.py:464
  40.6 2.5 %copy-done.1 = bf16[5120,512]{1,0:T(8,128)(2,1)S(1)} copy-done((bf16[5120,512]{1,0:T(8,128)(2,1)S(1)}, bf16[5120,512]{1,0:T(8,128)(2,1)}, u32[]{:S(2)}) %copy-start.1) | copy-done | bytes 5242904
  43.1 1.2 %copy-done.7 = bf16[2048,256]{1,0:T(8,128)(2,1)S(1)} copy-done((bf16[2048,256]{1,0:T(8,128)(2,1)S(1)}, bf16[2048,256]{1,0:T(8,128)(2,1)}, u32[]{:S(2)}) %copy-start.7) | copy-done | bytes 1048600
  44.3 1.6 %copy-done.9 = bf16[2048,512]{1,0:T(8,128)(2,1)S(1)} copy-done((bf16[2048,512]{1,0:T(8,128)(2,1)S(1)}, bf16[2048,512]{1,0:T(8,128)(2,1)}, u32[]{:S(2)}) %copy-start.9) | copy-done | bytes 2097176
  45.9 10.2 %project.2 = (bf16[2048,512]{1,0:T(8,128)(2,1)S(1)}, bf16[2048,256]{1,0:T(8,128)(2,1)S(1)}) custom-call(bf16[2048,5120]{1,0:T(8,128)(2,1)} %refs_0_.3, bf16[5120,512]{1,0:T(8,128)(2,1)S(1)} %copy-done.1, bf16[5120,256]{1,0:T(8,128)(2,1)S(1)} %copy-done.3, bf16[2048,512]{1,0:T(8,128)(2,1)S(1)} %copy-done.9, ...), custom_call_target="tpu_custom_call", output_to_operand_aliasing={{0}: (3, {}), {1}: (4, {})} | custom-call | flops 6039797760 | bytes 16908288 | tf_op jit(solution)/shard_map/project/pallas_call | solution.py:148
  56.1 0.0 collective-permute-done.8.refs_0_
  56.1 1.9 %collective-permute-start.12 = (f32[8,128]{1,0:T(8,128)S(1)}, f32[8,128]{1,0:T(8,128)S(1)}, u32[]{:S(2)}, u32[]{:S(2)}) collective-permute-start(f32[8,128]{1,0:T(8,128)S(1)} %get-tuple-element.56), channel_id=1, source_target_pairs={{0,12},{1,13},{2,14},{3,15},{4,8},{5,9},{6,10},{7,11},{8,4},{9,5},... | collective-permute-start | bytes 12296 | tf_op jit(solution)/shard_map/ppermute | solution.py:464
  57.9 0.0 collective-permute-done.9.refs_1_
  57.9 3.1 %collective-permute-start.13 = (f32[8,128]{1,0:T(8,128)S(1)}, f32[8,128]{1,0:T(8,128)S(1)}, u32[]{:S(2)}, u32[]{:S(2)}) collective-permute-start(f32[8,128]{1,0:T(8,128)S(1)} %get-tuple-element.57), channel_id=1, source_target_pairs={{0,13},{1,14},{2,15},{3,8},{4,9},{5,10},{6,11},{7,12},{8,5},{9,6},... | collective-permute-start | bytes 12296 | tf_op jit(solution)/shard_map/ppermute | solution.py:464
  61.1 0.0 collective-permute-done.10.refs_2_
  61.1 0.2 collective-permute-start.14
  61.3 0.0 collective-permute-done.11.refs_3_
  61.3 1.0 collective-permute-start.15
  62.3 10.2 %project.3 = (bf16[2048,512]{1,0:T(8,128)(2,1)S(1)}, bf16[2048,256]{1,0:T(8,128)(2,1)S(1)}) custom-call(bf16[2048,5120]{1,0:T(8,128)(2,1)} %refs_0_.3, bf16[5120,512]{1,0:T(8,128)(2,1)S(1)} %copy-done.1, bf16[5120,256]{1,0:T(8,128)(2,1)S(1)} %copy-done.3, ...), custom_call_target="tpu_custom_call", output_to_operand_aliasing={{0}: (3, {}), {1}: (4, {})} | custom-call | flops 6039797760 | bytes 16908288 | tf_op jit(solution)/shard_map/project/pallas_call | solution.py:148
  72.5 0.0 collective-permute-done.12.refs_4_
  72.5 0.0 collective-permute-done.13.refs_5_
  72.5 0.0 collective-permute-done.14.refs_6_
  72.5 0.0 collective-permute-done.7.q_ref
  72.5 1.6 %handed_attention.1 = (f32[32,128]{1,0:T(8,128)S(1)}, f32[32,128]{1,0:T(8,128)S(1)}, f32[32,128]{1,0:T(8,128)S(1)}, f32[32,128]{1,0:T(8,128)S(1)}, f32[32,128]{1...) custom-call(bf16[2048,256]{1,0:T(8,128)(2,1)S(1)} %get-tuple-element.40.kv_ref, ...), custom_call_target="tpu_custom_call" | custom-call | flops 268435456 | bytes 2097152 | tf_op jit(solution)/shard_map/handed_attention/pallas_call | solution.py:384
  74.1 0.5 collective-permute-start.16
  74.6 0.4 collective-permute-start.17
  75.0 1.5 %collective-permute-start.18 = (f32[32,128]{1,0:T(8,128)S(1)}, f32[32,128]{1,0:T(8,128)S(1)}, u32[]{:S(2)}, u32[]{:S(2)}) collective-permute-start(f32[32,128]{1,0:T(8,128)S(1)} %get-tuple-element.62), channel_id=1, source_target_pairs={{0,10},{1,11},{2,12},{3,13},{4,14},{5,15},{6,8},{7,9},{8,2},{9,3},... | collective-permute-start | bytes 49160 | tf_op jit(solution)/shard_map/ppermute | solution.py:464
  76.5 1.0 collective-permute-start.19
  77.5 2.6 %collective-permute-start.20 = (f32[32,128]{1,0:T(8,128)S(1)}, f32[32,128]{1,0:T(8,128)S(1)}, u32[]{:S(2)}, u32[]{:S(2)}) collective-permute-start(f32[32,128]{1,0:T(8,128)S(1)} %get-tuple-element.64), channel_id=1, source_target_pairs={{0,12},{1,13},{2,14},{3,15},{4,8},{5,9},{6,10},{7,11},{8,4},{9,5},... | collective-permute-start | bytes 49160 | tf_op jit(solution)/shard_map/ppermute | solution.py:464
  80.1 0.1 collective-permute-start.21
  80.2 0.3 collective-permute-done.17.refs_9_
  80.5 2.4 %collective-permute-start.22 = (f32[32,128]{1,0:T(8,128)S(1)}, f32[32,128]{1,0:T(8,128)S(1)}, u32[]{:S(2)}, u32[]{:S(2)}) collective-permute-start(f32[32,128]{1,0:T(8,128)S(1)} %get-tuple-element.66), channel_id=1, source_target_pairs={{0,14},{1,15},{2,8},{3,9},{4,10},{5,11},{6,12},{7,13},{8,6},{9,7},... | collective-permute-start | bytes 49160 | tf_op jit(solution)/shard_map/ppermute | solution.py:464
  82.9 0.0 collective-permute-done.18.refs_10_
  82.9 2.3 %collective-permute-start.23 = (f32[32,128]{1,0:T(8,128)S(1)}, f32[32,128]{1,0:T(8,128)S(1)}, u32[]{:S(2)}, u32[]{:S(2)}) collective-permute-start(f32[32,128]{1,0:T(8,128)S(1)} %get-tuple-element.67), channel_id=1, source_target_pairs={{0,15},{1,8},{2,9},{3,10},{4,11},{5,12},{6,13},{7,14},{8,7},{9,0},... | collective-permute-start | bytes 49160 | tf_op jit(solution)/shard_map/ppermute | solution.py:464
  85.2 26.0 %prompt_attention.1 = bf16[2048,512]{1,0:T(8,128)(2,1)} custom-call(s32[2,3]{1,0:T(2,128)S(1)} %copy-done.12, bf16[2048,512]{1,0:T(8,128)(2,1)S(1)} %get-tuple-element.39.q_ref, bf16[2048,256]{1,0:T(8,128)(2,1)S(1)} %get-tuple-element.40.kv_ref), custom_call_target="tpu_custom_call" | custom-call | flops 8589934592 | bytes 8388608 | tf_op jit(solution)/shard_map/prompt_attention/pallas_call | solution.py:198
  111.3 0.0 collective-permute-done.22.refs_14_
  111.3 0.0 collective-permute-done.23.refs_15_
  111.3 0.7 decode_mix.1
  112.0 0.7 copy.18
  (26 shorter events, 0.1 us)
Async XLA Ops:
  0.6 2.5 %copy-start = (bf16[5120,512]{1,0:T(8,128)(2,1)S(1)}, bf16[5120,512]{1,0:T(8,128)(2,1)}, u32[]{:S(2)}) copy-start(bf16[5120,512]{1,0:T(8,128)(2,1)} %refs_1_.5) | copy-start | bytes 15728644
  3.1 1.7 %copy-start.2 = (bf16[5120,256]{1,0:T(8,128)(2,1)S(1)}, bf16[5120,256]{1,0:T(8,128)(2,1)}, u32[]{:S(2)}) copy-start(bf16[5120,256]{1,0:T(8,128)(2,1)} %refs_2_.5) | copy-start | bytes 7864324
  4.9 1.0 copy-start.10
  5.9 24.7 %copy-start.14 = (s32[2,16,2]{1,2,0:T(2,128)S(1)}, s32[2,16,2]{1,2,0:T(2,128)}, u32[]{:S(2)}) copy-start(s32[2,16,2]{1,2,0:T(2,128)} %param.15) | copy-start | bytes 772
  5.9 24.8 %copy-start.15 = (s32[3,2]{0,1:T(2,128)S(1)}, s32[3,2]{0,1:T(2,128)}, u32[]{:S(2)}) copy-start(s32[3,2]{0,1:T(2,128)} %param.16) | copy-start | bytes 76
  5.9 27.2 %copy-start.11 = (s32[2,3]{1,0:T(2,128)S(1)}, s32[2,3]{1,0:T(2,128)}, u32[]{:S(2)}) copy-start(s32[2,3]{1,0:T(2,128)} %done.1) | copy-start | bytes 76
  5.9 27.2 %copy-start.12 = (s32[2,3]{1,0:T(2,128)S(1)}, s32[2,3]{1,0:T(2,128)}, u32[]{:S(2)}) copy-start(s32[2,3]{1,0:T(2,128)} %counts.3) | copy-start | bytes 76
  5.9 27.2 %copy-start.13 = (s32[3]{0:T(128)S(1)}, s32[3]{0:T(128)}, u32[]{:S(2)}) copy-start(s32[3]{0:T(128)} %lens.1) | copy-start | bytes 40
  14.6 1.0 copy-start.6
  15.6 1.3 %copy-start.8 = (bf16[2048,512]{1,0:T(8,128)(2,1)}, bf16[2048,512]{1,0:T(8,128)(2,1)S(1)}, u32[]{:S(2)}) copy-start(bf16[2048,512]{1,0:T(8,128)(2,1)S(1)} %get-tuple-element.35.refs_3_) | copy-start | bytes 6291460
  16.9 23.7 %copy-start.3 = (bf16[5120,256]{1,0:T(8,128)(2,1)S(1)}, bf16[5120,256]{1,0:T(8,128)(2,1)}, u32[]{:S(2)}) copy-start(bf16[5120,256]{1,0:T(8,128)(2,1)} %refs_2_.5) | copy-start | bytes 7864324
  16.9 11.0 %collective-permute-start = (f32[8,768]{1,0:T(8,128)S(1)}, f32[8,768]{1,0:T(8,128)S(1)}, u32[]{:S(2)}, u32[]{:S(2)}) collective-permute-start(f32[8,768]{1,0:T(8,128)S(1)} %get-tuple-element.42), channel_id=1, source_target_pairs={{0,1},{1,2},{2,3},{3,4},{4,5},{5,6},{6,7},{7,0},{8,9},{9,10},{10,1... | collective-permute-start | bytes 73736 | tf_op jit(solution)/shard_map/ppermute | solution.py:457
  19.9 9.3 %collective-permute-start.1 = (f32[8,768]{1,0:T(8,128)S(1)}, f32[8,768]{1,0:T(8,128)S(1)}, u32[]{:S(2)}, u32[]{:S(2)}) collective-permute-start(f32[8,768]{1,0:T(8,128)S(1)} %get-tuple-element.43), channel_id=1, source_target_pairs={{0,2},{1,3},{2,4},{3,5},{4,6},{5,7},{6,0},{7,1},{8,10},{9,11},{10,... | collective-permute-start | bytes 73736 | tf_op jit(solution)/shard_map/ppermute | solution.py:457
  21.4 9.4 %collective-permute-start.2 = (f32[8,768]{1,0:T(8,128)S(1)}, f32[8,768]{1,0:T(8,128)S(1)}, u32[]{:S(2)}, u32[]{:S(2)}) collective-permute-start(f32[8,768]{1,0:T(8,128)S(1)} %get-tuple-element.44), channel_id=1, source_target_pairs={{0,3},{1,4},{2,5},{3,6},{4,7},{5,0},{6,1},{7,2},{8,11},{9,12},{10,... | collective-permute-start | bytes 73736 | tf_op jit(solution)/shard_map/ppermute | solution.py:457
  24.0 6.8 %collective-permute-start.3 = (f32[8,768]{1,0:T(8,128)S(1)}, f32[8,768]{1,0:T(8,128)S(1)}, u32[]{:S(2)}, u32[]{:S(2)}) collective-permute-start(f32[8,768]{1,0:T(8,128)S(1)} %get-tuple-element.45), channel_id=1, source_target_pairs={{0,4},{1,5},{2,6},{3,7},{4,0},{5,1},{6,2},{7,3},{8,12},{9,13},{10,... | collective-permute-start | bytes 73736 | tf_op jit(solution)/shard_map/ppermute | solution.py:457
  25.2 5.6 %collective-permute-start.4 = (f32[8,768]{1,0:T(8,128)S(1)}, f32[8,768]{1,0:T(8,128)S(1)}, u32[]{:S(2)}, u32[]{:S(2)}) collective-permute-start(f32[8,768]{1,0:T(8,128)S(1)} %get-tuple-element.46), channel_id=1, source_target_pairs={{0,5},{1,6},{2,7},{3,0},{4,1},{5,2},{6,3},{7,4},{8,13},{9,14},{10,... | collective-permute-start | bytes 73736 | tf_op jit(solution)/shard_map/ppermute | solution.py:457
  27.9 3.8 %collective-permute-start.5 = (f32[8,768]{1,0:T(8,128)S(1)}, f32[8,768]{1,0:T(8,128)S(1)}, u32[]{:S(2)}, u32[]{:S(2)}) collective-permute-start(f32[8,768]{1,0:T(8,128)S(1)} %get-tuple-element.47), channel_id=1, source_target_pairs={{0,6},{1,7},{2,0},{3,1},{4,2},{5,3},{6,4},{7,5},{8,14},{9,15},{10,... | collective-permute-start | bytes 73736 | tf_op jit(solution)/shard_map/ppermute | solution.py:457
  29.2 3.8 %collective-permute-start.6 = (f32[8,768]{1,0:T(8,128)S(1)}, f32[8,768]{1,0:T(8,128)S(1)}, u32[]{:S(2)}, u32[]{:S(2)}) collective-permute-start(f32[8,768]{1,0:T(8,128)S(1)} %get-tuple-element.48), channel_id=1, source_target_pairs={{0,7},{1,0},{2,1},{3,2},{4,3},{5,4},{6,5},{7,6},{8,15},{9,8},{10,9... | collective-permute-start | bytes 73736 | tf_op jit(solution)/shard_map/ppermute | solution.py:457
  30.8 41.7 %collective-permute-start.7 = (bf16[256,128]{1,0:T(8,128)(2,1)S(1)}, bf16[256,128]{1,0:T(8,128)(2,1)S(1)}, u32[]{:S(2)}, u32[]{:S(2)}) collective-permute-start(bf16[256,128]{1,0:T(8,128)(2,1)S(1)} %get-tuple-element.51), channel_id=1, source_target_pairs={{0,8},{8,0},{1,9},{9,1},{2,10},{10,2},{3,11},{11,3},{4,12},{12,4},... | collective-permute-start | bytes 196616 | tf_op jit(solution)/shard_map/ppermute | solution.py:495
  33.1 1.9 %copy-start.4 = (bf16[6,128,2048]{2,1,0:T(8,128)(2,1)S(1)}, bf16[6,128,2048]{2,1,0:T(8,128)(2,1)}, u32[]{:S(2)}) copy-start(bf16[6,128,2048]{2,1,0:T(8,128)(2,1)} %param.18) | copy-start | bytes 9437188
  36.8 19.2 %collective-permute-start.8 = (f32[8,128]{1,0:T(8,128)S(1)}, f32[8,128]{1,0:T(8,128)S(1)}, u32[]{:S(2)}, u32[]{:S(2)}) collective-permute-start(f32[8,128]{1,0:T(8,128)S(1)} %get-tuple-element.52), channel_id=1, source_target_pairs={{0,8},{1,9},{2,10},{3,11},{4,12},{5,13},{6,14},{7,15},{8,0},{9,1},... | collective-permute-start | bytes 12296 | tf_op jit(solution)/shard_map/ppermute | solution.py:464
  36.9 21.0 %collective-permute-start.9 = (f32[8,128]{1,0:T(8,128)S(1)}, f32[8,128]{1,0:T(8,128)S(1)}, u32[]{:S(2)}, u32[]{:S(2)}) collective-permute-start(f32[8,128]{1,0:T(8,128)S(1)} %get-tuple-element.53), channel_id=1, source_target_pairs={{0,9},{1,10},{2,11},{3,12},{4,13},{5,14},{6,15},{7,8},{8,1},{9,2},... | collective-permute-start | bytes 12296 | tf_op jit(solution)/shard_map/ppermute | solution.py:464
  38.5 22.6 %collective-permute-start.10 = (f32[8,128]{1,0:T(8,128)S(1)}, f32[8,128]{1,0:T(8,128)S(1)}, u32[]{:S(2)}, u32[]{:S(2)}) collective-permute-start(f32[8,128]{1,0:T(8,128)S(1)} %get-tuple-element.54), channel_id=1, source_target_pairs={{0,10},{1,11},{2,12},{3,13},{4,14},{5,15},{6,8},{7,9},{8,2},{9,3},... | collective-permute-start | bytes 12296 | tf_op jit(solution)/shard_map/ppermute | solution.py:464
  38.5 22.7 %collective-permute-start.11 = (f32[8,128]{1,0:T(8,128)S(1)}, f32[8,128]{1,0:T(8,128)S(1)}, u32[]{:S(2)}, u32[]{:S(2)}) collective-permute-start(f32[8,128]{1,0:T(8,128)S(1)} %get-tuple-element.55), channel_id=1, source_target_pairs={{0,11},{1,12},{2,13},{3,14},{4,15},{5,8},{6,9},{7,10},{8,3},{9,4},... | collective-permute-start | bytes 12296 | tf_op jit(solution)/shard_map/ppermute | solution.py:464
  40.6 2.5 %copy-start.1 = (bf16[5120,512]{1,0:T(8,128)(2,1)S(1)}, bf16[5120,512]{1,0:T(8,128)(2,1)}, u32[]{:S(2)}) copy-start(bf16[5120,512]{1,0:T(8,128)(2,1)} %refs_1_.5) | copy-start | bytes 15728644
  43.1 1.2 %copy-start.7 = (bf16[2048,256]{1,0:T(8,128)(2,1)S(1)}, bf16[2048,256]{1,0:T(8,128)(2,1)}, u32[]{:S(2)}) copy-start(bf16[2048,256]{1,0:T(8,128)(2,1)} %copy-done.6) | copy-start | bytes 3145732
  44.3 1.6 %copy-start.9 = (bf16[2048,512]{1,0:T(8,128)(2,1)S(1)}, bf16[2048,512]{1,0:T(8,128)(2,1)}, u32[]{:S(2)}) copy-start(bf16[2048,512]{1,0:T(8,128)(2,1)} %copy-done.8) | copy-start | bytes 6291460
  56.1 16.4 %collective-permute-start.12 = (f32[8,128]{1,0:T(8,128)S(1)}, f32[8,128]{1,0:T(8,128)S(1)}, u32[]{:S(2)}, u32[]{:S(2)}) collective-permute-start(f32[8,128]{1,0:T(8,128)S(1)} %get-tuple-element.56), channel_id=1, source_target_pairs={{0,12},{1,13},{2,14},{3,15},{4,8},{5,9},{6,10},{7,11},{8,4},{9,5},... | collective-permute-start | bytes 12296 | tf_op jit(solution)/shard_map/ppermute | solution.py:464
  57.9 14.6 %collective-permute-start.13 = (f32[8,128]{1,0:T(8,128)S(1)}, f32[8,128]{1,0:T(8,128)S(1)}, u32[]{:S(2)}, u32[]{:S(2)}) collective-permute-start(f32[8,128]{1,0:T(8,128)S(1)} %get-tuple-element.57), channel_id=1, source_target_pairs={{0,13},{1,14},{2,15},{3,8},{4,9},{5,10},{6,11},{7,12},{8,5},{9,6},... | collective-permute-start | bytes 12296 | tf_op jit(solution)/shard_map/ppermute | solution.py:464
  61.1 11.4 %collective-permute-start.14 = (f32[8,128]{1,0:T(8,128)S(1)}, f32[8,128]{1,0:T(8,128)S(1)}, u32[]{:S(2)}, u32[]{:S(2)}) collective-permute-start(f32[8,128]{1,0:T(8,128)S(1)} %get-tuple-element.58), channel_id=1, source_target_pairs={{0,14},{1,15},{2,8},{3,9},{4,10},{5,11},{6,12},{7,13},{8,6},{9,7},... | collective-permute-start | bytes 12296 | tf_op jit(solution)/shard_map/ppermute | solution.py:464
  61.3 11.2 %collective-permute-start.15 = (f32[8,128]{1,0:T(8,128)S(1)}, f32[8,128]{1,0:T(8,128)S(1)}, u32[]{:S(2)}, u32[]{:S(2)}) collective-permute-start(f32[8,128]{1,0:T(8,128)S(1)} %get-tuple-element.59), channel_id=1, source_target_pairs={{0,15},{1,8},{2,9},{3,10},{4,11},{5,12},{6,13},{7,14},{8,7},{9,0},... | collective-permute-start | bytes 12296 | tf_op jit(solution)/shard_map/ppermute | solution.py:464
  74.1 6.0 %collective-permute-start.16 = (f32[32,128]{1,0:T(8,128)S(1)}, f32[32,128]{1,0:T(8,128)S(1)}, u32[]{:S(2)}, u32[]{:S(2)}) collective-permute-start(f32[32,128]{1,0:T(8,128)S(1)} %get-tuple-element.60), channel_id=1, source_target_pairs={{0,8},{1,9},{2,10},{3,11},{4,12},{5,13},{6,14},{7,15},{8,0},{9,1},... | collective-permute-start | bytes 49160 | tf_op jit(solution)/shard_map/ppermute | solution.py:464
  74.6 5.9 %collective-permute-start.17 = (f32[32,128]{1,0:T(8,128)S(1)}, f32[32,128]{1,0:T(8,128)S(1)}, u32[]{:S(2)}, u32[]{:S(2)}) collective-permute-start(f32[32,128]{1,0:T(8,128)S(1)} %get-tuple-element.61), channel_id=1, source_target_pairs={{0,9},{1,10},{2,11},{3,12},{4,13},{5,14},{6,15},{7,8},{8,1},{9,2},... | collective-permute-start | bytes 49160 | tf_op jit(solution)/shard_map/ppermute | solution.py:464
  75.0 7.8 %collective-permute-start.18 = (f32[32,128]{1,0:T(8,128)S(1)}, f32[32,128]{1,0:T(8,128)S(1)}, u32[]{:S(2)}, u32[]{:S(2)}) collective-permute-start(f32[32,128]{1,0:T(8,128)S(1)} %get-tuple-element.62), channel_id=1, source_target_pairs={{0,10},{1,11},{2,12},{3,13},{4,14},{5,15},{6,8},{7,9},{8,2},{9,3},... | collective-permute-start | bytes 49160 | tf_op jit(solution)/shard_map/ppermute | solution.py:464
  76.5 34.7 %collective-permute-start.19 = (f32[32,128]{1,0:T(8,128)S(1)}, f32[32,128]{1,0:T(8,128)S(1)}, u32[]{:S(2)}, u32[]{:S(2)}) collective-permute-start(f32[32,128]{1,0:T(8,128)S(1)} %get-tuple-element.63), channel_id=1, source_target_pairs={{0,11},{1,12},{2,13},{3,14},{4,15},{5,8},{6,9},{7,10},{8,3},{9,4},... | collective-permute-start | bytes 49160 | tf_op jit(solution)/shard_map/ppermute | solution.py:464
  77.5 33.8 %collective-permute-start.20 = (f32[32,128]{1,0:T(8,128)S(1)}, f32[32,128]{1,0:T(8,128)S(1)}, u32[]{:S(2)}, u32[]{:S(2)}) collective-permute-start(f32[32,128]{1,0:T(8,128)S(1)} %get-tuple-element.64), channel_id=1, source_target_pairs={{0,12},{1,13},{2,14},{3,15},{4,8},{5,9},{6,10},{7,11},{8,4},{9,5},... | collective-permute-start | bytes 49160 | tf_op jit(solution)/shard_map/ppermute | solution.py:464
  80.1 31.1 %collective-permute-start.21 = (f32[32,128]{1,0:T(8,128)S(1)}, f32[32,128]{1,0:T(8,128)S(1)}, u32[]{:S(2)}, u32[]{:S(2)}) collective-permute-start(f32[32,128]{1,0:T(8,128)S(1)} %get-tuple-element.65), channel_id=1, source_target_pairs={{0,13},{1,14},{2,15},{3,8},{4,9},{5,10},{6,11},{7,12},{8,5},{9,6},... | collective-permute-start | bytes 49160 | tf_op jit(solution)/shard_map/ppermute | solution.py:464
  80.5 30.8 %collective-permute-start.22 = (f32[32,128]{1,0:T(8,128)S(1)}, f32[32,128]{1,0:T(8,128)S(1)}, u32[]{:S(2)}, u32[]{:S(2)}) collective-permute-start(f32[32,128]{1,0:T(8,128)S(1)} %get-tuple-element.66), channel_id=1, source_target_pairs={{0,14},{1,15},{2,8},{3,9},{4,10},{5,11},{6,12},{7,13},{8,6},{9,7},... | collective-permute-start | bytes 49160 | tf_op jit(solution)/shard_map/ppermute | solution.py:464
  82.9 28.4 %collective-permute-start.23 = (f32[32,128]{1,0:T(8,128)S(1)}, f32[32,128]{1,0:T(8,128)S(1)}, u32[]{:S(2)}, u32[]{:S(2)}) collective-permute-start(f32[32,128]{1,0:T(8,128)S(1)} %get-tuple-element.67), channel_id=1, source_target_pairs={{0,15},{1,8},{2,9},{3,10},{4,11},{5,12},{6,13},{7,14},{8,7},{9,0},... | collective-permute-start | bytes 49160 | tf_op jit(solution)/shard_map/ppermute | solution.py:464
  85.2 26.1 %copy-start.5 = (bf16[6,128,2048]{2,1,0:T(8,128)(2,1)S(1)}, bf16[6,128,2048]{2,1,0:T(8,128)(2,1)}, u32[]{:S(2)}) copy-start(bf16[6,128,2048]{2,1,0:T(8,128)(2,1)} %param.18) | copy-start | bytes 9437188

commit v2 on v0

v2 whole, which is shorter than its diff:
```python
import functools

import jax
import jax.numpy as jnp
from jax import lax
from jax.experimental import pallas as pl
from jax.experimental.pallas import tpu as pltpu
from jax.sharding import PartitionSpec as P

QH = 32
KVH = 8
GQ = QH // KVH
HD = 128
BLOCK_TOKENS = 128
PTOK = 2048
NPROMPT = 3
MOST_BLOCKS = 8
PAGES = 2
STEPS = 2
NBLK = 16
DEVICE_SLOTS = 6
ROWS_DEV = 3
GROUP_ROWS = 8
KEY_VALUE_COLUMNS = 2048
SCALE = HD ** (-0.5)
MASKED = -1e30
PIECES = 5
MIB = 1 << 20
VMEM = pltpu.VMEM
SMEM = pltpu.SMEM


def dot(a, b):
    return jnp.dot(a, b, preferred_element_type=jnp.float32)


def dot_t(a, b):
    return lax.dot_general(a, b, (((1,), (1,)), ((), ())), preferred_element_type=jnp.float32)


def iota(shape, axis):
    return lax.broadcasted_iota(jnp.int32, shape, axis)


def row_of(rs):
    return jnp.where(rs >= 2 * ROWS_DEV, ROWS_DEV, jnp.where(rs >= ROWS_DEV, rs - ROWS_DEV, rs))


def block_of_pages(counts, done, placed, table):
    me = lax.axis_index("tp")
    other = 1 - lax.axis_index("pool")
    first_end = counts[other, 0]
    second_end = first_end + counts[other, 1]
    found = [[jnp.int32(-1)] * PAGES for _ in range(ROWS_DEV)]
    for b in range(NBLK):
        live = jnp.where(
            b < first_end, done[other, 0], jnp.where(b < second_end, done[other, 1], done[other, 2])
        )
        slot = jnp.where((live > 0) & (placed[other, b, 0] == me), placed[other, b, 1], -1)
        for r in range(ROWS_DEV):
            for p in range(PAGES):
                found[r][p] = jnp.where(slot == table[r, p], b, found[r][p])
    return found


def by_row(r, values, rest):
    out = jnp.full(r.shape, rest, jnp.int32)
    for k in range(ROWS_DEV):
        out = jnp.where(r == k, values[k], out)
    return out


def project(n, lq, blocks, with_q, with_kv, with_decode, *refs):
    refs = list(refs)
    if with_decode:
        counts, done, placed, table, lens, dx_ref = refs[:6]
        del refs[:6]
    x_hbm, wq_hbm = refs[:2]
    del refs[:2]
    wkv_hbm = refs.pop(0) if with_kv else None
    if not with_decode:
        refs.pop(0)
    q_hbm = refs.pop(0)
    kv_hbm = refs.pop(0) if with_kv else None
    if with_decode:
        qh_ref, msg_ref = refs[:2]
        del refs[:2]
    xs, w, q_out, kv_out, x_sems, w_sems, out_sems = refs
    size, depth = xs.shape[1:]
    cq = lq * HD
    piece = depth // PIECES

    def w_copies(c):
        part = pl.ds(c * piece, piece)
        copies = [pltpu.make_async_copy(wq_hbm.at[part], w.at[part, pl.ds(0, cq)], w_sems.at[0, c])]
        if with_kv:
            cols = pl.ds(cq, 2 * HD)
            copies.append(pltpu.make_async_copy(wkv_hbm.at[part], w.at[part, cols], w_sems.at[1, c]))
        return copies

    def x_piece(c):
        rows, cols = pl.ds(blocks[0] * size, size), pl.ds(c * piece, piece)
        return pltpu.make_async_copy(x_hbm.at[rows, cols], xs.at[0, :, cols], x_sems.at[c])

    def x_copy(k):
        rows = pl.ds(blocks[k] * size, size)
        return pltpu.make_async_copy(x_hbm.at[rows], xs.at[k % 2], x_sems.at[PIECES + k % 2])

    for c in range(PIECES):
        x_piece(c).start()
        for copy in w_copies(c):
            copy.start()
    pending = {}
    for k, block in enumerate(blocks):
        if k + 1 < len(blocks):
            x_copy(k + 1).start()
        low = 0 if block in with_q else cq
        high = cq + 2 * HD if with_kv else cq
        if k == 0:
            total, own = 0.0, 0.0
            for c in range(PIECES):
                x_piece(c).wait()
                for copy in w_copies(c):
                    copy.wait()
                part = slice(c * piece, (c + 1) * piece)
                total += dot(xs[0, :, part], w[part, low:high])
                if with_decode:
                    own += dot(dx_ref[:, part], w[part, :])
        else:
            x_copy(k).wait()
            total = dot(xs[k % 2], w[:, low:high])
        slot = k % 2
        for copy in pending.pop(slot, []):
            copy.wait()
        rows = pl.ds(block * size, size)
        copies = []
        if low == 0:
            q_out[slot] = total[:, :cq].astype(jnp.bfloat16)
            copies.append(pltpu.make_async_copy(q_out.at[slot], q_hbm.at[rows], out_sems.at[0, slot]))
        if with_kv:
            kv_out[slot] = total[:, cq - low :].astype(jnp.bfloat16)
            copies.append(pltpu.make_async_copy(kv_out.at[slot], kv_hbm.at[rows], out_sems.at[1, slot]))
        for copy in copies:
            copy.start()
        pending[slot] = copies
        if with_decode and k == 0:
            rows = STEPS * ROWS_DEV * n
            shape = (n * GROUP_ROWS, rows)
            to, fro = iota(shape, 0), iota(shape, 1)
            owner, rs = to // GROUP_ROWS, to % GROUP_ROWS
            wanted = owner * ROWS_DEV + row_of(rs) + jnp.where(rs >= ROWS_DEV, ROWS_DEV * n, 0)
            pick = ((fro == wanted) & (rs < STEPS * ROWS_DEV)).astype(jnp.float32).astype(jnp.bfloat16)
            own = dot(pick, own.astype(jnp.bfloat16))
            for h in range(lq):
                part = slice(h * n * GROUP_ROWS, (h + 1) * n * GROUP_ROWS)
                qh_ref[part, :] = own[:, h * HD : (h + 1) * HD].astype(jnp.bfloat16)
            found = block_of_pages(counts, done, placed, table)
            lane = iota((n * GROUP_ROWS, HD), 1)
            r = row_of(lane % GROUP_ROWS)
            kind = lane // GROUP_ROWS
            facts = jnp.where(
                kind == 0,
                by_row(r, [found[i][0] for i in range(ROWS_DEV)], -1),
                jnp.where(
                    kind == 1,
                    by_row(r, [found[i][1] for i in range(ROWS_DEV)], -1),
                    by_row(r, [lens[i] for i in range(ROWS_DEV)], 0),
                ),
            ).astype(jnp.float32)
            sixth = iota((n * GROUP_ROWS, HD), 0) % GROUP_ROWS == 6
            msg_ref[:, :HD] = jnp.where(sixth, facts, own[:, :HD])
            msg_ref[:, HD:] = own[:, HD:]
    for copies in pending.values():
        for copy in copies:
            copy.wait()


def project_first(ints, dx, x, wq, wkv, n, size, q_blocks):
    rows, depth = x.shape
    cq = wq.shape[1]
    lq = cq // HD
    blocks = list(range(rows // size))
    smem, vmem = pl.BlockSpec(memory_space=SMEM), pl.BlockSpec(memory_space=VMEM)
    hbm = pl.BlockSpec(memory_space=pl.ANY)
    return pl.pallas_call(
        functools.partial(project, n, lq, blocks, blocks[:q_blocks], True, True),
        in_specs=[smem] * 5 + [vmem] + [hbm] * 3,
        out_specs=[hbm, hbm, vmem, vmem],
        out_shape=[
            jax.ShapeDtypeStruct((rows, cq), jnp.bfloat16),
            jax.ShapeDtypeStruct((rows, 2 * HD), jnp.bfloat16),
            jax.ShapeDtypeStruct((lq * n * GROUP_ROWS, HD), jnp.bfloat16),
            jax.ShapeDtypeStruct((n * GROUP_ROWS, cq + 2 * HD), jnp.float32),
        ],
        scratch_shapes=projection_scratch(size, depth, cq, 2 * HD),
        compiler_params=pltpu.CompilerParams(vmem_limit_bytes=62 * MIB),
        cost_estimate=pl.CostEstimate(
            flops=2 * rows * depth * (2 * HD + cq * q_blocks * size // rows),
            bytes_accessed=2 * rows * depth + 2 * depth * (cq + 2 * HD),
            transcendentals=0,
        ),
        name="project_first",
    )(*ints, dx, x, wq, wkv)


def projection_scratch(size, depth, cq, ckv):
    return [
        VMEM((2, size, depth), jnp.bfloat16),
        VMEM((depth, cq + ckv), jnp.bfloat16),
        VMEM((2, size, cq), jnp.bfloat16),
        VMEM((2, size, 2 * HD), jnp.bfloat16),
        pltpu.SemaphoreType.DMA((PIECES + 2,)),
        pltpu.SemaphoreType.DMA((2, PIECES)),
        pltpu.SemaphoreType.DMA((2, 2)),
    ]


def project_rest(x, wq, q, size, q_blocks):
    rows, depth = x.shape
    cq = wq.shape[1]
    blocks = list(range(q_blocks, rows // size))
    hbm = pl.BlockSpec(memory_space=pl.ANY)
    return pl.pallas_call(
        functools.partial(project, 0, cq // HD, blocks, blocks, False, False),
        in_specs=[hbm] * 3,
        out_specs=hbm,
        out_shape=jax.ShapeDtypeStruct((rows, cq), jnp.bfloat16),
        scratch_shapes=projection_scratch(size, depth, cq, 0),
        input_output_aliases={2: 0},
        compiler_params=pltpu.CompilerParams(vmem_limit_bytes=62 * MIB),
        cost_estimate=pl.CostEstimate(
            flops=2 * len(blocks) * size * depth * cq,
            bytes_accessed=2 * len(blocks) * size * depth + 2 * depth * cq,
            transcendentals=0,
        ),
        name="project_rest",
    )(x, wq, q)


LOG2E = 1.4426950408889634
SLAB = 32


def attend_prompt(lq, counts, q_ref, kv_ref, o_ref, held):
    group = lax.axis_index("pool")
    c0, c1 = counts[group, 0], counts[group, 1]
    big = jnp.where(c0 == MOST_BLOCKS, 0, jnp.where(c1 == MOST_BLOCKS, c0, c0 + c1))
    cut = jnp.where(c0 == MOST_BLOCKS, c1, c0)
    causal = iota((SLAB, BLOCK_TOKENS), 1) - iota((SLAB, BLOCK_TOKENS), 0)
    for half in range(2):

        def rows_at(j, half=half):
            block = big + j if half == 0 else j + jnp.where(j >= big, MOST_BLOCKS, 0)
            return pl.ds(pl.multiple_of(block * BLOCK_TOKENS, BLOCK_TOKENS), BLOCK_TOKENS)

        for j in range(MOST_BLOCKS):
            held[half, j * BLOCK_TOKENS : (j + 1) * BLOCK_TOKENS, :] = kv_ref[rows_at(j), :]

        def scores_of(j, half=half):
            q = q_ref[rows_at(j), :]
            q = jnp.concatenate([q[:, h * HD : (h + 1) * HD] for h in range(lq)], axis=0)
            return dot_t(q, held[half, : (j + 1) * BLOCK_TOKENS, :HD])

        scores = scores_of(0)
        for j in range(MOST_BLOCKS):
            later = scores_of(j + 1) if j + 1 < MOST_BLOCKS else None
            weights = []
            for at in range(0, lq * BLOCK_TOKENS, SLAB):
                tiles = []
                for i in range(j + 1):
                    tile = scores[at : at + SLAB, i * BLOCK_TOKENS : (i + 1) * BLOCK_TOKENS]
                    if i == j:
                        tile = jnp.where(causal <= at % BLOCK_TOKENS, tile, MASKED)
                    elif half == 1:
                        tile = tile + jnp.where((i < cut) & (cut <= j), MASKED, 0.0)
                    tiles.append(tile)
                peak = jnp.max(functools.reduce(jnp.maximum, tiles), axis=1, keepdims=True)
                raised = [jnp.exp2((tile - peak) * (SCALE * LOG2E)) for tile in tiles]
                inverse = 1.0 / jnp.sum(functools.reduce(jnp.add, raised), axis=1, keepdims=True)
                weights.append(jnp.concatenate([(t * inverse).astype(jnp.bfloat16) for t in raised], axis=1))
            mixed = dot(jnp.concatenate(weights, axis=0), held[half, : (j + 1) * BLOCK_TOKENS, HD:])
            for h in range(lq):
                part = mixed[h * BLOCK_TOKENS : (h + 1) * BLOCK_TOKENS]
                o_ref[rows_at(j), h * HD : (h + 1) * HD] = part.astype(jnp.bfloat16)
            scores = later


def prompt_attention(counts, q, kv):
    rows, cq = q.shape
    vmem = pl.BlockSpec(memory_space=VMEM)
    return pl.pallas_call(
        functools.partial(attend_prompt, cq // HD),
        in_specs=[pl.BlockSpec(memory_space=SMEM), vmem, vmem],
        out_specs=vmem,
        out_shape=jax.ShapeDtypeStruct((rows, cq), jnp.bfloat16),
        scratch_shapes=[VMEM((2, MOST_BLOCKS * BLOCK_TOKENS, 2 * HD), jnp.bfloat16)],
        compiler_params=pltpu.CompilerParams(vmem_limit_bytes=48 * MIB),
        cost_estimate=pl.CostEstimate(flops=2 * rows * rows * cq, bytes_accessed=8 * rows * cq, transcendentals=rows * rows),
        name="prompt_attention",
    )(counts, q, kv)


def row_head(n, lq, h, hh):
    at = h * GQ + hh
    return at // lq, at % lq


def handed_part(n, lq, kv_ref, q_ref, msg_ref, o_ref):
    rows = lq * n * GROUP_ROWS
    shape = (rows, HD)
    at_row, lane = iota(shape, 0), iota(shape, 1)
    rs = at_row % GROUP_ROWS
    facts = msg_ref[:, :HD].reshape(n, GROUP_ROWS, HD)[:, 6:7, :]
    facts = jnp.broadcast_to(facts, (n, GROUP_ROWS, HD)).reshape(n * GROUP_ROWS, HD)
    facts = jnp.concatenate([facts] * lq, axis=0)

    def column(kind):
        return jnp.sum(jnp.where(lane == kind * GROUP_ROWS + rs, facts, 0.0), axis=1, keepdims=True)

    first_block, second_block, length = [column(kind) for kind in range(3)]
    scores = dot_t(q_ref[...], kv_ref[:, :HD]) * SCALE
    lane_f = lane.astype(jnp.float32)
    parts = []
    for b in range(NBLK):
        limit = jnp.where(
            first_block == b, length, jnp.where(second_block == b, length - BLOCK_TOKENS, 0.0)
        )
        part = scores[:, b * BLOCK_TOKENS : (b + 1) * BLOCK_TOKENS]
        parts.append(jnp.where(lane_f < limit, part, MASKED))
    scores = jnp.concatenate(parts, axis=1)
    top = jnp.max(scores, axis=1, keepdims=True)
    raised = jnp.exp(scores - top)
    total = jnp.sum(raised, axis=1, keepdims=True)
    near = raised.astype(jnp.bfloat16)
    rest = (raised - near.astype(jnp.float32)).astype(jnp.bfloat16)
    values = kv_ref[:, HD:]
    mixed = (dot(near, values) + dot(rest, values)).reshape(lq * n, GROUP_ROWS, HD)

    def line(col):
        spread = jnp.where(lane == rs, col, 0.0).reshape(lq * n, GROUP_ROWS, HD)
        return jnp.sum(spread, axis=1, keepdims=True)

    rs3 = rs.reshape(lq * n, GROUP_ROWS, HD)
    mixed = jnp.where(rs3 == 6, line(top), jnp.where(rs3 == 7, line(total), mixed))
    for h in range(lq):
        o_ref[:, h * GROUP_ROWS : (h + 1) * GROUP_ROWS, :] = mixed[h * n : (h + 1) * n]


def handed_attention(kv, q_own, msgs, n, lq):
    rows = lq * n * GROUP_ROWS
    vmem = pl.BlockSpec(memory_space=VMEM)
    return pl.pallas_call(
        functools.partial(handed_part, n, lq),
        in_specs=[vmem] * 3,
        out_specs=vmem,
        out_shape=jax.ShapeDtypeStruct((n, lq * GROUP_ROWS, HD), jnp.float32),
        compiler_params=pltpu.CompilerParams(vmem_limit_bytes=32 * MIB),
        cost_estimate=pl.CostEstimate(flops=6 * rows * HD * PTOK, bytes_accessed=2 * MIB, transcendentals=rows * PTOK),
        name="handed_attention",
    )(kv, q_own, msgs)


def owner_part(n, lq, counts, done, placed, table, lens, cache_hbm, held, handed, o_ref, cache, sems, slot_row, slot_limit):
    def slot_copy(slot):
        rows = pl.ds(slot * BLOCK_TOKENS, BLOCK_TOKENS)
        return pltpu.make_async_copy(cache_hbm.at[rows], cache.at[rows], sems.at[slot])

    for slot in range(DEVICE_SLOTS):
        slot_copy(slot).start()
    found = block_of_pages(counts, done, placed, table)
    for r in range(ROWS_DEV):
        for p in range(PAGES):
            slot_row[table[r, p]] = jnp.int32(r)
            slot_limit[table[r, p]] = jnp.where(found[r][p] < 0, lens[r] - p * BLOCK_TOKENS, 0)

    cq = lq * HD
    groups = QH
    rows = groups * GROUP_ROWS
    span = GQ * GROUP_ROWS
    queries, keys = [], []
    for h in range(KVH):
        for hh in range(GQ):
            t, at = row_head(n, lq, h, hh)
            queries.append(held[t * GROUP_ROWS : (t + 1) * GROUP_ROWS, at * HD : (at + 1) * HD])
        t, _ = row_head(n, lq, h, 0)
        keys += [held[t * GROUP_ROWS : (t + 1) * GROUP_ROWS, cq : cq + HD]] * GQ
    queries = jnp.concatenate(queries, axis=0)
    earlier = jnp.concatenate([pltpu.roll(key, ROWS_DEV, 0) for key in keys], axis=0)
    keys = jnp.concatenate(keys, axis=0)
    at_row, lane = iota((rows, HD), 0), iota((rows, HD), 1)
    r = row_of(at_row % GROUP_ROWS)
    rounded = queries.astype(jnp.bfloat16)
    scores = []
    for slot in range(DEVICE_SLOTS):
        slot_copy(slot).wait()
        part = slice(slot * BLOCK_TOKENS, (slot + 1) * BLOCK_TOKENS)
        some = [
            dot_t(rounded[h * span : (h + 1) * span], cache[part, 2 * h * HD : (2 * h + 1) * HD])
            for h in range(KVH)
        ]
        usable = (r == slot_row[slot]) & (lane < slot_limit[slot])
        scores.append(jnp.where(usable, jnp.concatenate(some, axis=0) * SCALE, MASKED))
    scores = jnp.concatenate(scores, axis=1)
    now = jnp.sum(queries * keys, axis=1, keepdims=True) * SCALE
    before = jnp.sum(queries * earlier, axis=1, keepdims=True) * SCALE
    rs1 = iota((rows, 1), 0) % GROUP_ROWS
    before = jnp.where((rs1 >= ROWS_DEV) & (rs1 < STEPS * ROWS_DEV), before, MASKED)

    mixed = handed[...].reshape(groups, GROUP_ROWS, HD)
    shape = (groups, GROUP_ROWS, HD)
    mine = iota(shape, 1) == iota(shape, 2)

    def column(at):
        line = jnp.broadcast_to(mixed[:, at : at + 1, :], shape)
        return jnp.sum(jnp.where(mine, line, 0.0), axis=2, keepdims=True).reshape(rows, 1)

    other_peak, other_total = column(6), column(7)
    peak = jnp.maximum(jnp.max(scores, axis=1, keepdims=True), jnp.maximum(now, before))
    peak = jnp.maximum(peak, other_peak)
    raised, now, before = jnp.exp(scores - peak), jnp.exp(now - peak), jnp.exp(before - peak)
    other = jnp.exp(other_peak - peak)
    inverse = 1.0 / (jnp.sum(raised, axis=1, keepdims=True) + now + before + other * other_total)
    weights = (raised * inverse).astype(jnp.bfloat16)
    now = (now * inverse).astype(jnp.bfloat16).astype(jnp.float32)
    before = (before * inverse).astype(jnp.bfloat16).astype(jnp.float32)
    mixed = mixed.reshape(rows, HD) * (other * inverse)
    out = []
    for h in range(KVH):
        part = slice(h * span, (h + 1) * span)
        own = mixed[part] + dot(weights[part], cache[:, (2 * h + 1) * HD : (2 * h + 2) * HD])
        t, _ = row_head(n, lq, h, 0)
        value = held[t * GROUP_ROWS : (t + 1) * GROUP_ROWS, cq + HD : cq + 2 * HD]
        last = pltpu.roll(value, ROWS_DEV, 0)
        for hh in range(GQ):
            some = slice(h * span + hh * GROUP_ROWS, h * span + (hh + 1) * GROUP_ROWS)
            line = own[hh * GROUP_ROWS : (hh + 1) * GROUP_ROWS]
            out.append(line + now[some] * value + before[some] * last)
    out = jnp.concatenate(out, axis=1)
    for s in range(STEPS):
        o_ref[s] = out[s * ROWS_DEV : (s + 1) * ROWS_DEV].astype(jnp.bfloat16)


def decode_attention(ints, cache, msgs, parts, n, lq):
    smem, vmem = pl.BlockSpec(memory_space=SMEM), pl.BlockSpec(memory_space=VMEM)
    return pl.pallas_call(
        functools.partial(owner_part, n, lq),
        in_specs=[smem] * 5 + [pl.BlockSpec(memory_space=pl.ANY), vmem, vmem],
        out_specs=vmem,
        out_shape=jax.ShapeDtypeStruct((STEPS, ROWS_DEV, QH * HD), jnp.bfloat16),
        scratch_shapes=[
            VMEM(cache.shape, jnp.bfloat16),
            pltpu.SemaphoreType.DMA((DEVICE_SLOTS,)),
            SMEM((DEVICE_SLOTS,), jnp.int32),
            SMEM((DEVICE_SLOTS,), jnp.int32),
        ],
        compiler_params=pltpu.CompilerParams(vmem_limit_bytes=48 * MIB),
        cost_estimate=pl.CostEstimate(flops=4 * 256 * HD * 768, bytes_accessed=4 * MIB, transcendentals=256 * 768),
        name="decode_attention",
    )(*ints, cache, msgs, parts)


def local(
    prompt_x,
    q_weight,
    kv_weight,
    prompt_blocks,
    finished,
    placement,
    page_table,
    row_lens,
    kv_cache,
    decode_x,
):
    n = lax.axis_size("tp")
    lq = q_weight.shape[1] // HD
    share = GQ // lq
    if share > 1:
        sets = [[k * share + i for i in range(share)] for k in range(n // share)]
        kv_weight = lax.all_gather(kv_weight, "tp", axis=1, tiled=True, axis_index_groups=sets)
    cache = kv_cache.reshape(-1, kv_cache.shape[2])
    dx = decode_x.reshape(-1, decode_x.shape[2])
    ints = (prompt_blocks, finished, placement, page_table, row_lens)
    size, q_blocks = 512, 1
    q, kv, q_own, msgs = project_first(ints, dx, prompt_x, q_weight, kv_weight, n, size, q_blocks)
    kv_other = lax.ppermute(kv, "pool", [(0, 1), (1, 0)])
    msgs = lax.all_to_all(msgs, "tp", split_axis=0, concat_axis=0, tiled=True)
    q = project_rest(prompt_x, q_weight, q, size, q_blocks)
    parts = handed_attention(kv_other, q_own, msgs, n, lq)
    parts = lax.all_to_all(parts, "tp", split_axis=0, concat_axis=0, tiled=True)
    prompt_attn = prompt_attention(prompt_blocks, q, kv)
    decode_attn = decode_attention(ints, cache, msgs, parts, n, lq)
    return prompt_attn, decode_attn


def solution(mesh):
    return jax.shard_map(
        local,
        mesh=mesh,
        in_specs=(
            P(("rep", "pool"), None),
            P(None, "tp"),
            P(None, "tp"),
            P("rep", None),
            P("rep", None),
            P("rep", None, None),
            P(("rep", "pool", "tp"), None),
            P(("rep", "pool", "tp")),
            P(("rep", "pool", "tp"), None, None),
            P(None, ("rep", "pool"), None),
        ),
        out_specs=(P(("rep", "pool"), "tp"), P(None, ("rep", "pool", "tp"), None)),
        check_vma=False,
    )
```

time: 262 us -> 69.4 us (0.26)
  matrix products: 92 us -> 0 us
  waiting for transfers between devices: 84.6 us -> 0.01 us
  Pallas kernels: 0 us -> 48.6 us
  local copies, waits for them, and re-layouts: 41.8 us -> 6.24 us
  between operations: 14.4 us -> 0.75 us
  other arithmetic: 11.2 us -> 0 us
  starting transfers between devices: 16.9 us -> 13.4 us
    all_gather x1 -> x0, waiting for transfers between devices: 77.2 us -> none  [local(): kv_whole = lax.all_gather(kv_local, 'tp', axis=1, tiled=True)]
    dot_general x11 -> x0, matrix products: 60.8 us -> none  [the longest x1 22.3 us: local(): jnp.einsum('hij,jd->ihd', weights, head_kv[:, 1], preferred_element_type=...]
    pallas_call x0 -> x5, Pallas kernels: none -> 48.6 us  [the longest x1 21 us: project_first(): pl.pallas_call(functools.partial(project, n, lq, blocks, blocks[:q_blocks...]
    sub x1 -> x0, matrix products: 31.3 us -> none  [local(): raised = jnp.exp(scores - row_peak)]
    reshape x9 -> x0, local copies, waits for them, and re-layouts: 21.1 us -> none  [the longest x1 14.3 us: local(): kv_split = kv_whole.reshape(PTOK, KVH, 2, HD)]
    all_to_all x3 -> x2, waiting for transfers between devices: 7.4 us -> 0.01 us  [the longest x1 0.01 us: local(): parts = lax.all_to_all(parts, 'tp', split_axis=0, concat_axis=0, tiled=True)]
    and x1 -> x0, other arithmetic: 5.42 us -> none  [local(): (segment[:, None] == segment[None, :]) & (position[:, None] >= position[N...]
    slice x2 -> x0, local copies, waits for them, and re-layouts: 4.47 us -> none  [the longest x1 4.47 us: local(): context[:, :, :, 1]]
  transfers between devices with their start and end apart: 5 -> 3, of which waited for: 2 -> 0; matrix products, arithmetic and copies ran while one was open for 40% -> 0% of each run, Pallas kernels for 0% -> 31%
where the time goes in v2:
time: 69.4 us; the launch traced here: 68.9 us
  Pallas kernels  48.6 us (70%)
  starting transfers between devices  13.4 us (19%)
  local copies, waits for them, and re-layouts  6.24 us (9%)
  between operations  0.75 us (1%)
    pallas_call x1, Pallas kernels, project_first(): pl.pallas_call(functools.partial(project, n, lq, blocks, blocks[:q_blocks...  21 us
    pallas_call x1, Pallas kernels, project_rest(): pl.pallas_call(functools.partial(project, 0, cq // HD, blocks, blocks, Fa...  12.4 us
    pallas_call x1, Pallas kernels, prompt_attention(): pl.pallas_call(functools.partial(attend_prompt, cq // HD), in_specs=[pl.B...  9.3 us
    all_to_all x1, starting transfers between devices, local(): msgs = lax.all_to_all(msgs, 'tp', split_axis=0, concat_axis=0, tiled=True)  6.85 us
    unnamed x21, local copies, waits for them, and re-layouts  6.24 us
    all_to_all x1, starting transfers between devices, local(): parts = lax.all_to_all(parts, 'tp', split_axis=0, concat_axis=0, tiled=True)  5.98 us
    pallas_call x1, Pallas kernels, decode_attention(): pl.pallas_call(functools.partial(owner_part, n, lq), in_specs=[smem] * 5...  3.53 us
    pallas_call x1, Pallas kernels, handed_attention(): pl.pallas_call(functools.partial(handed_part, n, lq), in_specs=[vmem] * 3...  2.4 us
  transfers between devices with their start and end apart: 3, of which 0 were waited for; matrix products, arithmetic and copies ran while one was open for 0% of the time, Pallas kernels for 31%

profile of v2, /device:TPU:0, one launch (start us, length us, event | category | flops | bytes accessed | tf_op | source)
XLA Modules:
  0.0 68.9 jit_solution(8802603266172882046)
XLA Ops:
  0.6 1.4 %copy.13.refs_2_.placed = s32[2,16,2]{2,1,0:T(8,128)} copy(s32[2,16,2]{1,2,0:T(2,128)} %param.15) | data formatting | bytes 512 | tf_op args[5]
  2.0 1.4 %copy.14.refs_3_.table = s32[3,2]{1,0:T(4,128)} copy(s32[3,2]{0,1:T(2,128)} %param.16) | data formatting | bytes 48 | tf_op args[6]
  3.3 21.0 %project_first.1 = (bf16[2048,512]{1,0:T(8,128)(2,1)}, bf16[2048,256]{1,0:T(8,128)(2,1)}, bf16[256,128]{1,0:T(8,128)(2,1)}, f32[64,768]{1,0:T(8,128)}) custom-call(s32[2,3]{1,0:T(2,128)} %counts.3, s32[2,3]{1,0:T(2,128)} %done.1, s32[2,16,2]{2,1,0:T(8,128)} %copy.13.refs_2_.placed, s32[3,2]{1,0:T(4,128)} %copy.14.refs_3_.table, s32[3]{0:T(128)} %lens.1, ...), custom_call_target="tpu_custom_call" | custom-call | flops 8053063680 | bytes 28835840 | tf_op jit(solution)/shard_map/project_first/pallas_call | solution.py:185
  24.3 0.5 collective-permute-start
  24.8 6.9 %all-to-all-start = ((f32[8,8,768]{2,1,0:T(8,128)}), f32[8,8,768]{2,1,0:T(8,128)S(1)}, u32[]{:S(2)}, u32[]{:S(2)}) async-start(f32[8,8,768]{2,1,0:T(8,128)} %bitcast.7), calls=%async_computation | async-start | bytes 393216 | tf_op jit(solution)/shard_map/all_to_all | solution.py:486
  31.7 0.0 copy-start.8
  31.7 0.0 copy-start.4
  31.7 12.4 %project_rest.1.q_ref = bf16[2048,512]{1,0:T(8,128)(2,1)} custom-call(bf16[2048,5120]{1,0:T(8,128)(2,1)} %refs_0_.3, bf16[5120,512]{1,0:T(8,128)(2,1)} %refs_1_.3, bf16[2048,512]{1,0:T(8,128)(2,1)} %get-tuple-element.6.refs_2_), custom_call_target="tpu_custom_call", output_to_operand_aliasing={{}: (2, {})} | custom-call | flops 8053063680 | bytes 20971520 | tf_op jit(solution)/shard_map/project_rest/pallas_call | solution.py:223
  44.1 0.0 all-to-all-done
  44.1 0.0 collective-permute-done.kv_ref
  44.1 0.0 copy-done.8
  44.1 2.4 %handed_attention.1 = f32[8,32,128]{2,1,0:T(8,128)} custom-call(bf16[2048,256]{1,0:T(8,128)(2,1)S(1)} %collective-permute-done.kv_ref, bf16[256,128]{1,0:T(8,128)(2,1)S(1)} %copy-done.8, f32[64,768]{1,0:T(8,128)S(1)} %bitcast.5), custom_call_target="tpu_custom_call" | custom-call | flops 402653184 | bytes 2097152 | tf_op jit(solution)/shard_map/handed_attention/pallas_call | solution.py:352
  46.5 6.0 %all-to-all-start.1 = ((f32[8,32,128]{2,1,0:T(8,128)}), f32[8,32,128]{2,1,0:T(8,128)S(1)}, u32[]{:S(2)}, u32[]{:S(2)}) async-start(f32[8,32,128]{2,1,0:T(8,128)} %handed_attention.1), calls=%async_computation.1 | async-start | bytes 262144 | tf_op jit(solution)/shard_map/all_to_all | solution.py:489
  52.5 0.0 copy-done.4
  52.5 0.0 copy-start.1
  52.5 1.6 %copy-done.1 = bf16[2048,512]{1,0:T(8,128)(2,1)S(1)} copy-done((bf16[2048,512]{1,0:T(8,128)(2,1)S(1)}, bf16[2048,512]{1,0:T(8,128)(2,1)}, u32[]{:S(2)}) %copy-start.1) | copy-done | bytes 2097176
  54.1 0.0 copy-start.7
  54.1 1.2 %copy-done.7 = bf16[2048,256]{1,0:T(8,128)(2,1)S(1)} copy-done((bf16[2048,256]{1,0:T(8,128)(2,1)S(1)}, bf16[2048,256]{1,0:T(8,128)(2,1)}, u32[]{:S(2)}) %copy-start.7) | copy-done | bytes 1048600
  55.3 0.0 copy-start
  55.3 0.0 copy-start.2
  55.3 0.0 copy-start.3
  55.3 0.0 copy-start.5
  55.3 0.0 copy-start.6
  55.4 9.3 %prompt_attention.1 = bf16[2048,512]{1,0:T(8,128)(2,1)} custom-call(s32[2,3]{1,0:T(2,128)S(1)} %copy-done.4, bf16[2048,512]{1,0:T(8,128)(2,1)S(1)} %copy-done.1, bf16[2048,256]{1,0:T(8,128)(2,1)S(1)} %copy-done.7), custom_call_target="tpu_custom_call" | custom-call | flops 4294967296 | bytes 8388608 | tf_op jit(solution)/shard_map/prompt_attention/pallas_call | solution.py:291
  64.7 0.0 all-to-all-done.1.handed
  64.7 0.0 copy-done
  64.7 0.0 copy-done.2
  64.7 0.0 copy-done.3
  64.7 0.0 copy-done.5
  64.7 0.0 copy-done.6
  64.7 3.5 %decode_attention.1 = bf16[2,3,4096]{2,1,0:T(4,128)(2,1)S(1)} custom-call(s32[2,3]{1,0:T(2,128)S(1)} %copy-done.4, s32[2,3]{1,0:T(2,128)S(1)} %copy-done.5, s32[2,16,2]{2,1,0:T(8,128)S(1)} %copy-done.2, s32[3,2]{1,0:T(4,128)S(1)} %copy-done.3, s32[3]{0:T(128)S(1)} %copy-done.6, bf16[768,2048]{1,0:T(8,128)(2,1)S(1)} %bitcast.4, f32[64,768]{1,0:T(8,128)S(1)} %bitcast.6, ...), custom_call_target="tpu_custom_call" | custom-call | flops 100663296 | bytes 4194304 | tf_op jit(solution)/shard_map/decode_attention/pallas_call | solution.py:445
  68.2 0.7 copy.17
Async XLA Ops:
  24.3 19.8 %collective-permute-start = (bf16[2048,256]{1,0:T(8,128)(2,1)}, bf16[2048,256]{1,0:T(8,128)(2,1)S(1)}, u32[]{:S(2)}, u32[]{:S(2)}) collective-permute-start(bf16[2048,256]{1,0:T(8,128)(2,1)} %get-tuple-element.7.kv_ref), channel_id=1, source_target_pairs={{0,8},{8,0},{1,9},{9,1},{2,10},{10,2},{3,11},{11,3},{4,12},{12,4},... | collective-permute-start | bytes 3145736 | tf_op jit(solution)/shard_map/ppermute | solution.py:485
  24.8 19.3 %all-to-all-start = ((f32[8,8,768]{2,1,0:T(8,128)}), f32[8,8,768]{2,1,0:T(8,128)S(1)}, u32[]{:S(2)}, u32[]{:S(2)}) async-start(f32[8,8,768]{2,1,0:T(8,128)} %bitcast.7), calls=%async_computation | async-start | bytes 393216 | tf_op jit(solution)/shard_map/all_to_all | solution.py:486
  31.7 12.4 %copy-start.8 = (bf16[256,128]{1,0:T(8,128)(2,1)S(1)}, bf16[256,128]{1,0:T(8,128)(2,1)}, u32[]{:S(2)}) copy-start(bf16[256,128]{1,0:T(8,128)(2,1)} %get-tuple-element.9.q_ref) | copy-start | bytes 196612
  31.7 20.8 %copy-start.4 = (s32[2,3]{1,0:T(2,128)S(1)}, s32[2,3]{1,0:T(2,128)}, u32[]{:S(2)}) copy-start(s32[2,3]{1,0:T(2,128)} %counts.3) | copy-start | bytes 76
  46.5 18.1 %all-to-all-start.1 = ((f32[8,32,128]{2,1,0:T(8,128)}), f32[8,32,128]{2,1,0:T(8,128)S(1)}, u32[]{:S(2)}, u32[]{:S(2)}) async-start(f32[8,32,128]{2,1,0:T(8,128)} %handed_attention.1), calls=%async_computation.1 | async-start | bytes 262144 | tf_op jit(solution)/shard_map/all_to_all | solution.py:489
  52.5 1.6 %copy-start.1 = (bf16[2048,512]{1,0:T(8,128)(2,1)S(1)}, bf16[2048,512]{1,0:T(8,128)(2,1)}, u32[]{:S(2)}) copy-start(bf16[2048,512]{1,0:T(8,128)(2,1)} %project_rest.1.q_ref) | copy-start | bytes 6291460
  54.1 1.2 %copy-start.7 = (bf16[2048,256]{1,0:T(8,128)(2,1)S(1)}, bf16[2048,256]{1,0:T(8,128)(2,1)}, u32[]{:S(2)}) copy-start(bf16[2048,256]{1,0:T(8,128)(2,1)} %get-tuple-element.7.kv_ref) | copy-start | bytes 3145732
  55.3 9.3 %copy-start = (bf16[6,128,2048]{2,1,0:T(8,128)(2,1)S(1)}, bf16[6,128,2048]{2,1,0:T(8,128)(2,1)}, u32[]{:S(2)}) copy-start(bf16[6,128,2048]{2,1,0:T(8,128)(2,1)} %param.18) | copy-start | bytes 9437188
  55.3 9.3 %copy-start.2 = (s32[2,16,2]{2,1,0:T(8,128)S(1)}, s32[2,16,2]{2,1,0:T(8,128)}, u32[]{:S(2)}) copy-start(s32[2,16,2]{2,1,0:T(8,128)} %copy.13.refs_2_.placed) | copy-start | bytes 772
  55.3 9.3 %copy-start.3 = (s32[3,2]{1,0:T(4,128)S(1)}, s32[3,2]{1,0:T(4,128)}, u32[]{:S(2)}) copy-start(s32[3,2]{1,0:T(4,128)} %copy.14.refs_3_.table) | copy-start | bytes 76
  55.3 9.3 %copy-start.5 = (s32[2,3]{1,0:T(2,128)S(1)}, s32[2,3]{1,0:T(2,128)}, u32[]{:S(2)}) copy-start(s32[2,3]{1,0:T(2,128)} %done.1) | copy-start | bytes 76
  55.3 9.4 %copy-start.6 = (s32[3]{0:T(128)S(1)}, s32[3]{0:T(128)}, u32[]{:S(2)}) copy-start(s32[3]{0:T(128)} %lens.1) | copy-start | bytes 40

commit v3 on v2

v3 whole, which is shorter than its diff:
```python
import functools

import jax
import jax.numpy as jnp
from jax import lax
from jax.experimental import pallas as pl
from jax.experimental.pallas import tpu as pltpu
from jax.sharding import PartitionSpec as P

QH = 32
KVH = 8
GQ = QH // KVH
HD = 128
BLOCK_TOKENS = 128
PTOK = 2048
NPROMPT = 3
MOST_BLOCKS = 8
PAGES = 2
STEPS = 2
NBLK = 16
DEVICE_SLOTS = 6
ROWS_DEV = 3
GROUP_ROWS = 8
KEY_VALUE_COLUMNS = 2048
SCALE = HD ** (-0.5)
MASKED = -1e30
PIECES = 5
MIB = 1 << 20
VMEM = pltpu.VMEM
SMEM = pltpu.SMEM


def dot(a, b):
    return jnp.dot(a, b, preferred_element_type=jnp.float32)


def dot_t(a, b):
    return lax.dot_general(a, b, (((1,), (1,)), ((), ())), preferred_element_type=jnp.float32)


def iota(shape, axis):
    return lax.broadcasted_iota(jnp.int32, shape, axis)


def row_of(rs):
    return jnp.where(rs >= 2 * ROWS_DEV, ROWS_DEV, jnp.where(rs >= ROWS_DEV, rs - ROWS_DEV, rs))


def block_of_pages(counts, done, placed, table):
    me = lax.axis_index("tp")
    other = 1 - lax.axis_index("pool")
    first_end = counts[other, 0]
    second_end = first_end + counts[other, 1]
    found = [[jnp.int32(-1)] * PAGES for _ in range(ROWS_DEV)]
    for b in range(NBLK):
        live = jnp.where(
            b < first_end, done[other, 0], jnp.where(b < second_end, done[other, 1], done[other, 2])
        )
        slot = jnp.where((live > 0) & (placed[other, 0, b] == me), placed[other, 1, b], -1)
        for r in range(ROWS_DEV):
            for p in range(PAGES):
                found[r][p] = jnp.where(slot == table[p, r], b, found[r][p])
    return found


def by_row(r, values, rest):
    out = jnp.full(r.shape, rest, jnp.int32)
    for k in range(ROWS_DEV):
        out = jnp.where(r == k, values[k], out)
    return out


def project(n, lq, start, with_decode, *refs):
    refs = list(refs)
    if with_decode:
        counts, done, placed, table, lens, dx_ref = refs[:6]
        x_hbm, wq_hbm, wkv_hbm, q_ref, kv_ref, qh_ref, msg_ref = refs[6:13]
        del refs[:13]
    else:
        x_hbm, wq_hbm, wkv_hbm, _, _, q_ref, kv_ref = refs[:7]
        del refs[:7]
    xs, w, x_sems, w_sems = refs
    size, depth = xs.shape[1:]
    cq = lq * HD
    piece = depth // PIECES
    step, steps = pl.program_id(0), pl.num_programs(0)
    slot = lax.rem(step, 2)

    def w_copies(c):
        part = pl.ds(c * piece, piece)
        return [
            pltpu.make_async_copy(wq_hbm.at[part], w.at[part, pl.ds(0, cq)], w_sems.at[0, c]),
            pltpu.make_async_copy(wkv_hbm.at[part], w.at[part, pl.ds(cq, 2 * HD)], w_sems.at[1, c]),
        ]

    def x_copy(at, c):
        rows = pl.ds(pl.multiple_of((start + at) * size, size), size)
        cols = pl.ds(c * piece, piece)
        to = lax.rem(at, 2)
        return pltpu.make_async_copy(x_hbm.at[rows, cols], xs.at[to, :, cols], x_sems.at[to, c])

    @pl.when(step == 0)
    def _():
        for c in range(PIECES):
            x_copy(step, c).start()
            for copy in w_copies(c):
                copy.start()

    @pl.when(step + 1 < steps)
    def _():
        for c in range(PIECES):
            x_copy(step + 1, c).start()

    total = 0.0
    for c in range(PIECES):
        x_copy(step, c).wait()

        @pl.when(step == 0)
        def _(c=c):
            for copy in w_copies(c):
                copy.wait()

        part = slice(c * piece, (c + 1) * piece)
        total += dot(xs[slot, :, part], w[part, :])
    q_ref[...] = total[:, :cq].astype(jnp.bfloat16)
    kv_ref[...] = total[:, cq:].astype(jnp.bfloat16)
    if with_decode:

        @pl.when(step == 0)
        def _():
            rows = STEPS * ROWS_DEV * n
            shape = (n * GROUP_ROWS, rows)
            to, fro = iota(shape, 0), iota(shape, 1)
            owner, rs = to // GROUP_ROWS, to % GROUP_ROWS
            wanted = owner * ROWS_DEV + row_of(rs) + jnp.where(rs >= ROWS_DEV, ROWS_DEV * n, 0)
            pick = ((fro == wanted) & (rs < STEPS * ROWS_DEV)).astype(jnp.float32).astype(jnp.bfloat16)
            own = dot(pick, dot(dx_ref[...], w[...]).astype(jnp.bfloat16))
            for h in range(lq):
                part = slice(h * n * GROUP_ROWS, (h + 1) * n * GROUP_ROWS)
                qh_ref[part, :] = own[:, h * HD : (h + 1) * HD].astype(jnp.bfloat16)
            found = block_of_pages(counts, done, placed, table)
            lane = iota((n * GROUP_ROWS, HD), 1)
            r = row_of(lane % GROUP_ROWS)
            kind = lane // GROUP_ROWS
            facts = jnp.where(
                kind == 0,
                by_row(r, [found[i][0] for i in range(ROWS_DEV)], -1),
                jnp.where(
                    kind == 1,
                    by_row(r, [found[i][1] for i in range(ROWS_DEV)], -1),
                    by_row(r, [lens[i] for i in range(ROWS_DEV)], 0),
                ),
            ).astype(jnp.float32)
            sixth = iota((n * GROUP_ROWS, HD), 0) % GROUP_ROWS == 6
            msg_ref[:, :HD] = jnp.where(sixth, facts, own[:, :HD])
            msg_ref[:, HD:] = own[:, HD:]


def project_rows(x, wq, wkv, start, count, size, held=None, ints=None, dx=None, n=None):
    rows, depth = x.shape
    cq, ckv = wq.shape[1], wkv.shape[1]
    lq = cq // HD
    first = held is None
    offset = start // size
    smem, vmem = pl.BlockSpec(memory_space=SMEM), pl.BlockSpec(memory_space=VMEM)
    hbm = pl.BlockSpec(memory_space=pl.ANY)
    out_shape = [
        jax.ShapeDtypeStruct((rows, cq), jnp.bfloat16),
        jax.ShapeDtypeStruct((rows, ckv), jnp.bfloat16),
    ]
    out_specs = [
        pl.BlockSpec((size, cq), lambda i: (i + offset, 0)),
        pl.BlockSpec((size, ckv), lambda i: (i + offset, 0)),
    ]
    if first:
        args = tuple(ints) + (dx, x, wq, wkv)
        in_specs = [smem] * 5 + [vmem] + [hbm] * 3
        out_shape += [
            jax.ShapeDtypeStruct((lq * n * GROUP_ROWS, HD), jnp.bfloat16),
            jax.ShapeDtypeStruct((n * GROUP_ROWS, cq + ckv), jnp.float32),
        ]
        out_specs += [vmem, vmem]
        aliases = {}
    else:
        args = (x, wq, wkv) + held
        in_specs = [hbm] * 5
        aliases = {3: 0, 4: 1}
    return pl.pallas_call(
        functools.partial(project, n, lq, offset, first),
        grid=(count // size,),
        in_specs=in_specs,
        out_specs=out_specs,
        out_shape=out_shape,
        scratch_shapes=[
            VMEM((2, size, depth), jnp.bfloat16),
            VMEM((depth, cq + ckv), jnp.bfloat16),
            pltpu.SemaphoreType.DMA((2, PIECES)),
            pltpu.SemaphoreType.DMA((2, PIECES)),
        ],
        input_output_aliases=aliases,
        compiler_params=pltpu.CompilerParams(vmem_limit_bytes=62 * MIB),
        cost_estimate=pl.CostEstimate(
            flops=2 * count * depth * (cq + ckv),
            bytes_accessed=2 * (count + cq + ckv) * depth + 2 * count * (cq + ckv),
            transcendentals=0,
        ),
        name="project_first" if first else "project_rest",
    )(*args)


LOG2E = 1.4426950408889634
SLAB = 32


def attend_prompt(lq, half, counts, q_hbm, kv_hbm, *refs):
    o_hbm, qs, kvs, outs, sems = refs[-5:]
    group = lax.axis_index("pool")
    c0, c1 = counts[group, 0], counts[group, 1]
    big = jnp.where(c0 == MOST_BLOCKS, 0, jnp.where(c1 == MOST_BLOCKS, c0, c0 + c1))
    cut = jnp.where(c0 == MOST_BLOCKS, c1, c0)

    loads, stores = [], []
    for j in range(MOST_BLOCKS):
        block = big + j if half == 0 else j + jnp.where(j >= big, MOST_BLOCKS, 0)
        rows = pl.ds(pl.multiple_of(block * BLOCK_TOKENS, BLOCK_TOKENS), BLOCK_TOKENS)
        here = pl.ds(j * BLOCK_TOKENS, BLOCK_TOKENS)
        loads.append(
            (
                pltpu.make_async_copy(kv_hbm.at[rows], kvs.at[here], sems.at[0, j]),
                pltpu.make_async_copy(q_hbm.at[rows], qs.at[here], sems.at[1, j]),
            )
        )
        stores.append(pltpu.make_async_copy(outs.at[here], o_hbm.at[rows], sems.at[2, j]))
        for copy in loads[j]:
            copy.start()

    def scores_of(j):
        for copy in loads[j]:
            copy.wait()
        q = qs[j * BLOCK_TOKENS : (j + 1) * BLOCK_TOKENS, :]
        q = jnp.concatenate([q[:, h * HD : (h + 1) * HD] for h in range(lq)], axis=0)
        return dot_t(q, kvs[: (j + 1) * BLOCK_TOKENS, :HD])

    causal = iota((SLAB, BLOCK_TOKENS), 1) - iota((SLAB, BLOCK_TOKENS), 0)
    scores = scores_of(0)
    for j in range(MOST_BLOCKS):
        later = scores_of(j + 1) if j + 1 < MOST_BLOCKS else None
        weights = []
        for at in range(0, lq * BLOCK_TOKENS, SLAB):
            tiles = []
            for i in range(j + 1):
                tile = scores[at : at + SLAB, i * BLOCK_TOKENS : (i + 1) * BLOCK_TOKENS]
                if i == j:
                    tile = jnp.where(causal <= at % BLOCK_TOKENS, tile, MASKED)
                elif half == 1:
                    tile = tile + jnp.where((i < cut) & (cut <= j), MASKED, 0.0)
                tiles.append(tile)
            peak = jnp.max(functools.reduce(jnp.maximum, tiles), axis=1, keepdims=True)
            raised = [jnp.exp2((tile - peak) * (SCALE * LOG2E)) for tile in tiles]
            inverse = 1.0 / jnp.sum(functools.reduce(jnp.add, raised), axis=1, keepdims=True)
            weights.append(jnp.concatenate([(t * inverse).astype(jnp.bfloat16) for t in raised], axis=1))
        mixed = dot(jnp.concatenate(weights, axis=0), kvs[: (j + 1) * BLOCK_TOKENS, HD:])
        for h in range(lq):
            part = mixed[h * BLOCK_TOKENS : (h + 1) * BLOCK_TOKENS]
            outs[j * BLOCK_TOKENS : (j + 1) * BLOCK_TOKENS, h * HD : (h + 1) * HD] = part.astype(jnp.bfloat16)
        stores[j].start()
        scores = later
    for copy in stores:
        copy.wait()


def prompt_attention(counts, q, kv, half, so_far=None, after=None):
    rows, cq = q.shape
    hbm = pl.BlockSpec(memory_space=pl.ANY)
    more = () if so_far is None else (so_far, after)
    tokens = MOST_BLOCKS * BLOCK_TOKENS
    return pl.pallas_call(
        functools.partial(attend_prompt, cq // HD, half),
        in_specs=[pl.BlockSpec(memory_space=SMEM), hbm, hbm] + [hbm] * len(more),
        out_specs=hbm,
        out_shape=jax.ShapeDtypeStruct((rows, cq), jnp.bfloat16),
        scratch_shapes=[
            VMEM((tokens, cq), jnp.bfloat16),
            VMEM((tokens, 2 * HD), jnp.bfloat16),
            VMEM((tokens, cq), jnp.bfloat16),
            pltpu.SemaphoreType.DMA((3, MOST_BLOCKS)),
        ],
        input_output_aliases={3: 0} if more else {},
        compiler_params=pltpu.CompilerParams(vmem_limit_bytes=62 * MIB),
        cost_estimate=pl.CostEstimate(flops=rows * rows * cq, bytes_accessed=4 * rows * cq, transcendentals=rows * rows // 2),
        name="long_prompt" if half == 0 else "short_prompts",
    )(counts, q, kv, *more)


def row_head(n, lq, h, hh):
    at = h * GQ + hh
    return at // lq, at % lq


def handed_part(n, lq, kv_ref, q_ref, msg_ref, o_ref):
    rows = lq * n * GROUP_ROWS
    shape = (rows, HD)
    at_row, lane = iota(shape, 0), iota(shape, 1)
    rs = at_row % GROUP_ROWS
    facts = msg_ref[:, :HD].reshape(n, GROUP_ROWS, HD)[:, 6:7, :]
    facts = jnp.broadcast_to(facts, (n, GROUP_ROWS, HD)).reshape(n * GROUP_ROWS, HD)
    facts = jnp.concatenate([facts] * lq, axis=0)

    def column(kind):
        return jnp.sum(jnp.where(lane == kind * GROUP_ROWS + rs, facts, 0.0), axis=1, keepdims=True)

    first_block, second_block, length = [column(kind) for kind in range(3)]
    scores = dot_t(q_ref[...], kv_ref[:, :HD]) * SCALE
    lane_f = lane.astype(jnp.float32)
    parts = []
    for b in range(NBLK):
        limit = jnp.where(
            first_block == b, length, jnp.where(second_block == b, length - BLOCK_TOKENS, 0.0)
        )
        part = scores[:, b * BLOCK_TOKENS : (b + 1) * BLOCK_TOKENS]
        parts.append(jnp.where(lane_f < limit, part, MASKED))
    scores = jnp.concatenate(parts, axis=1)
    top = jnp.max(scores, axis=1, keepdims=True)
    raised = jnp.exp(scores - top)
    total = jnp.sum(raised, axis=1, keepdims=True)
    near = raised.astype(jnp.bfloat16)
    rest = (raised - near.astype(jnp.float32)).astype(jnp.bfloat16)
    values = kv_ref[:, HD:]
    mixed = (dot(near, values) + dot(rest, values)).reshape(lq * n, GROUP_ROWS, HD)

    def line(col):
        spread = jnp.where(lane == rs, col, 0.0).reshape(lq * n, GROUP_ROWS, HD)
        return jnp.sum(spread, axis=1, keepdims=True)

    rs3 = rs.reshape(lq * n, GROUP_ROWS, HD)
    mixed = jnp.where(rs3 == 6, line(top), jnp.where(rs3 == 7, line(total), mixed))
    for h in range(lq):
        o_ref[:, h * GROUP_ROWS : (h + 1) * GROUP_ROWS, :] = mixed[h * n : (h + 1) * n]


def handed_attention(kv, q_own, msgs, n, lq):
    rows = lq * n * GROUP_ROWS
    vmem = pl.BlockSpec(memory_space=VMEM)
    return pl.pallas_call(
        functools.partial(handed_part, n, lq),
        in_specs=[vmem] * 3,
        out_specs=vmem,
        out_shape=jax.ShapeDtypeStruct((n, lq * GROUP_ROWS, HD), jnp.float32),
        compiler_params=pltpu.CompilerParams(vmem_limit_bytes=32 * MIB),
        cost_estimate=pl.CostEstimate(flops=6 * rows * HD * PTOK, bytes_accessed=2 * MIB, transcendentals=rows * PTOK),
        name="handed_attention",
    )(kv, q_own, msgs)


def owner_part(n, lq, counts, done, placed, table, lens, cache_hbm, held, handed, o_ref, cache, sems, slot_row, slot_limit):
    def slot_copy(slot):
        rows = pl.ds(slot * BLOCK_TOKENS, BLOCK_TOKENS)
        return pltpu.make_async_copy(cache_hbm.at[rows], cache.at[rows], sems.at[slot])

    for slot in range(DEVICE_SLOTS):
        slot_copy(slot).start()
    found = block_of_pages(counts, done, placed, table)
    for r in range(ROWS_DEV):
        for p in range(PAGES):
            slot_row[table[p, r]] = jnp.int32(r)
            slot_limit[table[p, r]] = jnp.where(found[r][p] < 0, lens[r] - p * BLOCK_TOKENS, 0)

    cq = lq * HD
    groups = QH
    rows = groups * GROUP_ROWS
    span = GQ * GROUP_ROWS
    queries, keys = [], []
    for h in range(KVH):
        for hh in range(GQ):
            t, at = row_head(n, lq, h, hh)
            queries.append(held[t * GROUP_ROWS : (t + 1) * GROUP_ROWS, at * HD : (at + 1) * HD])
        t, _ = row_head(n, lq, h, 0)
        keys += [held[t * GROUP_ROWS : (t + 1) * GROUP_ROWS, cq : cq + HD]] * GQ
    queries = jnp.concatenate(queries, axis=0)
    earlier = jnp.concatenate([pltpu.roll(key, ROWS_DEV, 0) for key in keys], axis=0)
    keys = jnp.concatenate(keys, axis=0)
    at_row, lane = iota((rows, HD), 0), iota((rows, HD), 1)
    r = row_of(at_row % GROUP_ROWS)
    rounded = queries.astype(jnp.bfloat16)
    scores = []
    for slot in range(DEVICE_SLOTS):
        slot_copy(slot).wait()
        part = slice(slot * BLOCK_TOKENS, (slot + 1) * BLOCK_TOKENS)
        some = [
            dot_t(rounded[h * span : (h + 1) * span], cache[part, 2 * h * HD : (2 * h + 1) * HD])
            for h in range(KVH)
        ]
        usable = (r == slot_row[slot]) & (lane < slot_limit[slot])
        scores.append(jnp.where(usable, jnp.concatenate(some, axis=0) * SCALE, MASKED))
    scores = jnp.concatenate(scores, axis=1)
    now = jnp.sum(queries * keys, axis=1, keepdims=True) * SCALE
    before = jnp.sum(queries * earlier, axis=1, keepdims=True) * SCALE
    rs1 = iota((rows, 1), 0) % GROUP_ROWS
    before = jnp.where((rs1 >= ROWS_DEV) & (rs1 < STEPS * ROWS_DEV), before, MASKED)

    mixed = handed[...].reshape(groups, GROUP_ROWS, HD)
    shape = (groups, GROUP_ROWS, HD)
    mine = iota(shape, 1) == iota(shape, 2)

    def column(at):
        line = jnp.broadcast_to(mixed[:, at : at + 1, :], shape)
        return jnp.sum(jnp.where(mine, line, 0.0), axis=2, keepdims=True).reshape(rows, 1)

    other_peak, other_total = column(6), column(7)
    peak = jnp.maximum(jnp.max(scores, axis=1, keepdims=True), jnp.maximum(now, before))
    peak = jnp.maximum(peak, other_peak)
    raised, now, before = jnp.exp(scores - peak), jnp.exp(now - peak), jnp.exp(before - peak)
    other = jnp.exp(other_peak - peak)
    inverse = 1.0 / (jnp.sum(raised, axis=1, keepdims=True) + now + before + other * other_total)
    weights = (raised * inverse).astype(jnp.bfloat16)
    now = (now * inverse).astype(jnp.bfloat16).astype(jnp.float32)
    before = (before * inverse).astype(jnp.bfloat16).astype(jnp.float32)
    mixed = mixed.reshape(rows, HD) * (other * inverse)
    out = []
    for h in range(KVH):
        part = slice(h * span, (h + 1) * span)
        own = mixed[part] + dot(weights[part], cache[:, (2 * h + 1) * HD : (2 * h + 2) * HD])
        t, _ = row_head(n, lq, h, 0)
        value = held[t * GROUP_ROWS : (t + 1) * GROUP_ROWS, cq + HD : cq + 2 * HD]
        last = pltpu.roll(value, ROWS_DEV, 0)
        for hh in range(GQ):
            some = slice(h * span + hh * GROUP_ROWS, h * span + (hh + 1) * GROUP_ROWS)
            line = own[hh * GROUP_ROWS : (hh + 1) * GROUP_ROWS]
            out.append(line + now[some] * value + before[some] * last)
    out = jnp.concatenate(out, axis=1)
    for k in range(ROWS_DEV):
        steps = [out[s * ROWS_DEV + k : s * ROWS_DEV + k + 1] for s in range(STEPS)]
        o_ref[k] = jnp.concatenate(steps, axis=0).astype(jnp.bfloat16)


def decode_attention(ints, cache, msgs, parts, n, lq):
    smem, vmem = pl.BlockSpec(memory_space=SMEM), pl.BlockSpec(memory_space=VMEM)
    return pl.pallas_call(
        functools.partial(owner_part, n, lq),
        in_specs=[smem] * 5 + [pl.BlockSpec(memory_space=pl.ANY), vmem, vmem],
        out_specs=vmem,
        out_shape=jax.ShapeDtypeStruct((ROWS_DEV, STEPS, QH * HD), jnp.bfloat16),
        scratch_shapes=[
            VMEM(cache.shape, jnp.bfloat16),
            pltpu.SemaphoreType.DMA((DEVICE_SLOTS,)),
            SMEM((DEVICE_SLOTS,), jnp.int32),
            SMEM((DEVICE_SLOTS,), jnp.int32),
        ],
        compiler_params=pltpu.CompilerParams(vmem_limit_bytes=62 * MIB),
        cost_estimate=pl.CostEstimate(flops=4 * 256 * HD * 768, bytes_accessed=4 * MIB, transcendentals=256 * 768),
        name="decode_attention",
    )(*ints, cache, msgs, parts)


def local(
    prompt_x,
    q_weight,
    kv_weight,
    prompt_blocks,
    finished,
    placement,
    page_table,
    row_lens,
    kv_cache,
    decode_x,
):
    n = lax.axis_size("tp")
    lq = q_weight.shape[1] // HD
    share = GQ // lq
    if share > 1:
        sets = [[k * share + i for i in range(share)] for k in range(n // share)]
        kv_weight = lax.all_gather(kv_weight, "tp", axis=1, tiled=True, axis_index_groups=sets)
    cache = kv_cache.reshape(-1, kv_cache.shape[2])
    dx = decode_x.reshape(-1, decode_x.shape[2])
    placement = placement.transpose(0, 2, 1)
    page_table = page_table.transpose(1, 0)
    ints = (prompt_blocks, finished, placement, page_table, row_lens)
    size = 256
    first = 2 * size
    q, kv, q_own, msgs = project_rows(
        prompt_x, q_weight, kv_weight, 0, first, size, ints=ints, dx=dx, n=n
    )
    msgs = lax.all_to_all(msgs, "tp", split_axis=0, concat_axis=0, tiled=True)
    rest = prompt_x.shape[0] - first
    q, kv = project_rows(prompt_x, q_weight, kv_weight, first, rest, size, held=(q, kv))
    kv_other = lax.ppermute(kv, "pool", [(0, 1), (1, 0)])
    prompt_attn = prompt_attention(prompt_blocks, q, kv, 0)
    handed = handed_attention(kv_other, q_own, msgs, n, lq)
    parts = lax.all_to_all(handed, "tp", split_axis=0, concat_axis=0, tiled=True)
    prompt_attn = prompt_attention(prompt_blocks, q, kv, 1, prompt_attn, handed)
    decode_attn = decode_attention(ints, cache, msgs, parts, n, lq)
    return prompt_attn, decode_attn.transpose(1, 0, 2)


def solution(mesh):
    return jax.shard_map(
        local,
        mesh=mesh,
        in_specs=(
            P(("rep", "pool"), None),
            P(None, "tp"),
            P(None, "tp"),
            P("rep", None),
            P("rep", None),
            P("rep", None, None),
            P(("rep", "pool", "tp"), None),
            P(("rep", "pool", "tp")),
            P(("rep", "pool", "tp"), None, None),
            P(None, ("rep", "pool"), None),
        ),
        out_specs=(P(("rep", "pool"), "tp"), P(None, ("rep", "pool", "tp"), None)),
        check_vma=False,
    )
```

time: 69.4 us -> 80.3 us (1.16)
  blocking collectives: 0 us -> 15.2 us
  Pallas kernels: 48.6 us -> 59.1 us
  starting transfers between devices: 13.4 us -> 4.07 us
  local copies, waits for them, and re-layouts: 6.24 us -> 0.66 us
    all_to_all x0 -> x1, blocking collectives: none -> 15.2 us  [local(): msgs = lax.all_to_all(msgs, 'tp', split_axis=0, concat_axis=0, tiled=True)]
    all_to_all x2 -> x1, starting transfers between devices: 12.8 us -> 3.55 us  [local(): lax.all_to_all(handed, 'tp', split_axis=0, concat_axis=0, tiled=True)]
    pallas_call x3 -> x4, Pallas kernels: 42.6 us -> 51.8 us  [the longest x2 35.4 us: project_rows(): pl.pallas_call(functools.partial(project, n, lq, offset, first), grid=(co...]
    unnamed x21 -> x8, local copies, waits for them, and re-layouts: 6.24 us -> 0.66 us
    pallas_call x1, Pallas kernels: 3.53 us -> 4.96 us  [decode_attention(): pl.pallas_call(functools.partial(owner_part, n, lq), in_specs=[smem] * 5...]
  transfers between devices with their start and end apart: 3 -> 2, of which waited for: 0 -> 0; matrix products, arithmetic and copies ran while one was open for 0% -> 0% of each run, Pallas kernels for 31% -> 20%
where the time goes in v3:
time: 80.3 us; the launch traced here: 80 us
  Pallas kernels  59.1 us (74%)
  blocking collectives  15.2 us (19%)
  starting transfers between devices  4.07 us (5%)
  between operations  0.88 us (1%)
    pallas_call x2, Pallas kernels, project_rows(): pl.pallas_call(functools.partial(project, n, lq, offset, first), grid=(co...  35.4 us
    pallas_call x2, Pallas kernels, prompt_attention(): pl.pallas_call(functools.partial(attend_prompt, cq // HD, half), in_specs...  16.3 us
    all_to_all x1, blocking collectives, local(): msgs = lax.all_to_all(msgs, 'tp', split_axis=0, concat_axis=0, tiled=True)  15.2 us
    pallas_call x1, Pallas kernels, decode_attention(): pl.pallas_call(functools.partial(owner_part, n, lq), in_specs=[smem] * 5...  4.96 us
    all_to_all x1, starting transfers between devices, local(): lax.all_to_all(handed, 'tp', split_axis=0, concat_axis=0, tiled=True)  3.55 us
    pallas_call x1, Pallas kernels, handed_attention(): pl.pallas_call(functools.partial(handed_part, n, lq), in_specs=[vmem] * 3...  2.4 us
  transfers between devices with their start and end apart: 2, of which 0 were waited for; matrix products, arithmetic and copies ran while one was open for 0% of the time, Pallas kernels for 20%

profile of v3, /device:TPU:0, one launch (start us, length us, event | category | flops | bytes accessed | tf_op | source)
XLA Modules:
  0.0 80.0 jit_solution(37515525441876862)
XLA Ops:
  0.6 12.5 %project_first.1 = (bf16[2048,512]{1,0:T(8,128)(2,1)}, bf16[2048,256]{1,0:T(8,128)(2,1)}, bf16[256,128]{1,0:T(8,128)(2,1)}, f32[64,768]{1,0:T(8,128)}) custom-call(s32[2,3]{1,0:T(2,128)} %counts.5, s32[2,3]{1,0:T(2,128)} %done.1, s32[2,2,16]{2,1,0:T(2,128)} %bitcast.13, s32[2,3]{1,0:T(2,128)} %bitcast.15, s32[3]{0:T(128)} %lens.1, ...), custom_call_target="tpu_custom_call" | custom-call | flops 4026531840 | bytes 13893632 | tf_op jit(solution)/shard_map/project_first/pallas_call | solution.py:188
  13.2 0.0 copy-start.3
  13.2 0.0 copy-start.1
  13.2 22.9 %project_rest.1 = (bf16[2048,512]{1,0:T(8,128)(2,1)}, bf16[2048,256]{1,0:T(8,128)(2,1)}) custom-call(bf16[2048,5120]{1,0:T(8,128)(2,1)} %refs_0_.3, bf16[5120,512]{1,0:T(8,128)(2,1)} %refs_1_.3, bf16[5120,256]{1,0:T(8,128)(2,1)} %refs_2_.1, bf16[2048,512]{1,0:T(8,128)(2,1)} %get-tuple-element.8.refs_3_, ...), custom_call_target="tpu_custom_call", output_to_operand_aliasing={{0}: (3, {}), {1}: (4, {})} | custom-call | flops 12079595520 | bytes 25952256 | tf_op jit(solution)/shard_map/project_rest/pallas_call | solution.py:188
  36.1 0.5 collective-permute-start
  36.6 0.0 copy-done.3
  36.6 15.2 %all_to_all.16 = f32[8,8,768]{2,1,0:T(8,128)S(1)} all-to-all(f32[8,8,768]{2,1,0:T(8,128)S(1)} %bitcast.11), channel_id=1, replica_groups=mesh['rep'=2,'pool'=2,'tp'=8] {'tp'}, dimensions={0} | all-to-all | bytes 393216 | tf_op jit(solution)/shard_map/all_to_all | solution.py:483
  51.9 0.0 copy-start
  51.9 0.0 collective-permute-done.kv_ref
  51.9 0.0 copy-done.1
  51.9 2.4 %handed_attention.1.refs_1_ = f32[8,32,128]{2,1,0:T(8,128)} custom-call(bf16[2048,256]{1,0:T(8,128)(2,1)S(1)} %collective-permute-done.kv_ref, bf16[256,128]{1,0:T(8,128)(2,1)S(1)} %copy-done.1, f32[64,768]{1,0:T(8,128)S(1)} %bitcast.7), custom_call_target="tpu_custom_call" | custom-call | flops 402653184 | bytes 2097152 | tf_op jit(solution)/shard_map/handed_attention/pallas_call | solution.py:344
  54.3 3.5 %all-to-all-start.1 = ((f32[8,32,128]{2,1,0:T(8,128)}), f32[8,32,128]{2,1,0:T(8,128)S(1)}, u32[]{:S(2)}, u32[]{:S(2)}) async-start(f32[8,32,128]{2,1,0:T(8,128)} %handed_attention.1.refs_1_), calls=%async_computation.1 | async-start | bytes 262144 | tf_op jit(solution)/shard_map/all_to_all | solution.py:489
  57.8 8.1 %long_prompt.1.refs_0_ = bf16[2048,512]{1,0:T(8,128)(2,1)} custom-call(s32[2,3]{1,0:T(2,128)} %counts.5, bf16[2048,512]{1,0:T(8,128)(2,1)} %get-tuple-element.10.q_hbm, bf16[2048,256]{1,0:T(8,128)(2,1)} %get-tuple-element.11.kv_hbm), custom_call_target="tpu_custom_call" | custom-call | flops 2147483648 | bytes 4194304 | tf_op jit(solution)/shard_map/long_prompt/pallas_call | solution.py:277
  65.9 0.0 copy-done
  66.0 8.2 %short_prompts.1 = bf16[2048,512]{1,0:T(8,128)(2,1)} custom-call(s32[2,3]{1,0:T(2,128)} %counts.5, bf16[2048,512]{1,0:T(8,128)(2,1)} %get-tuple-element.10.q_hbm, bf16[2048,256]{1,0:T(8,128)(2,1)} %get-tuple-element.11.kv_hbm, bf16[2048,512]{1,0:T(8,128)(2,1)} %long_prompt.1.refs_0_, ...), custom_call_target="tpu_custom_call", output_to_operand_aliasing={{}: (3, {})} | custom-call | flops 2147483648 | bytes 4194304 | tf_op jit(solution)/shard_map/short_prompts/pallas_call | solution.py:277
  74.2 0.0 all-to-all-done.1.handed
  74.2 0.0 copy-start.2
  74.2 0.6 copy-done.2
  74.8 5.0 %decode_attention.1 = bf16[3,2,4096]{2,1,0:T(2,128)(2,1)} custom-call(s32[2,3]{1,0:T(2,128)} %counts.5, s32[2,3]{1,0:T(2,128)} %done.1, s32[2,2,16]{2,1,0:T(2,128)} %bitcast.14, s32[2,3]{1,0:T(2,128)} %bitcast.16, s32[3]{0:T(128)} %lens.1, bf16[768,2048]{1,0:T(8,128)(2,1)} %bitcast.9, f32[64,768]{1,0:T(8,128)} %bitcast.8, f32[8,32,128]{2,1,0:T(8,128)} %copy-done.2), custom_call_target="tpu_custom_call" | custom-call | flops 100663296 | bytes 4194304 | tf_op jit(solution)/shard_map/decode_attention/pallas_call | solution.py:438
Async XLA Ops:
  13.2 23.5 %copy-start.3 = (f32[64,768]{1,0:T(8,128)S(1)}, f32[64,768]{1,0:T(8,128)}, u32[]{:S(2)}) copy-start(f32[64,768]{1,0:T(8,128)} %get-tuple-element.13) | copy-start | bytes 589828
  13.2 38.7 %copy-start.1 = (bf16[256,128]{1,0:T(8,128)(2,1)S(1)}, bf16[256,128]{1,0:T(8,128)(2,1)}, u32[]{:S(2)}) copy-start(bf16[256,128]{1,0:T(8,128)(2,1)} %get-tuple-element.12.q_ref) | copy-start | bytes 196612
  36.1 15.8 %collective-permute-start = (bf16[2048,256]{1,0:T(8,128)(2,1)}, bf16[2048,256]{1,0:T(8,128)(2,1)S(1)}, u32[]{:S(2)}, u32[]{:S(2)}) collective-permute-start(bf16[2048,256]{1,0:T(8,128)(2,1)} %get-tuple-element.11.kv_hbm), channel_id=1, source_target_pairs={{0,8},{8,0},{1,9},{9,1},{2,10},{10,2},{3,11},{11,3},{4,12},{12,4},... | collective-permute-start | bytes 3145736 | tf_op jit(solution)/shard_map/ppermute | solution.py:486
  51.9 14.1 %copy-start = (f32[8,8,768]{2,1,0:T(8,128)}, f32[8,8,768]{2,1,0:T(8,128)S(1)}, u32[]{:S(2)}) copy-start(f32[8,8,768]{2,1,0:T(8,128)S(1)} %all_to_all.16) | copy-start | bytes 589828
  54.3 19.9 %all-to-all-start.1 = ((f32[8,32,128]{2,1,0:T(8,128)}), f32[8,32,128]{2,1,0:T(8,128)S(1)}, u32[]{:S(2)}, u32[]{:S(2)}) async-start(f32[8,32,128]{2,1,0:T(8,128)} %handed_attention.1.refs_1_), calls=%async_computation.1 | async-start | bytes 262144 | tf_op jit(solution)/shard_map/all_to_all | solution.py:489
  74.2 0.7 copy-start.2

commit v4 on v3

--- a/solution.py
+++ b/solution.py
@@ -25,6 +25,7 @@
 SCALE = HD ** (-0.5)
 MASKED = -1e30
 PIECES = 5
+STRIPS = 4
 MIB = 1 << 20
 VMEM = pltpu.VMEM
 SMEM = pltpu.SMEM
@@ -70,142 +71,146 @@
     return out
 
 
-def project(n, lq, start, with_decode, *refs):
-    refs = list(refs)
-    if with_decode:
-        counts, done, placed, table, lens, dx_ref = refs[:6]
-        x_hbm, wq_hbm, wkv_hbm, q_ref, kv_ref, qh_ref, msg_ref = refs[6:13]
-        del refs[:13]
-    else:
-        x_hbm, wq_hbm, wkv_hbm, _, _, q_ref, kv_ref = refs[:7]
-        del refs[:7]
-    xs, w, x_sems, w_sems = refs
-    size, depth = xs.shape[1:]
+def project(n, lq, first, size, *refs):
+    counts, done, placed, table, lens, dx_hbm, x_hbm, wq_hbm, wkv_hbm = refs[:9]
+    q_hbm, kv_hbm, qh_ref, msg_ref = refs[9:13]
+    x0, xs, w, q_out, kv_out, x_sems, w_sems, out_sems = refs[13:]
+    depth = w.shape[0]
+    count = xs.shape[0]
     cq = lq * HD
     piece = depth // PIECES
-    step, steps = pl.program_id(0), pl.num_programs(0)
-    slot = lax.rem(step, 2)
-
-    def w_copies(c):
+    own_rows = dx_hbm.shape[0]
+    step = pl.program_id(0)
+
+    def piece_copies(c):
         part = pl.ds(c * piece, piece)
         return [
-            pltpu.make_async_copy(wq_hbm.at[part], w.at[part, pl.ds(0, cq)], w_sems.at[0, c]),
-            pltpu.make_async_copy(wkv_hbm.at[part], w.at[part, pl.ds(cq, 2 * HD)], w_sems.at[1, c]),
+            pltpu.make_async_copy(x_hbm.at[pl.ds(0, first), part], x0.at[pl.ds(0, first), part], w_sems.at[0, c]),
+            pltpu.make_async_copy(dx_hbm.at[:, part], x0.at[pl.ds(first, own_rows), part], w_sems.at[1, c]),
+            pltpu.make_async_copy(wq_hbm.at[part], w.at[part, pl.ds(0, cq)], w_sems.at[2, c]),
+            pltpu.make_async_copy(wkv_hbm.at[part], w.at[part, pl.ds(cq, 2 * HD)], w_sems.at[3, c]),
         ]
 
-    def x_copy(at, c):
-        rows = pl.ds(pl.multiple_of((start + at) * size, size), size)
-        cols = pl.ds(c * piece, piece)
-        to = lax.rem(at, 2)
-        return pltpu.make_async_copy(x_hbm.at[rows, cols], xs.at[to, :, cols], x_sems.at[to, c])
+    def x_copies(k):
+        strip = size // STRIPS
+        copies = []
+        for i in range(STRIPS):
+            rows = pl.ds(pl.multiple_of(first + k * size + i * strip, 16), strip)
+            copies.append(
+                pltpu.make_async_copy(x_hbm.at[rows], xs.at[k, pl.ds(i * strip, strip)], x_sems.at[k, i])
+            )
+        return copies
+
+    def out_copies(k):
+        if isinstance(k, int):
+            rows = pl.ds(0, first)
+        else:
+            rows = pl.ds(pl.multiple_of(first + (k - 1) * size, BLOCK_TOKENS), size)
+        return [
+            pltpu.make_async_copy(q_out.at[rows], q_hbm.at[rows], out_sems.at[0, k]),
+            pltpu.make_async_copy(kv_out.at[rows], kv_hbm.at[rows], out_sems.at[1, k]),
+        ]
+
+    def keep(total, rows):
+        q_out[rows, :] = total[:, :cq].astype(jnp.bfloat16)
+        kv_out[rows, :] = total[:, cq:].astype(jnp.bfloat16)
 
     @pl.when(step == 0)
     def _():
         for c in range(PIECES):
-            x_copy(step, c).start()
-            for copy in w_copies(c):
+            for copy in piece_copies(c):
                 copy.start()
-
-    @pl.when(step + 1 < steps)
+        for k in range(count):
+            for copy in x_copies(k):
+                copy.start()
+        total = 0.0
+        for c in range(PIECES):
+            for copy in piece_copies(c):
+                copy.wait()
+            part = slice(c * piece, (c + 1) * piece)
+            total += dot(x0[:, part], w[part, :])
+        keep(total[:first], pl.ds(0, first))
+        for copy in out_copies(0):
+            copy.start()
+        shape = (n * GROUP_ROWS, own_rows)
+        to, fro = iota(shape, 0), iota(shape, 1)
+        owner, rs = to // GROUP_ROWS, to % GROUP_ROWS
+        wanted = owner * ROWS_DEV + row_of(rs) + jnp.where(rs >= ROWS_DEV, ROWS_DEV * n, 0)
+        pick = ((fro == wanted) & (rs < STEPS * ROWS_DEV)).astype(jnp.float32).astype(jnp.bfloat16)
+        own = dot(pick, total[first:].astype(jnp.bfloat16))
+        for h in range(lq):
+            part = slice(h * n * GROUP_ROWS, (h + 1) * n * GROUP_ROWS)
+            qh_ref[part, :] = own[:, h * HD : (h + 1) * HD].astype(jnp.bfloat16)
+        found = block_of_pages(counts, done, placed, table)
+        lane = iota((n * GROUP_ROWS, HD), 1)
+        r = row_of(lane % GROUP_ROWS)
+        kind = lane // GROUP_ROWS
+        facts = jnp.where(
+            kind == 0,
+            by_row(r, [found[i][0] for i in range(ROWS_DEV)], -1),
+            jnp.where(
+                kind == 1,
+                by_row(r, [found[i][1] for i in range(ROWS_DEV)], -1),
+                by_row(r, [lens[i] for i in range(ROWS_DEV)], 0),
+            ),
+        ).astype(jnp.float32)
+        sixth = iota((n * GROUP_ROWS, HD), 0) % GROUP_ROWS == 6
+        msg_ref[:, :HD] = jnp.where(sixth, facts, own[:, :HD])
+        msg_ref[:, HD:] = own[:, HD:]
+
+    @pl.when(step > 0)
     def _():
-        for c in range(PIECES):
-            x_copy(step + 1, c).start()
-
-    total = 0.0
-    for c in range(PIECES):
-        x_copy(step, c).wait()
-
-        @pl.when(step == 0)
-        def _(c=c):
-            for copy in w_copies(c):
+        for copy in x_copies(step - 1):
+            copy.wait()
+        keep(dot(xs[step - 1], w[...]), pl.ds(pl.multiple_of(first + (step - 1) * size, BLOCK_TOKENS), size))
+        for copy in out_copies(step):
+            copy.start()
+
+    @pl.when(step == count)
+    def _():
+        for copy in out_copies(0):
+            copy.wait()
+        for k in range(1, count + 1):
+            for copy in out_copies(jnp.int32(k)):
                 copy.wait()
 
-        part = slice(c * piece, (c + 1) * piece)
-        total += dot(xs[slot, :, part], w[part, :])
-    q_ref[...] = total[:, :cq].astype(jnp.bfloat16)
-    kv_ref[...] = total[:, cq:].astype(jnp.bfloat16)
-    if with_decode:
-
-        @pl.when(step == 0)
-        def _():
-            rows = STEPS * ROWS_DEV * n
-            shape = (n * GROUP_ROWS, rows)
-            to, fro = iota(shape, 0), iota(shape, 1)
-            owner, rs = to // GROUP_ROWS, to % GROUP_ROWS
-            wanted = owner * ROWS_DEV + row_of(rs) + jnp.where(rs >= ROWS_DEV, ROWS_DEV * n, 0)
-            pick = ((fro == wanted) & (rs < STEPS * ROWS_DEV)).astype(jnp.float32).astype(jnp.bfloat16)
-            own = dot(pick, dot(dx_ref[...], w[...]).astype(jnp.bfloat16))
-            for h in range(lq):
-                part = slice(h * n * GROUP_ROWS, (h + 1) * n * GROUP_ROWS)
-                qh_ref[part, :] = own[:, h * HD : (h + 1) * HD].astype(jnp.bfloat16)
-            found = block_of_pages(counts, done, placed, table)
-            lane = iota((n * GROUP_ROWS, HD), 1)
-            r = row_of(lane % GROUP_ROWS)
-            kind = lane // GROUP_ROWS
-            facts = jnp.where(
-                kind == 0,
-                by_row(r, [found[i][0] for i in range(ROWS_DEV)], -1),
-                jnp.where(
-                    kind == 1,
-                    by_row(r, [found[i][1] for i in range(ROWS_DEV)], -1),
-                    by_row(r, [lens[i] for i in range(ROWS_DEV)], 0),
-                ),
-            ).astype(jnp.float32)
-            sixth = iota((n * GROUP_ROWS, HD), 0) % GROUP_ROWS == 6
-            msg_ref[:, :HD] = jnp.where(sixth, facts, own[:, :HD])
-            msg_ref[:, HD:] = own[:, HD:]
-
-
-def project_rows(x, wq, wkv, start, count, size, held=None, ints=None, dx=None, n=None):
+
+def project_all(ints, dx, x, wq, wkv, n, first, size):
     rows, depth = x.shape
     cq, ckv = wq.shape[1], wkv.shape[1]
     lq = cq // HD
-    first = held is None
-    offset = start // size
+    count = (rows - first) // size
     smem, vmem = pl.BlockSpec(memory_space=SMEM), pl.BlockSpec(memory_space=VMEM)
     hbm = pl.BlockSpec(memory_space=pl.ANY)
-    out_shape = [
-        jax.ShapeDtypeStruct((rows, cq), jnp.bfloat16),
-        jax.ShapeDtypeStruct((rows, ckv), jnp.bfloat16),
-    ]
-    out_specs = [
-        pl.BlockSpec((size, cq), lambda i: (i + offset, 0)),
-        pl.BlockSpec((size, ckv), lambda i: (i + offset, 0)),
-    ]
-    if first:
-        args = tuple(ints) + (dx, x, wq, wkv)
-        in_specs = [smem] * 5 + [vmem] + [hbm] * 3
-        out_shape += [
+    return pl.pallas_call(
+        functools.partial(project, n, lq, first, size),
+        grid=(1 + count,),
+        in_specs=[smem] * 5 + [hbm] * 4,
+        out_specs=[hbm, hbm, vmem, vmem],
+        out_shape=[
+            jax.ShapeDtypeStruct((rows, cq), jnp.bfloat16),
+            jax.ShapeDtypeStruct((rows, ckv), jnp.bfloat16),
             jax.ShapeDtypeStruct((lq * n * GROUP_ROWS, HD), jnp.bfloat16),
             jax.ShapeDtypeStruct((n * GROUP_ROWS, cq + ckv), jnp.float32),
-        ]
-        out_specs += [vmem, vmem]
-        aliases = {}
-    else:
-        args = (x, wq, wkv) + held
-        in_specs = [hbm] * 5
-        aliases = {3: 0, 4: 1}
-    return pl.pallas_call(
-        functools.partial(project, n, lq, offset, first),
-        grid=(count // size,),
-        in_specs=in_specs,
-        out_specs=out_specs,
-        out_shape=out_shape,
+        ],
         scratch_shapes=[
-            VMEM((2, size, depth), jnp.bfloat16),
+            VMEM((first + dx.shape[0], depth), jnp.bfloat16),
+            VMEM((count, size, depth), jnp.bfloat16),
             VMEM((depth, cq + ckv), jnp.bfloat16),
-            pltpu.SemaphoreType.DMA((2, PIECES)),
-            pltpu.SemaphoreType.DMA((2, PIECES)),
+            VMEM((rows, cq), jnp.bfloat16),
+            VMEM((rows, ckv), jnp.bfloat16),
+            pltpu.SemaphoreType.DMA((count, STRIPS)),
+            pltpu.SemaphoreType.DMA((4, PIECES)),
+            pltpu.SemaphoreType.DMA((2, count + 1)),
         ],
-        input_output_aliases=aliases,
         compiler_params=pltpu.CompilerParams(vmem_limit_bytes=62 * MIB),
         cost_estimate=pl.CostEstimate(
-            flops=2 * count * depth * (cq + ckv),
-            bytes_accessed=2 * (count + cq + ckv) * depth + 2 * count * (cq + ckv),
+            flops=2 * rows * depth * (cq + ckv),
+            bytes_accessed=2 * (rows + cq + ckv) * depth + 2 * rows * (cq + ckv),
             transcendentals=0,
         ),
-        name="project_first" if first else "project_rest",
-    )(*args)
+        name="project",
+    )(*ints, dx, x, wq, wkv)
 
 
 LOG2E = 1.4426950408889634
@@ -213,7 +218,8 @@
 
 
 def attend_prompt(lq, half, counts, q_hbm, kv_hbm, *refs):
-    o_hbm, qs, kvs, outs, sems = refs[-5:]
+    o_hbm, done_ref, qs, kvs, outs, sems = refs[-6:]
+    done_ref[...] = jnp.zeros_like(done_ref)
     group = lax.axis_index("pool")
     c0, c1 = counts[group, 0], counts[group, 1]
     big = jnp.where(c0 == MOST_BLOCKS, 0, jnp.where(c1 == MOST_BLOCKS, c0, c0 + c1))
@@ -224,19 +230,15 @@
         block = big + j if half == 0 else j + jnp.where(j >= big, MOST_BLOCKS, 0)
         rows = pl.ds(pl.multiple_of(block * BLOCK_TOKENS, BLOCK_TOKENS), BLOCK_TOKENS)
         here = pl.ds(j * BLOCK_TOKENS, BLOCK_TOKENS)
-        loads.append(
-            (
-                pltpu.make_async_copy(kv_hbm.at[rows], kvs.at[here], sems.at[0, j]),
-                pltpu.make_async_copy(q_hbm.at[rows], qs.at[here], sems.at[1, j]),
-            )
-        )
+        loads.append(pltpu.make_async_copy(kv_hbm.at[rows], kvs.at[here], sems.at[0, j]))
+        loads.append(pltpu.make_async_copy(q_hbm.at[rows], qs.at[here], sems.at[1, j]))
         stores.append(pltpu.make_async_copy(outs.at[here], o_hbm.at[rows], sems.at[2, j]))
-        for copy in loads[j]:
-            copy.start()
+    for copy in loads:
+        copy.start()
+    for copy in loads:
+        copy.wait()
 
     def scores_of(j):
-        for copy in loads[j]:
-            copy.wait()
         q = qs[j * BLOCK_TOKENS : (j + 1) * BLOCK_TOKENS, :]
         q = jnp.concatenate([q[:, h * HD : (h + 1) * HD] for h in range(lq)], axis=0)
         return dot_t(q, kvs[: (j + 1) * BLOCK_TOKENS, :HD])
@@ -263,8 +265,9 @@
         for h in range(lq):
             part = mixed[h * BLOCK_TOKENS : (h + 1) * BLOCK_TOKENS]
             outs[j * BLOCK_TOKENS : (j + 1) * BLOCK_TOKENS, h * HD : (h + 1) * HD] = part.astype(jnp.bfloat16)
-        stores[j].start()
         scores = later
+    for copy in stores:
+        copy.start()
     for copy in stores:
         copy.wait()
 
@@ -277,8 +280,11 @@
     return pl.pallas_call(
         functools.partial(attend_prompt, cq // HD, half),
         in_specs=[pl.BlockSpec(memory_space=SMEM), hbm, hbm] + [hbm] * len(more),
-        out_specs=hbm,
-        out_shape=jax.ShapeDtypeStruct((rows, cq), jnp.bfloat16),
+        out_specs=[hbm, pl.BlockSpec(memory_space=VMEM)],
+        out_shape=[
+            jax.ShapeDtypeStruct((rows, cq), jnp.bfloat16),
+            jax.ShapeDtypeStruct((8, HD), jnp.float32),
+        ],
         scratch_shapes=[
             VMEM((tokens, cq), jnp.bfloat16),
             VMEM((tokens, 2 * HD), jnp.bfloat16),
@@ -297,7 +303,7 @@
     return at // lq, at % lq
 
 
-def handed_part(n, lq, kv_ref, q_ref, msg_ref, o_ref):
+def handed_part(n, lq, kv_ref, q_ref, msg_ref, _, o_ref):
     rows = lq * n * GROUP_ROWS
     shape = (rows, HD)
     at_row, lane = iota(shape, 0), iota(shape, 1)
@@ -338,27 +344,23 @@
         o_ref[:, h * GROUP_ROWS : (h + 1) * GROUP_ROWS, :] = mixed[h * n : (h + 1) * n]
 
 
-def handed_attention(kv, q_own, msgs, n, lq):
+def handed_attention(kv, q_own, msgs, after, n, lq):
     rows = lq * n * GROUP_ROWS
     vmem = pl.BlockSpec(memory_space=VMEM)
     return pl.pallas_call(
         functools.partial(handed_part, n, lq),
-        in_specs=[vmem] * 3,
+        in_specs=[vmem] * 3 + [pl.BlockSpec(memory_space=pl.ANY)],
         out_specs=vmem,
         out_shape=jax.ShapeDtypeStruct((n, lq * GROUP_ROWS, HD), jnp.float32),
-        compiler_params=pltpu.CompilerParams(vmem_limit_bytes=32 * MIB),
+        compiler_params=pltpu.CompilerParams(vmem_limit_bytes=24 * MIB),
         cost_estimate=pl.CostEstimate(flops=6 * rows * HD * PTOK, bytes_accessed=2 * MIB, transcendentals=rows * PTOK),
         name="handed_attention",
-    )(kv, q_own, msgs)
-
-
-def owner_part(n, lq, counts, done, placed, table, lens, cache_hbm, held, handed, o_ref, cache, sems, slot_row, slot_limit):
-    def slot_copy(slot):
-        rows = pl.ds(slot * BLOCK_TOKENS, BLOCK_TOKENS)
-        return pltpu.make_async_copy(cache_hbm.at[rows], cache.at[rows], sems.at[slot])
-
-    for slot in range(DEVICE_SLOTS):
-        slot_copy(slot).start()
+    )(kv, q_own, msgs, after)
+
+
+def owner_part(n, lq, counts, done, placed, table, lens, cache_hbm, held, handed, o_ref, cache, sem, slot_row, slot_limit):
+    load = pltpu.make_async_copy(cache_hbm, cache, sem)
+    load.start()
     found = block_of_pages(counts, done, placed, table)
     for r in range(ROWS_DEV):
         for p in range(PAGES):
@@ -382,19 +384,19 @@
     at_row, lane = iota((rows, HD), 0), iota((rows, HD), 1)
     r = row_of(at_row % GROUP_ROWS)
     rounded = queries.astype(jnp.bfloat16)
-    scores = []
-    for slot in range(DEVICE_SLOTS):
-        slot_copy(slot).wait()
-        part = slice(slot * BLOCK_TOKENS, (slot + 1) * BLOCK_TOKENS)
-        some = [
-            dot_t(rounded[h * span : (h + 1) * span], cache[part, 2 * h * HD : (2 * h + 1) * HD])
-            for h in range(KVH)
-        ]
-        usable = (r == slot_row[slot]) & (lane < slot_limit[slot])
-        scores.append(jnp.where(usable, jnp.concatenate(some, axis=0) * SCALE, MASKED))
-    scores = jnp.concatenate(scores, axis=1)
     now = jnp.sum(queries * keys, axis=1, keepdims=True) * SCALE
     before = jnp.sum(queries * earlier, axis=1, keepdims=True) * SCALE
+    load.wait()
+    scores = jnp.concatenate(
+        [dot_t(rounded[h * span : (h + 1) * span], cache[:, 2 * h * HD : (2 * h + 1) * HD]) for h in range(KVH)],
+        axis=0,
+    )
+    parts = []
+    for slot in range(DEVICE_SLOTS):
+        part = scores[:, slot * BLOCK_TOKENS : (slot + 1) * BLOCK_TOKENS]
+        usable = (r == slot_row[slot]) & (lane < slot_limit[slot])
+        parts.append(jnp.where(usable, part * SCALE, MASKED))
+    scores = jnp.concatenate(parts, axis=1)
     rs1 = iota((rows, 1), 0) % GROUP_ROWS
     before = jnp.where((rs1 >= ROWS_DEV) & (rs1 < STEPS * ROWS_DEV), before, MASKED)
 
@@ -442,7 +444,7 @@
         out_shape=jax.ShapeDtypeStruct((ROWS_DEV, STEPS, QH * HD), jnp.bfloat16),
         scratch_shapes=[
             VMEM(cache.shape, jnp.bfloat16),
-            pltpu.SemaphoreType.DMA((DEVICE_SLOTS,)),
+            pltpu.SemaphoreType.DMA,
             SMEM((DEVICE_SLOTS,), jnp.int32),
             SMEM((DEVICE_SLOTS,), jnp.int32),
         ],
@@ -475,19 +477,14 @@
     placement = placement.transpose(0, 2, 1)
     page_table = page_table.transpose(1, 0)
     ints = (prompt_blocks, finished, placement, page_table, row_lens)
-    size = 256
-    first = 2 * size
-    q, kv, q_own, msgs = project_rows(
-        prompt_x, q_weight, kv_weight, 0, first, size, ints=ints, dx=dx, n=n
-    )
+    first, size = 256, 896
+    q, kv, q_own, msgs = project_all(ints, dx, prompt_x, q_weight, kv_weight, n, first, size)
     msgs = lax.all_to_all(msgs, "tp", split_axis=0, concat_axis=0, tiled=True)
-    rest = prompt_x.shape[0] - first
-    q, kv = project_rows(prompt_x, q_weight, kv_weight, first, rest, size, held=(q, kv))
     kv_other = lax.ppermute(kv, "pool", [(0, 1), (1, 0)])
-    prompt_attn = prompt_attention(prompt_blocks, q, kv, 0)
-    handed = handed_attention(kv_other, q_own, msgs, n, lq)
+    prompt_attn, made = prompt_attention(prompt_blocks, q, kv, 0)
+    handed = handed_attention(kv_other, q_own, msgs, made, n, lq)
     parts = lax.all_to_all(handed, "tp", split_axis=0, concat_axis=0, tiled=True)
-    prompt_attn = prompt_attention(prompt_blocks, q, kv, 1, prompt_attn, handed)
+    prompt_attn, _ = prompt_attention(prompt_blocks, q, kv, 1, prompt_attn, handed)
     decode_attn = decode_attention(ints, cache, msgs, parts, n, lq)
     return prompt_attn, decode_attn.transpose(1, 0, 2)
 

time: 80.3 us -> 66.1 us (0.82)
  blocking collectives: 15.2 us -> 0 us
  Pallas kernels: 59.1 us -> 49.9 us
  starting transfers between devices: 4.07 us -> 12.6 us
  waiting for transfers between devices: 0.01 us -> 0.86 us
    all_to_all x1 -> x0, blocking collectives: 15.2 us -> none  [local(): msgs = lax.all_to_all(msgs, 'tp', split_axis=0, concat_axis=0, tiled=True)]
    pallas_call x2 -> x1, Pallas kernels: 35.4 us -> 27.1 us  [project_all(): pl.pallas_call(functools.partial(project, n, lq, first, size), grid=(1 +...]
    all_to_all x0 -> x1, starting transfers between devices: none -> 6.85 us  [local(): msgs = lax.all_to_all(msgs, 'tp', split_axis=0, concat_axis=0, tiled=True)]
    all_to_all x1, starting transfers between devices: 3.55 us -> 5.18 us  [local(): lax.all_to_all(handed, 'tp', split_axis=0, concat_axis=0, tiled=True)]
    all_to_all x0 -> x1, waiting for transfers between devices: none -> 0.85 us  [local(): msgs = lax.all_to_all(msgs, 'tp', split_axis=0, concat_axis=0, tiled=True)]
  transfers between devices with their start and end apart: 2 -> 3, of which waited for: 0 -> 1; matrix products, arithmetic and copies ran while one was open for 0% -> 0% of each run, Pallas kernels for 20% -> 24%
where the time goes in v4:
time: 66.1 us; the launch traced here: 65.5 us
  Pallas kernels  49.9 us (75%)
  starting transfers between devices  12.6 us (19%)
  local copies, waits for them, and re-layouts  1.34 us (2%)
  waiting for transfers between devices  0.86 us (1%)
  between operations  0.86 us (1%)
    pallas_call x1, Pallas kernels, project_all(): pl.pallas_call(functools.partial(project, n, lq, first, size), grid=(1 +...  27.1 us
    pallas_call x2, Pallas kernels, prompt_attention(): pl.pallas_call(functools.partial(attend_prompt, cq // HD, half), in_specs...  15.6 us
    all_to_all x1, starting transfers between devices, local(): msgs = lax.all_to_all(msgs, 'tp', split_axis=0, concat_axis=0, tiled=True)  6.85 us
    all_to_all x1, starting transfers between devices, local(): lax.all_to_all(handed, 'tp', split_axis=0, concat_axis=0, tiled=True)  5.18 us
    pallas_call x1, Pallas kernels, decode_attention(): pl.pallas_call(functools.partial(owner_part, n, lq), in_specs=[smem] * 5...  4.84 us
    pallas_call x1, Pallas kernels, handed_attention(): pl.pallas_call(functools.partial(handed_part, n, lq), in_specs=[vmem] * 3...  2.39 us
    unnamed x8, local copies, waits for them, and re-layouts  1.34 us
  transfers between devices with their start and end apart: 3, of which 1 were waited for; matrix products, arithmetic and copies ran while one was open for 0% of the time, Pallas kernels for 24%

profile of v4, /device:TPU:0, one launch (start us, length us, event | category | flops | bytes accessed | tf_op | source)
XLA Modules:
  0.0 65.5 jit_solution(10721517295291515205)
XLA Ops:
  0.6 27.1 %project.1 = (bf16[2048,512]{1,0:T(8,128)(2,1)}, bf16[2048,256]{1,0:T(8,128)(2,1)}, bf16[256,128]{1,0:T(8,128)(2,1)}, f32[64,768]{1,0:T(8,128)}) custom-call(s32[2,3]{1,0:T(2,128)} %counts.5, s32[2,3]{1,0:T(2,128)} %done.1, s32[2,2,16]{2,1,0:T(2,128)} %bitcast.12, s32[2,3]{1,0:T(2,128)} %bitcast.14, s32[3]{0:T(128)} %lens.1, bf16[48,5120]{1,0:T(8,128)(2,1)} %bitcast.16, ...), custom_call_target="tpu_custom_call" | custom-call | flops 16106127360 | bytes 31981568 | tf_op jit(solution)/shard_map/project/pallas_call | solution.py:185
  27.7 0.5 collective-permute-start
  28.3 6.8 %all-to-all-start = ((f32[8,8,768]{2,1,0:T(8,128)}), f32[8,8,768]{2,1,0:T(8,128)S(1)}, u32[]{:S(2)}, u32[]{:S(2)}) async-start(f32[8,8,768]{2,1,0:T(8,128)} %bitcast.10), calls=%async_computation | async-start | bytes 393216 | tf_op jit(solution)/shard_map/all_to_all | solution.py:482
  35.1 0.0 copy-start.1
  35.1 7.7 %long_prompt.1 = (bf16[2048,512]{1,0:T(8,128)(2,1)}, f32[8,128]{1,0:T(8,128)}) custom-call(s32[2,3]{1,0:T(2,128)} %counts.5, bf16[2048,512]{1,0:T(8,128)(2,1)} %get-tuple-element.9.q_hbm, bf16[2048,256]{1,0:T(8,128)(2,1)} %get-tuple-element.10.kv_hbm), custom_call_target="tpu_custom_call" | custom-call | flops 2147483648 | bytes 4194304 | tf_op jit(solution)/shard_map/long_prompt/pallas_call | solution.py:280
  42.9 0.8 %all-to-all-done = f32[8,8,768]{2,1,0:T(8,128)S(1)} async-done(((f32[8,8,768]{2,1,0:T(8,128)}), f32[8,8,768]{2,1,0:T(8,128)S(1)}, u32[]{:S(2)}, u32[]{:S(2)}) %all-to-all-start) | async-done | bytes 196640 | tf_op jit(solution)/shard_map/all_to_all | solution.py:482
  43.7 0.0 copy-start
  43.7 0.0 collective-permute-done.kv_ref
  43.7 0.0 copy-done.1
  43.7 0.0 copy-start.2
  43.7 0.7 %copy-done.2 = f32[8,128]{1,0:T(8,128)S(1)} copy-done((f32[8,128]{1,0:T(8,128)S(1)}, f32[8,128]{1,0:T(8,128)}, u32[]{:S(2)}) %copy-start.2) | copy-done | bytes 4120
  44.4 2.4 %handed_attention.1.refs_1_ = f32[8,32,128]{2,1,0:T(8,128)} custom-call(bf16[2048,256]{1,0:T(8,128)(2,1)S(1)} %collective-permute-done.kv_ref, bf16[256,128]{1,0:T(8,128)(2,1)S(1)} %copy-done.1, f32[64,768]{1,0:T(8,128)S(1)} %bitcast.7, f32[8,128]{1,0:T(8,128)S(1)} %copy-done.2), custom_call_target="tpu_custom_call" | custom-call | flops 402653184 | bytes 2097152 | tf_op jit(solution)/shard_map/handed_attention/pallas_call | solution.py:350
  46.8 5.2 %all-to-all-start.1 = ((f32[8,32,128]{2,1,0:T(8,128)}), f32[8,32,128]{2,1,0:T(8,128)S(1)}, u32[]{:S(2)}, u32[]{:S(2)}) async-start(f32[8,32,128]{2,1,0:T(8,128)} %handed_attention.1.refs_1_), calls=%async_computation.1 | async-start | bytes 262144 | tf_op jit(solution)/shard_map/all_to_all | solution.py:486
  52.0 7.9 %short_prompts.1 = (bf16[2048,512]{1,0:T(8,128)(2,1)}, f32[8,128]{1,0:T(8,128)}) custom-call(s32[2,3]{1,0:T(2,128)} %counts.5, bf16[2048,512]{1,0:T(8,128)(2,1)} %get-tuple-element.9.q_hbm, bf16[2048,256]{1,0:T(8,128)(2,1)} %get-tuple-element.10.kv_hbm, bf16[2048,512]{1,0:T(8,128)(2,1)} %get-tuple-element.11.refs_0_, ...), custom_call_target="tpu_custom_call", output_to_operand_aliasing={{0}: (3, {})} | custom-call | flops 2147483648 | bytes 4194304 | tf_op jit(solution)/shard_map/short_prompts/pallas_call | solution.py:280
  59.9 0.0 copy-done
  59.9 0.0 all-to-all-done.1.handed
  59.9 0.0 copy-start.3
  59.9 0.6 copy-done.3
  60.5 4.8 %decode_attention.1 = bf16[3,2,4096]{2,1,0:T(2,128)(2,1)} custom-call(s32[2,3]{1,0:T(2,128)} %counts.5, s32[2,3]{1,0:T(2,128)} %done.1, s32[2,2,16]{2,1,0:T(2,128)} %bitcast.13, s32[2,3]{1,0:T(2,128)} %bitcast.15, s32[3]{0:T(128)} %lens.1, bf16[768,2048]{1,0:T(8,128)(2,1)} %bitcast.9, f32[64,768]{1,0:T(8,128)} %bitcast.8, f32[8,32,128]{2,1,0:T(8,128)} %copy-done.3), custom_call_target="tpu_custom_call" | custom-call | flops 100663296 | bytes 4194304 | tf_op jit(solution)/shard_map/decode_attention/pallas_call | solution.py:440
Async XLA Ops:
  27.7 16.0 %collective-permute-start = (bf16[2048,256]{1,0:T(8,128)(2,1)}, bf16[2048,256]{1,0:T(8,128)(2,1)S(1)}, u32[]{:S(2)}, u32[]{:S(2)}) collective-permute-start(bf16[2048,256]{1,0:T(8,128)(2,1)} %get-tuple-element.10.kv_hbm), channel_id=1, source_target_pairs={{0,8},{8,0},{1,9},{9,1},{2,10},{10,2},{3,11},{11,3},{4,12},{12,4},... | collective-permute-start | bytes 3145736 | tf_op jit(solution)/shard_map/ppermute | solution.py:483
  28.3 15.5 %all-to-all-start = ((f32[8,8,768]{2,1,0:T(8,128)}), f32[8,8,768]{2,1,0:T(8,128)S(1)}, u32[]{:S(2)}, u32[]{:S(2)}) async-start(f32[8,8,768]{2,1,0:T(8,128)} %bitcast.10), calls=%async_computation | async-start | bytes 393216 | tf_op jit(solution)/shard_map/all_to_all | solution.py:482
  35.1 8.6 %copy-start.1 = (bf16[256,128]{1,0:T(8,128)(2,1)S(1)}, bf16[256,128]{1,0:T(8,128)(2,1)}, u32[]{:S(2)}) copy-start(bf16[256,128]{1,0:T(8,128)(2,1)} %get-tuple-element.12.q_ref) | copy-start | bytes 196612
  43.7 16.2 %copy-start = (f32[8,8,768]{2,1,0:T(8,128)}, f32[8,8,768]{2,1,0:T(8,128)S(1)}, u32[]{:S(2)}) copy-start(f32[8,8,768]{2,1,0:T(8,128)S(1)} %all-to-all-done) | copy-start | bytes 589828
  43.7 0.7 %copy-start.2 = (f32[8,128]{1,0:T(8,128)S(1)}, f32[8,128]{1,0:T(8,128)}, u32[]{:S(2)}) copy-start(f32[8,128]{1,0:T(8,128)} %get-tuple-element.14._) | copy-start | bytes 12292
  46.8 13.1 %all-to-all-start.1 = ((f32[8,32,128]{2,1,0:T(8,128)}), f32[8,32,128]{2,1,0:T(8,128)S(1)}, u32[]{:S(2)}, u32[]{:S(2)}) async-start(f32[8,32,128]{2,1,0:T(8,128)} %handed_attention.1.refs_1_), calls=%async_computation.1 | async-start | bytes 262144 | tf_op jit(solution)/shard_map/all_to_all | solution.py:486
  59.9 0.6 copy-start.3

commit v5 on v4

--- a/solution.py
+++ b/solution.py
@@ -155,14 +155,19 @@
             ),
         ).astype(jnp.float32)
         sixth = iota((n * GROUP_ROWS, HD), 0) % GROUP_ROWS == 6
-        msg_ref[:, :HD] = jnp.where(sixth, facts, own[:, :HD])
-        msg_ref[:, HD:] = own[:, HD:]
+        msg_ref[:, :HD] = jnp.where(sixth, facts, own[:, :HD]).astype(jnp.bfloat16)
+        msg_ref[:, HD:] = own[:, HD:].astype(jnp.bfloat16)
 
     @pl.when(step > 0)
     def _():
         for copy in x_copies(step - 1):
             copy.wait()
-        keep(dot(xs[step - 1], w[...]), pl.ds(pl.multiple_of(first + (step - 1) * size, BLOCK_TOKENS), size))
+        rows = pl.ds(pl.multiple_of(first + (step - 1) * size, BLOCK_TOKENS), size)
+        half = depth // 2
+        x = xs.at[step - 1]
+        q_out[rows, :] = dot(x[...], w[:, :cq]).astype(jnp.bfloat16)
+        low, high = dot(x[:, :half], w[:half, cq:]), dot(x[:, half:], w[half:, cq:])
+        kv_out[rows, :] = (low + high).astype(jnp.bfloat16)
         for copy in out_copies(step):
             copy.start()
 
@@ -191,7 +196,7 @@
             jax.ShapeDtypeStruct((rows, cq), jnp.bfloat16),
             jax.ShapeDtypeStruct((rows, ckv), jnp.bfloat16),
             jax.ShapeDtypeStruct((lq * n * GROUP_ROWS, HD), jnp.bfloat16),
-            jax.ShapeDtypeStruct((n * GROUP_ROWS, cq + ckv), jnp.float32),
+            jax.ShapeDtypeStruct((n * GROUP_ROWS, cq + ckv), jnp.bfloat16),
         ],
         scratch_shapes=[
             VMEM((first + dx.shape[0], depth), jnp.bfloat16),
@@ -214,57 +219,61 @@
 
 
 LOG2E = 1.4426950408889634
-SLAB = 32
-
-
-def attend_prompt(lq, half, counts, q_hbm, kv_hbm, *refs):
-    o_hbm, done_ref, qs, kvs, outs, sems = refs[-6:]
-    done_ref[...] = jnp.zeros_like(done_ref)
+
+
+def attend_prompt(lq, counts, q_hbm, kv_hbm, o_hbm, made_ref, qs, kvs, outs, sems):
+    made_ref[...] = jnp.zeros_like(made_ref)
     group = lax.axis_index("pool")
     c0, c1 = counts[group, 0], counts[group, 1]
     big = jnp.where(c0 == MOST_BLOCKS, 0, jnp.where(c1 == MOST_BLOCKS, c0, c0 + c1))
     cut = jnp.where(c0 == MOST_BLOCKS, c1, c0)
-
     loads, stores = [], []
-    for j in range(MOST_BLOCKS):
-        block = big + j if half == 0 else j + jnp.where(j >= big, MOST_BLOCKS, 0)
-        rows = pl.ds(pl.multiple_of(block * BLOCK_TOKENS, BLOCK_TOKENS), BLOCK_TOKENS)
-        here = pl.ds(j * BLOCK_TOKENS, BLOCK_TOKENS)
-        loads.append(pltpu.make_async_copy(kv_hbm.at[rows], kvs.at[here], sems.at[0, j]))
-        loads.append(pltpu.make_async_copy(q_hbm.at[rows], qs.at[here], sems.at[1, j]))
-        stores.append(pltpu.make_async_copy(outs.at[here], o_hbm.at[rows], sems.at[2, j]))
+    for half in range(2):
+        for j in range(MOST_BLOCKS):
+            block = big + j if half == 0 else j + jnp.where(j >= big, MOST_BLOCKS, 0)
+            rows = pl.ds(pl.multiple_of(block * BLOCK_TOKENS, BLOCK_TOKENS), BLOCK_TOKENS)
+            here = pl.ds(j * BLOCK_TOKENS, BLOCK_TOKENS)
+            loads.append(pltpu.make_async_copy(kv_hbm.at[rows], kvs.at[half, here], sems.at[0, half, j]))
+            loads.append(pltpu.make_async_copy(q_hbm.at[rows], qs.at[half, here], sems.at[1, half, j]))
+            stores.append(pltpu.make_async_copy(outs.at[half, here], o_hbm.at[rows], sems.at[2, half, j]))
     for copy in loads:
         copy.start()
     for copy in loads:
         copy.wait()
-
-    def scores_of(j):
-        q = qs[j * BLOCK_TOKENS : (j + 1) * BLOCK_TOKENS, :]
+    tokens = MOST_BLOCKS * BLOCK_TOKENS
+    shape = (BLOCK_TOKENS, lq * BLOCK_TOKENS)
+    causal = iota(shape, 0) <= iota(shape, 1) % BLOCK_TOKENS
+    flipped = [kvs[half, :, HD:].T for half in range(2)]
+
+    def scores_of(half, j):
+        q = qs[half, j * BLOCK_TOKENS : (j + 1) * BLOCK_TOKENS, :]
         q = jnp.concatenate([q[:, h * HD : (h + 1) * HD] for h in range(lq)], axis=0)
-        return dot_t(q, kvs[: (j + 1) * BLOCK_TOKENS, :HD])
-
-    causal = iota((SLAB, BLOCK_TOKENS), 1) - iota((SLAB, BLOCK_TOKENS), 0)
-    scores = scores_of(0)
-    for j in range(MOST_BLOCKS):
-        later = scores_of(j + 1) if j + 1 < MOST_BLOCKS else None
+        return dot_t(kvs[half, : (j + 1) * BLOCK_TOKENS, :HD], q)
+
+    order = [(half, j) for half in range(2) for j in range(MOST_BLOCKS)]
+    scores = scores_of(*order[0])
+    for k, (half, j) in enumerate(order):
+        later = scores_of(*order[k + 1]) if k + 1 < len(order) else None
         weights = []
-        for at in range(0, lq * BLOCK_TOKENS, SLAB):
+        for h in range(lq):
+            cols = slice(h * BLOCK_TOKENS, (h + 1) * BLOCK_TOKENS)
             tiles = []
             for i in range(j + 1):
-                tile = scores[at : at + SLAB, i * BLOCK_TOKENS : (i + 1) * BLOCK_TOKENS]
+                tile = scores[i * BLOCK_TOKENS : (i + 1) * BLOCK_TOKENS, cols]
                 if i == j:
-                    tile = jnp.where(causal <= at % BLOCK_TOKENS, tile, MASKED)
+                    tile = jnp.where(causal[:, cols], tile, MASKED)
                 elif half == 1:
                     tile = tile + jnp.where((i < cut) & (cut <= j), MASKED, 0.0)
                 tiles.append(tile)
-            peak = jnp.max(functools.reduce(jnp.maximum, tiles), axis=1, keepdims=True)
+            peak = jnp.max(functools.reduce(jnp.maximum, tiles), axis=0, keepdims=True)
             raised = [jnp.exp2((tile - peak) * (SCALE * LOG2E)) for tile in tiles]
-            inverse = 1.0 / jnp.sum(functools.reduce(jnp.add, raised), axis=1, keepdims=True)
-            weights.append(jnp.concatenate([(t * inverse).astype(jnp.bfloat16) for t in raised], axis=1))
-        mixed = dot(jnp.concatenate(weights, axis=0), kvs[: (j + 1) * BLOCK_TOKENS, HD:])
+            inverse = 1.0 / jnp.sum(functools.reduce(jnp.add, raised), axis=0, keepdims=True)
+            weights.append(jnp.concatenate([(t * inverse).astype(jnp.bfloat16) for t in raised], axis=0))
+        mixed = dot(flipped[half][:, : (j + 1) * BLOCK_TOKENS], jnp.concatenate(weights, axis=1))
+        mixed = mixed.astype(jnp.bfloat16)
         for h in range(lq):
-            part = mixed[h * BLOCK_TOKENS : (h + 1) * BLOCK_TOKENS]
-            outs[j * BLOCK_TOKENS : (j + 1) * BLOCK_TOKENS, h * HD : (h + 1) * HD] = part.astype(jnp.bfloat16)
+            part = mixed[:, h * BLOCK_TOKENS : (h + 1) * BLOCK_TOKENS].T
+            outs[half, j * BLOCK_TOKENS : (j + 1) * BLOCK_TOKENS, h * HD : (h + 1) * HD] = part
         scores = later
     for copy in stores:
         copy.start()
@@ -272,30 +281,28 @@
         copy.wait()
 
 
-def prompt_attention(counts, q, kv, half, so_far=None, after=None):
+def prompt_attention(counts, q, kv):
     rows, cq = q.shape
     hbm = pl.BlockSpec(memory_space=pl.ANY)
-    more = () if so_far is None else (so_far, after)
     tokens = MOST_BLOCKS * BLOCK_TOKENS
     return pl.pallas_call(
-        functools.partial(attend_prompt, cq // HD, half),
-        in_specs=[pl.BlockSpec(memory_space=SMEM), hbm, hbm] + [hbm] * len(more),
+        functools.partial(attend_prompt, cq // HD),
+        in_specs=[pl.BlockSpec(memory_space=SMEM), hbm, hbm],
         out_specs=[hbm, pl.BlockSpec(memory_space=VMEM)],
         out_shape=[
             jax.ShapeDtypeStruct((rows, cq), jnp.bfloat16),
             jax.ShapeDtypeStruct((8, HD), jnp.float32),
         ],
         scratch_shapes=[
-            VMEM((tokens, cq), jnp.bfloat16),
-            VMEM((tokens, 2 * HD), jnp.bfloat16),
-            VMEM((tokens, cq), jnp.bfloat16),
-            pltpu.SemaphoreType.DMA((3, MOST_BLOCKS)),
+            VMEM((2, tokens, cq), jnp.bfloat16),
+            VMEM((2, tokens, 2 * HD), jnp.bfloat16),
+            VMEM((2, tokens, cq), jnp.bfloat16),
+            pltpu.SemaphoreType.DMA((3, 2, MOST_BLOCKS)),
         ],
-        input_output_aliases={3: 0} if more else {},
         compiler_params=pltpu.CompilerParams(vmem_limit_bytes=62 * MIB),
-        cost_estimate=pl.CostEstimate(flops=rows * rows * cq, bytes_accessed=4 * rows * cq, transcendentals=rows * rows // 2),
-        name="long_prompt" if half == 0 else "short_prompts",
-    )(counts, q, kv, *more)
+        cost_estimate=pl.CostEstimate(flops=2 * rows * rows * cq, bytes_accessed=8 * rows * cq, transcendentals=rows * rows),
+        name="prompt_attention",
+    )(counts, q, kv)
 
 
 def row_head(n, lq, h, hh):
@@ -308,7 +315,7 @@
     shape = (rows, HD)
     at_row, lane = iota(shape, 0), iota(shape, 1)
     rs = at_row % GROUP_ROWS
-    facts = msg_ref[:, :HD].reshape(n, GROUP_ROWS, HD)[:, 6:7, :]
+    facts = msg_ref[:, :HD].astype(jnp.float32).reshape(n, GROUP_ROWS, HD)[:, 6:7, :]
     facts = jnp.broadcast_to(facts, (n, GROUP_ROWS, HD)).reshape(n * GROUP_ROWS, HD)
     facts = jnp.concatenate([facts] * lq, axis=0)
 
@@ -358,18 +365,17 @@
     )(kv, q_own, msgs, after)
 
 
-def owner_part(n, lq, counts, done, placed, table, lens, cache_hbm, held, handed, o_ref, cache, sem, slot_row, slot_limit):
+def owner_scores(n, lq, counts, done, placed, table, lens, cache_hbm, msgs, _, s_ref, v_ref, new_ref, cache, sem, slot_row, slot_limit):
     load = pltpu.make_async_copy(cache_hbm, cache, sem)
     load.start()
+    held = msgs[...].astype(jnp.float32)
     found = block_of_pages(counts, done, placed, table)
     for r in range(ROWS_DEV):
         for p in range(PAGES):
             slot_row[table[p, r]] = jnp.int32(r)
             slot_limit[table[p, r]] = jnp.where(found[r][p] < 0, lens[r] - p * BLOCK_TOKENS, 0)
-
     cq = lq * HD
-    groups = QH
-    rows = groups * GROUP_ROWS
+    rows = QH * GROUP_ROWS
     span = GQ * GROUP_ROWS
     queries, keys = [], []
     for h in range(KVH):
@@ -378,28 +384,63 @@
             queries.append(held[t * GROUP_ROWS : (t + 1) * GROUP_ROWS, at * HD : (at + 1) * HD])
         t, _ = row_head(n, lq, h, 0)
         keys += [held[t * GROUP_ROWS : (t + 1) * GROUP_ROWS, cq : cq + HD]] * GQ
+        new_ref[h * GROUP_ROWS : (h + 1) * GROUP_ROWS, :] = held[
+            t * GROUP_ROWS : (t + 1) * GROUP_ROWS, cq + HD : cq + 2 * HD
+        ]
     queries = jnp.concatenate(queries, axis=0)
     earlier = jnp.concatenate([pltpu.roll(key, ROWS_DEV, 0) for key in keys], axis=0)
     keys = jnp.concatenate(keys, axis=0)
     at_row, lane = iota((rows, HD), 0), iota((rows, HD), 1)
-    r = row_of(at_row % GROUP_ROWS)
+    rs = at_row % GROUP_ROWS
+    r = row_of(rs)
     rounded = queries.astype(jnp.bfloat16)
     now = jnp.sum(queries * keys, axis=1, keepdims=True) * SCALE
     before = jnp.sum(queries * earlier, axis=1, keepdims=True) * SCALE
+    second = (rs >= ROWS_DEV) & (rs < STEPS * ROWS_DEV)
+    before = jnp.where(second, before, MASKED)
     load.wait()
     scores = jnp.concatenate(
         [dot_t(rounded[h * span : (h + 1) * span], cache[:, 2 * h * HD : (2 * h + 1) * HD]) for h in range(KVH)],
         axis=0,
     )
-    parts = []
     for slot in range(DEVICE_SLOTS):
-        part = scores[:, slot * BLOCK_TOKENS : (slot + 1) * BLOCK_TOKENS]
+        part = slice(slot * BLOCK_TOKENS, (slot + 1) * BLOCK_TOKENS)
         usable = (r == slot_row[slot]) & (lane < slot_limit[slot])
-        parts.append(jnp.where(usable, part * SCALE, MASKED))
-    scores = jnp.concatenate(parts, axis=1)
-    rs1 = iota((rows, 1), 0) % GROUP_ROWS
-    before = jnp.where((rs1 >= ROWS_DEV) & (rs1 < STEPS * ROWS_DEV), before, MASKED)
-
+        s_ref[:, part] = jnp.where(usable, scores[:, part] * SCALE, MASKED)
+    last = jnp.where(lane == 0, now, jnp.where(lane == 1, before, MASKED))
+    s_ref[:, DEVICE_SLOTS * BLOCK_TOKENS :] = last
+    for h in range(KVH):
+        v_ref[:, h * HD : (h + 1) * HD] = cache[:, (2 * h + 1) * HD : (2 * h + 2) * HD]
+
+
+def decode_scores(ints, cache, msgs, after, n, lq):
+    smem, vmem, hbm = [pl.BlockSpec(memory_space=space) for space in (SMEM, VMEM, pl.ANY)]
+    rows = QH * GROUP_ROWS
+    return pl.pallas_call(
+        functools.partial(owner_scores, n, lq),
+        in_specs=[smem] * 5 + [hbm, vmem, hbm],
+        out_specs=[vmem] * 3,
+        out_shape=[
+            jax.ShapeDtypeStruct((rows, (DEVICE_SLOTS + 1) * BLOCK_TOKENS), jnp.float32),
+            jax.ShapeDtypeStruct((cache.shape[0], KVH * HD), jnp.bfloat16),
+            jax.ShapeDtypeStruct((KVH * GROUP_ROWS, HD), jnp.float32),
+        ],
+        scratch_shapes=[
+            VMEM(cache.shape, jnp.bfloat16),
+            pltpu.SemaphoreType.DMA,
+            SMEM((DEVICE_SLOTS,), jnp.int32),
+            SMEM((DEVICE_SLOTS,), jnp.int32),
+        ],
+        compiler_params=pltpu.CompilerParams(vmem_limit_bytes=24 * MIB),
+        cost_estimate=pl.CostEstimate(flops=2 * rows * HD * 768, bytes_accessed=4 * MIB, transcendentals=0),
+        name="decode_scores",
+    )(*ints, cache, msgs, after)
+
+
+def owner_mix(s_ref, v_ref, new_ref, handed, o_ref):
+    groups = QH
+    rows = groups * GROUP_ROWS
+    span = GQ * GROUP_ROWS
     mixed = handed[...].reshape(groups, GROUP_ROWS, HD)
     shape = (groups, GROUP_ROWS, HD)
     mine = iota(shape, 1) == iota(shape, 2)
@@ -409,21 +450,21 @@
         return jnp.sum(jnp.where(mine, line, 0.0), axis=2, keepdims=True).reshape(rows, 1)
 
     other_peak, other_total = column(6), column(7)
-    peak = jnp.maximum(jnp.max(scores, axis=1, keepdims=True), jnp.maximum(now, before))
-    peak = jnp.maximum(peak, other_peak)
-    raised, now, before = jnp.exp(scores - peak), jnp.exp(now - peak), jnp.exp(before - peak)
+    scores = s_ref[...]
+    peak = jnp.maximum(jnp.max(scores, axis=1, keepdims=True), other_peak)
+    raised = jnp.exp(scores - peak)
     other = jnp.exp(other_peak - peak)
-    inverse = 1.0 / (jnp.sum(raised, axis=1, keepdims=True) + now + before + other * other_total)
+    inverse = 1.0 / (jnp.sum(raised, axis=1, keepdims=True) + other * other_total)
     weights = (raised * inverse).astype(jnp.bfloat16)
-    now = (now * inverse).astype(jnp.bfloat16).astype(jnp.float32)
-    before = (before * inverse).astype(jnp.bfloat16).astype(jnp.float32)
+    old = DEVICE_SLOTS * BLOCK_TOKENS
+    fresh = weights[:, old:].astype(jnp.float32)
+    now, before = fresh[:, 0:1], fresh[:, 1:2]
     mixed = mixed.reshape(rows, HD) * (other * inverse)
     out = []
     for h in range(KVH):
         part = slice(h * span, (h + 1) * span)
-        own = mixed[part] + dot(weights[part], cache[:, (2 * h + 1) * HD : (2 * h + 2) * HD])
-        t, _ = row_head(n, lq, h, 0)
-        value = held[t * GROUP_ROWS : (t + 1) * GROUP_ROWS, cq + HD : cq + 2 * HD]
+        own = mixed[part] + dot(weights[part, :old], v_ref[:, h * HD : (h + 1) * HD])
+        value = new_ref[h * GROUP_ROWS : (h + 1) * GROUP_ROWS, :]
         last = pltpu.roll(value, ROWS_DEV, 0)
         for hh in range(GQ):
             some = slice(h * span + hh * GROUP_ROWS, h * span + (hh + 1) * GROUP_ROWS)
@@ -435,23 +476,18 @@
         o_ref[k] = jnp.concatenate(steps, axis=0).astype(jnp.bfloat16)
 
 
-def decode_attention(ints, cache, msgs, parts, n, lq):
-    smem, vmem = pl.BlockSpec(memory_space=SMEM), pl.BlockSpec(memory_space=VMEM)
+def decode_mix(scores, values, new, parts):
+    vmem = pl.BlockSpec(memory_space=VMEM)
+    rows = QH * GROUP_ROWS
     return pl.pallas_call(
-        functools.partial(owner_part, n, lq),
-        in_specs=[smem] * 5 + [pl.BlockSpec(memory_space=pl.ANY), vmem, vmem],
+        owner_mix,
+        in_specs=[vmem] * 4,
         out_specs=vmem,
         out_shape=jax.ShapeDtypeStruct((ROWS_DEV, STEPS, QH * HD), jnp.bfloat16),
-        scratch_shapes=[
-            VMEM(cache.shape, jnp.bfloat16),
-            pltpu.SemaphoreType.DMA,
-            SMEM((DEVICE_SLOTS,), jnp.int32),
-            SMEM((DEVICE_SLOTS,), jnp.int32),
-        ],
-        compiler_params=pltpu.CompilerParams(vmem_limit_bytes=62 * MIB),
-        cost_estimate=pl.CostEstimate(flops=4 * 256 * HD * 768, bytes_accessed=4 * MIB, transcendentals=256 * 768),
-        name="decode_attention",
-    )(*ints, cache, msgs, parts)
+        compiler_params=pltpu.CompilerParams(vmem_limit_bytes=24 * MIB),
+        cost_estimate=pl.CostEstimate(flops=2 * rows * HD * 768, bytes_accessed=4 * MIB, transcendentals=rows * 768),
+        name="decode_mix",
+    )(scores, values, new, parts)
 
 
 def local(
@@ -481,11 +517,11 @@
     q, kv, q_own, msgs = project_all(ints, dx, prompt_x, q_weight, kv_weight, n, first, size)
     msgs = lax.all_to_all(msgs, "tp", split_axis=0, concat_axis=0, tiled=True)
     kv_other = lax.ppermute(kv, "pool", [(0, 1), (1, 0)])
-    prompt_attn, made = prompt_attention(prompt_blocks, q, kv, 0)
+    prompt_attn, made = prompt_attention(prompt_blocks, q, kv)
     handed = handed_attention(kv_other, q_own, msgs, made, n, lq)
     parts = lax.all_to_all(handed, "tp", split_axis=0, concat_axis=0, tiled=True)
-    prompt_attn, _ = prompt_attention(prompt_blocks, q, kv, 1, prompt_attn, handed)
-    decode_attn = decode_attention(ints, cache, msgs, parts, n, lq)
+    scores, values, new = decode_scores(ints, cache, msgs, handed, n, lq)
+    decode_attn = decode_mix(scores, values, new, parts)
     return prompt_attn, decode_attn.transpose(1, 0, 2)
 
 

time: 66.1 us -> 65.7 us (level)
  Pallas kernels: 49.9 us -> 45.1 us
  waiting for transfers between devices: 0.86 us -> 3.43 us
  local copies, waits for them, and re-layouts: 1.34 us -> 2.6 us
  starting transfers between devices: 12.6 us -> 13.3 us
    pallas_call x3, Pallas kernels: 20.4 us -> 15.7 us  [the longest x1 12.3 us: prompt_attention(): pl.pallas_call(functools.partial(attend_prompt, cq // HD), in_specs=[pl.B...]
    all_to_all x1, waiting for transfers between devices: 0.01 us -> 3.42 us  [local(): lax.all_to_all(handed, 'tp', split_axis=0, concat_axis=0, tiled=True)]
    unnamed x8 -> x16, local copies, waits for them, and re-layouts: 1.34 us -> 2.6 us
    all_to_all x1, waiting for transfers between devices: 0.85 us -> 0.01 us  [local(): msgs = lax.all_to_all(msgs, 'tp', split_axis=0, concat_axis=0, tiled=True)]
    all_to_all x1, starting transfers between devices: 5.18 us -> 5.97 us  [local(): lax.all_to_all(handed, 'tp', split_axis=0, concat_axis=0, tiled=True)]
  transfers between devices with their start and end apart: 3 -> 3, of which waited for: 1 -> 1; matrix products, arithmetic and copies ran while one was open for 0% -> 0% of each run, Pallas kernels for 24% -> 22%
where the time goes in v5:
time: 65.7 us; the launch traced here: 65.3 us
  Pallas kernels  45.1 us (69%)
  starting transfers between devices  13.3 us (20%)
  waiting for transfers between devices  3.43 us (5%)
  local copies, waits for them, and re-layouts  2.6 us (4%)
  between operations  0.78 us (1%)
    pallas_call x1, Pallas kernels, project_all(): pl.pallas_call(functools.partial(project, n, lq, first, size), grid=(1 +...  27 us
    pallas_call x1, Pallas kernels, prompt_attention(): pl.pallas_call(functools.partial(attend_prompt, cq // HD), in_specs=[pl.B...  12.3 us
    all_to_all x1, starting transfers between devices, local(): msgs = lax.all_to_all(msgs, 'tp', split_axis=0, concat_axis=0, tiled=True)  6.86 us
    all_to_all x1, starting transfers between devices, local(): lax.all_to_all(handed, 'tp', split_axis=0, concat_axis=0, tiled=True)  5.97 us
    all_to_all x1, waiting for transfers between devices, local(): lax.all_to_all(handed, 'tp', split_axis=0, concat_axis=0, tiled=True)  3.42 us
    unnamed x16, local copies, waits for them, and re-layouts  2.6 us
    pallas_call x1, Pallas kernels, handed_attention(): pl.pallas_call(functools.partial(handed_part, n, lq), in_specs=[vmem] * 3...  2.4 us
    pallas_call x1, Pallas kernels, decode_scores(): pl.pallas_call(functools.partial(owner_scores, n, lq), in_specs=[smem] *...  1.97 us
  transfers between devices with their start and end apart: 3, of which 1 were waited for; matrix products, arithmetic and copies ran while one was open for 0% of the time, Pallas kernels for 22%

profile of v5, /device:TPU:0, one launch (start us, length us, event | category | flops | bytes accessed | tf_op | source)
XLA Modules:
  0.0 65.3 jit_solution(7644640362115251900)
XLA Ops:
  0.6 27.0 %project.1 = (bf16[2048,512]{1,0:T(8,128)(2,1)}, bf16[2048,256]{1,0:T(8,128)(2,1)}, bf16[256,128]{1,0:T(8,128)(2,1)}, bf16[64,768]{1,0:T(8,128)(2,1)}) custom-call(s32[2,3]{1,0:T(2,128)} %counts.3, s32[2,3]{1,0:T(2,128)} %done.1, s32[2,2,16]{2,1,0:T(2,128)} %bitcast.10, s32[2,3]{1,0:T(2,128)} %bitcast.12, s32[3]{0:T(128)} %lens.1, ...), custom_call_target="tpu_custom_call" | custom-call | flops 16106127360 | bytes 31981568 | tf_op jit(solution)/shard_map/project/pallas_call | solution.py:190
  27.7 0.5 collective-permute-start
  28.2 6.9 %all-to-all-start = ((bf16[8,8,768]{2,1,0:T(8,128)(2,1)}), bf16[8,8,768]{2,1,0:T(8,128)(2,1)S(1)}, u32[]{:S(2)}, u32[]{:S(2)}) async-start(bf16[8,8,768]{2,1,0:T(8,128)(2,1)} %bitcast.14), calls=%async_computation | async-start | bytes 196608 | tf_op jit(solution)/shard_map/all_to_all | solution.py:518
  35.1 0.0 copy-start.6
  35.1 0.0 copy-start.1
  35.1 0.0 copy-start.2
  35.1 0.0 copy-start.3
  35.1 0.0 copy-start.4
  35.1 0.0 copy-start.5
  35.1 12.3 %prompt_attention.1 = (bf16[2048,512]{1,0:T(8,128)(2,1)}, f32[8,128]{1,0:T(8,128)}) custom-call(s32[2,3]{1,0:T(2,128)} %counts.3, bf16[2048,512]{1,0:T(8,128)(2,1)} %get-tuple-element.11.q_hbm, bf16[2048,256]{1,0:T(8,128)(2,1)} %get-tuple-element.12.kv_hbm), custom_call_target="tpu_custom_call" | custom-call | flops 4294967296 | bytes 8388608 | tf_op jit(solution)/shard_map/prompt_attention/pallas_call | solution.py:288
  47.5 0.0 all-to-all-done
  47.5 0.0 collective-permute-done.kv_ref
  47.5 0.0 copy-done.6
  47.5 0.0 copy-start.7
  47.5 0.7 %copy-done.7 = f32[8,128]{1,0:T(8,128)S(1)} copy-done((f32[8,128]{1,0:T(8,128)S(1)}, f32[8,128]{1,0:T(8,128)}, u32[]{:S(2)}) %copy-start.7) | copy-done | bytes 4120
  48.2 2.4 %handed_attention.1._ = f32[8,32,128]{2,1,0:T(8,128)} custom-call(bf16[2048,256]{1,0:T(8,128)(2,1)S(1)} %collective-permute-done.kv_ref, bf16[256,128]{1,0:T(8,128)(2,1)S(1)} %copy-done.6, bf16[64,768]{1,0:T(8,128)(2,1)S(1)} %bitcast.8, f32[8,128]{1,0:T(8,128)S(1)} %copy-done.7), custom_call_target="tpu_custom_call" | custom-call | flops 402653184 | bytes 2097152 | tf_op jit(solution)/shard_map/handed_attention/pallas_call | solution.py:357
  50.6 6.0 %all-to-all-start.1 = ((f32[8,32,128]{2,1,0:T(8,128)}), f32[8,32,128]{2,1,0:T(8,128)S(1)}, u32[]{:S(2)}, u32[]{:S(2)}) async-start(f32[8,32,128]{2,1,0:T(8,128)} %handed_attention.1._), calls=%async_computation.1 | async-start | bytes 262144 | tf_op jit(solution)/shard_map/all_to_all | solution.py:522
  56.6 0.0 copy-done.1
  56.6 0.0 copy-done.2
  56.6 0.0 copy-done.3
  56.6 0.0 copy-done.4
  56.6 0.0 copy-done.5
  56.6 0.0 copy-start
  56.6 1.9 %copy-done = bf16[6,128,2048]{2,1,0:T(8,128)(2,1)S(1)} copy-done((bf16[6,128,2048]{2,1,0:T(8,128)(2,1)S(1)}, bf16[6,128,2048]{2,1,0:T(8,128)(2,1)}, u32[]{:S(2)}) %copy-start) | copy-done | bytes 3145752
  58.5 2.0 %decode_scores.1 = (f32[256,896]{1,0:T(8,128)S(1)}, bf16[768,1024]{1,0:T(8,128)(2,1)S(1)}, f32[64,128]{1,0:T(8,128)S(1)}) custom-call(s32[2,3]{1,0:T(2,128)S(1)} %copy-done.2, s32[2,3]{1,0:T(2,128)S(1)} %copy-done.3, s32[2,2,16]{2,1,0:T(2,128)S(1)} %bitcast.11, s32[2,3]{1,0:T(2,128)S(1)} %bitcast.13, s32[3]{0:T(128)S(1)} %copy-done.5, ...), custom_call_target="tpu_custom_call" | custom-call | flops 50331648 | bytes 4194304 | tf_op jit(solution)/shard_map/decode_scores/pallas_call | solution.py:419
  60.5 3.4 %all-to-all-done.1.handed = f32[8,32,128]{2,1,0:T(8,128)S(1)} async-done(((f32[8,32,128]{2,1,0:T(8,128)}), f32[8,32,128]{2,1,0:T(8,128)S(1)}, u32[]{:S(2)}, u32[]{:S(2)}) %all-to-all-start.1) | async-done | bytes 131104 | tf_op jit(solution)/shard_map/all_to_all | solution.py:522
  63.9 1.4 %decode_mix.1 = bf16[3,2,4096]{2,1,0:T(2,128)(2,1)} custom-call(f32[256,896]{1,0:T(8,128)S(1)} %get-tuple-element.17.s_ref, bf16[768,1024]{1,0:T(8,128)(2,1)S(1)} %get-tuple-element.18.v_ref, f32[64,128]{1,0:T(8,128)S(1)} %get-tuple-element.19.new_ref, f32[8,32,128]{2,1,0:T(8,128)S(1)} %all-to-all-done.1.handed), custom_call_target="tpu_custom_call" | custom-call | flops 50331648 | bytes 4194304 | tf_op jit(solution)/shard_map/decode_mix/pallas_call | solution.py:482
Async XLA Ops:
  27.7 19.8 %collective-permute-start = (bf16[2048,256]{1,0:T(8,128)(2,1)}, bf16[2048,256]{1,0:T(8,128)(2,1)S(1)}, u32[]{:S(2)}, u32[]{:S(2)}) collective-permute-start(bf16[2048,256]{1,0:T(8,128)(2,1)} %get-tuple-element.12.kv_hbm), channel_id=1, source_target_pairs={{0,8},{8,0},{1,9},{9,1},{2,10},{10,2},{3,11},{11,3},{4,12},{12,4},... | collective-permute-start | bytes 3145736 | tf_op jit(solution)/shard_map/ppermute | solution.py:519
  28.2 19.3 %all-to-all-start = ((bf16[8,8,768]{2,1,0:T(8,128)(2,1)}), bf16[8,8,768]{2,1,0:T(8,128)(2,1)S(1)}, u32[]{:S(2)}, u32[]{:S(2)}) async-start(bf16[8,8,768]{2,1,0:T(8,128)(2,1)} %bitcast.14), calls=%async_computation | async-start | bytes 196608 | tf_op jit(solution)/shard_map/all_to_all | solution.py:518
  35.1 12.4 %copy-start.6 = (bf16[256,128]{1,0:T(8,128)(2,1)S(1)}, bf16[256,128]{1,0:T(8,128)(2,1)}, u32[]{:S(2)}) copy-start(bf16[256,128]{1,0:T(8,128)(2,1)} %get-tuple-element.15.q_ref) | copy-start | bytes 196612
  35.1 21.5 %copy-start.1 = (s32[2,16,2]{1,2,0:T(2,128)S(1)}, s32[2,16,2]{1,2,0:T(2,128)}, u32[]{:S(2)}) copy-start(s32[2,16,2]{1,2,0:T(2,128)} %param.15) | copy-start | bytes 772
  35.1 21.5 %copy-start.2 = (s32[2,3]{1,0:T(2,128)S(1)}, s32[2,3]{1,0:T(2,128)}, u32[]{:S(2)}) copy-start(s32[2,3]{1,0:T(2,128)} %counts.3) | copy-start | bytes 76
  35.1 21.5 %copy-start.3 = (s32[2,3]{1,0:T(2,128)S(1)}, s32[2,3]{1,0:T(2,128)}, u32[]{:S(2)}) copy-start(s32[2,3]{1,0:T(2,128)} %done.1) | copy-start | bytes 76
  35.1 21.5 %copy-start.4 = (s32[3,2]{0,1:T(2,128)S(1)}, s32[3,2]{0,1:T(2,128)}, u32[]{:S(2)}) copy-start(s32[3,2]{0,1:T(2,128)} %param.16) | copy-start | bytes 76
  35.1 21.5 %copy-start.5 = (s32[3]{0:T(128)S(1)}, s32[3]{0:T(128)}, u32[]{:S(2)}) copy-start(s32[3]{0:T(128)} %lens.1) | copy-start | bytes 40
  47.5 0.7 %copy-start.7 = (f32[8,128]{1,0:T(8,128)S(1)}, f32[8,128]{1,0:T(8,128)}, u32[]{:S(2)}) copy-start(f32[8,128]{1,0:T(8,128)} %get-tuple-element.16._) | copy-start | bytes 12292
  50.6 13.3 %all-to-all-start.1 = ((f32[8,32,128]{2,1,0:T(8,128)}), f32[8,32,128]{2,1,0:T(8,128)S(1)}, u32[]{:S(2)}, u32[]{:S(2)}) async-start(f32[8,32,128]{2,1,0:T(8,128)} %handed_attention.1._), calls=%async_computation.1 | async-start | bytes 262144 | tf_op jit(solution)/shard_map/all_to_all | solution.py:522
  56.6 1.9 %copy-start = (bf16[6,128,2048]{2,1,0:T(8,128)(2,1)S(1)}, bf16[6,128,2048]{2,1,0:T(8,128)(2,1)}, u32[]{:S(2)}) copy-start(bf16[6,128,2048]{2,1,0:T(8,128)(2,1)} %param.18) | copy-start | bytes 9437188

commit v6 on v5

--- a/solution.py
+++ b/solution.py
@@ -26,6 +26,7 @@
 MASKED = -1e30
 PIECES = 5
 STRIPS = 4
+AHEAD = 2
 MIB = 1 << 20
 VMEM = pltpu.VMEM
 SMEM = pltpu.SMEM
@@ -117,16 +118,19 @@
 
     @pl.when(step == 0)
     def _():
-        for c in range(PIECES):
+        for c in range(AHEAD):
             for copy in piece_copies(c):
-                copy.start()
-        for k in range(count):
-            for copy in x_copies(k):
                 copy.start()
         total = 0.0
         for c in range(PIECES):
             for copy in piece_copies(c):
                 copy.wait()
+            if c + AHEAD < PIECES:
+                for copy in piece_copies(c + AHEAD):
+                    copy.start()
+            if c + AHEAD == PIECES:
+                for copy in x_copies(0):
+                    copy.start()
             part = slice(c * piece, (c + 1) * piece)
             total += dot(x0[:, part], w[part, :])
         keep(total[:first], pl.ds(0, first))
@@ -158,16 +162,16 @@
         msg_ref[:, :HD] = jnp.where(sixth, facts, own[:, :HD]).astype(jnp.bfloat16)
         msg_ref[:, HD:] = own[:, HD:].astype(jnp.bfloat16)
 
+    @pl.when((step > 0) & (step < count))
+    def _():
+        for copy in x_copies(step):
+            copy.start()
+
     @pl.when(step > 0)
     def _():
         for copy in x_copies(step - 1):
             copy.wait()
-        rows = pl.ds(pl.multiple_of(first + (step - 1) * size, BLOCK_TOKENS), size)
-        half = depth // 2
-        x = xs.at[step - 1]
-        q_out[rows, :] = dot(x[...], w[:, :cq]).astype(jnp.bfloat16)
-        low, high = dot(x[:, :half], w[:half, cq:]), dot(x[:, half:], w[half:, cq:])
-        kv_out[rows, :] = (low + high).astype(jnp.bfloat16)
+        keep(dot(xs[step - 1], w[...]), pl.ds(pl.multiple_of(first + (step - 1) * size, BLOCK_TOKENS), size))
         for copy in out_copies(step):
             copy.start()
 
@@ -218,9 +222,6 @@
     )(*ints, dx, x, wq, wkv)
 
 
-LOG2E = 1.4426950408889634
-
-
 def attend_prompt(lq, counts, q_hbm, kv_hbm, o_hbm, made_ref, qs, kvs, outs, sems):
     made_ref[...] = jnp.zeros_like(made_ref)
     group = lax.axis_index("pool")
@@ -266,7 +267,7 @@
                     tile = tile + jnp.where((i < cut) & (cut <= j), MASKED, 0.0)
                 tiles.append(tile)
             peak = jnp.max(functools.reduce(jnp.maximum, tiles), axis=0, keepdims=True)
-            raised = [jnp.exp2((tile - peak) * (SCALE * LOG2E)) for tile in tiles]
+            raised = [jnp.exp((tile - peak) * SCALE) for tile in tiles]
             inverse = 1.0 / jnp.sum(functools.reduce(jnp.add, raised), axis=0, keepdims=True)
             weights.append(jnp.concatenate([(t * inverse).astype(jnp.bfloat16) for t in raised], axis=0))
         mixed = dot(flipped[half][:, : (j + 1) * BLOCK_TOKENS], jnp.concatenate(weights, axis=1))

time: 65.7 us -> 65 us (0.989)
  Pallas kernels: 45.1 us -> 44.4 us
    pallas_call x1, Pallas kernels: 27 us -> 25.7 us  [project_all(): pl.pallas_call(functools.partial(project, n, lq, first, size), grid=(1 +...]
    pallas_call x1, Pallas kernels: 12.3 us -> 13 us  [prompt_attention(): pl.pallas_call(functools.partial(attend_prompt, cq // HD), in_specs=[pl.B...]
  transfers between devices with their start and end apart: 3 -> 3, of which waited for: 1 -> 1; matrix products, arithmetic and copies ran while one was open for 0% -> 0% of each run, Pallas kernels for 22% -> 23%
where the time goes in v6:
time: 65 us; the launch traced here: 64.6 us
  Pallas kernels  44.4 us (68%)
  starting transfers between devices  13.3 us (20%)
  waiting for transfers between devices  3.43 us (5%)
  local copies, waits for them, and re-layouts  2.6 us (4%)
  between operations  0.78 us (1%)
    pallas_call x1, Pallas kernels, project_all(): pl.pallas_call(functools.partial(project, n, lq, first, size), grid=(1 +...  25.7 us
    pallas_call x1, Pallas kernels, prompt_attention(): pl.pallas_call(functools.partial(attend_prompt, cq // HD), in_specs=[pl.B...  13 us
    all_to_all x1, starting transfers between devices, local(): msgs = lax.all_to_all(msgs, 'tp', split_axis=0, concat_axis=0, tiled=True)  6.85 us
    all_to_all x1, starting transfers between devices, local(): lax.all_to_all(handed, 'tp', split_axis=0, concat_axis=0, tiled=True)  5.98 us
    all_to_all x1, waiting for transfers between devices, local(): lax.all_to_all(handed, 'tp', split_axis=0, concat_axis=0, tiled=True)  3.42 us
    unnamed x16, local copies, waits for them, and re-layouts  2.6 us
    pallas_call x1, Pallas kernels, handed_attention(): pl.pallas_call(functools.partial(handed_part, n, lq), in_specs=[vmem] * 3...  2.4 us
    pallas_call x1, Pallas kernels, decode_scores(): pl.pallas_call(functools.partial(owner_scores, n, lq), in_specs=[smem] *...  1.97 us
  transfers between devices with their start and end apart: 3, of which 1 were waited for; matrix products, arithmetic and copies ran while one was open for 0% of the time, Pallas kernels for 23%

profile of v6, /device:TPU:0, one launch (start us, length us, event | category | flops | bytes accessed | tf_op | source)
XLA Modules:
  0.0 64.6 jit_solution(10702995316724264974)
XLA Ops:
  0.6 25.7 %project.1 = (bf16[2048,512]{1,0:T(8,128)(2,1)}, bf16[2048,256]{1,0:T(8,128)(2,1)}, bf16[256,128]{1,0:T(8,128)(2,1)}, bf16[64,768]{1,0:T(8,128)(2,1)}) custom-call(s32[2,3]{1,0:T(2,128)} %counts.3, s32[2,3]{1,0:T(2,128)} %done.1, s32[2,2,16]{2,1,0:T(2,128)} %bitcast.10, s32[2,3]{1,0:T(2,128)} %bitcast.12, s32[3]{0:T(128)} %lens.1, ...), custom_call_target="tpu_custom_call" | custom-call | flops 16106127360 | bytes 31981568 | tf_op jit(solution)/shard_map/project/pallas_call | solution.py:194
  26.3 0.5 collective-permute-start
  26.8 6.9 %all-to-all-start = ((bf16[8,8,768]{2,1,0:T(8,128)(2,1)}), bf16[8,8,768]{2,1,0:T(8,128)(2,1)S(1)}, u32[]{:S(2)}, u32[]{:S(2)}) async-start(bf16[8,8,768]{2,1,0:T(8,128)(2,1)} %bitcast.14), calls=%async_computation | async-start | bytes 196608 | tf_op jit(solution)/shard_map/all_to_all | solution.py:519
  33.7 0.0 copy-start.6
  33.7 0.0 copy-start.1
  33.7 0.0 copy-start.2
  33.7 0.0 copy-start.3
  33.7 0.0 copy-start.4
  33.7 0.0 copy-start.5
  33.7 13.0 %prompt_attention.1 = (bf16[2048,512]{1,0:T(8,128)(2,1)}, f32[8,128]{1,0:T(8,128)}) custom-call(s32[2,3]{1,0:T(2,128)} %counts.3, bf16[2048,512]{1,0:T(8,128)(2,1)} %get-tuple-element.11.q_hbm, bf16[2048,256]{1,0:T(8,128)(2,1)} %get-tuple-element.12.kv_hbm), custom_call_target="tpu_custom_call" | custom-call | flops 4294967296 | bytes 8388608 | tf_op jit(solution)/shard_map/prompt_attention/pallas_call | solution.py:289
  46.7 0.0 all-to-all-done
  46.8 0.0 collective-permute-done.kv_ref
  46.8 0.0 copy-done.6
  46.8 0.0 copy-start.7
  46.8 0.7 %copy-done.7 = f32[8,128]{1,0:T(8,128)S(1)} copy-done((f32[8,128]{1,0:T(8,128)S(1)}, f32[8,128]{1,0:T(8,128)}, u32[]{:S(2)}) %copy-start.7) | copy-done | bytes 4120
  47.5 2.4 %handed_attention.1._ = f32[8,32,128]{2,1,0:T(8,128)} custom-call(bf16[2048,256]{1,0:T(8,128)(2,1)S(1)} %collective-permute-done.kv_ref, bf16[256,128]{1,0:T(8,128)(2,1)S(1)} %copy-done.6, bf16[64,768]{1,0:T(8,128)(2,1)S(1)} %bitcast.8, f32[8,128]{1,0:T(8,128)S(1)} %copy-done.7), custom_call_target="tpu_custom_call" | custom-call | flops 402653184 | bytes 2097152 | tf_op jit(solution)/shard_map/handed_attention/pallas_call | solution.py:358
  49.9 6.0 %all-to-all-start.1 = ((f32[8,32,128]{2,1,0:T(8,128)}), f32[8,32,128]{2,1,0:T(8,128)S(1)}, u32[]{:S(2)}, u32[]{:S(2)}) async-start(f32[8,32,128]{2,1,0:T(8,128)} %handed_attention.1._), calls=%async_computation.1 | async-start | bytes 262144 | tf_op jit(solution)/shard_map/all_to_all | solution.py:523
  55.8 0.0 copy-done.1
  55.8 0.0 copy-done.2
  55.9 0.0 copy-done.3
  55.9 0.0 copy-done.4
  55.9 0.0 copy-done.5
  55.9 0.0 copy-start
  55.9 1.9 %copy-done = bf16[6,128,2048]{2,1,0:T(8,128)(2,1)S(1)} copy-done((bf16[6,128,2048]{2,1,0:T(8,128)(2,1)S(1)}, bf16[6,128,2048]{2,1,0:T(8,128)(2,1)}, u32[]{:S(2)}) %copy-start) | copy-done | bytes 3145752
  57.8 2.0 %decode_scores.1 = (f32[256,896]{1,0:T(8,128)S(1)}, bf16[768,1024]{1,0:T(8,128)(2,1)S(1)}, f32[64,128]{1,0:T(8,128)S(1)}) custom-call(s32[2,3]{1,0:T(2,128)S(1)} %copy-done.2, s32[2,3]{1,0:T(2,128)S(1)} %copy-done.3, s32[2,2,16]{2,1,0:T(2,128)S(1)} %bitcast.11, s32[2,3]{1,0:T(2,128)S(1)} %bitcast.13, s32[3]{0:T(128)S(1)} %copy-done.5, ...), custom_call_target="tpu_custom_call" | custom-call | flops 50331648 | bytes 4194304 | tf_op jit(solution)/shard_map/decode_scores/pallas_call | solution.py:420
  59.8 3.4 %all-to-all-done.1.handed = f32[8,32,128]{2,1,0:T(8,128)S(1)} async-done(((f32[8,32,128]{2,1,0:T(8,128)}), f32[8,32,128]{2,1,0:T(8,128)S(1)}, u32[]{:S(2)}, u32[]{:S(2)}) %all-to-all-start.1) | async-done | bytes 131104 | tf_op jit(solution)/shard_map/all_to_all | solution.py:523
  63.2 1.4 %decode_mix.1 = bf16[3,2,4096]{2,1,0:T(2,128)(2,1)} custom-call(f32[256,896]{1,0:T(8,128)S(1)} %get-tuple-element.17.s_ref, bf16[768,1024]{1,0:T(8,128)(2,1)S(1)} %get-tuple-element.18.v_ref, f32[64,128]{1,0:T(8,128)S(1)} %get-tuple-element.19.new_ref, f32[8,32,128]{2,1,0:T(8,128)S(1)} %all-to-all-done.1.handed), custom_call_target="tpu_custom_call" | custom-call | flops 50331648 | bytes 4194304 | tf_op jit(solution)/shard_map/decode_mix/pallas_call | solution.py:483
Async XLA Ops:
  26.3 20.5 %collective-permute-start = (bf16[2048,256]{1,0:T(8,128)(2,1)}, bf16[2048,256]{1,0:T(8,128)(2,1)S(1)}, u32[]{:S(2)}, u32[]{:S(2)}) collective-permute-start(bf16[2048,256]{1,0:T(8,128)(2,1)} %get-tuple-element.12.kv_hbm), channel_id=1, source_target_pairs={{0,8},{8,0},{1,9},{9,1},{2,10},{10,2},{3,11},{11,3},{4,12},{12,4},... | collective-permute-start | bytes 3145736 | tf_op jit(solution)/shard_map/ppermute | solution.py:520
  26.8 19.9 %all-to-all-start = ((bf16[8,8,768]{2,1,0:T(8,128)(2,1)}), bf16[8,8,768]{2,1,0:T(8,128)(2,1)S(1)}, u32[]{:S(2)}, u32[]{:S(2)}) async-start(bf16[8,8,768]{2,1,0:T(8,128)(2,1)} %bitcast.14), calls=%async_computation | async-start | bytes 196608 | tf_op jit(solution)/shard_map/all_to_all | solution.py:519
  33.7 13.1 %copy-start.6 = (bf16[256,128]{1,0:T(8,128)(2,1)S(1)}, bf16[256,128]{1,0:T(8,128)(2,1)}, u32[]{:S(2)}) copy-start(bf16[256,128]{1,0:T(8,128)(2,1)} %get-tuple-element.15.q_ref) | copy-start | bytes 196612
  33.7 22.2 %copy-start.1 = (s32[2,16,2]{1,2,0:T(2,128)S(1)}, s32[2,16,2]{1,2,0:T(2,128)}, u32[]{:S(2)}) copy-start(s32[2,16,2]{1,2,0:T(2,128)} %param.15) | copy-start | bytes 772
  33.7 22.2 %copy-start.2 = (s32[2,3]{1,0:T(2,128)S(1)}, s32[2,3]{1,0:T(2,128)}, u32[]{:S(2)}) copy-start(s32[2,3]{1,0:T(2,128)} %counts.3) | copy-start | bytes 76
  33.7 22.2 %copy-start.3 = (s32[2,3]{1,0:T(2,128)S(1)}, s32[2,3]{1,0:T(2,128)}, u32[]{:S(2)}) copy-start(s32[2,3]{1,0:T(2,128)} %done.1) | copy-start | bytes 76
  33.7 22.2 %copy-start.4 = (s32[3,2]{0,1:T(2,128)S(1)}, s32[3,2]{0,1:T(2,128)}, u32[]{:S(2)}) copy-start(s32[3,2]{0,1:T(2,128)} %param.16) | copy-start | bytes 76
  33.7 22.2 %copy-start.5 = (s32[3]{0:T(128)S(1)}, s32[3]{0:T(128)}, u32[]{:S(2)}) copy-start(s32[3]{0:T(128)} %lens.1) | copy-start | bytes 40
  46.8 0.7 %copy-start.7 = (f32[8,128]{1,0:T(8,128)S(1)}, f32[8,128]{1,0:T(8,128)}, u32[]{:S(2)}) copy-start(f32[8,128]{1,0:T(8,128)} %get-tuple-element.16._) | copy-start | bytes 12292
  49.9 13.3 %all-to-all-start.1 = ((f32[8,32,128]{2,1,0:T(8,128)}), f32[8,32,128]{2,1,0:T(8,128)S(1)}, u32[]{:S(2)}, u32[]{:S(2)}) async-start(f32[8,32,128]{2,1,0:T(8,128)} %handed_attention.1._), calls=%async_computation.1 | async-start | bytes 262144 | tf_op jit(solution)/shard_map/all_to_all | solution.py:523
  55.9 1.9 %copy-start = (bf16[6,128,2048]{2,1,0:T(8,128)(2,1)S(1)}, bf16[6,128,2048]{2,1,0:T(8,128)(2,1)}, u32[]{:S(2)}) copy-start(bf16[6,128,2048]{2,1,0:T(8,128)(2,1)} %param.18) | copy-start | bytes 9437188

commit v7 on v6

--- a/solution.py
+++ b/solution.py
@@ -25,7 +25,8 @@
 SCALE = HD ** (-0.5)
 MASKED = -1e30
 PIECES = 5
-STRIPS = 4
+STRIPS = 2
+LOG2E = 1.4426950408889634
 AHEAD = 2
 MIB = 1 << 20
 VMEM = pltpu.VMEM
@@ -128,8 +129,8 @@
             if c + AHEAD < PIECES:
                 for copy in piece_copies(c + AHEAD):
                     copy.start()
-            if c + AHEAD == PIECES:
-                for copy in x_copies(0):
+            if c + AHEAD >= PIECES:
+                for copy in x_copies(c + AHEAD - PIECES):
                     copy.start()
             part = slice(c * piece, (c + 1) * piece)
             total += dot(x0[:, part], w[part, :])
@@ -162,9 +163,9 @@
         msg_ref[:, :HD] = jnp.where(sixth, facts, own[:, :HD]).astype(jnp.bfloat16)
         msg_ref[:, HD:] = own[:, HD:].astype(jnp.bfloat16)
 
-    @pl.when((step > 0) & (step < count))
+    @pl.when((step > 0) & (step + AHEAD <= count))
     def _():
-        for copy in x_copies(step):
+        for copy in x_copies(step + AHEAD - 1):
             copy.start()
 
     @pl.when(step > 0)
@@ -222,39 +223,37 @@
     )(*ints, dx, x, wq, wkv)
 
 
-def attend_prompt(lq, counts, q_hbm, kv_hbm, o_hbm, made_ref, qs, kvs, outs, sems):
+def attend_prompt(lq, half, counts, q_hbm, kv_hbm, *refs):
+    o_hbm, made_ref, qs, kvs, outs, sems = refs[-6:]
     made_ref[...] = jnp.zeros_like(made_ref)
     group = lax.axis_index("pool")
     c0, c1 = counts[group, 0], counts[group, 1]
     big = jnp.where(c0 == MOST_BLOCKS, 0, jnp.where(c1 == MOST_BLOCKS, c0, c0 + c1))
     cut = jnp.where(c0 == MOST_BLOCKS, c1, c0)
     loads, stores = [], []
-    for half in range(2):
-        for j in range(MOST_BLOCKS):
-            block = big + j if half == 0 else j + jnp.where(j >= big, MOST_BLOCKS, 0)
-            rows = pl.ds(pl.multiple_of(block * BLOCK_TOKENS, BLOCK_TOKENS), BLOCK_TOKENS)
-            here = pl.ds(j * BLOCK_TOKENS, BLOCK_TOKENS)
-            loads.append(pltpu.make_async_copy(kv_hbm.at[rows], kvs.at[half, here], sems.at[0, half, j]))
-            loads.append(pltpu.make_async_copy(q_hbm.at[rows], qs.at[half, here], sems.at[1, half, j]))
-            stores.append(pltpu.make_async_copy(outs.at[half, here], o_hbm.at[rows], sems.at[2, half, j]))
+    for j in range(MOST_BLOCKS):
+        block = big + j if half == 0 else j + jnp.where(j >= big, MOST_BLOCKS, 0)
+        rows = pl.ds(pl.multiple_of(block * BLOCK_TOKENS, BLOCK_TOKENS), BLOCK_TOKENS)
+        here = pl.ds(j * BLOCK_TOKENS, BLOCK_TOKENS)
+        loads.append(pltpu.make_async_copy(kv_hbm.at[rows], kvs.at[here], sems.at[0, j]))
+        loads.append(pltpu.make_async_copy(q_hbm.at[rows], qs.at[here], sems.at[1, j]))
+        stores.append(pltpu.make_async_copy(outs.at[here], o_hbm.at[rows], sems.at[2, j]))
     for copy in loads:
         copy.start()
     for copy in loads:
         copy.wait()
-    tokens = MOST_BLOCKS * BLOCK_TOKENS
     shape = (BLOCK_TOKENS, lq * BLOCK_TOKENS)
     causal = iota(shape, 0) <= iota(shape, 1) % BLOCK_TOKENS
-    flipped = [kvs[half, :, HD:].T for half in range(2)]
-
-    def scores_of(half, j):
-        q = qs[half, j * BLOCK_TOKENS : (j + 1) * BLOCK_TOKENS, :]
+    flipped = kvs[:, HD:].T
+
+    def scores_of(j):
+        q = qs[j * BLOCK_TOKENS : (j + 1) * BLOCK_TOKENS, :]
         q = jnp.concatenate([q[:, h * HD : (h + 1) * HD] for h in range(lq)], axis=0)
-        return dot_t(kvs[half, : (j + 1) * BLOCK_TOKENS, :HD], q)
-
-    order = [(half, j) for half in range(2) for j in range(MOST_BLOCKS)]
-    scores = scores_of(*order[0])
-    for k, (half, j) in enumerate(order):
-        later = scores_of(*order[k + 1]) if k + 1 < len(order) else None
+        return dot_t(kvs[: (j + 1) * BLOCK_TOKENS, :HD], q)
+
+    scores = scores_of(0)
+    for j in range(MOST_BLOCKS):
+        later = scores_of(j + 1) if j + 1 < MOST_BLOCKS else None
         weights = []
         for h in range(lq):
             cols = slice(h * BLOCK_TOKENS, (h + 1) * BLOCK_TOKENS)
@@ -267,43 +266,48 @@
                     tile = tile + jnp.where((i < cut) & (cut <= j), MASKED, 0.0)
                 tiles.append(tile)
             peak = jnp.max(functools.reduce(jnp.maximum, tiles), axis=0, keepdims=True)
-            raised = [jnp.exp((tile - peak) * SCALE) for tile in tiles]
+            raised = [jnp.exp2((tile - peak) * (SCALE * LOG2E)) for tile in tiles]
             inverse = 1.0 / jnp.sum(functools.reduce(jnp.add, raised), axis=0, keepdims=True)
             weights.append(jnp.concatenate([(t * inverse).astype(jnp.bfloat16) for t in raised], axis=0))
-        mixed = dot(flipped[half][:, : (j + 1) * BLOCK_TOKENS], jnp.concatenate(weights, axis=1))
+        mixed = dot(flipped[:, : (j + 1) * BLOCK_TOKENS], jnp.concatenate(weights, axis=1))
         mixed = mixed.astype(jnp.bfloat16)
         for h in range(lq):
             part = mixed[:, h * BLOCK_TOKENS : (h + 1) * BLOCK_TOKENS].T
-            outs[half, j * BLOCK_TOKENS : (j + 1) * BLOCK_TOKENS, h * HD : (h + 1) * HD] = part
+            outs[j * BLOCK_TOKENS : (j + 1) * BLOCK_TOKENS, h * HD : (h + 1) * HD] = part
         scores = later
-    for copy in stores:
+        if j == MOST_BLOCKS - 3:
+            for copy in stores[: j + 1]:
+                copy.start()
+    for copy in stores[MOST_BLOCKS - 2 :]:
         copy.start()
     for copy in stores:
         copy.wait()
 
 
-def prompt_attention(counts, q, kv):
+def prompt_attention(counts, q, kv, half, so_far=None, after=None):
     rows, cq = q.shape
     hbm = pl.BlockSpec(memory_space=pl.ANY)
+    more = () if so_far is None else (so_far, after)
     tokens = MOST_BLOCKS * BLOCK_TOKENS
     return pl.pallas_call(
-        functools.partial(attend_prompt, cq // HD),
-        in_specs=[pl.BlockSpec(memory_space=SMEM), hbm, hbm],
+        functools.partial(attend_prompt, cq // HD, half),
+        in_specs=[pl.BlockSpec(memory_space=SMEM), hbm, hbm] + [hbm] * len(more),
         out_specs=[hbm, pl.BlockSpec(memory_space=VMEM)],
         out_shape=[
             jax.ShapeDtypeStruct((rows, cq), jnp.bfloat16),
             jax.ShapeDtypeStruct((8, HD), jnp.float32),
         ],
         scratch_shapes=[
-            VMEM((2, tokens, cq), jnp.bfloat16),
-            VMEM((2, tokens, 2 * HD), jnp.bfloat16),
-            VMEM((2, tokens, cq), jnp.bfloat16),
-            pltpu.SemaphoreType.DMA((3, 2, MOST_BLOCKS)),
+            VMEM((tokens, cq), jnp.bfloat16),
+            VMEM((tokens, 2 * HD), jnp.bfloat16),
+            VMEM((tokens, cq), jnp.bfloat16),
+            pltpu.SemaphoreType.DMA((3, MOST_BLOCKS)),
         ],
+        input_output_aliases={3: 0} if more else {},
         compiler_params=pltpu.CompilerParams(vmem_limit_bytes=62 * MIB),
-        cost_estimate=pl.CostEstimate(flops=2 * rows * rows * cq, bytes_accessed=8 * rows * cq, transcendentals=rows * rows),
-        name="prompt_attention",
-    )(counts, q, kv)
+        cost_estimate=pl.CostEstimate(flops=2 * rows * rows * cq, bytes_accessed=4 * rows * cq, transcendentals=rows * rows // 2),
+        name="long_prompt" if half == 0 else "short_prompts",
+    )(counts, q, kv, *more)
 
 
 def row_head(n, lq, h, hh):
@@ -311,7 +315,7 @@
     return at // lq, at % lq
 
 
-def handed_part(n, lq, kv_ref, q_ref, msg_ref, _, o_ref):
+def handed_part(n, lq, kv_ref, q_ref, msg_ref, o_ref):
     rows = lq * n * GROUP_ROWS
     shape = (rows, HD)
     at_row, lane = iota(shape, 0), iota(shape, 1)
@@ -352,23 +356,12 @@
         o_ref[:, h * GROUP_ROWS : (h + 1) * GROUP_ROWS, :] = mixed[h * n : (h + 1) * n]
 
 
-def handed_attention(kv, q_own, msgs, after, n, lq):
-    rows = lq * n * GROUP_ROWS
-    vmem = pl.BlockSpec(memory_space=VMEM)
-    return pl.pallas_call(
-        functools.partial(handed_part, n, lq),
-        in_specs=[vmem] * 3 + [pl.BlockSpec(memory_space=pl.ANY)],
-        out_specs=vmem,
-        out_shape=jax.ShapeDtypeStruct((n, lq * GROUP_ROWS, HD), jnp.float32),
-        compiler_params=pltpu.CompilerParams(vmem_limit_bytes=24 * MIB),
-        cost_estimate=pl.CostEstimate(flops=6 * rows * HD * PTOK, bytes_accessed=2 * MIB, transcendentals=rows * PTOK),
-        name="handed_attention",
-    )(kv, q_own, msgs, after)
-
-
-def owner_scores(n, lq, counts, done, placed, table, lens, cache_hbm, msgs, _, s_ref, v_ref, new_ref, cache, sem, slot_row, slot_limit):
+def exchange_part(n, lq, *refs):
+    counts, done, placed, table, lens, cache_hbm, msgs, kv_ref, q_ref, _ = refs[:10]
+    handed_ref, s_ref, v_ref, new_ref, cache, sem, slot_row, slot_limit = refs[10:]
     load = pltpu.make_async_copy(cache_hbm, cache, sem)
     load.start()
+    handed_part(n, lq, kv_ref, q_ref, msgs, handed_ref)
     held = msgs[...].astype(jnp.float32)
     found = block_of_pages(counts, done, placed, table)
     for r in range(ROWS_DEV):
@@ -414,14 +407,15 @@
         v_ref[:, h * HD : (h + 1) * HD] = cache[:, (2 * h + 1) * HD : (2 * h + 2) * HD]
 
 
-def decode_scores(ints, cache, msgs, after, n, lq):
+def decode_scores(ints, cache, msgs, kv, q_own, after, n, lq):
     smem, vmem, hbm = [pl.BlockSpec(memory_space=space) for space in (SMEM, VMEM, pl.ANY)]
     rows = QH * GROUP_ROWS
     return pl.pallas_call(
-        functools.partial(owner_scores, n, lq),
-        in_specs=[smem] * 5 + [hbm, vmem, hbm],
-        out_specs=[vmem] * 3,
+        functools.partial(exchange_part, n, lq),
+        in_specs=[smem] * 5 + [hbm, vmem, vmem, vmem, hbm],
+        out_specs=[vmem] * 4,
         out_shape=[
+            jax.ShapeDtypeStruct((n, lq * GROUP_ROWS, HD), jnp.float32),
             jax.ShapeDtypeStruct((rows, (DEVICE_SLOTS + 1) * BLOCK_TOKENS), jnp.float32),
             jax.ShapeDtypeStruct((cache.shape[0], KVH * HD), jnp.bfloat16),
             jax.ShapeDtypeStruct((KVH * GROUP_ROWS, HD), jnp.float32),
@@ -432,10 +426,10 @@
             SMEM((DEVICE_SLOTS,), jnp.int32),
             SMEM((DEVICE_SLOTS,), jnp.int32),
         ],
-        compiler_params=pltpu.CompilerParams(vmem_limit_bytes=24 * MIB),
+        compiler_params=pltpu.CompilerParams(vmem_limit_bytes=61 * MIB),
         cost_estimate=pl.CostEstimate(flops=2 * rows * HD * 768, bytes_accessed=4 * MIB, transcendentals=0),
         name="decode_scores",
-    )(*ints, cache, msgs, after)
+    )(*ints, cache, msgs, kv, q_own, after)
 
 
 def owner_mix(s_ref, v_ref, new_ref, handed, o_ref):
@@ -485,7 +479,7 @@
         in_specs=[vmem] * 4,
         out_specs=vmem,
         out_shape=jax.ShapeDtypeStruct((ROWS_DEV, STEPS, QH * HD), jnp.bfloat16),
-        compiler_params=pltpu.CompilerParams(vmem_limit_bytes=24 * MIB),
+        compiler_params=pltpu.CompilerParams(vmem_limit_bytes=62 * MIB),
         cost_estimate=pl.CostEstimate(flops=2 * rows * HD * 768, bytes_accessed=4 * MIB, transcendentals=rows * 768),
         name="decode_mix",
     )(scores, values, new, parts)
@@ -514,14 +508,14 @@
     placement = placement.transpose(0, 2, 1)
     page_table = page_table.transpose(1, 0)
     ints = (prompt_blocks, finished, placement, page_table, row_lens)
-    first, size = 256, 896
+    first, size = 256, 256
     q, kv, q_own, msgs = project_all(ints, dx, prompt_x, q_weight, kv_weight, n, first, size)
     msgs = lax.all_to_all(msgs, "tp", split_axis=0, concat_axis=0, tiled=True)
     kv_other = lax.ppermute(kv, "pool", [(0, 1), (1, 0)])
-    prompt_attn, made = prompt_attention(prompt_blocks, q, kv)
-    handed = handed_attention(kv_other, q_own, msgs, made, n, lq)
+    prompt_attn, made = prompt_attention(prompt_blocks, q, kv, 0)
+    handed, scores, values, new = decode_scores(ints, cache, msgs, kv_other, q_own, made, n, lq)
     parts = lax.all_to_all(handed, "tp", split_axis=0, concat_axis=0, tiled=True)
-    scores, values, new = decode_scores(ints, cache, msgs, handed, n, lq)
+    prompt_attn, _ = prompt_attention(prompt_blocks, q, kv, 1, prompt_attn, handed)
     decode_attn = decode_mix(scores, values, new, parts)
     return prompt_attn, decode_attn.transpose(1, 0, 2)
 

time: 65 us -> 64.3 us (0.989)
  Pallas kernels: 44.4 us -> 48 us
  waiting for transfers between devices: 3.43 us -> 0.01 us
  local copies, waits for them, and re-layouts: 2.6 us -> 1.64 us
    all_to_all x1, waiting for transfers between devices: 3.42 us -> 0.01 us  [local(): lax.all_to_all(handed, 'tp', split_axis=0, concat_axis=0, tiled=True)]
    pallas_call x3, Pallas kernels: 17.4 us -> 20.3 us  [the longest x2 15 us: prompt_attention(): pl.pallas_call(functools.partial(attend_prompt, cq // HD, half), in_specs...]
    pallas_call x1, Pallas kernels: 1.37 us -> 3.04 us  [decode_mix(): pl.pallas_call(owner_mix, in_specs=[vmem] * 4, out_specs=vmem, out_shape=...]
    pallas_call x1, Pallas kernels: 25.7 us -> 24.7 us  [project_all(): pl.pallas_call(functools.partial(project, n, lq, first, size), grid=(1 +...]
    unnamed x16 -> x6, local copies, waits for them, and re-layouts: 2.6 us -> 1.64 us
  transfers between devices with their start and end apart: 3 -> 3, of which waited for: 1 -> 0; matrix products, arithmetic and copies ran while one was open for 0% -> 0% of each run, Pallas kernels for 23% -> 24%
where the time goes in v7:
time: 64.3 us; the launch traced here: 63.8 us
  Pallas kernels  48 us (75%)
  starting transfers between devices  13.4 us (21%)
  local copies, waits for them, and re-layouts  1.64 us (3%)
  between operations  0.71 us (1%)
    pallas_call x1, Pallas kernels, project_all(): pl.pallas_call(functools.partial(project, n, lq, first, size), grid=(1 +...  24.7 us
    pallas_call x2, Pallas kernels, prompt_attention(): pl.pallas_call(functools.partial(attend_prompt, cq // HD, half), in_specs...  15 us
    all_to_all x1, starting transfers between devices, local(): msgs = lax.all_to_all(msgs, 'tp', split_axis=0, concat_axis=0, tiled=True)  6.86 us
    all_to_all x1, starting transfers between devices, local(): lax.all_to_all(handed, 'tp', split_axis=0, concat_axis=0, tiled=True)  6.02 us
    pallas_call x1, Pallas kernels, decode_scores(): pl.pallas_call(functools.partial(exchange_part, n, lq), in_specs=[smem] *...  5.29 us
    pallas_call x1, Pallas kernels, decode_mix(): pl.pallas_call(owner_mix, in_specs=[vmem] * 4, out_specs=vmem, out_shape=...  3.04 us
    unnamed x6, local copies, waits for them, and re-layouts  1.64 us
  transfers between devices with their start and end apart: 3, of which 0 were waited for; matrix products, arithmetic and copies ran while one was open for 0% of the time, Pallas kernels for 24%

profile of v7, /device:TPU:0, one launch (start us, length us, event | category | flops | bytes accessed | tf_op | source)
XLA Modules:
  0.0 63.8 jit_solution(2795230127889564311)
XLA Ops:
  0.6 24.7 %project.1 = (bf16[2048,512]{1,0:T(8,128)(2,1)}, bf16[2048,256]{1,0:T(8,128)(2,1)}, bf16[256,128]{1,0:T(8,128)(2,1)}, bf16[64,768]{1,0:T(8,128)(2,1)}) custom-call(s32[2,3]{1,0:T(2,128)} %counts.3, s32[2,3]{1,0:T(2,128)} %refs_1_.3, s32[2,2,16]{2,1,0:T(2,128)} %bitcast.11, s32[2,3]{1,0:T(2,128)} %bitcast.13, s32[3]{0:T(128)} %refs_4_.3, ...), custom_call_target="tpu_custom_call" | custom-call | flops 16106127360 | bytes 31981568 | tf_op jit(solution)/shard_map/project/pallas_call | solution.py:195
  25.3 0.5 collective-permute-start
  25.8 6.9 %all-to-all-start = ((bf16[8,8,768]{2,1,0:T(8,128)(2,1)}), bf16[8,8,768]{2,1,0:T(8,128)(2,1)S(1)}, u32[]{:S(2)}, u32[]{:S(2)}) async-start(bf16[8,8,768]{2,1,0:T(8,128)(2,1)} %bitcast.9), calls=%async_computation | async-start | bytes 196608 | tf_op jit(solution)/shard_map/all_to_all | solution.py:513
  32.7 7.4 %long_prompt.1 = (bf16[2048,512]{1,0:T(8,128)(2,1)}, f32[8,128]{1,0:T(8,128)}) custom-call(s32[2,3]{1,0:T(2,128)} %counts.3, bf16[2048,512]{1,0:T(8,128)(2,1)} %get-tuple-element.13.q_hbm, bf16[2048,256]{1,0:T(8,128)(2,1)} %get-tuple-element.14.kv_hbm), custom_call_target="tpu_custom_call" | custom-call | flops 4294967296 | bytes 4194304 | tf_op jit(solution)/shard_map/long_prompt/pallas_call | solution.py:292
  40.1 0.0 all-to-all-done
  40.1 0.0 copy-start.2
  40.1 0.0 collective-permute-done.refs_7_
  40.2 0.0 copy-start
  40.2 0.6 copy-done.2
  40.8 0.4 copy-done
  41.2 5.3 %decode_scores.1 = (f32[8,32,128]{2,1,0:T(8,128)}, f32[256,896]{1,0:T(8,128)}, bf16[768,1024]{1,0:T(8,128)(2,1)}, f32[64,128]{1,0:T(8,128)}) custom-call(s32[2,3]{1,0:T(2,128)} %counts.3, s32[2,3]{1,0:T(2,128)} %refs_1_.3, s32[2,2,16]{2,1,0:T(2,128)} %bitcast.12, s32[2,3]{1,0:T(2,128)} %bitcast.14, s32[3]{0:T(128)} %refs_4_.3, bf16[768,2048]{1,0:T(8,128)(2,1)} %bitcast.7, ...), custom_call_target="tpu_custom_call" | custom-call | flops 50331648 | bytes 4194304 | tf_op jit(solution)/shard_map/decode_scores/pallas_call | solution.py:413
  46.5 6.0 %all-to-all-start.1 = ((f32[8,32,128]{2,1,0:T(8,128)}), f32[8,32,128]{2,1,0:T(8,128)S(1)}, u32[]{:S(2)}, u32[]{:S(2)}) async-start(f32[8,32,128]{2,1,0:T(8,128)} %get-tuple-element.19.refs_1_), calls=%async_computation.1 | async-start | bytes 262144 | tf_op jit(solution)/shard_map/all_to_all | solution.py:517
  52.5 7.6 %short_prompts.1 = (bf16[2048,512]{1,0:T(8,128)(2,1)}, f32[8,128]{1,0:T(8,128)}) custom-call(s32[2,3]{1,0:T(2,128)} %counts.3, bf16[2048,512]{1,0:T(8,128)(2,1)} %get-tuple-element.13.q_hbm, bf16[2048,256]{1,0:T(8,128)(2,1)} %get-tuple-element.14.kv_hbm, bf16[2048,512]{1,0:T(8,128)(2,1)} %get-tuple-element.15.refs_0_, ...), custom_call_target="tpu_custom_call", output_to_operand_aliasing={{0}: (3, {})} | custom-call | flops 4294967296 | bytes 4194304 | tf_op jit(solution)/shard_map/short_prompts/pallas_call | solution.py:292
  60.1 0.0 all-to-all-done.1.handed
  60.1 0.0 copy-start.1
  60.1 0.6 copy-done.1
  60.7 3.0 %decode_mix.1 = bf16[3,2,4096]{2,1,0:T(2,128)(2,1)} custom-call(f32[256,896]{1,0:T(8,128)} %get-tuple-element.21.s_ref, bf16[768,1024]{1,0:T(8,128)(2,1)} %get-tuple-element.22.v_ref, f32[64,128]{1,0:T(8,128)} %get-tuple-element.23.new_ref, f32[8,32,128]{2,1,0:T(8,128)} %copy-done.1), custom_call_target="tpu_custom_call" | custom-call | flops 50331648 | bytes 4194304 | tf_op jit(solution)/shard_map/decode_mix/pallas_call | solution.py:477
Async XLA Ops:
  25.3 14.8 %collective-permute-start = (bf16[2048,256]{1,0:T(8,128)(2,1)}, bf16[2048,256]{1,0:T(8,128)(2,1)S(1)}, u32[]{:S(2)}, u32[]{:S(2)}) collective-permute-start(bf16[2048,256]{1,0:T(8,128)(2,1)} %get-tuple-element.14.kv_hbm), channel_id=1, source_target_pairs={{0,8},{8,0},{1,9},{9,1},{2,10},{10,2},{3,11},{11,3},{4,12},{12,4},... | collective-permute-start | bytes 3145736 | tf_op jit(solution)/shard_map/ppermute | solution.py:514
  25.8 14.3 %all-to-all-start = ((bf16[8,8,768]{2,1,0:T(8,128)(2,1)}), bf16[8,8,768]{2,1,0:T(8,128)(2,1)S(1)}, u32[]{:S(2)}, u32[]{:S(2)}) async-start(bf16[8,8,768]{2,1,0:T(8,128)(2,1)} %bitcast.9), calls=%async_computation | async-start | bytes 196608 | tf_op jit(solution)/shard_map/all_to_all | solution.py:513
  40.1 0.6 copy-start.2
  40.2 1.0 %copy-start = (bf16[2048,256]{1,0:T(8,128)(2,1)}, bf16[2048,256]{1,0:T(8,128)(2,1)S(1)}, u32[]{:S(2)}) copy-start(bf16[2048,256]{1,0:T(8,128)(2,1)S(1)} %collective-permute-done.refs_7_) | copy-start | bytes 3145732
  46.5 13.6 %all-to-all-start.1 = ((f32[8,32,128]{2,1,0:T(8,128)}), f32[8,32,128]{2,1,0:T(8,128)S(1)}, u32[]{:S(2)}, u32[]{:S(2)}) async-start(f32[8,32,128]{2,1,0:T(8,128)} %get-tuple-element.19.refs_1_), calls=%async_computation.1 | async-start | bytes 262144 | tf_op jit(solution)/shard_map/all_to_all | solution.py:517
  60.1 0.6 copy-start.1

commit v8 on v6

v8 whole, which is shorter than its diff:
```python
import functools

import jax
import jax.numpy as jnp
from jax import lax
from jax.experimental import pallas as pl
from jax.experimental.pallas import tpu as pltpu
from jax.sharding import PartitionSpec as P

QH = 32
KVH = 8
GQ = QH // KVH
HD = 128
BLOCK_TOKENS = 128
PTOK = 2048
NPROMPT = 3
MOST_BLOCKS = 8
PAGES = 2
STEPS = 2
NBLK = 16
DEVICE_SLOTS = 6
ROWS_DEV = 3
GROUP_ROWS = 8
KEY_VALUE_COLUMNS = 2048
SCALE = HD ** (-0.5)
MASKED = -1e30
PIECES = 5
STRIPS = 4
LOG2E = 1.4426950408889634
AHEAD = 2
MIB = 1 << 20
VMEM = pltpu.VMEM
SMEM = pltpu.SMEM


def dot(a, b):
    return jnp.dot(a, b, preferred_element_type=jnp.float32)


def dot_t(a, b):
    return lax.dot_general(a, b, (((1,), (1,)), ((), ())), preferred_element_type=jnp.float32)


def iota(shape, axis):
    return lax.broadcasted_iota(jnp.int32, shape, axis)


def row_of(rs):
    return jnp.where(rs >= 2 * ROWS_DEV, ROWS_DEV, jnp.where(rs >= ROWS_DEV, rs - ROWS_DEV, rs))


def block_of_pages(counts, done, placed, table):
    me = lax.axis_index("tp")
    other = 1 - lax.axis_index("pool")
    first_end = counts[other, 0]
    second_end = first_end + counts[other, 1]
    found = [[jnp.int32(-1)] * PAGES for _ in range(ROWS_DEV)]
    for b in range(NBLK):
        live = jnp.where(
            b < first_end, done[other, 0], jnp.where(b < second_end, done[other, 1], done[other, 2])
        )
        slot = jnp.where((live > 0) & (placed[other, 0, b] == me), placed[other, 1, b], -1)
        for r in range(ROWS_DEV):
            for p in range(PAGES):
                found[r][p] = jnp.where(slot == table[p, r], b, found[r][p])
    return found


def project(n, lq, first, size, *refs):
    dx_hbm, x_hbm, wq_hbm, wkv_hbm, q_hbm, kv_hbm, own_ref = refs[:7]
    x0, xs, w, q_out, kv_out, x_sems, w_sems, out_sems = refs[7:]
    depth = w.shape[0]
    count = xs.shape[0]
    cq = lq * HD
    piece = depth // PIECES
    own_rows = dx_hbm.shape[0]
    step = pl.program_id(0)

    def piece_copies(c):
        part = pl.ds(c * piece, piece)
        return [
            pltpu.make_async_copy(x_hbm.at[pl.ds(0, first), part], x0.at[pl.ds(0, first), part], w_sems.at[0, c]),
            pltpu.make_async_copy(dx_hbm.at[:, part], x0.at[pl.ds(first, own_rows), part], w_sems.at[1, c]),
            pltpu.make_async_copy(wq_hbm.at[part], w.at[part, pl.ds(0, cq)], w_sems.at[2, c]),
            pltpu.make_async_copy(wkv_hbm.at[part], w.at[part, pl.ds(cq, 2 * HD)], w_sems.at[3, c]),
        ]

    def x_copies(k):
        strip = size // STRIPS
        copies = []
        for i in range(STRIPS):
            rows = pl.ds(pl.multiple_of(first + k * size + i * strip, 16), strip)
            copies.append(
                pltpu.make_async_copy(x_hbm.at[rows], xs.at[k, pl.ds(i * strip, strip)], x_sems.at[k, i])
            )
        return copies

    def out_copies(k):
        if isinstance(k, int):
            rows = pl.ds(0, first)
        else:
            rows = pl.ds(pl.multiple_of(first + (k - 1) * size, 64), size)
        return [
            pltpu.make_async_copy(q_out.at[rows], q_hbm.at[rows], out_sems.at[0, k]),
            pltpu.make_async_copy(kv_out.at[rows], kv_hbm.at[rows], out_sems.at[1, k]),
        ]

    def keep(total, rows):
        q_out[rows, :] = total[:, :cq].astype(jnp.bfloat16)
        kv_out[rows, :] = total[:, cq:].astype(jnp.bfloat16)

    @pl.when(step == 0)
    def _():
        for c in range(AHEAD):
            for copy in piece_copies(c):
                copy.start()
        total = 0.0
        for c in range(PIECES):
            for copy in piece_copies(c):
                copy.wait()
            if c + AHEAD < PIECES:
                for copy in piece_copies(c + AHEAD):
                    copy.start()
            if c + AHEAD >= PIECES:
                for copy in x_copies(c + AHEAD - PIECES):
                    copy.start()
            part = slice(c * piece, (c + 1) * piece)
            total += dot(x0[:, part], w[part, :])
        keep(total[:first], pl.ds(0, first))
        for copy in out_copies(0):
            copy.start()
        shape = (n * GROUP_ROWS, own_rows)
        to, fro = iota(shape, 0), iota(shape, 1)
        owner, rs = to // GROUP_ROWS, to % GROUP_ROWS
        wanted = owner * ROWS_DEV + row_of(rs) + jnp.where(rs >= ROWS_DEV, ROWS_DEV * n, 0)
        pick = ((fro == wanted) & (rs < STEPS * ROWS_DEV)).astype(jnp.float32).astype(jnp.bfloat16)
        own_ref[...] = dot(pick, total[first:].astype(jnp.bfloat16)).astype(jnp.bfloat16)

    @pl.when((step > 0) & (step + AHEAD <= count))
    def _():
        for copy in x_copies(step + AHEAD - 1):
            copy.start()

    @pl.when(step > 0)
    def _():
        for copy in x_copies(step - 1):
            copy.wait()
        keep(dot(xs[step - 1], w[...]), pl.ds(pl.multiple_of(first + (step - 1) * size, 64), size))
        for copy in out_copies(step):
            copy.start()

    @pl.when(step == count)
    def _():
        for copy in out_copies(0):
            copy.wait()
        for k in range(1, count + 1):
            for copy in out_copies(jnp.int32(k)):
                copy.wait()


def project_all(dx, x, wq, wkv, n, first, size):
    rows, depth = x.shape
    cq, ckv = wq.shape[1], wkv.shape[1]
    lq = cq // HD
    count = (rows - first) // size
    vmem, hbm = pl.BlockSpec(memory_space=VMEM), pl.BlockSpec(memory_space=pl.ANY)
    return pl.pallas_call(
        functools.partial(project, n, lq, first, size),
        grid=(1 + count,),
        in_specs=[hbm] * 4,
        out_specs=[hbm, hbm, vmem],
        out_shape=[
            jax.ShapeDtypeStruct((rows, cq), jnp.bfloat16),
            jax.ShapeDtypeStruct((rows, ckv), jnp.bfloat16),
            jax.ShapeDtypeStruct((n * GROUP_ROWS, cq + ckv), jnp.bfloat16),
        ],
        scratch_shapes=[
            VMEM((first + dx.shape[0], depth), jnp.bfloat16),
            VMEM((count, size, depth), jnp.bfloat16),
            VMEM((depth, cq + ckv), jnp.bfloat16),
            VMEM((rows, cq), jnp.bfloat16),
            VMEM((rows, ckv), jnp.bfloat16),
            pltpu.SemaphoreType.DMA((count, STRIPS)),
            pltpu.SemaphoreType.DMA((4, PIECES)),
            pltpu.SemaphoreType.DMA((2, count + 1)),
        ],
        compiler_params=pltpu.CompilerParams(vmem_limit_bytes=62 * MIB),
        cost_estimate=pl.CostEstimate(
            flops=2 * rows * depth * (cq + ckv),
            bytes_accessed=2 * (rows + cq + ckv) * depth + 2 * rows * (cq + ckv),
            transcendentals=0,
        ),
        name="project",
    )(dx, x, wq, wkv)


def attend_prompt(lq, counts, q_hbm, kv_hbm, _, o_hbm, qs, kvs, outs, sems):
    group = lax.axis_index("pool")
    c0, c1 = counts[group, 0], counts[group, 1]
    big = jnp.where(c0 == MOST_BLOCKS, 0, jnp.where(c1 == MOST_BLOCKS, c0, c0 + c1))
    cut = jnp.where(c0 == MOST_BLOCKS, c1, c0)
    loads, stores = [], []
    for half in range(2):
        for j in range(MOST_BLOCKS):
            block = big + j if half == 0 else j + jnp.where(j >= big, MOST_BLOCKS, 0)
            rows = pl.ds(pl.multiple_of(block * BLOCK_TOKENS, BLOCK_TOKENS), BLOCK_TOKENS)
            here = pl.ds(j * BLOCK_TOKENS, BLOCK_TOKENS)
            loads.append(pltpu.make_async_copy(kv_hbm.at[rows], kvs.at[half, here], sems.at[0, half, j]))
            loads.append(pltpu.make_async_copy(q_hbm.at[rows], qs.at[half, here], sems.at[1, half, j]))
            stores.append(pltpu.make_async_copy(outs.at[half, here], o_hbm.at[rows], sems.at[2, half, j]))
    for copy in loads:
        copy.start()
    for copy in loads[: len(loads) // 2]:
        copy.wait()
    shape = (BLOCK_TOKENS, lq * BLOCK_TOKENS)
    causal = iota(shape, 0) <= iota(shape, 1) % BLOCK_TOKENS

    def scores_of(half, j):
        q = qs[half, j * BLOCK_TOKENS : (j + 1) * BLOCK_TOKENS, :]
        q = jnp.concatenate([q[:, h * HD : (h + 1) * HD] for h in range(lq)], axis=0)
        return dot_t(kvs[half, : (j + 1) * BLOCK_TOKENS, :HD], q)

    flipped = [kvs[0, :, HD:].T, None]
    order = [(half, j) for half in range(2) for j in range(MOST_BLOCKS)]
    scores = scores_of(*order[0])
    for k, (half, j) in enumerate(order):
        if k + 1 == MOST_BLOCKS:
            for copy in loads[len(loads) // 2 :]:
                copy.wait()
            flipped[1] = kvs[1, :, HD:].T
        later = scores_of(*order[k + 1]) if k + 1 < len(order) else None
        weights = []
        for h in range(lq):
            cols = slice(h * BLOCK_TOKENS, (h + 1) * BLOCK_TOKENS)
            tiles = []
            for i in range(j + 1):
                tile = scores[i * BLOCK_TOKENS : (i + 1) * BLOCK_TOKENS, cols]
                if i == j:
                    tile = jnp.where(causal[:, cols], tile, MASKED)
                elif half == 1:
                    tile = tile + jnp.where((i < cut) & (cut <= j), MASKED, 0.0)
                tiles.append(tile)
            peak = jnp.max(functools.reduce(jnp.maximum, tiles), axis=0, keepdims=True) * (SCALE * LOG2E)
            raised = [jnp.exp2(tile * (SCALE * LOG2E) - peak) for tile in tiles]
            total = jnp.sum(functools.reduce(jnp.add, raised), axis=0, keepdims=True)
            peak = peak + jnp.log2(total)
            raised = [jnp.exp2(tile * (SCALE * LOG2E) - peak).astype(jnp.bfloat16) for tile in tiles]
            weights.append(jnp.concatenate(raised, axis=0))
        mixed = dot(flipped[half][:, : (j + 1) * BLOCK_TOKENS], jnp.concatenate(weights, axis=1))
        mixed = mixed.astype(jnp.bfloat16)
        for h in range(lq):
            part = mixed[:, h * BLOCK_TOKENS : (h + 1) * BLOCK_TOKENS].T
            outs[half, j * BLOCK_TOKENS : (j + 1) * BLOCK_TOKENS, h * HD : (h + 1) * HD] = part
        scores = later
        if k + 1 == MOST_BLOCKS:
            for copy in stores[:MOST_BLOCKS]:
                copy.start()
    for copy in stores[MOST_BLOCKS:]:
        copy.start()
    for copy in stores:
        copy.wait()


def prompt_attention(counts, q, kv, after):
    rows, cq = q.shape
    hbm = pl.BlockSpec(memory_space=pl.ANY)
    tokens = MOST_BLOCKS * BLOCK_TOKENS
    return pl.pallas_call(
        functools.partial(attend_prompt, cq // HD),
        in_specs=[pl.BlockSpec(memory_space=SMEM)] + [hbm] * 3,
        out_specs=hbm,
        out_shape=jax.ShapeDtypeStruct((rows, cq), jnp.bfloat16),
        scratch_shapes=[
            VMEM((2, tokens, cq), jnp.bfloat16),
            VMEM((2, tokens, 2 * HD), jnp.bfloat16),
            VMEM((2, tokens, cq), jnp.bfloat16),
            pltpu.SemaphoreType.DMA((3, 2, MOST_BLOCKS)),
        ],
        compiler_params=pltpu.CompilerParams(vmem_limit_bytes=62 * MIB),
        cost_estimate=pl.CostEstimate(flops=4 * rows * rows * cq, bytes_accessed=8 * rows * cq, transcendentals=rows * rows),
        name="prompt_attention",
    )(counts, q, kv, after)


def row_head(n, lq, h, hh):
    at = h * GQ + hh
    return at // lq, at % lq


def pass_on(*refs):
    pass


def wait_for(kv, facts):
    hbm = pl.BlockSpec(memory_space=pl.ANY)
    return pl.pallas_call(
        pass_on,
        in_specs=[hbm, hbm],
        out_specs=hbm,
        out_shape=jax.ShapeDtypeStruct(kv.shape, kv.dtype),
        input_output_aliases={0: 0},
        compiler_params=pltpu.CompilerParams(vmem_limit_bytes=62 * MIB),
        name="wait_for",
    )(kv, facts)


def handed_part(n, lq, counts, done, placed, facts_ref, kv_ref, own_ref, o_ref):
    rows = lq * n * GROUP_ROWS
    shape = (rows, HD)
    at_row, lane = iota(shape, 0), iota(shape, 1)
    rs = at_row % GROUP_ROWS
    owner = (iota((rows, 1), 0) // GROUP_ROWS) % n
    own = own_ref[...]
    queries = jnp.concatenate([own[:, h * HD : (h + 1) * HD] for h in range(lq)], axis=0)
    scores = dot_t(queries, kv_ref[:, :HD]) * SCALE
    facts = jnp.broadcast_to(facts_ref[...], (n, GROUP_ROWS, HD)).reshape(n * GROUP_ROWS, HD)
    facts = jnp.concatenate([facts] * lq, axis=0)

    def column(kind):
        return jnp.sum(jnp.where(lane == kind * GROUP_ROWS + rs, facts, 0.0), axis=1, keepdims=True)

    slots = [column(page) for page in range(PAGES)]
    length = column(PAGES)
    other = 1 - lax.axis_index("pool")
    first_end = counts[other, 0]
    second_end = first_end + counts[other, 1]
    lane_f = lane.astype(jnp.float32)
    parts = []
    for b in range(NBLK):
        live = jnp.where(
            b < first_end, done[other, 0], jnp.where(b < second_end, done[other, 1], done[other, 2])
        )
        to = jnp.where(live > 0, placed[other, 0, b], -1)
        slot = placed[other, 1, b].astype(jnp.float32)
        limit = jnp.where(slots[0] == slot, length, jnp.where(slots[1] == slot, length - BLOCK_TOKENS, 0.0))
        limit = jnp.where(owner == to, limit, 0.0)
        part = scores[:, b * BLOCK_TOKENS : (b + 1) * BLOCK_TOKENS]
        parts.append(jnp.where(lane_f < limit, part, MASKED))
    scores = jnp.concatenate(parts, axis=1)
    top = jnp.max(scores, axis=1, keepdims=True)
    raised = jnp.exp(scores - top)
    total = jnp.sum(raised, axis=1, keepdims=True)
    near = raised.astype(jnp.bfloat16)
    rest = (raised - near.astype(jnp.float32)).astype(jnp.bfloat16)
    values = kv_ref[:, HD:]
    mixed = (dot(near, values) + dot(rest, values)).reshape(lq * n, GROUP_ROWS, HD)

    def line(col):
        spread = jnp.where(lane == rs, col, 0.0).reshape(lq * n, GROUP_ROWS, HD)
        return jnp.sum(spread, axis=1, keepdims=True)

    rs3 = rs.reshape(lq * n, GROUP_ROWS, HD)
    mixed = jnp.where(rs3 == 6, line(top), jnp.where(rs3 == 7, line(total), mixed))
    for h in range(lq):
        o_ref[:, h * GROUP_ROWS : (h + 1) * GROUP_ROWS, :] = mixed[h * n : (h + 1) * n]
    for k in range(lq + 2):
        tile = own[:, k * HD : (k + 1) * HD].astype(jnp.float32).reshape(n, GROUP_ROWS, HD)
        o_ref[:, (lq + k) * GROUP_ROWS : (lq + k + 1) * GROUP_ROWS, :] = tile


def handed_attention(ints, facts, kv, own, n, lq):
    rows = lq * n * GROUP_ROWS
    smem, vmem = pl.BlockSpec(memory_space=SMEM), pl.BlockSpec(memory_space=VMEM)
    return pl.pallas_call(
        functools.partial(handed_part, n, lq),
        in_specs=[smem] * 3 + [vmem] * 3,
        out_specs=vmem,
        out_shape=jax.ShapeDtypeStruct((n, 2 * (lq + 1) * GROUP_ROWS, HD), jnp.float32),
        compiler_params=pltpu.CompilerParams(vmem_limit_bytes=24 * MIB),
        cost_estimate=pl.CostEstimate(flops=6 * rows * HD * PTOK, bytes_accessed=2 * MIB, transcendentals=rows * PTOK),
        name="handed_attention",
    )(*ints[:3], facts, kv, own)


def owner_part(n, lq, counts, done, placed, table, lens, cache_hbm, msgs, o_ref, cache, sems, slot_row, slot_limit):
    loads = []
    for slot in range(DEVICE_SLOTS):
        part = pl.ds(slot * BLOCK_TOKENS, BLOCK_TOKENS)
        loads.append(pltpu.make_async_copy(cache_hbm.at[part], cache.at[part], sems.at[slot]))
    for load in loads:
        load.start()
    found = block_of_pages(counts, done, placed, table)
    for r in range(ROWS_DEV):
        for p in range(PAGES):
            slot_row[table[p, r]] = jnp.int32(r)
            slot_limit[table[p, r]] = jnp.where(found[r][p] < 0, lens[r] - p * BLOCK_TOKENS, 0)

    def tile(t, k):
        return msgs[t, k * GROUP_ROWS : (k + 1) * GROUP_ROWS, :]

    groups = QH
    rows = groups * GROUP_ROWS
    span = GQ * GROUP_ROWS
    queries, keys, values, mixed = [], [], [], []
    for h in range(KVH):
        for hh in range(GQ):
            t, at = row_head(n, lq, h, hh)
            queries.append(tile(t, lq + at))
            mixed.append(tile(t, at))
        t, _ = row_head(n, lq, h, 0)
        keys += [tile(t, 2 * lq)] * GQ
        values.append(tile(t, 2 * lq + 1))
    queries = jnp.concatenate(queries, axis=0)
    earlier = jnp.concatenate([pltpu.roll(key, ROWS_DEV, 0) for key in keys], axis=0)
    keys = jnp.concatenate(keys, axis=0)
    at_row, lane = iota((rows, HD), 0), iota((rows, HD), 1)
    r = row_of(at_row % GROUP_ROWS)
    rounded = queries.astype(jnp.bfloat16)
    now = jnp.sum(queries * keys, axis=1, keepdims=True) * SCALE
    before = jnp.sum(queries * earlier, axis=1, keepdims=True) * SCALE
    rs1 = iota((rows, 1), 0) % GROUP_ROWS
    before = jnp.where((rs1 >= ROWS_DEV) & (rs1 < STEPS * ROWS_DEV), before, MASKED)
    mixed = jnp.concatenate(mixed, axis=0).reshape(groups, GROUP_ROWS, HD)
    shape = (groups, GROUP_ROWS, HD)
    mine = iota(shape, 1) == iota(shape, 2)

    def column(at):
        line = jnp.broadcast_to(mixed[:, at : at + 1, :], shape)
        return jnp.sum(jnp.where(mine, line, 0.0), axis=2, keepdims=True).reshape(rows, 1)

    other_peak, other_total = column(6), column(7)
    for load in loads:
        load.wait()
    scores = jnp.concatenate(
        [dot_t(rounded[h * span : (h + 1) * span], cache[:, 2 * h * HD : (2 * h + 1) * HD]) for h in range(KVH)],
        axis=0,
    )
    parts = []
    for slot in range(DEVICE_SLOTS):
        part = scores[:, slot * BLOCK_TOKENS : (slot + 1) * BLOCK_TOKENS]
        usable = (r == slot_row[slot]) & (lane < slot_limit[slot])
        parts.append(jnp.where(usable, part * SCALE, MASKED))
    scores = jnp.concatenate(parts, axis=1)
    peak = jnp.maximum(jnp.max(scores, axis=1, keepdims=True), jnp.maximum(now, before))
    peak = jnp.maximum(peak, other_peak)
    raised, now, before = jnp.exp(scores - peak), jnp.exp(now - peak), jnp.exp(before - peak)
    other = jnp.exp(other_peak - peak)
    inverse = 1.0 / (jnp.sum(raised, axis=1, keepdims=True) + now + before + other * other_total)
    weights = (raised * inverse).astype(jnp.bfloat16)
    now = (now * inverse).astype(jnp.bfloat16).astype(jnp.float32)
    before = (before * inverse).astype(jnp.bfloat16).astype(jnp.float32)
    mixed = mixed.reshape(rows, HD) * (other * inverse)
    out = []
    for h in range(KVH):
        part = slice(h * span, (h + 1) * span)
        own = mixed[part] + dot(weights[part], cache[:, (2 * h + 1) * HD : (2 * h + 2) * HD])
        last = pltpu.roll(values[h], ROWS_DEV, 0)
        for hh in range(GQ):
            some = slice(h * span + hh * GROUP_ROWS, h * span + (hh + 1) * GROUP_ROWS)
            line = own[hh * GROUP_ROWS : (hh + 1) * GROUP_ROWS]
            out.append(line + now[some] * values[h] + before[some] * last)
    out = jnp.concatenate(out, axis=1)
    for k in range(ROWS_DEV):
        steps = [out[s * ROWS_DEV + k : s * ROWS_DEV + k + 1] for s in range(STEPS)]
        o_ref[k] = jnp.concatenate(steps, axis=0).astype(jnp.bfloat16)


def decode_attention(ints, cache, msgs, n, lq):
    smem, vmem, hbm = [pl.BlockSpec(memory_space=space) for space in (SMEM, VMEM, pl.ANY)]
    rows = QH * GROUP_ROWS
    return pl.pallas_call(
        functools.partial(owner_part, n, lq),
        in_specs=[smem] * 5 + [hbm, vmem],
        out_specs=vmem,
        out_shape=jax.ShapeDtypeStruct((ROWS_DEV, STEPS, QH * HD), jnp.bfloat16),
        scratch_shapes=[
            VMEM(cache.shape, jnp.bfloat16),
            pltpu.SemaphoreType.DMA((DEVICE_SLOTS,)),
            SMEM((DEVICE_SLOTS,), jnp.int32),
            SMEM((DEVICE_SLOTS,), jnp.int32),
        ],
        compiler_params=pltpu.CompilerParams(vmem_limit_bytes=62 * MIB),
        cost_estimate=pl.CostEstimate(flops=4 * rows * HD * 768, bytes_accessed=4 * MIB, transcendentals=rows * 768),
        name="decode_attention",
    )(*ints, cache, msgs)


def local(
    prompt_x,
    q_weight,
    kv_weight,
    prompt_blocks,
    finished,
    placement,
    page_table,
    row_lens,
    kv_cache,
    decode_x,
):
    n = lax.axis_size("tp")
    lq = q_weight.shape[1] // HD
    share = GQ // lq
    if share > 1:
        sets = [[k * share + i for i in range(share)] for k in range(n // share)]
        kv_weight = lax.all_gather(kv_weight, "tp", axis=1, tiled=True, axis_index_groups=sets)
    cache = kv_cache.reshape(-1, kv_cache.shape[2])
    dx = decode_x.reshape(-1, decode_x.shape[2])
    placement = placement.transpose(0, 2, 1)
    page_table = page_table.transpose(1, 0)
    ints = (prompt_blocks, finished, placement, page_table, row_lens)
    spare = jnp.zeros((GROUP_ROWS - STEPS * ROWS_DEV,), jnp.int32)
    facts = []
    for fact in (page_table[0], page_table[1], row_lens):
        facts += [fact] * STEPS + [spare]
    facts.append(jnp.zeros((HD - 3 * GROUP_ROWS,), jnp.int32))
    facts = jnp.broadcast_to(jnp.concatenate(facts).astype(jnp.float32), (n, 1, HD))
    facts = lax.all_to_all(facts, "tp", split_axis=0, concat_axis=0, tiled=True)
    first, size = 256, 448
    q, kv, own = project_all(dx, prompt_x, q_weight, kv_weight, n, first, size)
    kv = wait_for(kv, facts)
    kv_other = lax.ppermute(kv, "pool", [(0, 1), (1, 0)])
    msgs = handed_attention(ints, facts, kv_other, own, n, lq)
    prompt_attn = prompt_attention(prompt_blocks, q, kv, msgs)
    msgs = lax.all_to_all(msgs, "tp", split_axis=0, concat_axis=0, tiled=True)
    decode_attn = decode_attention(ints, cache, msgs, n, lq)
    return prompt_attn, decode_attn.transpose(1, 0, 2)


def solution(mesh):
    return jax.shard_map(
        local,
        mesh=mesh,
        in_specs=(
            P(("rep", "pool"), None),
            P(None, "tp"),
            P(None, "tp"),
            P("rep", None),
            P("rep", None),
            P("rep", None, None),
            P(("rep", "pool", "tp"), None),
            P(("rep", "pool", "tp")),
            P(("rep", "pool", "tp"), None, None),
            P(None, ("rep", "pool"), None),
        ),
        out_specs=(P(("rep", "pool"), "tp"), P(None, ("rep", "pool", "tp"), None)),
        check_vma=False,
    )
```

time: 65 us -> 66.6 us (1.025)
  local copies, waits for them, and re-layouts: 2.6 us -> 5.06 us
    all_to_all x1, waiting for transfers between devices: 3.42 us -> 0.01 us  [local(): facts = lax.all_to_all(facts, 'tp', split_axis=0, concat_axis=0, tiled=True)]
    ppermute x1, waiting for transfers between devices: 0.01 us -> 2.87 us  [local(): kv_other = lax.ppermute(kv, 'pool', [(0, 1), (1, 0)])]
    pallas_call x3, Pallas kernels: 5.74 us -> 8.01 us  [the longest x1 4.8 us: decode_attention(): pl.pallas_call(functools.partial(owner_part, n, lq), in_specs=[smem] * 5...]
    pallas_call x1, Pallas kernels: 25.7 us -> 23.6 us  [project_all(): pl.pallas_call(functools.partial(project, n, lq, first, size), grid=(1 +...]
    all_to_all x1, starting transfers between devices: 5.98 us -> 7.28 us  [local(): facts = lax.all_to_all(facts, 'tp', split_axis=0, concat_axis=0, tiled=True)]
    all_to_all x1, starting transfers between devices: 6.85 us -> 6 us  [local(): msgs = lax.all_to_all(msgs, 'tp', split_axis=0, concat_axis=0, tiled=True)]
    concatenate x0 -> x1, local copies, waits for them, and re-layouts: none -> 0.81 us  [local(): jnp.concatenate(facts).astype(jnp.float32)]
    squeeze x0 -> x1, local copies, waits for them, and re-layouts: none -> 0.76 us  [local(): page_table[1]]
  transfers between devices with their start and end apart: 3 -> 3, of which waited for: 1 -> 1; matrix products, arithmetic and copies ran while one was open for 0% -> 0% of each run, Pallas kernels for 23% -> 55%
where the time goes in v8:
time: 66.6 us; the launch traced here: 66.1 us
  Pallas kernels  44 us (66%)
  starting transfers between devices  13.3 us (20%)
  local copies, waits for them, and re-layouts  5.06 us (8%)
  waiting for transfers between devices  2.87 us (4%)
  between operations  0.88 us (1%)
    pallas_call x1, Pallas kernels, project_all(): pl.pallas_call(functools.partial(project, n, lq, first, size), grid=(1 +...  23.6 us
    pallas_call x1, Pallas kernels, prompt_attention(): pl.pallas_call(functools.partial(attend_prompt, cq // HD), in_specs=[pl.B...  12.4 us
    all_to_all x1, starting transfers between devices, local(): facts = lax.all_to_all(facts, 'tp', split_axis=0, concat_axis=0, tiled=True)  7.28 us
    all_to_all x1, starting transfers between devices, local(): msgs = lax.all_to_all(msgs, 'tp', split_axis=0, concat_axis=0, tiled=True)  6 us
    pallas_call x1, Pallas kernels, decode_attention(): pl.pallas_call(functools.partial(owner_part, n, lq), in_specs=[smem] * 5...  4.8 us
    pallas_call x1, Pallas kernels, handed_attention(): pl.pallas_call(functools.partial(handed_part, n, lq), in_specs=[smem] * 3...  3.21 us
    unnamed x14, local copies, waits for them, and re-layouts  2.88 us
    ppermute x1, waiting for transfers between devices, local(): kv_other = lax.ppermute(kv, 'pool', [(0, 1), (1, 0)])  2.87 us
  transfers between devices with their start and end apart: 3, of which 1 were waited for; matrix products, arithmetic and copies ran while one was open for 0% of the time, Pallas kernels for 55%

profile of v8, /device:TPU:0, one launch (start us, length us, event | category | flops | bytes accessed | tf_op | source)
XLA Modules:
  0.0 66.1 jit_solution(2489958871837592129)
XLA Ops:
  0.6 0.8 %slice_bitcast_fusion = (s32[3]{0:T(128)S(1)}, s32[3]{0:T(128)S(1)}) fusion(s32[2,3]{1,0:T(2,128)} %bitcast.13), kind=kLoop, calls=%fused_computation | loop fusion | bytes 48 | tf_op jit(solution)/shard_map/squeeze | solution.py:503
  1.4 0.8 %concatenate.3 = s32[128]{0:T(128)S(1)} concatenate(s32[3]{0:T(128)S(1)} %get-tuple-element.9, s32[3]{0:T(128)S(1)} %get-tuple-element.9, s32[2]{0:T(128)S(1)} %broadcast.3, s32[3]{0:T(128)S(1)} %get-tuple-element.8, s32[3]{0:T(128)S(1)} %get-tuple-element.8, s32[2]{0:T(128)S(1)} %broadcast.3, s32[3]{0:T(128)} %lens.1, s32[3]{0:T(128)} %lens.1, s32[2]{0:T(128)S(1)} %broadcast.3, ...), dimensions={0} | concatenate | bytes 1024 | tf_op jit(solution)/shard_map/concatenate | solution.py:506
  2.2 0.6 broadcast_in_dim.7
  2.8 7.3 %all-to-all-start = ((f32[8,1,128]{2,1,0:T(1,128)}), f32[8,1,128]{2,1,0:T(1,128)S(1)}, u32[]{:S(2)}, u32[]{:S(2)}) async-start(f32[8,1,128]{2,1,0:T(1,128)} %broadcast_in_dim.7), calls=%async_computation | async-start | bytes 8192 | tf_op jit(solution)/shard_map/all_to_all | solution.py:507
  10.1 0.0 copy-start.2
  10.1 0.0 copy-start.3
  10.1 0.0 copy-start.4
  10.1 23.6 %project.1 = (bf16[2048,512]{1,0:T(8,128)(2,1)}, bf16[2048,256]{1,0:T(8,128)(2,1)}, bf16[64,768]{1,0:T(8,128)(2,1)}) custom-call(bf16[48,5120]{1,0:T(8,128)(2,1)} %bitcast.15, bf16[2048,5120]{1,0:T(8,128)(2,1)} %refs_1_.1, bf16[5120,512]{1,0:T(8,128)(2,1)} %refs_2_.1, bf16[5120,256]{1,0:T(8,128)(2,1)} %refs_3_.1), custom_call_target="tpu_custom_call" | custom-call | flops 16106127360 | bytes 31981568 | tf_op jit(solution)/shard_map/project/pallas_call | solution.py:167
  33.8 0.0 all-to-all-done.refs_1_.facts_ref
  33.8 0.0 copy-start
  33.8 0.6 copy-done
  34.4 0.0 collective-permute-start
  34.4 2.9 %collective-permute-done.kv_ref = bf16[2048,256]{1,0:T(8,128)(2,1)S(1)} collective-permute-done((bf16[2048,256]{1,0:T(8,128)(2,1)}, bf16[2048,256]{1,0:T(8,128)(2,1)S(1)}, u32[]{:S(2)}, u32[]{:S(2)}) %collective-permute-start) | collective-permute-done | bytes 1048608 | tf_op jit(solution)/shard_map/ppermute | solution.py:511
  37.3 0.0 copy-done.2
  37.3 0.0 copy-done.3
  37.3 0.0 copy-done.4
  37.3 0.0 copy-start.1
  37.3 0.7 %copy-done.1 = f32[8,1,128]{2,1,0:T(1,128)S(1)} copy-done((f32[8,1,128]{2,1,0:T(1,128)S(1)}, f32[8,1,128]{2,1,0:T(1,128)}, u32[]{:S(2)}) %copy-start.1) | copy-done | bytes 4120
  38.0 0.0 copy-start.5
  38.0 0.9 %copy-done.5 = bf16[64,768]{1,0:T(8,128)(2,1)S(1)} copy-done((bf16[64,768]{1,0:T(8,128)(2,1)S(1)}, bf16[64,768]{1,0:T(8,128)(2,1)}, u32[]{:S(2)}) %copy-start.5) | copy-done | bytes 98328
  38.9 3.2 %handed_attention.1._ = f32[8,80,128]{2,1,0:T(8,128)} custom-call(s32[2,3]{1,0:T(2,128)S(1)} %copy-done.3, s32[2,3]{1,0:T(2,128)S(1)} %copy-done.4, s32[2,2,16]{2,1,0:T(2,128)S(1)} %bitcast.10, f32[8,1,128]{2,1,0:T(1,128)S(1)} %copy-done.1, bf16[2048,256]{1,0:T(8,128)(2,1)S(1)} %collective-permute-done.kv_ref, bf16[64,768]{1,0:T(8,128)(2,1)S(1)} %copy-done.5), custom_call_target="tpu_custom_call" | custom-call | flops 402653184 | bytes 2097152 | tf_op jit(solution)/shard_map/handed_attention/pallas_call | solution.py:364
  42.1 6.0 %all-to-all-start.1 = ((f32[8,80,128]{2,1,0:T(8,128)}), f32[8,80,128]{2,1,0:T(8,128)S(1)}, u32[]{:S(2)}, u32[]{:S(2)}) async-start(f32[8,80,128]{2,1,0:T(8,128)} %handed_attention.1._), calls=%async_computation.1 | async-start | bytes 655360 | tf_op jit(solution)/shard_map/all_to_all | solution.py:514
  48.1 12.4 %prompt_attention.1 = bf16[2048,512]{1,0:T(8,128)(2,1)} custom-call(s32[2,3]{1,0:T(2,128)} %counts.5, bf16[2048,512]{1,0:T(8,128)(2,1)} %get-tuple-element.5.q_hbm, bf16[2048,256]{1,0:T(8,128)(2,1)} %wait_for.1.kv_hbm, f32[8,80,128]{2,1,0:T(8,128)} %handed_attention.1._), custom_call_target="tpu_custom_call" | custom-call | flops 8589934592 | bytes 8388608 | tf_op jit(solution)/shard_map/prompt_attention/pallas_call | solution.py:268
  60.4 0.0 all-to-all-done.1.msgs
  60.5 0.0 copy-start.6
  60.5 0.7 %copy-done.6 = f32[8,80,128]{2,1,0:T(8,128)} copy-done((f32[8,80,128]{2,1,0:T(8,128)}, f32[8,80,128]{2,1,0:T(8,128)S(1)}, u32[]{:S(2)}) %copy-start.6) | copy-done | bytes 327704
  61.2 4.8 %decode_attention.1 = bf16[3,2,4096]{2,1,0:T(2,128)(2,1)} custom-call(s32[2,3]{1,0:T(2,128)} %counts.5, s32[2,3]{1,0:T(2,128)} %done.3, s32[2,2,16]{2,1,0:T(2,128)} %bitcast.9, s32[2,3]{1,0:T(2,128)} %bitcast.14, s32[3]{0:T(128)} %lens.1, bf16[768,2048]{1,0:T(8,128)(2,1)} %bitcast.11, f32[8,80,128]{2,1,0:T(8,128)} %copy-done.6), custom_call_target="tpu_custom_call" | custom-call | flops 100663296 | bytes 4194304 | tf_op jit(solution)/shard_map/decode_attention/pallas_call | solution.py:461
  (4 shorter events, 0.0 us)
Async XLA Ops:
  2.8 31.0 %all-to-all-start = ((f32[8,1,128]{2,1,0:T(1,128)}), f32[8,1,128]{2,1,0:T(1,128)S(1)}, u32[]{:S(2)}, u32[]{:S(2)}) async-start(f32[8,1,128]{2,1,0:T(1,128)} %broadcast_in_dim.7), calls=%async_computation | async-start | bytes 8192 | tf_op jit(solution)/shard_map/all_to_all | solution.py:507
  10.1 27.2 %copy-start.2 = (s32[2,16,2]{1,2,0:T(2,128)S(1)}, s32[2,16,2]{1,2,0:T(2,128)}, u32[]{:S(2)}) copy-start(s32[2,16,2]{1,2,0:T(2,128)} %param.15) | copy-start | bytes 772
  10.1 27.2 %copy-start.3 = (s32[2,3]{1,0:T(2,128)S(1)}, s32[2,3]{1,0:T(2,128)}, u32[]{:S(2)}) copy-start(s32[2,3]{1,0:T(2,128)} %counts.5) | copy-start | bytes 76
  10.1 27.2 %copy-start.4 = (s32[2,3]{1,0:T(2,128)S(1)}, s32[2,3]{1,0:T(2,128)}, u32[]{:S(2)}) copy-start(s32[2,3]{1,0:T(2,128)} %done.3) | copy-start | bytes 76
  33.8 0.6 copy-start
  34.4 2.9 %collective-permute-start = (bf16[2048,256]{1,0:T(8,128)(2,1)}, bf16[2048,256]{1,0:T(8,128)(2,1)S(1)}, u32[]{:S(2)}, u32[]{:S(2)}) collective-permute-start(bf16[2048,256]{1,0:T(8,128)(2,1)} %wait_for.1.kv_hbm), channel_id=1, source_target_pairs={{0,8},{8,0},{1,9},{9,1},{2,10},{10,2},{3,11},{11,3},{4,12},{12,4},... | collective-permute-start | bytes 3145736 | tf_op jit(solution)/shard_map/ppermute | solution.py:511
  37.3 0.7 %copy-start.1 = (f32[8,1,128]{2,1,0:T(1,128)S(1)}, f32[8,1,128]{2,1,0:T(1,128)}, u32[]{:S(2)}) copy-start(f32[8,1,128]{2,1,0:T(1,128)} %copy-done) | copy-start | bytes 12292
  38.0 0.9 %copy-start.5 = (bf16[64,768]{1,0:T(8,128)(2,1)S(1)}, bf16[64,768]{1,0:T(8,128)(2,1)}, u32[]{:S(2)}) copy-start(bf16[64,768]{1,0:T(8,128)(2,1)} %get-tuple-element.7.own_ref) | copy-start | bytes 294916
  42.1 18.4 %all-to-all-start.1 = ((f32[8,80,128]{2,1,0:T(8,128)}), f32[8,80,128]{2,1,0:T(8,128)S(1)}, u32[]{:S(2)}, u32[]{:S(2)}) async-start(f32[8,80,128]{2,1,0:T(8,128)} %handed_attention.1._), calls=%async_computation.1 | async-start | bytes 655360 | tf_op jit(solution)/shard_map/all_to_all | solution.py:514
  60.5 0.7 %copy-start.6 = (f32[8,80,128]{2,1,0:T(8,128)}, f32[8,80,128]{2,1,0:T(8,128)S(1)}, u32[]{:S(2)}) copy-start(f32[8,80,128]{2,1,0:T(8,128)S(1)} %all-to-all-done.1.msgs) | copy-start | bytes 983044

commit v9 on v7

--- a/solution.py
+++ b/solution.py
@@ -25,7 +25,7 @@
 SCALE = HD ** (-0.5)
 MASKED = -1e30
 PIECES = 5
-STRIPS = 2
+STRIPS = 4
 LOG2E = 1.4426950408889634
 AHEAD = 2
 MIB = 1 << 20
@@ -74,9 +74,8 @@
 
 
 def project(n, lq, first, size, *refs):
-    counts, done, placed, table, lens, dx_hbm, x_hbm, wq_hbm, wkv_hbm = refs[:9]
-    q_hbm, kv_hbm, qh_ref, msg_ref = refs[9:13]
-    x0, xs, w, q_out, kv_out, x_sems, w_sems, out_sems = refs[13:]
+    dx_hbm, x_hbm, wq_hbm, wkv_hbm, q_hbm, kv_hbm, own_ref = refs[:7]
+    x0, xs, w, q_out, kv_out, x_sems, w_sems, out_sems = refs[7:]
     depth = w.shape[0]
     count = xs.shape[0]
     cq = lq * HD
@@ -107,7 +106,7 @@
         if isinstance(k, int):
             rows = pl.ds(0, first)
         else:
-            rows = pl.ds(pl.multiple_of(first + (k - 1) * size, BLOCK_TOKENS), size)
+            rows = pl.ds(pl.multiple_of(first + (k - 1) * size, 64), size)
         return [
             pltpu.make_async_copy(q_out.at[rows], q_hbm.at[rows], out_sems.at[0, k]),
             pltpu.make_async_copy(kv_out.at[rows], kv_hbm.at[rows], out_sems.at[1, k]),
@@ -142,26 +141,7 @@
         owner, rs = to // GROUP_ROWS, to % GROUP_ROWS
         wanted = owner * ROWS_DEV + row_of(rs) + jnp.where(rs >= ROWS_DEV, ROWS_DEV * n, 0)
         pick = ((fro == wanted) & (rs < STEPS * ROWS_DEV)).astype(jnp.float32).astype(jnp.bfloat16)
-        own = dot(pick, total[first:].astype(jnp.bfloat16))
-        for h in range(lq):
-            part = slice(h * n * GROUP_ROWS, (h + 1) * n * GROUP_ROWS)
-            qh_ref[part, :] = own[:, h * HD : (h + 1) * HD].astype(jnp.bfloat16)
-        found = block_of_pages(counts, done, placed, table)
-        lane = iota((n * GROUP_ROWS, HD), 1)
-        r = row_of(lane % GROUP_ROWS)
-        kind = lane // GROUP_ROWS
-        facts = jnp.where(
-            kind == 0,
-            by_row(r, [found[i][0] for i in range(ROWS_DEV)], -1),
-            jnp.where(
-                kind == 1,
-                by_row(r, [found[i][1] for i in range(ROWS_DEV)], -1),
-                by_row(r, [lens[i] for i in range(ROWS_DEV)], 0),
-            ),
-        ).astype(jnp.float32)
-        sixth = iota((n * GROUP_ROWS, HD), 0) % GROUP_ROWS == 6
-        msg_ref[:, :HD] = jnp.where(sixth, facts, own[:, :HD]).astype(jnp.bfloat16)
-        msg_ref[:, HD:] = own[:, HD:].astype(jnp.bfloat16)
+        own_ref[...] = dot(pick, total[first:].astype(jnp.bfloat16)).astype(jnp.bfloat16)
 
     @pl.when((step > 0) & (step + AHEAD <= count))
     def _():
@@ -172,7 +152,7 @@
     def _():
         for copy in x_copies(step - 1):
             copy.wait()
-        keep(dot(xs[step - 1], w[...]), pl.ds(pl.multiple_of(first + (step - 1) * size, BLOCK_TOKENS), size))
+        keep(dot(xs[step - 1], w[...]), pl.ds(pl.multiple_of(first + (step - 1) * size, 64), size))
         for copy in out_copies(step):
             copy.start()
 
@@ -185,22 +165,20 @@
                 copy.wait()
 
 
-def project_all(ints, dx, x, wq, wkv, n, first, size):
+def project_all(dx, x, wq, wkv, n, first, size):
     rows, depth = x.shape
     cq, ckv = wq.shape[1], wkv.shape[1]
     lq = cq // HD
     count = (rows - first) // size
-    smem, vmem = pl.BlockSpec(memory_space=SMEM), pl.BlockSpec(memory_space=VMEM)
-    hbm = pl.BlockSpec(memory_space=pl.ANY)
+    vmem, hbm = pl.BlockSpec(memory_space=VMEM), pl.BlockSpec(memory_space=pl.ANY)
     return pl.pallas_call(
         functools.partial(project, n, lq, first, size),
         grid=(1 + count,),
-        in_specs=[smem] * 5 + [hbm] * 4,
-        out_specs=[hbm, hbm, vmem, vmem],
+        in_specs=[hbm] * 4,
+        out_specs=[hbm, hbm, vmem],
         out_shape=[
             jax.ShapeDtypeStruct((rows, cq), jnp.bfloat16),
             jax.ShapeDtypeStruct((rows, ckv), jnp.bfloat16),
-            jax.ShapeDtypeStruct((lq * n * GROUP_ROWS, HD), jnp.bfloat16),
             jax.ShapeDtypeStruct((n * GROUP_ROWS, cq + ckv), jnp.bfloat16),
         ],
         scratch_shapes=[
@@ -213,41 +191,73 @@
             pltpu.SemaphoreType.DMA((4, PIECES)),
             pltpu.SemaphoreType.DMA((2, count + 1)),
         ],
-        compiler_params=pltpu.CompilerParams(vmem_limit_bytes=62 * MIB),
+        compiler_params=pltpu.CompilerParams(vmem_limit_bytes=50 * MIB),
         cost_estimate=pl.CostEstimate(
             flops=2 * rows * depth * (cq + ckv),
             bytes_accessed=2 * (rows + cq + ckv) * depth + 2 * rows * (cq + ckv),
             transcendentals=0,
         ),
         name="project",
-    )(*ints, dx, x, wq, wkv)
-
-
-def attend_prompt(lq, half, counts, q_hbm, kv_hbm, *refs):
-    o_hbm, made_ref, qs, kvs, outs, sems = refs[-6:]
+    )(dx, x, wq, wkv)
+
+
+def add_facts(n, counts, done, placed, table, lens, own_ref, msg_ref):
+    found = block_of_pages(counts, done, placed, table)
+    shape = (n * GROUP_ROWS, HD)
+    lane = iota(shape, 1)
+    r = row_of(lane % GROUP_ROWS)
+    kind = lane // GROUP_ROWS
+    facts = jnp.where(
+        kind == 0,
+        by_row(r, [found[i][0] for i in range(ROWS_DEV)], -1),
+        jnp.where(
+            kind == 1,
+            by_row(r, [found[i][1] for i in range(ROWS_DEV)], -1),
+            by_row(r, [lens[i] for i in range(ROWS_DEV)], 0),
+        ),
+    ).astype(jnp.float32)
+    sixth = iota(shape, 0) % GROUP_ROWS == 6
+    head = jnp.where(sixth, facts, own_ref[:, :HD].astype(jnp.float32))
+    msg_ref[:, :HD] = head.astype(jnp.bfloat16)
+    msg_ref[:, HD:] = own_ref[:, HD:]
+
+
+def make_messages(ints, own, n):
+    smem, vmem = pl.BlockSpec(memory_space=SMEM), pl.BlockSpec(memory_space=VMEM)
+    return pl.pallas_call(
+        functools.partial(add_facts, n),
+        in_specs=[smem] * 5 + [vmem],
+        out_specs=vmem,
+        out_shape=jax.ShapeDtypeStruct(own.shape, own.dtype),
+        compiler_params=pltpu.CompilerParams(vmem_limit_bytes=24 * MIB),
+        cost_estimate=pl.CostEstimate(flops=0, bytes_accessed=4 * own.size, transcendentals=0),
+        name="make_messages",
+    )(*ints, own)
+
+
+def attend_prompt(lq, half, counts, q_ref, kv_ref, *refs):
+    o_hbm, made_ref, kvs, outs, sems = refs[-5:]
     made_ref[...] = jnp.zeros_like(made_ref)
     group = lax.axis_index("pool")
     c0, c1 = counts[group, 0], counts[group, 1]
     big = jnp.where(c0 == MOST_BLOCKS, 0, jnp.where(c1 == MOST_BLOCKS, c0, c0 + c1))
     cut = jnp.where(c0 == MOST_BLOCKS, c1, c0)
-    loads, stores = [], []
+    places, stores = [], []
+    strip, early = (4, 3) if half == 0 else (1, 5)
     for j in range(MOST_BLOCKS):
         block = big + j if half == 0 else j + jnp.where(j >= big, MOST_BLOCKS, 0)
-        rows = pl.ds(pl.multiple_of(block * BLOCK_TOKENS, BLOCK_TOKENS), BLOCK_TOKENS)
-        here = pl.ds(j * BLOCK_TOKENS, BLOCK_TOKENS)
-        loads.append(pltpu.make_async_copy(kv_hbm.at[rows], kvs.at[here], sems.at[0, j]))
-        loads.append(pltpu.make_async_copy(q_hbm.at[rows], qs.at[here], sems.at[1, j]))
-        stores.append(pltpu.make_async_copy(outs.at[here], o_hbm.at[rows], sems.at[2, j]))
-    for copy in loads:
-        copy.start()
-    for copy in loads:
-        copy.wait()
+        at = pl.multiple_of(block * BLOCK_TOKENS, BLOCK_TOKENS)
+        places.append(pl.ds(at, BLOCK_TOKENS))
+        kvs[j * BLOCK_TOKENS : (j + 1) * BLOCK_TOKENS, :] = kv_ref[places[j], :]
+        if j % strip == 0:
+            rows, here = pl.ds(at, strip * BLOCK_TOKENS), pl.ds(j * BLOCK_TOKENS, strip * BLOCK_TOKENS)
+            stores.append(pltpu.make_async_copy(outs.at[here], o_hbm.at[rows], sems.at[j]))
     shape = (BLOCK_TOKENS, lq * BLOCK_TOKENS)
     causal = iota(shape, 0) <= iota(shape, 1) % BLOCK_TOKENS
     flipped = kvs[:, HD:].T
 
     def scores_of(j):
-        q = qs[j * BLOCK_TOKENS : (j + 1) * BLOCK_TOKENS, :]
+        q = q_ref[places[j], :]
         q = jnp.concatenate([q[:, h * HD : (h + 1) * HD] for h in range(lq)], axis=0)
         return dot_t(kvs[: (j + 1) * BLOCK_TOKENS, :HD], q)
 
@@ -275,10 +285,10 @@
             part = mixed[:, h * BLOCK_TOKENS : (h + 1) * BLOCK_TOKENS].T
             outs[j * BLOCK_TOKENS : (j + 1) * BLOCK_TOKENS, h * HD : (h + 1) * HD] = part
         scores = later
-        if j == MOST_BLOCKS - 3:
-            for copy in stores[: j + 1]:
+        if j == early:
+            for copy in stores[: (j + 1) // strip]:
                 copy.start()
-    for copy in stores[MOST_BLOCKS - 2 :]:
+    for copy in stores[(early + 1) // strip :]:
         copy.start()
     for copy in stores:
         copy.wait()
@@ -286,25 +296,24 @@
 
 def prompt_attention(counts, q, kv, half, so_far=None, after=None):
     rows, cq = q.shape
-    hbm = pl.BlockSpec(memory_space=pl.ANY)
+    hbm, vmem = pl.BlockSpec(memory_space=pl.ANY), pl.BlockSpec(memory_space=VMEM)
     more = () if so_far is None else (so_far, after)
     tokens = MOST_BLOCKS * BLOCK_TOKENS
     return pl.pallas_call(
         functools.partial(attend_prompt, cq // HD, half),
-        in_specs=[pl.BlockSpec(memory_space=SMEM), hbm, hbm] + [hbm] * len(more),
+        in_specs=[pl.BlockSpec(memory_space=SMEM), vmem, vmem] + [hbm] * len(more),
         out_specs=[hbm, pl.BlockSpec(memory_space=VMEM)],
         out_shape=[
             jax.ShapeDtypeStruct((rows, cq), jnp.bfloat16),
             jax.ShapeDtypeStruct((8, HD), jnp.float32),
         ],
         scratch_shapes=[
-            VMEM((tokens, cq), jnp.bfloat16),
             VMEM((tokens, 2 * HD), jnp.bfloat16),
             VMEM((tokens, cq), jnp.bfloat16),
-            pltpu.SemaphoreType.DMA((3, MOST_BLOCKS)),
+            pltpu.SemaphoreType.DMA((MOST_BLOCKS,)),
         ],
         input_output_aliases={3: 0} if more else {},
-        compiler_params=pltpu.CompilerParams(vmem_limit_bytes=62 * MIB),
+        compiler_params=pltpu.CompilerParams(vmem_limit_bytes=24 * MIB),
         cost_estimate=pl.CostEstimate(flops=2 * rows * rows * cq, bytes_accessed=4 * rows * cq, transcendentals=rows * rows // 2),
         name="long_prompt" if half == 0 else "short_prompts",
     )(counts, q, kv, *more)
@@ -315,7 +324,7 @@
     return at // lq, at % lq
 
 
-def handed_part(n, lq, kv_ref, q_ref, msg_ref, o_ref):
+def handed_part(n, lq, kv_ref, own_ref, msg_ref, o_ref):
     rows = lq * n * GROUP_ROWS
     shape = (rows, HD)
     at_row, lane = iota(shape, 0), iota(shape, 1)
@@ -328,7 +337,9 @@
         return jnp.sum(jnp.where(lane == kind * GROUP_ROWS + rs, facts, 0.0), axis=1, keepdims=True)
 
     first_block, second_block, length = [column(kind) for kind in range(3)]
-    scores = dot_t(q_ref[...], kv_ref[:, :HD]) * SCALE
+    own = own_ref[...]
+    queries = jnp.concatenate([own[:, h * HD : (h + 1) * HD] for h in range(lq)], axis=0)
+    scores = dot_t(queries, kv_ref[:, :HD]) * SCALE
     lane_f = lane.astype(jnp.float32)
     parts = []
     for b in range(NBLK):
@@ -357,11 +368,9 @@
 
 
 def exchange_part(n, lq, *refs):
-    counts, done, placed, table, lens, cache_hbm, msgs, kv_ref, q_ref, _ = refs[:10]
-    handed_ref, s_ref, v_ref, new_ref, cache, sem, slot_row, slot_limit = refs[10:]
-    load = pltpu.make_async_copy(cache_hbm, cache, sem)
-    load.start()
-    handed_part(n, lq, kv_ref, q_ref, msgs, handed_ref)
+    counts, done, placed, table, lens, cache, msgs, kv_ref, own_ref, _ = refs[:10]
+    handed_ref, s_ref, v_ref, new_ref, slot_row, slot_limit = refs[10:]
+    handed_part(n, lq, kv_ref, own_ref, msgs, handed_ref)
     held = msgs[...].astype(jnp.float32)
     found = block_of_pages(counts, done, placed, table)
     for r in range(ROWS_DEV):
@@ -392,7 +401,6 @@
     before = jnp.sum(queries * earlier, axis=1, keepdims=True) * SCALE
     second = (rs >= ROWS_DEV) & (rs < STEPS * ROWS_DEV)
     before = jnp.where(second, before, MASKED)
-    load.wait()
     scores = jnp.concatenate(
         [dot_t(rounded[h * span : (h + 1) * span], cache[:, 2 * h * HD : (2 * h + 1) * HD]) for h in range(KVH)],
         axis=0,
@@ -407,12 +415,12 @@
         v_ref[:, h * HD : (h + 1) * HD] = cache[:, (2 * h + 1) * HD : (2 * h + 2) * HD]
 
 
-def decode_scores(ints, cache, msgs, kv, q_own, after, n, lq):
+def decode_scores(ints, cache, msgs, kv, own, after, n, lq):
     smem, vmem, hbm = [pl.BlockSpec(memory_space=space) for space in (SMEM, VMEM, pl.ANY)]
     rows = QH * GROUP_ROWS
     return pl.pallas_call(
         functools.partial(exchange_part, n, lq),
-        in_specs=[smem] * 5 + [hbm, vmem, vmem, vmem, hbm],
+        in_specs=[smem] * 5 + [vmem] * 4 + [hbm],
         out_specs=[vmem] * 4,
         out_shape=[
             jax.ShapeDtypeStruct((n, lq * GROUP_ROWS, HD), jnp.float32),
@@ -421,15 +429,13 @@
             jax.ShapeDtypeStruct((KVH * GROUP_ROWS, HD), jnp.float32),
         ],
         scratch_shapes=[
-            VMEM(cache.shape, jnp.bfloat16),
-            pltpu.SemaphoreType.DMA,
             SMEM((DEVICE_SLOTS,), jnp.int32),
             SMEM((DEVICE_SLOTS,), jnp.int32),
         ],
-        compiler_params=pltpu.CompilerParams(vmem_limit_bytes=61 * MIB),
+        compiler_params=pltpu.CompilerParams(vmem_limit_bytes=24 * MIB),
         cost_estimate=pl.CostEstimate(flops=2 * rows * HD * 768, bytes_accessed=4 * MIB, transcendentals=0),
         name="decode_scores",
-    )(*ints, cache, msgs, kv, q_own, after)
+    )(*ints, cache, msgs, kv, own, after)
 
 
 def owner_mix(s_ref, v_ref, new_ref, handed, o_ref):
@@ -479,7 +485,7 @@
         in_specs=[vmem] * 4,
         out_specs=vmem,
         out_shape=jax.ShapeDtypeStruct((ROWS_DEV, STEPS, QH * HD), jnp.bfloat16),
-        compiler_params=pltpu.CompilerParams(vmem_limit_bytes=62 * MIB),
+        compiler_params=pltpu.CompilerParams(vmem_limit_bytes=24 * MIB),
         cost_estimate=pl.CostEstimate(flops=2 * rows * HD * 768, bytes_accessed=4 * MIB, transcendentals=rows * 768),
         name="decode_mix",
     )(scores, values, new, parts)
@@ -508,12 +514,13 @@
     placement = placement.transpose(0, 2, 1)
     page_table = page_table.transpose(1, 0)
     ints = (prompt_blocks, finished, placement, page_table, row_lens)
-    first, size = 256, 256
-    q, kv, q_own, msgs = project_all(ints, dx, prompt_x, q_weight, kv_weight, n, first, size)
+    first, size = 512, 512
+    q, kv, own = project_all(dx, prompt_x, q_weight, kv_weight, n, first, size)
+    msgs = make_messages(ints, own, n)
     msgs = lax.all_to_all(msgs, "tp", split_axis=0, concat_axis=0, tiled=True)
     kv_other = lax.ppermute(kv, "pool", [(0, 1), (1, 0)])
     prompt_attn, made = prompt_attention(prompt_blocks, q, kv, 0)
-    handed, scores, values, new = decode_scores(ints, cache, msgs, kv_other, q_own, made, n, lq)
+    handed, scores, values, new = decode_scores(ints, cache, msgs, kv_other, own, made, n, lq)
     parts = lax.all_to_all(handed, "tp", split_axis=0, concat_axis=0, tiled=True)
     prompt_attn, _ = prompt_attention(prompt_blocks, q, kv, 1, prompt_attn, handed)
     decode_attn = decode_mix(scores, values, new, parts)

time: 64.3 us -> 64.7 us (level)
  local copies, waits for them, and re-layouts: 1.64 us -> 7.65 us
  Pallas kernels: 48 us -> 42.5 us
    unnamed x6 -> x28, local copies, waits for them, and re-layouts: 1.64 us -> 7.65 us
    pallas_call x2, Pallas kernels: 15 us -> 12.6 us  [prompt_attention(): pl.pallas_call(functools.partial(attend_prompt, cq // HD, half), in_specs...]
    pallas_call x1, Pallas kernels: 3.04 us -> 1.37 us  [decode_mix(): pl.pallas_call(owner_mix, in_specs=[vmem] * 4, out_specs=vmem, out_shape=...]
    pallas_call x1, Pallas kernels: 24.7 us -> 23.2 us  [project_all(): pl.pallas_call(functools.partial(project, n, lq, first, size), grid=(1 +...]
    pallas_call x0 -> x1, Pallas kernels: none -> 1.39 us  [make_messages(): pl.pallas_call(functools.partial(add_facts, n), in_specs=[smem] * 5 + [vm...]
    pallas_call x1, Pallas kernels: 5.29 us -> 3.95 us  [decode_scores(): pl.pallas_call(functools.partial(exchange_part, n, lq), in_specs=[smem] *...]
  transfers between devices with their start and end apart: 3 -> 3, of which waited for: 0 -> 0; matrix products, arithmetic and copies ran while one was open for 0% -> 0% of each run, Pallas kernels for 24% -> 22%
where the time goes in v9:
time: 64.7 us; the launch traced here: 64.3 us
  Pallas kernels  42.5 us (66%)
  starting transfers between devices  13.3 us (21%)
  local copies, waits for them, and re-layouts  7.65 us (12%)
  between operations  0.76 us (1%)
    pallas_call x1, Pallas kernels, project_all(): pl.pallas_call(functools.partial(project, n, lq, first, size), grid=(1 +...  23.2 us
    pallas_call x2, Pallas kernels, prompt_attention(): pl.pallas_call(functools.partial(attend_prompt, cq // HD, half), in_specs...  12.6 us
    unnamed x28, local copies, waits for them, and re-layouts  7.65 us
    all_to_all x1, starting transfers between devices, local(): msgs = lax.all_to_all(msgs, 'tp', split_axis=0, concat_axis=0, tiled=True)  6.85 us
    all_to_all x1, starting transfers between devices, local(): lax.all_to_all(handed, 'tp', split_axis=0, concat_axis=0, tiled=True)  6 us
    pallas_call x1, Pallas kernels, decode_scores(): pl.pallas_call(functools.partial(exchange_part, n, lq), in_specs=[smem] *...  3.95 us
    pallas_call x1, Pallas kernels, make_messages(): pl.pallas_call(functools.partial(add_facts, n), in_specs=[smem] * 5 + [vm...  1.39 us
    pallas_call x1, Pallas kernels, decode_mix(): pl.pallas_call(owner_mix, in_specs=[vmem] * 4, out_specs=vmem, out_shape=...  1.37 us
  transfers between devices with their start and end apart: 3, of which 0 were waited for; matrix products, arithmetic and copies ran while one was open for 0% of the time, Pallas kernels for 22%

profile of v9, /device:TPU:0, one launch (start us, length us, event | category | flops | bytes accessed | tf_op | source)
XLA Modules:
  0.0 64.3 jit_solution(17186305263665775026)
XLA Ops:
  0.6 0.0 copy-start.10
  0.6 1.0 %copy-done.10 = bf16[2,24,5120]{2,1,0:T(8,128)(2,1)S(1)} copy-done((bf16[2,24,5120]{2,1,0:T(8,128)(2,1)S(1)}, bf16[2,24,5120]{2,1,0:T(8,128)(2,1)}, u32[]{:S(2)}) %copy-start.10) | copy-done | bytes 491544
  1.7 0.0 copy-start.5
  1.7 0.0 copy-start.6
  1.7 0.0 copy-start.7
  1.7 0.0 copy-start.8
  1.7 0.0 copy-start.9
  1.7 23.2 %project.1 = (bf16[2048,512]{1,0:T(8,128)(2,1)S(1)}, bf16[2048,256]{1,0:T(8,128)(2,1)}, bf16[64,768]{1,0:T(8,128)(2,1)S(1)}) custom-call(bf16[48,5120]{1,0:T(8,128)(2,1)S(1)} %bitcast.13, bf16[2048,5120]{1,0:T(8,128)(2,1)} %refs_1_.2, bf16[5120,512]{1,0:T(8,128)(2,1)} %refs_2_.1, bf16[5120,256]{1,0:T(8,128)(2,1)} %refs_3_.1), custom_call_target="tpu_custom_call" | custom-call | flops 16106127360 | bytes 31981568 | tf_op jit(solution)/shard_map/project/pallas_call | solution.py:174
  24.9 0.0 copy-start.11
  24.9 1.3 %copy-done.11 = bf16[2048,512]{1,0:T(8,128)(2,1)} copy-done((bf16[2048,512]{1,0:T(8,128)(2,1)}, bf16[2048,512]{1,0:T(8,128)(2,1)S(1)}, u32[]{:S(2)}) %copy-start.11) | copy-done | bytes 2097176
  26.2 0.5 collective-permute-start
  26.7 0.0 copy-done.5
  26.7 0.0 copy-done.6
  26.7 0.0 copy-done.7
  26.7 0.0 copy-done.8
  26.7 0.0 copy-done.9
  26.7 1.4 %make_messages.1 = bf16[64,768]{1,0:T(8,128)(2,1)} custom-call(s32[2,3]{1,0:T(2,128)S(1)} %copy-done.8, s32[2,3]{1,0:T(2,128)S(1)} %copy-done.6, s32[2,2,16]{2,1,0:T(2,128)S(1)} %bitcast.9, s32[2,3]{1,0:T(2,128)S(1)} %bitcast.11, s32[3]{0:T(128)S(1)} %copy-done.9, bf16[64,768]{1,0:T(8,128)(2,1)S(1)} %get-tuple-element.15.own_ref.refs_8_), custom_call_target="tpu_custom_call" | custom-call | bytes 196608 | tf_op jit(solution)/shard_map/make_messages/pallas_call | solution.py:227
  28.1 6.8 %all-to-all-start = ((bf16[8,8,768]{2,1,0:T(8,128)(2,1)}), bf16[8,8,768]{2,1,0:T(8,128)(2,1)S(1)}, u32[]{:S(2)}, u32[]{:S(2)}) async-start(bf16[8,8,768]{2,1,0:T(8,128)(2,1)} %bitcast.4), calls=%async_computation | async-start | bytes 196608 | tf_op jit(solution)/shard_map/all_to_all | solution.py:520
  35.0 0.0 copy-start.12
  35.0 1.6 %copy-done.12 = bf16[2048,512]{1,0:T(8,128)(2,1)S(1)} copy-done((bf16[2048,512]{1,0:T(8,128)(2,1)S(1)}, bf16[2048,512]{1,0:T(8,128)(2,1)}, u32[]{:S(2)}) %copy-start.12) | copy-done | bytes 2097176
  36.5 0.0 copy-start
  36.6 5.9 %long_prompt.1 = (bf16[2048,512]{1,0:T(8,128)(2,1)}, f32[8,128]{1,0:T(8,128)S(1)}) custom-call(s32[2,3]{1,0:T(2,128)S(1)} %copy-done.8, bf16[2048,512]{1,0:T(8,128)(2,1)S(1)} %copy-done.12, bf16[2048,256]{1,0:T(8,128)(2,1)} %get-tuple-element.13.kv_ref), custom_call_target="tpu_custom_call" | custom-call | flops 4294967296 | bytes 4194304 | tf_op jit(solution)/shard_map/long_prompt/pallas_call | solution.py:302
  42.5 0.0 all-to-all-done
  42.5 0.0 collective-permute-done.refs_7_
  42.5 0.0 copy-done
  42.5 3.9 %decode_scores.1 = (f32[8,32,128]{2,1,0:T(8,128)}, f32[256,896]{1,0:T(8,128)S(1)}, bf16[768,1024]{1,0:T(8,128)(2,1)S(1)}, f32[64,128]{1,0:T(8,128)S(1)}) custom-call(s32[2,3]{1,0:T(2,128)S(1)} %copy-done.8, s32[2,3]{1,0:T(2,128)S(1)} %copy-done.6, s32[2,2,16]{2,1,0:T(2,128)S(1)} %bitcast.10, s32[2,3]{1,0:T(2,128)S(1)} %bitcast.12, s32[3]{0:T(128)S(1)} %copy-done.9, ...), custom_call_target="tpu_custom_call" | custom-call | flops 50331648 | bytes 4194304 | tf_op jit(solution)/shard_map/decode_scores/pallas_call | solution.py:421
  46.5 0.0 copy-start.1
  46.5 1.1 %copy-done.1 = bf16[768,1024]{1,0:T(8,128)(2,1)} copy-done((bf16[768,1024]{1,0:T(8,128)(2,1)}, bf16[768,1024]{1,0:T(8,128)(2,1)S(1)}, u32[]{:S(2)}) %copy-start.1) | copy-done | bytes 1572888
  47.6 0.0 copy-start.3
  47.6 1.0 %copy-done.3 = f32[256,896]{1,0:T(8,128)} copy-done((f32[256,896]{1,0:T(8,128)}, f32[256,896]{1,0:T(8,128)S(1)}, u32[]{:S(2)}) %copy-start.3) | copy-done | bytes 917528
  48.6 6.0 %all-to-all-start.1 = ((f32[8,32,128]{2,1,0:T(8,128)}), f32[8,32,128]{2,1,0:T(8,128)S(1)}, u32[]{:S(2)}, u32[]{:S(2)}) async-start(f32[8,32,128]{2,1,0:T(8,128)} %get-tuple-element.17.refs_1_), calls=%async_computation.1 | async-start | bytes 262144 | tf_op jit(solution)/shard_map/all_to_all | solution.py:524
  54.6 0.0 copy-start.13
  54.6 1.6 %copy-done.13 = bf16[2048,512]{1,0:T(8,128)(2,1)S(1)} copy-done((bf16[2048,512]{1,0:T(8,128)(2,1)S(1)}, bf16[2048,512]{1,0:T(8,128)(2,1)}, u32[]{:S(2)}) %copy-start.13) | copy-done | bytes 2097176
  56.2 0.0 copy-start.2
  56.2 0.0 copy-start.4
  56.2 6.7 %short_prompts.1 = (bf16[2048,512]{1,0:T(8,128)(2,1)}, f32[8,128]{1,0:T(8,128)}) custom-call(s32[2,3]{1,0:T(2,128)S(1)} %copy-done.8, bf16[2048,512]{1,0:T(8,128)(2,1)S(1)} %copy-done.13, bf16[2048,256]{1,0:T(8,128)(2,1)} %get-tuple-element.13.kv_ref, bf16[2048,512]{1,0:T(8,128)(2,1)} %get-tuple-element.14.refs_0_, ...), custom_call_target="tpu_custom_call", output_to_operand_aliasing={{0}: (3, {})} | custom-call | flops 4294967296 | bytes 4194304 | tf_op jit(solution)/shard_map/short_prompts/pallas_call | solution.py:302
  62.9 0.0 all-to-all-done.1.handed
  62.9 0.0 copy-done.2
  62.9 0.0 copy-done.4
  62.9 1.4 %decode_mix.1 = bf16[3,2,4096]{2,1,0:T(2,128)(2,1)} custom-call(f32[256,896]{1,0:T(8,128)S(1)} %copy-done.4, bf16[768,1024]{1,0:T(8,128)(2,1)S(1)} %copy-done.2, f32[64,128]{1,0:T(8,128)S(1)} %get-tuple-element.21.new_ref, f32[8,32,128]{2,1,0:T(8,128)S(1)} %all-to-all-done.1.handed), custom_call_target="tpu_custom_call" | custom-call | flops 50331648 | bytes 4194304 | tf_op jit(solution)/shard_map/decode_mix/pallas_call | solution.py:483
Async XLA Ops:
  0.6 1.0 %copy-start.10 = (bf16[2,24,5120]{2,1,0:T(8,128)(2,1)S(1)}, bf16[2,24,5120]{2,1,0:T(8,128)(2,1)}, u32[]{:S(2)}) copy-start(bf16[2,24,5120]{2,1,0:T(8,128)(2,1)} %param.19) | copy-start | bytes 1474564
  1.7 25.0 %copy-start.5 = (s32[2,16,2]{1,2,0:T(2,128)S(1)}, s32[2,16,2]{1,2,0:T(2,128)}, u32[]{:S(2)}) copy-start(s32[2,16,2]{1,2,0:T(2,128)} %param.15) | copy-start | bytes 772
  1.7 25.0 %copy-start.6 = (s32[2,3]{1,0:T(2,128)S(1)}, s32[2,3]{1,0:T(2,128)}, u32[]{:S(2)}) copy-start(s32[2,3]{1,0:T(2,128)} %refs_1_.3) | copy-start | bytes 76
  1.7 25.0 %copy-start.7 = (s32[3,2]{0,1:T(2,128)S(1)}, s32[3,2]{0,1:T(2,128)}, u32[]{:S(2)}) copy-start(s32[3,2]{0,1:T(2,128)} %param.16) | copy-start | bytes 76
  1.7 25.0 %copy-start.8 = (s32[2,3]{1,0:T(2,128)S(1)}, s32[2,3]{1,0:T(2,128)}, u32[]{:S(2)}) copy-start(s32[2,3]{1,0:T(2,128)} %counts.5) | copy-start | bytes 76
  1.7 25.0 %copy-start.9 = (s32[3]{0:T(128)S(1)}, s32[3]{0:T(128)}, u32[]{:S(2)}) copy-start(s32[3]{0:T(128)} %refs_4_.1) | copy-start | bytes 40
  24.9 1.3 %copy-start.11 = (bf16[2048,512]{1,0:T(8,128)(2,1)}, bf16[2048,512]{1,0:T(8,128)(2,1)S(1)}, u32[]{:S(2)}) copy-start(bf16[2048,512]{1,0:T(8,128)(2,1)S(1)} %get-tuple-element.12.q_ref) | copy-start | bytes 6291460
  26.2 16.3 %collective-permute-start = (bf16[2048,256]{1,0:T(8,128)(2,1)}, bf16[2048,256]{1,0:T(8,128)(2,1)}, u32[]{:S(2)}, u32[]{:S(2)}) collective-permute-start(bf16[2048,256]{1,0:T(8,128)(2,1)} %get-tuple-element.13.kv_ref), channel_id=1, source_target_pairs={{0,8},{8,0},{1,9},{9,1},{2,10},{10,2},{3,11},{11,3},{4,12},{12,4},... | collective-permute-start | bytes 3145736 | tf_op jit(solution)/shard_map/ppermute | solution.py:521
  28.1 14.4 %all-to-all-start = ((bf16[8,8,768]{2,1,0:T(8,128)(2,1)}), bf16[8,8,768]{2,1,0:T(8,128)(2,1)S(1)}, u32[]{:S(2)}, u32[]{:S(2)}) async-start(bf16[8,8,768]{2,1,0:T(8,128)(2,1)} %bitcast.4), calls=%async_computation | async-start | bytes 196608 | tf_op jit(solution)/shard_map/all_to_all | solution.py:520
  35.0 1.6 %copy-start.12 = (bf16[2048,512]{1,0:T(8,128)(2,1)S(1)}, bf16[2048,512]{1,0:T(8,128)(2,1)}, u32[]{:S(2)}) copy-start(bf16[2048,512]{1,0:T(8,128)(2,1)} %copy-done.11) | copy-start | bytes 6291460
  36.5 6.0 %copy-start = (bf16[6,128,2048]{2,1,0:T(8,128)(2,1)S(1)}, bf16[6,128,2048]{2,1,0:T(8,128)(2,1)}, u32[]{:S(2)}) copy-start(bf16[6,128,2048]{2,1,0:T(8,128)(2,1)} %param.18) | copy-start | bytes 9437188
  46.5 1.1 %copy-start.1 = (bf16[768,1024]{1,0:T(8,128)(2,1)}, bf16[768,1024]{1,0:T(8,128)(2,1)S(1)}, u32[]{:S(2)}) copy-start(bf16[768,1024]{1,0:T(8,128)(2,1)S(1)} %get-tuple-element.20.v_ref) | copy-start | bytes 4718596
  47.6 1.0 %copy-start.3 = (f32[256,896]{1,0:T(8,128)}, f32[256,896]{1,0:T(8,128)S(1)}, u32[]{:S(2)}) copy-start(f32[256,896]{1,0:T(8,128)S(1)} %get-tuple-element.19.s_ref) | copy-start | bytes 2752516
  48.6 14.3 %all-to-all-start.1 = ((f32[8,32,128]{2,1,0:T(8,128)}), f32[8,32,128]{2,1,0:T(8,128)S(1)}, u32[]{:S(2)}, u32[]{:S(2)}) async-start(f32[8,32,128]{2,1,0:T(8,128)} %get-tuple-element.17.refs_1_), calls=%async_computation.1 | async-start | bytes 262144 | tf_op jit(solution)/shard_map/all_to_all | solution.py:524
  54.6 1.6 %copy-start.13 = (bf16[2048,512]{1,0:T(8,128)(2,1)S(1)}, bf16[2048,512]{1,0:T(8,128)(2,1)}, u32[]{:S(2)}) copy-start(bf16[2048,512]{1,0:T(8,128)(2,1)} %copy-done.11) | copy-start | bytes 6291460
  56.2 6.7 %copy-start.2 = (bf16[768,1024]{1,0:T(8,128)(2,1)S(1)}, bf16[768,1024]{1,0:T(8,128)(2,1)}, u32[]{:S(2)}) copy-start(bf16[768,1024]{1,0:T(8,128)(2,1)} %copy-done.1) | copy-start | bytes 4718596
  56.2 6.7 %copy-start.4 = (f32[256,896]{1,0:T(8,128)S(1)}, f32[256,896]{1,0:T(8,128)}, u32[]{:S(2)}) copy-start(f32[256,896]{1,0:T(8,128)} %copy-done.3) | copy-start | bytes 2752516

commit v10 on v7

--- a/solution.py
+++ b/solution.py
@@ -25,7 +25,9 @@
 SCALE = HD ** (-0.5)
 MASKED = -1e30
 PIECES = 5
-STRIPS = 2
+STRIPS = 4
+MIX_STRIPS = 4
+WIDE = 4096
 LOG2E = 1.4426950408889634
 AHEAD = 2
 MIB = 1 << 20
@@ -107,7 +109,7 @@
         if isinstance(k, int):
             rows = pl.ds(0, first)
         else:
-            rows = pl.ds(pl.multiple_of(first + (k - 1) * size, BLOCK_TOKENS), size)
+            rows = pl.ds(pl.multiple_of(first + (k - 1) * size, 64), size)
         return [
             pltpu.make_async_copy(q_out.at[rows], q_hbm.at[rows], out_sems.at[0, k]),
             pltpu.make_async_copy(kv_out.at[rows], kv_hbm.at[rows], out_sems.at[1, k]),
@@ -172,7 +174,7 @@
     def _():
         for copy in x_copies(step - 1):
             copy.wait()
-        keep(dot(xs[step - 1], w[...]), pl.ds(pl.multiple_of(first + (step - 1) * size, BLOCK_TOKENS), size))
+        keep(dot(xs[step - 1], w[...]), pl.ds(pl.multiple_of(first + (step - 1) * size, 64), size))
         for copy in out_copies(step):
             copy.start()
 
@@ -224,27 +226,29 @@
 
 
 def attend_prompt(lq, half, counts, q_hbm, kv_hbm, *refs):
-    o_hbm, made_ref, qs, kvs, outs, sems = refs[-6:]
-    made_ref[...] = jnp.zeros_like(made_ref)
+    o_hbm, qs, kvs, outs, sems = refs[-5:]
     group = lax.axis_index("pool")
     c0, c1 = counts[group, 0], counts[group, 1]
     big = jnp.where(c0 == MOST_BLOCKS, 0, jnp.where(c1 == MOST_BLOCKS, c0, c0 + c1))
     cut = jnp.where(c0 == MOST_BLOCKS, c1, c0)
     loads, stores = [], []
-    for j in range(MOST_BLOCKS):
+    strip, early = (4, 3) if half == 0 else (1, 5)
+    for j in range(0, MOST_BLOCKS, strip):
         block = big + j if half == 0 else j + jnp.where(j >= big, MOST_BLOCKS, 0)
-        rows = pl.ds(pl.multiple_of(block * BLOCK_TOKENS, BLOCK_TOKENS), BLOCK_TOKENS)
-        here = pl.ds(j * BLOCK_TOKENS, BLOCK_TOKENS)
+        rows = pl.ds(pl.multiple_of(block * BLOCK_TOKENS, BLOCK_TOKENS), strip * BLOCK_TOKENS)
+        here = pl.ds(j * BLOCK_TOKENS, strip * BLOCK_TOKENS)
         loads.append(pltpu.make_async_copy(kv_hbm.at[rows], kvs.at[here], sems.at[0, j]))
         loads.append(pltpu.make_async_copy(q_hbm.at[rows], qs.at[here], sems.at[1, j]))
         stores.append(pltpu.make_async_copy(outs.at[here], o_hbm.at[rows], sems.at[2, j]))
     for copy in loads:
         copy.start()
-    for copy in loads:
+    near = len(loads) // 2
+    for copy in loads[:near]:
         copy.wait()
     shape = (BLOCK_TOKENS, lq * BLOCK_TOKENS)
     causal = iota(shape, 0) <= iota(shape, 1) % BLOCK_TOKENS
-    flipped = kvs[:, HD:].T
+    tokens = MOST_BLOCKS * BLOCK_TOKENS
+    flipped = kvs[: tokens // 2, HD:].T
 
     def scores_of(j):
         q = qs[j * BLOCK_TOKENS : (j + 1) * BLOCK_TOKENS, :]
@@ -253,6 +257,10 @@
 
     scores = scores_of(0)
     for j in range(MOST_BLOCKS):
+        if j + 1 == MOST_BLOCKS // 2:
+            for copy in loads[near:]:
+                copy.wait()
+            flipped = jnp.concatenate([flipped, kvs[tokens // 2 :, HD:].T], axis=1)
         later = scores_of(j + 1) if j + 1 < MOST_BLOCKS else None
         weights = []
         for h in range(lq):
@@ -275,28 +283,25 @@
             part = mixed[:, h * BLOCK_TOKENS : (h + 1) * BLOCK_TOKENS].T
             outs[j * BLOCK_TOKENS : (j + 1) * BLOCK_TOKENS, h * HD : (h + 1) * HD] = part
         scores = later
-        if j == MOST_BLOCKS - 3:
-            for copy in stores[: j + 1]:
+        if j == early:
+            for copy in stores[: (j + 1) // strip]:
                 copy.start()
-    for copy in stores[MOST_BLOCKS - 2 :]:
+    for copy in stores[(early + 1) // strip :]:
         copy.start()
     for copy in stores:
         copy.wait()
 
 
-def prompt_attention(counts, q, kv, half, so_far=None, after=None):
+def prompt_attention(counts, q, kv, half, so_far=None):
     rows, cq = q.shape
     hbm = pl.BlockSpec(memory_space=pl.ANY)
-    more = () if so_far is None else (so_far, after)
+    more = () if so_far is None else (so_far,)
     tokens = MOST_BLOCKS * BLOCK_TOKENS
     return pl.pallas_call(
         functools.partial(attend_prompt, cq // HD, half),
         in_specs=[pl.BlockSpec(memory_space=SMEM), hbm, hbm] + [hbm] * len(more),
-        out_specs=[hbm, pl.BlockSpec(memory_space=VMEM)],
-        out_shape=[
-            jax.ShapeDtypeStruct((rows, cq), jnp.bfloat16),
-            jax.ShapeDtypeStruct((8, HD), jnp.float32),
-        ],
+        out_specs=hbm,
+        out_shape=jax.ShapeDtypeStruct((rows, cq), jnp.bfloat16),
         scratch_shapes=[
             VMEM((tokens, cq), jnp.bfloat16),
             VMEM((tokens, 2 * HD), jnp.bfloat16),
@@ -358,9 +363,13 @@
 
 def exchange_part(n, lq, *refs):
     counts, done, placed, table, lens, cache_hbm, msgs, kv_ref, q_ref, _ = refs[:10]
-    handed_ref, s_ref, v_ref, new_ref, cache, sem, slot_row, slot_limit = refs[10:]
-    load = pltpu.make_async_copy(cache_hbm, cache, sem)
-    load.start()
+    handed_ref, s_hbm, v_ref, new_ref, _, s_ref, cache, sems, slot_row, slot_limit = refs[10:]
+    loads = []
+    for slot in range(DEVICE_SLOTS):
+        part = pl.ds(slot * BLOCK_TOKENS, BLOCK_TOKENS)
+        loads.append(pltpu.make_async_copy(cache_hbm.at[part], cache.at[part], sems.at[slot]))
+    for load in loads:
+        load.start()
     handed_part(n, lq, kv_ref, q_ref, msgs, handed_ref)
     held = msgs[...].astype(jnp.float32)
     found = block_of_pages(counts, done, placed, table)
@@ -392,7 +401,8 @@
     before = jnp.sum(queries * earlier, axis=1, keepdims=True) * SCALE
     second = (rs >= ROWS_DEV) & (rs < STEPS * ROWS_DEV)
     before = jnp.where(second, before, MASKED)
-    load.wait()
+    for load in loads:
+        load.wait()
     scores = jnp.concatenate(
         [dot_t(rounded[h * span : (h + 1) * span], cache[:, 2 * h * HD : (2 * h + 1) * HD]) for h in range(KVH)],
         axis=0,
@@ -403,36 +413,50 @@
         s_ref[:, part] = jnp.where(usable, scores[:, part] * SCALE, MASKED)
     last = jnp.where(lane == 0, now, jnp.where(lane == 1, before, MASKED))
     s_ref[:, DEVICE_SLOTS * BLOCK_TOKENS :] = last
+    save = pltpu.make_async_copy(s_ref, s_hbm.at[:, pl.ds(0, s_ref.shape[1])], sems.at[DEVICE_SLOTS])
+    save.start()
     for h in range(KVH):
         v_ref[:, h * HD : (h + 1) * HD] = cache[:, (2 * h + 1) * HD : (2 * h + 2) * HD]
-
-
-def decode_scores(ints, cache, msgs, kv, q_own, after, n, lq):
+    save.wait()
+
+
+def decode_scores(ints, cache, msgs, kv, q_own, prompt_attn, n, lq):
     smem, vmem, hbm = [pl.BlockSpec(memory_space=space) for space in (SMEM, VMEM, pl.ANY)]
     rows = QH * GROUP_ROWS
     return pl.pallas_call(
         functools.partial(exchange_part, n, lq),
         in_specs=[smem] * 5 + [hbm, vmem, vmem, vmem, hbm],
-        out_specs=[vmem] * 4,
+        out_specs=[vmem, hbm, vmem, vmem, hbm],
         out_shape=[
             jax.ShapeDtypeStruct((n, lq * GROUP_ROWS, HD), jnp.float32),
-            jax.ShapeDtypeStruct((rows, (DEVICE_SLOTS + 1) * BLOCK_TOKENS), jnp.float32),
+            jax.ShapeDtypeStruct((rows, WIDE), jnp.float32),
             jax.ShapeDtypeStruct((cache.shape[0], KVH * HD), jnp.bfloat16),
             jax.ShapeDtypeStruct((KVH * GROUP_ROWS, HD), jnp.float32),
+            jax.ShapeDtypeStruct(prompt_attn.shape, prompt_attn.dtype),
         ],
+        input_output_aliases={9: 4},
         scratch_shapes=[
+            VMEM((rows, (DEVICE_SLOTS + 1) * BLOCK_TOKENS), jnp.float32),
             VMEM(cache.shape, jnp.bfloat16),
-            pltpu.SemaphoreType.DMA,
+            pltpu.SemaphoreType.DMA((DEVICE_SLOTS + 1,)),
             SMEM((DEVICE_SLOTS,), jnp.int32),
             SMEM((DEVICE_SLOTS,), jnp.int32),
         ],
-        compiler_params=pltpu.CompilerParams(vmem_limit_bytes=61 * MIB),
+        compiler_params=pltpu.CompilerParams(vmem_limit_bytes=103 * MIB // 2),
         cost_estimate=pl.CostEstimate(flops=2 * rows * HD * 768, bytes_accessed=4 * MIB, transcendentals=0),
         name="decode_scores",
-    )(*ints, cache, msgs, kv, q_own, after)
-
-
-def owner_mix(s_ref, v_ref, new_ref, handed, o_ref):
+    )(*ints, cache, msgs, kv, q_own, prompt_attn)
+
+
+def owner_mix(s_hbm, v_hbm, new_ref, handed, o_ref, s_ref, v_ref, sems):
+    loads = []
+    for k, (source, to) in enumerate(((s_hbm, s_ref), (v_hbm, v_ref))):
+        strip = to.shape[0] // MIX_STRIPS
+        for i in range(MIX_STRIPS):
+            part, cols = pl.ds(i * strip, strip), pl.ds(0, to.shape[1])
+            loads.append(pltpu.make_async_copy(source.at[part, cols], to.at[part], sems.at[k, i]))
+    for load in loads:
+        load.start()
     groups = QH
     rows = groups * GROUP_ROWS
     span = GQ * GROUP_ROWS
@@ -445,6 +469,8 @@
         return jnp.sum(jnp.where(mine, line, 0.0), axis=2, keepdims=True).reshape(rows, 1)
 
     other_peak, other_total = column(6), column(7)
+    for load in loads[:MIX_STRIPS]:
+        load.wait()
     scores = s_ref[...]
     peak = jnp.maximum(jnp.max(scores, axis=1, keepdims=True), other_peak)
     raised = jnp.exp(scores - peak)
@@ -455,6 +481,8 @@
     fresh = weights[:, old:].astype(jnp.float32)
     now, before = fresh[:, 0:1], fresh[:, 1:2]
     mixed = mixed.reshape(rows, HD) * (other * inverse)
+    for load in loads[MIX_STRIPS:]:
+        load.wait()
     out = []
     for h in range(KVH):
         part = slice(h * span, (h + 1) * span)
@@ -472,14 +500,19 @@
 
 
 def decode_mix(scores, values, new, parts):
-    vmem = pl.BlockSpec(memory_space=VMEM)
+    vmem, hbm = pl.BlockSpec(memory_space=VMEM), pl.BlockSpec(memory_space=pl.ANY)
     rows = QH * GROUP_ROWS
     return pl.pallas_call(
         owner_mix,
-        in_specs=[vmem] * 4,
+        in_specs=[hbm, hbm, vmem, vmem],
         out_specs=vmem,
         out_shape=jax.ShapeDtypeStruct((ROWS_DEV, STEPS, QH * HD), jnp.bfloat16),
-        compiler_params=pltpu.CompilerParams(vmem_limit_bytes=62 * MIB),
+        scratch_shapes=[
+            VMEM((rows, (DEVICE_SLOTS + 1) * BLOCK_TOKENS), jnp.float32),
+            VMEM(values.shape, values.dtype),
+            pltpu.SemaphoreType.DMA((2, MIX_STRIPS)),
+        ],
+        compiler_params=pltpu.CompilerParams(vmem_limit_bytes=533 * MIB // 10),
         cost_estimate=pl.CostEstimate(flops=2 * rows * HD * 768, bytes_accessed=4 * MIB, transcendentals=rows * 768),
         name="decode_mix",
     )(scores, values, new, parts)
@@ -508,14 +541,16 @@
     placement = placement.transpose(0, 2, 1)
     page_table = page_table.transpose(1, 0)
     ints = (prompt_blocks, finished, placement, page_table, row_lens)
-    first, size = 256, 256
+    first, size = 512, 512
     q, kv, q_own, msgs = project_all(ints, dx, prompt_x, q_weight, kv_weight, n, first, size)
     msgs = lax.all_to_all(msgs, "tp", split_axis=0, concat_axis=0, tiled=True)
     kv_other = lax.ppermute(kv, "pool", [(0, 1), (1, 0)])
-    prompt_attn, made = prompt_attention(prompt_blocks, q, kv, 0)
-    handed, scores, values, new = decode_scores(ints, cache, msgs, kv_other, q_own, made, n, lq)
+    prompt_attn = prompt_attention(prompt_blocks, q, kv, 0)
+    handed, scores, values, new, prompt_attn = decode_scores(
+        ints, cache, msgs, kv_other, q_own, prompt_attn, n, lq
+    )
     parts = lax.all_to_all(handed, "tp", split_axis=0, concat_axis=0, tiled=True)
-    prompt_attn, _ = prompt_attention(prompt_blocks, q, kv, 1, prompt_attn, handed)
+    prompt_attn = prompt_attention(prompt_blocks, q, kv, 1, prompt_attn)
     decode_attn = decode_mix(scores, values, new, parts)
     return prompt_attn, decode_attn.transpose(1, 0, 2)
 

time: 64.3 us -> 63.9 us (level)
  local copies, waits for them, and re-layouts: 1.64 us -> 0.04 us
  Pallas kernels: 48 us -> 48.8 us
    pallas_call x1, Pallas kernels: 5.29 us -> 7.32 us  [decode_scores(): pl.pallas_call(functools.partial(exchange_part, n, lq), in_specs=[smem] *...]
    unnamed x6 -> x12, local copies, waits for them, and re-layouts: 1.64 us -> 0.04 us
    pallas_call x2, Pallas kernels: 15 us -> 13.8 us  [prompt_attention(): pl.pallas_call(functools.partial(attend_prompt, cq // HD, half), in_specs...]
  transfers between devices with their start and end apart: 3 -> 3, of which waited for: 0 -> 2; matrix products, arithmetic and copies ran while one was open for 0% -> 0% of each run, Pallas kernels for 24% -> 22%
where the time goes in v10:
time: 63.9 us; the launch traced here: 63.4 us
  Pallas kernels  48.8 us (76%)
  starting transfers between devices  13.1 us (21%)
  between operations  0.9 us (1%)
    pallas_call x1, Pallas kernels, project_all(): pl.pallas_call(functools.partial(project, n, lq, first, size), grid=(1 +...  24.7 us
    pallas_call x2, Pallas kernels, prompt_attention(): pl.pallas_call(functools.partial(attend_prompt, cq // HD, half), in_specs...  13.8 us
    pallas_call x1, Pallas kernels, decode_scores(): pl.pallas_call(functools.partial(exchange_part, n, lq), in_specs=[smem] *...  7.32 us
    all_to_all x1, starting transfers between devices, local(): msgs = lax.all_to_all(msgs, 'tp', split_axis=0, concat_axis=0, tiled=True)  6.86 us
    all_to_all x1, starting transfers between devices, local(): lax.all_to_all(handed, 'tp', split_axis=0, concat_axis=0, tiled=True)  5.75 us
    pallas_call x1, Pallas kernels, decode_mix(): pl.pallas_call(owner_mix, in_specs=[hbm, hbm, vmem, vmem], out_specs=vmem...  2.94 us
  transfers between devices with their start and end apart: 3, of which 2 were waited for; matrix products, arithmetic and copies ran while one was open for 0% of the time, Pallas kernels for 22%

profile of v10, /device:TPU:0, one launch (start us, length us, event | category | flops | bytes accessed | tf_op | source)
XLA Modules:
  0.0 63.4 jit_solution(9816792693681330292)
XLA Ops:
  0.6 24.7 %project.1 = (bf16[2048,512]{1,0:T(8,128)(2,1)}, bf16[2048,256]{1,0:T(8,128)(2,1)}, bf16[256,128]{1,0:T(8,128)(2,1)}, bf16[64,768]{1,0:T(8,128)(2,1)}) custom-call(s32[2,3]{1,0:T(2,128)} %counts.3, s32[2,3]{1,0:T(2,128)} %refs_1_.3, s32[2,2,16]{2,1,0:T(2,128)} %bitcast.8, s32[2,3]{1,0:T(2,128)} %bitcast.10, s32[3]{0:T(128)} %refs_4_.3, ...), custom_call_target="tpu_custom_call" | custom-call | flops 16106127360 | bytes 31981568 | tf_op jit(solution)/shard_map/project/pallas_call | solution.py:197
  25.3 0.5 collective-permute-start
  25.9 6.9 %all-to-all-start = ((bf16[8,8,768]{2,1,0:T(8,128)(2,1)}), bf16[8,8,768]{2,1,0:T(8,128)(2,1)S(1)}, u32[]{:S(2)}, u32[]{:S(2)}) async-start(bf16[8,8,768]{2,1,0:T(8,128)(2,1)} %bitcast.13), calls=%async_computation | async-start | bytes 196608 | tf_op jit(solution)/shard_map/all_to_all | solution.py:546
  32.7 0.0 copy-start
  32.7 0.0 copy-start.1
  32.7 0.0 copy-start.2
  32.8 0.0 copy-start.3
  32.8 0.0 copy-start.4
  32.8 0.0 copy-start.5
  32.8 6.8 %long_prompt.1.refs_9_ = bf16[2048,512]{1,0:T(8,128)(2,1)} custom-call(s32[2,3]{1,0:T(2,128)} %counts.3, bf16[2048,512]{1,0:T(8,128)(2,1)} %get-tuple-element.11.q_hbm, bf16[2048,256]{1,0:T(8,128)(2,1)} %get-tuple-element.12.kv_hbm), custom_call_target="tpu_custom_call" | custom-call | flops 4294967296 | bytes 4194304 | tf_op jit(solution)/shard_map/long_prompt/pallas_call | solution.py:300
  39.6 0.3 all-to-all-done
  39.9 0.0 collective-permute-done.refs_7_
  39.9 0.0 copy-done
  39.9 0.0 copy-done.1
  39.9 0.0 copy-done.2
  39.9 0.0 copy-done.3
  39.9 0.0 copy-done.4
  39.9 0.0 copy-done.5
  39.9 7.3 %decode_scores.1 = (f32[8,32,128]{2,1,0:T(8,128)}, f32[256,4096]{1,0:T(8,128)}, bf16[768,1024]{1,0:T(8,128)(2,1)}, f32[64,128]{1,0:T(8,128)S(1)}, bf16[2048,512]{1,0:T(8,128)(2,1)}) custom-call(s32[2,3]{1,0:T(2,128)S(1)} %copy-done.4, s32[2,3]{1,0:T(2,128)S(1)} %copy-done.2, s32[2,2,16]{2,1,0:T(2,128)S(1)} %bitcast.9, ...), custom_call_target="tpu_custom_call", output_to_operand_aliasing={{4}: (9, {})} | custom-call | flops 50331648 | bytes 4194304 | tf_op jit(solution)/shard_map/decode_scores/pallas_call | solution.py:426
  47.3 5.7 %all-to-all-start.1 = ((f32[8,32,128]{2,1,0:T(8,128)}), f32[8,32,128]{2,1,0:T(8,128)S(1)}, u32[]{:S(2)}, u32[]{:S(2)}) async-start(f32[8,32,128]{2,1,0:T(8,128)} %get-tuple-element.19), calls=%async_computation.1 | async-start | bytes 262144 | tf_op jit(solution)/shard_map/all_to_all | solution.py:552
  53.0 7.0 %short_prompts.1 = bf16[2048,512]{1,0:T(8,128)(2,1)} custom-call(s32[2,3]{1,0:T(2,128)} %counts.3, bf16[2048,512]{1,0:T(8,128)(2,1)} %get-tuple-element.11.q_hbm, bf16[2048,256]{1,0:T(8,128)(2,1)} %get-tuple-element.12.kv_hbm, bf16[2048,512]{1,0:T(8,128)(2,1)} %get-tuple-element.15.refs_0_), custom_call_target="tpu_custom_call", output_to_operand_aliasing={{}: (3, {})} | custom-call | flops 4294967296 | bytes 4194304 | tf_op jit(solution)/shard_map/short_prompts/pallas_call | solution.py:300
  60.1 0.3 all-to-all-done.1.handed
  60.3 2.9 %decode_mix.1 = bf16[3,2,4096]{2,1,0:T(2,128)(2,1)} custom-call(f32[256,4096]{1,0:T(8,128)} %get-tuple-element.16.s_hbm, bf16[768,1024]{1,0:T(8,128)(2,1)} %get-tuple-element.17.v_hbm, f32[64,128]{1,0:T(8,128)S(1)} %get-tuple-element.18.new_ref, f32[8,32,128]{2,1,0:T(8,128)S(1)} %all-to-all-done.1.handed), custom_call_target="tpu_custom_call" | custom-call | flops 50331648 | bytes 4194304 | tf_op jit(solution)/shard_map/decode_mix/pallas_call | solution.py:505
Async XLA Ops:
  25.3 14.5 %collective-permute-start = (bf16[2048,256]{1,0:T(8,128)(2,1)}, bf16[2048,256]{1,0:T(8,128)(2,1)S(1)}, u32[]{:S(2)}, u32[]{:S(2)}) collective-permute-start(bf16[2048,256]{1,0:T(8,128)(2,1)} %get-tuple-element.12.kv_hbm), channel_id=1, source_target_pairs={{0,8},{8,0},{1,9},{9,1},{2,10},{10,2},{3,11},{11,3},{4,12},{12,4},... | collective-permute-start | bytes 3145736 | tf_op jit(solution)/shard_map/ppermute | solution.py:547
  25.9 14.0 %all-to-all-start = ((bf16[8,8,768]{2,1,0:T(8,128)(2,1)}), bf16[8,8,768]{2,1,0:T(8,128)(2,1)S(1)}, u32[]{:S(2)}, u32[]{:S(2)}) async-start(bf16[8,8,768]{2,1,0:T(8,128)(2,1)} %bitcast.13), calls=%async_computation | async-start | bytes 196608 | tf_op jit(solution)/shard_map/all_to_all | solution.py:546
  32.7 7.2 %copy-start = (bf16[256,128]{1,0:T(8,128)(2,1)S(1)}, bf16[256,128]{1,0:T(8,128)(2,1)}, u32[]{:S(2)}) copy-start(bf16[256,128]{1,0:T(8,128)(2,1)} %get-tuple-element.14.refs_8_) | copy-start | bytes 196612
  32.7 7.2 %copy-start.1 = (s32[2,16,2]{1,2,0:T(2,128)S(1)}, s32[2,16,2]{1,2,0:T(2,128)}, u32[]{:S(2)}) copy-start(s32[2,16,2]{1,2,0:T(2,128)} %param.15) | copy-start | bytes 772
  32.7 7.1 %copy-start.2 = (s32[2,3]{1,0:T(2,128)S(1)}, s32[2,3]{1,0:T(2,128)}, u32[]{:S(2)}) copy-start(s32[2,3]{1,0:T(2,128)} %refs_1_.3) | copy-start | bytes 76
  32.8 7.1 %copy-start.3 = (s32[3,2]{0,1:T(2,128)S(1)}, s32[3,2]{0,1:T(2,128)}, u32[]{:S(2)}) copy-start(s32[3,2]{0,1:T(2,128)} %param.16) | copy-start | bytes 76
  32.8 7.1 %copy-start.4 = (s32[2,3]{1,0:T(2,128)S(1)}, s32[2,3]{1,0:T(2,128)}, u32[]{:S(2)}) copy-start(s32[2,3]{1,0:T(2,128)} %counts.3) | copy-start | bytes 76
  32.8 7.1 %copy-start.5 = (s32[3]{0:T(128)S(1)}, s32[3]{0:T(128)}, u32[]{:S(2)}) copy-start(s32[3]{0:T(128)} %refs_4_.3) | copy-start | bytes 40
  47.3 13.1 %all-to-all-start.1 = ((f32[8,32,128]{2,1,0:T(8,128)}), f32[8,32,128]{2,1,0:T(8,128)S(1)}, u32[]{:S(2)}, u32[]{:S(2)}) async-start(f32[8,32,128]{2,1,0:T(8,128)} %get-tuple-element.19), calls=%async_computation.1 | async-start | bytes 262144 | tf_op jit(solution)/shard_map/all_to_all | solution.py:552

commit v11 on v10

--- a/solution.py
+++ b/solution.py
@@ -26,8 +26,6 @@
 MASKED = -1e30
 PIECES = 5
 STRIPS = 4
-MIX_STRIPS = 4
-WIDE = 4096
 LOG2E = 1.4426950408889634
 AHEAD = 2
 MIB = 1 << 20
@@ -75,10 +73,20 @@
     return out
 
 
+def int_scratch(ints):
+    return [SMEM(x.shape, jnp.int32) for x in ints] + [pltpu.SemaphoreType.DMA((len(ints),))]
+
+
+def int_copies(sources, targets, sems):
+    return [pltpu.make_async_copy(a, b, sems.at[i]) for i, (a, b) in enumerate(zip(sources, targets))]
+
+
 def project(n, lq, first, size, *refs):
-    counts, done, placed, table, lens, dx_hbm, x_hbm, wq_hbm, wkv_hbm = refs[:9]
-    q_hbm, kv_hbm, qh_ref, msg_ref = refs[9:13]
-    x0, xs, w, q_out, kv_out, x_sems, w_sems, out_sems = refs[13:]
+    dx_hbm, x_hbm, wq_hbm, wkv_hbm = refs[5:9]
+    q_hbm, kv_hbm, own_ref, msg_ref = refs[9:13]
+    x0, xs, w, q_out, kv_out, x_sems, w_sems, out_sems = refs[13:21]
+    counts, done, placed, table, lens, int_sems = refs[21:]
+    ints = int_copies(refs[:5], refs[21:26], int_sems)
     depth = w.shape[0]
     count = xs.shape[0]
     cq = lq * HD
@@ -124,6 +132,8 @@
         for c in range(AHEAD):
             for copy in piece_copies(c):
                 copy.start()
+        for copy in ints:
+            copy.start()
         total = 0.0
         for c in range(PIECES):
             for copy in piece_copies(c):
@@ -145,9 +155,9 @@
         wanted = owner * ROWS_DEV + row_of(rs) + jnp.where(rs >= ROWS_DEV, ROWS_DEV * n, 0)
         pick = ((fro == wanted) & (rs < STEPS * ROWS_DEV)).astype(jnp.float32).astype(jnp.bfloat16)
         own = dot(pick, total[first:].astype(jnp.bfloat16))
-        for h in range(lq):
-            part = slice(h * n * GROUP_ROWS, (h + 1) * n * GROUP_ROWS)
-            qh_ref[part, :] = own[:, h * HD : (h + 1) * HD].astype(jnp.bfloat16)
+        own_ref[...] = own.astype(jnp.bfloat16)
+        for copy in ints:
+            copy.wait()
         found = block_of_pages(counts, done, placed, table)
         lane = iota((n * GROUP_ROWS, HD), 1)
         r = row_of(lane % GROUP_ROWS)
@@ -192,17 +202,16 @@
     cq, ckv = wq.shape[1], wkv.shape[1]
     lq = cq // HD
     count = (rows - first) // size
-    smem, vmem = pl.BlockSpec(memory_space=SMEM), pl.BlockSpec(memory_space=VMEM)
-    hbm = pl.BlockSpec(memory_space=pl.ANY)
+    vmem, hbm = pl.BlockSpec(memory_space=VMEM), pl.BlockSpec(memory_space=pl.ANY)
     return pl.pallas_call(
         functools.partial(project, n, lq, first, size),
         grid=(1 + count,),
-        in_specs=[smem] * 5 + [hbm] * 4,
+        in_specs=[hbm] * 9,
         out_specs=[hbm, hbm, vmem, vmem],
         out_shape=[
             jax.ShapeDtypeStruct((rows, cq), jnp.bfloat16),
             jax.ShapeDtypeStruct((rows, ckv), jnp.bfloat16),
-            jax.ShapeDtypeStruct((lq * n * GROUP_ROWS, HD), jnp.bfloat16),
+            jax.ShapeDtypeStruct((n * GROUP_ROWS, cq + ckv), jnp.bfloat16),
             jax.ShapeDtypeStruct((n * GROUP_ROWS, cq + ckv), jnp.bfloat16),
         ],
         scratch_shapes=[
@@ -214,7 +223,8 @@
             pltpu.SemaphoreType.DMA((count, STRIPS)),
             pltpu.SemaphoreType.DMA((4, PIECES)),
             pltpu.SemaphoreType.DMA((2, count + 1)),
-        ],
+        ]
+        + int_scratch(ints),
         compiler_params=pltpu.CompilerParams(vmem_limit_bytes=62 * MIB),
         cost_estimate=pl.CostEstimate(
             flops=2 * rows * depth * (cq + ckv),
@@ -320,7 +330,7 @@
     return at // lq, at % lq
 
 
-def handed_part(n, lq, kv_ref, q_ref, msg_ref, o_ref):
+def handed_part(n, lq, kv_ref, own_ref, msg_ref, _, o_ref, __):
     rows = lq * n * GROUP_ROWS
     shape = (rows, HD)
     at_row, lane = iota(shape, 0), iota(shape, 1)
@@ -333,7 +343,9 @@
         return jnp.sum(jnp.where(lane == kind * GROUP_ROWS + rs, facts, 0.0), axis=1, keepdims=True)
 
     first_block, second_block, length = [column(kind) for kind in range(3)]
-    scores = dot_t(q_ref[...], kv_ref[:, :HD]) * SCALE
+    own = own_ref[...]
+    queries = jnp.concatenate([own[:, h * HD : (h + 1) * HD] for h in range(lq)], axis=0)
+    scores = dot_t(queries, kv_ref[:, :HD]) * SCALE
     lane_f = lane.astype(jnp.float32)
     parts = []
     for b in range(NBLK):
@@ -361,161 +373,133 @@
         o_ref[:, h * GROUP_ROWS : (h + 1) * GROUP_ROWS, :] = mixed[h * n : (h + 1) * n]
 
 
-def exchange_part(n, lq, *refs):
-    counts, done, placed, table, lens, cache_hbm, msgs, kv_ref, q_ref, _ = refs[:10]
-    handed_ref, s_hbm, v_ref, new_ref, _, s_ref, cache, sems, slot_row, slot_limit = refs[10:]
+def handed_attention(kv, own, msgs, prompt_attn, n, lq):
+    rows = lq * n * GROUP_ROWS
+    vmem, hbm = pl.BlockSpec(memory_space=VMEM), pl.BlockSpec(memory_space=pl.ANY)
+    return pl.pallas_call(
+        functools.partial(handed_part, n, lq),
+        in_specs=[vmem] * 3 + [hbm],
+        out_specs=[vmem, hbm],
+        out_shape=[
+            jax.ShapeDtypeStruct((n, lq * GROUP_ROWS, HD), jnp.float32),
+            jax.ShapeDtypeStruct(prompt_attn.shape, prompt_attn.dtype),
+        ],
+        input_output_aliases={3: 1},
+        compiler_params=pltpu.CompilerParams(vmem_limit_bytes=24 * MIB),
+        cost_estimate=pl.CostEstimate(flops=6 * rows * HD * PTOK, bytes_accessed=2 * MIB, transcendentals=rows * PTOK),
+        name="handed_attention",
+    )(kv, own, msgs, prompt_attn)
+
+
+def owner_part(n, lq, *refs):
+    cache_hbm, msgs, handed, o_ref, cache, sems, slot_row, slot_limit = refs[5:13]
+    counts, done, placed, table, lens, int_sems = refs[13:]
+    ints = int_copies(refs[:5], refs[13:18], int_sems)
+    for copy in ints:
+        copy.start()
     loads = []
     for slot in range(DEVICE_SLOTS):
         part = pl.ds(slot * BLOCK_TOKENS, BLOCK_TOKENS)
         loads.append(pltpu.make_async_copy(cache_hbm.at[part], cache.at[part], sems.at[slot]))
     for load in loads:
         load.start()
-    handed_part(n, lq, kv_ref, q_ref, msgs, handed_ref)
     held = msgs[...].astype(jnp.float32)
-    found = block_of_pages(counts, done, placed, table)
-    for r in range(ROWS_DEV):
-        for p in range(PAGES):
-            slot_row[table[p, r]] = jnp.int32(r)
-            slot_limit[table[p, r]] = jnp.where(found[r][p] < 0, lens[r] - p * BLOCK_TOKENS, 0)
-    cq = lq * HD
-    rows = QH * GROUP_ROWS
+
+    def tile(t, k):
+        return held[t * GROUP_ROWS : (t + 1) * GROUP_ROWS, k * HD : (k + 1) * HD]
+
+    groups = QH
+    rows = groups * GROUP_ROWS
     span = GQ * GROUP_ROWS
-    queries, keys = [], []
+    queries, keys, values = [], [], []
     for h in range(KVH):
         for hh in range(GQ):
             t, at = row_head(n, lq, h, hh)
-            queries.append(held[t * GROUP_ROWS : (t + 1) * GROUP_ROWS, at * HD : (at + 1) * HD])
+            queries.append(tile(t, at))
         t, _ = row_head(n, lq, h, 0)
-        keys += [held[t * GROUP_ROWS : (t + 1) * GROUP_ROWS, cq : cq + HD]] * GQ
-        new_ref[h * GROUP_ROWS : (h + 1) * GROUP_ROWS, :] = held[
-            t * GROUP_ROWS : (t + 1) * GROUP_ROWS, cq + HD : cq + 2 * HD
-        ]
+        keys += [tile(t, lq)] * GQ
+        values.append(tile(t, lq + 1))
     queries = jnp.concatenate(queries, axis=0)
     earlier = jnp.concatenate([pltpu.roll(key, ROWS_DEV, 0) for key in keys], axis=0)
     keys = jnp.concatenate(keys, axis=0)
     at_row, lane = iota((rows, HD), 0), iota((rows, HD), 1)
-    rs = at_row % GROUP_ROWS
-    r = row_of(rs)
+    r = row_of(at_row % GROUP_ROWS)
     rounded = queries.astype(jnp.bfloat16)
     now = jnp.sum(queries * keys, axis=1, keepdims=True) * SCALE
     before = jnp.sum(queries * earlier, axis=1, keepdims=True) * SCALE
-    second = (rs >= ROWS_DEV) & (rs < STEPS * ROWS_DEV)
-    before = jnp.where(second, before, MASKED)
+    rs1 = iota((rows, 1), 0) % GROUP_ROWS
+    before = jnp.where((rs1 >= ROWS_DEV) & (rs1 < STEPS * ROWS_DEV), before, MASKED)
+    mixed = handed[...].reshape(groups, GROUP_ROWS, HD)
+    shape = (groups, GROUP_ROWS, HD)
+    mine = iota(shape, 1) == iota(shape, 2)
+
+    def column(at):
+        line = jnp.broadcast_to(mixed[:, at : at + 1, :], shape)
+        return jnp.sum(jnp.where(mine, line, 0.0), axis=2, keepdims=True).reshape(rows, 1)
+
+    other_peak, other_total = column(6), column(7)
+    for copy in ints:
+        copy.wait()
+    found = block_of_pages(counts, done, placed, table)
+    for k in range(ROWS_DEV):
+        for p in range(PAGES):
+            slot_row[table[p, k]] = jnp.int32(k)
+            slot_limit[table[p, k]] = jnp.where(found[k][p] < 0, lens[k] - p * BLOCK_TOKENS, 0)
     for load in loads:
         load.wait()
     scores = jnp.concatenate(
         [dot_t(rounded[h * span : (h + 1) * span], cache[:, 2 * h * HD : (2 * h + 1) * HD]) for h in range(KVH)],
         axis=0,
     )
+    parts = []
     for slot in range(DEVICE_SLOTS):
-        part = slice(slot * BLOCK_TOKENS, (slot + 1) * BLOCK_TOKENS)
+        part = scores[:, slot * BLOCK_TOKENS : (slot + 1) * BLOCK_TOKENS]
         usable = (r == slot_row[slot]) & (lane < slot_limit[slot])
-        s_ref[:, part] = jnp.where(usable, scores[:, part] * SCALE, MASKED)
-    last = jnp.where(lane == 0, now, jnp.where(lane == 1, before, MASKED))
-    s_ref[:, DEVICE_SLOTS * BLOCK_TOKENS :] = last
-    save = pltpu.make_async_copy(s_ref, s_hbm.at[:, pl.ds(0, s_ref.shape[1])], sems.at[DEVICE_SLOTS])
-    save.start()
-    for h in range(KVH):
-        v_ref[:, h * HD : (h + 1) * HD] = cache[:, (2 * h + 1) * HD : (2 * h + 2) * HD]
-    save.wait()
-
-
-def decode_scores(ints, cache, msgs, kv, q_own, prompt_attn, n, lq):
-    smem, vmem, hbm = [pl.BlockSpec(memory_space=space) for space in (SMEM, VMEM, pl.ANY)]
-    rows = QH * GROUP_ROWS
-    return pl.pallas_call(
-        functools.partial(exchange_part, n, lq),
-        in_specs=[smem] * 5 + [hbm, vmem, vmem, vmem, hbm],
-        out_specs=[vmem, hbm, vmem, vmem, hbm],
-        out_shape=[
-            jax.ShapeDtypeStruct((n, lq * GROUP_ROWS, HD), jnp.float32),
-            jax.ShapeDtypeStruct((rows, WIDE), jnp.float32),
-            jax.ShapeDtypeStruct((cache.shape[0], KVH * HD), jnp.bfloat16),
-            jax.ShapeDtypeStruct((KVH * GROUP_ROWS, HD), jnp.float32),
-            jax.ShapeDtypeStruct(prompt_attn.shape, prompt_attn.dtype),
-        ],
-        input_output_aliases={9: 4},
-        scratch_shapes=[
-            VMEM((rows, (DEVICE_SLOTS + 1) * BLOCK_TOKENS), jnp.float32),
-            VMEM(cache.shape, jnp.bfloat16),
-            pltpu.SemaphoreType.DMA((DEVICE_SLOTS + 1,)),
-            SMEM((DEVICE_SLOTS,), jnp.int32),
-            SMEM((DEVICE_SLOTS,), jnp.int32),
-        ],
-        compiler_params=pltpu.CompilerParams(vmem_limit_bytes=103 * MIB // 2),
-        cost_estimate=pl.CostEstimate(flops=2 * rows * HD * 768, bytes_accessed=4 * MIB, transcendentals=0),
-        name="decode_scores",
-    )(*ints, cache, msgs, kv, q_own, prompt_attn)
-
-
-def owner_mix(s_hbm, v_hbm, new_ref, handed, o_ref, s_ref, v_ref, sems):
-    loads = []
-    for k, (source, to) in enumerate(((s_hbm, s_ref), (v_hbm, v_ref))):
-        strip = to.shape[0] // MIX_STRIPS
-        for i in range(MIX_STRIPS):
-            part, cols = pl.ds(i * strip, strip), pl.ds(0, to.shape[1])
-            loads.append(pltpu.make_async_copy(source.at[part, cols], to.at[part], sems.at[k, i]))
-    for load in loads:
-        load.start()
-    groups = QH
-    rows = groups * GROUP_ROWS
-    span = GQ * GROUP_ROWS
-    mixed = handed[...].reshape(groups, GROUP_ROWS, HD)
-    shape = (groups, GROUP_ROWS, HD)
-    mine = iota(shape, 1) == iota(shape, 2)
-
-    def column(at):
-        line = jnp.broadcast_to(mixed[:, at : at + 1, :], shape)
-        return jnp.sum(jnp.where(mine, line, 0.0), axis=2, keepdims=True).reshape(rows, 1)
-
-    other_peak, other_total = column(6), column(7)
-    for load in loads[:MIX_STRIPS]:
-        load.wait()
-    scores = s_ref[...]
-    peak = jnp.maximum(jnp.max(scores, axis=1, keepdims=True), other_peak)
-    raised = jnp.exp(scores - peak)
+        parts.append(jnp.where(usable, part * SCALE, MASKED))
+    scores = jnp.concatenate(parts, axis=1)
+    peak = jnp.maximum(jnp.max(scores, axis=1, keepdims=True), jnp.maximum(now, before))
+    peak = jnp.maximum(peak, other_peak)
+    raised, now, before = jnp.exp(scores - peak), jnp.exp(now - peak), jnp.exp(before - peak)
     other = jnp.exp(other_peak - peak)
-    inverse = 1.0 / (jnp.sum(raised, axis=1, keepdims=True) + other * other_total)
+    inverse = 1.0 / (jnp.sum(raised, axis=1, keepdims=True) + now + before + other * other_total)
     weights = (raised * inverse).astype(jnp.bfloat16)
-    old = DEVICE_SLOTS * BLOCK_TOKENS
-    fresh = weights[:, old:].astype(jnp.float32)
-    now, before = fresh[:, 0:1], fresh[:, 1:2]
+    now = (now * inverse).astype(jnp.bfloat16).astype(jnp.float32)
+    before = (before * inverse).astype(jnp.bfloat16).astype(jnp.float32)
     mixed = mixed.reshape(rows, HD) * (other * inverse)
-    for load in loads[MIX_STRIPS:]:
-        load.wait()
     out = []
     for h in range(KVH):
         part = slice(h * span, (h + 1) * span)
-        own = mixed[part] + dot(weights[part, :old], v_ref[:, h * HD : (h + 1) * HD])
-        value = new_ref[h * GROUP_ROWS : (h + 1) * GROUP_ROWS, :]
-        last = pltpu.roll(value, ROWS_DEV, 0)
+        own = mixed[part] + dot(weights[part], cache[:, (2 * h + 1) * HD : (2 * h + 2) * HD])
+        last = pltpu.roll(values[h], ROWS_DEV, 0)
         for hh in range(GQ):
             some = slice(h * span + hh * GROUP_ROWS, h * span + (hh + 1) * GROUP_ROWS)
             line = own[hh * GROUP_ROWS : (hh + 1) * GROUP_ROWS]
-            out.append(line + now[some] * value + before[some] * last)
+            out.append(line + now[some] * values[h] + before[some] * last)
     out = jnp.concatenate(out, axis=1)
     for k in range(ROWS_DEV):
         steps = [out[s * ROWS_DEV + k : s * ROWS_DEV + k + 1] for s in range(STEPS)]
         o_ref[k] = jnp.concatenate(steps, axis=0).astype(jnp.bfloat16)
 
 
-def decode_mix(scores, values, new, parts):
+def decode_attention(ints, cache, msgs, parts, n, lq):
     vmem, hbm = pl.BlockSpec(memory_space=VMEM), pl.BlockSpec(memory_space=pl.ANY)
     rows = QH * GROUP_ROWS
     return pl.pallas_call(
-        owner_mix,
-        in_specs=[hbm, hbm, vmem, vmem],
+        functools.partial(owner_part, n, lq),
+        in_specs=[hbm] * 6 + [vmem, vmem],
         out_specs=vmem,
         out_shape=jax.ShapeDtypeStruct((ROWS_DEV, STEPS, QH * HD), jnp.bfloat16),
         scratch_shapes=[
-            VMEM((rows, (DEVICE_SLOTS + 1) * BLOCK_TOKENS), jnp.float32),
-            VMEM(values.shape, values.dtype),
-            pltpu.SemaphoreType.DMA((2, MIX_STRIPS)),
-        ],
-        compiler_params=pltpu.CompilerParams(vmem_limit_bytes=533 * MIB // 10),
-        cost_estimate=pl.CostEstimate(flops=2 * rows * HD * 768, bytes_accessed=4 * MIB, transcendentals=rows * 768),
-        name="decode_mix",
-    )(scores, values, new, parts)
+            VMEM(cache.shape, jnp.bfloat16),
+            pltpu.SemaphoreType.DMA((DEVICE_SLOTS,)),
+            SMEM((DEVICE_SLOTS,), jnp.int32),
+            SMEM((DEVICE_SLOTS,), jnp.int32),
+        ]
+        + int_scratch(ints),
+        compiler_params=pltpu.CompilerParams(vmem_limit_bytes=54 * MIB),
+        cost_estimate=pl.CostEstimate(flops=4 * rows * HD * 768, bytes_accessed=4 * MIB, transcendentals=rows * 768),
+        name="decode_attention",
+    )(*ints, cache, msgs, parts)
 
 
 def local(
@@ -542,16 +526,14 @@
     page_table = page_table.transpose(1, 0)
     ints = (prompt_blocks, finished, placement, page_table, row_lens)
     first, size = 512, 512
-    q, kv, q_own, msgs = project_all(ints, dx, prompt_x, q_weight, kv_weight, n, first, size)
+    q, kv, own, msgs = project_all(ints, dx, prompt_x, q_weight, kv_weight, n, first, size)
+    kv_other = lax.ppermute(kv, "pool", [(0, 1), (1, 0)])
     msgs = lax.all_to_all(msgs, "tp", split_axis=0, concat_axis=0, tiled=True)
-    kv_other = lax.ppermute(kv, "pool", [(0, 1), (1, 0)])
     prompt_attn = prompt_attention(prompt_blocks, q, kv, 0)
-    handed, scores, values, new, prompt_attn = decode_scores(
-        ints, cache, msgs, kv_other, q_own, prompt_attn, n, lq
-    )
+    handed, prompt_attn = handed_attention(kv_other, own, msgs, prompt_attn, n, lq)
     parts = lax.all_to_all(handed, "tp", split_axis=0, concat_axis=0, tiled=True)
     prompt_attn = prompt_attention(prompt_blocks, q, kv, 1, prompt_attn)
-    decode_attn = decode_mix(scores, values, new, parts)
+    decode_attn = decode_attention(ints, cache, msgs, parts, n, lq)
     return prompt_attn, decode_attn.transpose(1, 0, 2)
 
 

time: 63.9 us -> 60.7 us (0.950)
  Pallas kernels: 48.8 us -> 45.1 us
    pallas_call x2, Pallas kernels: 10.3 us -> 7.17 us  [the longest x1 4.77 us: decode_attention(): pl.pallas_call(functools.partial(owner_part, n, lq), in_specs=[hbm] * 6 +...]
  transfers between devices with their start and end apart: 3 -> 3, of which waited for: 2 -> 2; matrix products, arithmetic and copies ran while one was open for 0% -> 0% of each run, Pallas kernels for 22% -> 23%
where the time goes in v11:
time: 60.7 us; the launch traced here: 60.3 us
  Pallas kernels  45.1 us (74%)
  starting transfers between devices  13.1 us (22%)
  between operations  0.83 us (1%)
  local copies, waits for them, and re-layouts  0.65 us (1%)
  waiting for transfers between devices  0.61 us (1%)
    pallas_call x1, Pallas kernels, project_all(): pl.pallas_call(functools.partial(project, n, lq, first, size), grid=(1 +...  24.1 us
    pallas_call x2, Pallas kernels, prompt_attention(): pl.pallas_call(functools.partial(attend_prompt, cq // HD, half), in_specs...  13.8 us
    all_to_all x1, starting transfers between devices, local(): msgs = lax.all_to_all(msgs, 'tp', split_axis=0, concat_axis=0, tiled=True)  6.86 us
    all_to_all x1, starting transfers between devices, local(): lax.all_to_all(handed, 'tp', split_axis=0, concat_axis=0, tiled=True)  5.68 us
    pallas_call x1, Pallas kernels, decode_attention(): pl.pallas_call(functools.partial(owner_part, n, lq), in_specs=[hbm] * 6 +...  4.77 us
    pallas_call x1, Pallas kernels, handed_attention(): pl.pallas_call(functools.partial(handed_part, n, lq), in_specs=[vmem] * 3...  2.4 us
  transfers between devices with their start and end apart: 3, of which 2 were waited for; matrix products, arithmetic and copies ran while one was open for 0% of the time, Pallas kernels for 23%

profile of v11, /device:TPU:0, one launch (start us, length us, event | category | flops | bytes accessed | tf_op | source)
XLA Modules:
  0.0 60.3 jit_solution(5589456122771444325)
XLA Ops:
  0.6 24.1 %project.1 = (bf16[2048,512]{1,0:T(8,128)(2,1)}, bf16[2048,256]{1,0:T(8,128)(2,1)}, bf16[64,768]{1,0:T(8,128)(2,1)}, bf16[64,768]{1,0:T(8,128)(2,1)}) custom-call(s32[2,3]{1,0:T(2,128)} %refs_0_.3, s32[2,3]{1,0:T(2,128)} %refs_1_.3, s32[2,2,16]{2,1,0:T(2,128)} %bitcast.12, s32[2,3]{1,0:T(2,128)} %bitcast.14, s32[3]{0:T(128)} %refs_4_.3, ...), custom_call_target="tpu_custom_call" | custom-call | flops 16106127360 | bytes 31981568 | tf_op jit(solution)/shard_map/project/pallas_call | solution.py:206
  24.7 0.5 collective-permute-start
  25.2 6.9 %all-to-all-start = ((bf16[8,8,768]{2,1,0:T(8,128)(2,1)}), bf16[8,8,768]{2,1,0:T(8,128)(2,1)S(1)}, u32[]{:S(2)}, u32[]{:S(2)}) async-start(bf16[8,8,768]{2,1,0:T(8,128)(2,1)} %bitcast.10), calls=%async_computation | async-start | bytes 196608 | tf_op jit(solution)/shard_map/all_to_all | solution.py:531
  32.1 0.0 copy-start.1
  32.1 6.8 %long_prompt.1._ = bf16[2048,512]{1,0:T(8,128)(2,1)} custom-call(s32[2,3]{1,0:T(2,128)} %refs_0_.3, bf16[2048,512]{1,0:T(8,128)(2,1)} %get-tuple-element.8.q_hbm, bf16[2048,256]{1,0:T(8,128)(2,1)} %get-tuple-element.9.kv_hbm), custom_call_target="tpu_custom_call" | custom-call | flops 4294967296 | bytes 4194304 | tf_op jit(solution)/shard_map/long_prompt/pallas_call | solution.py:310
  38.9 0.3 all-to-all-done
  39.2 0.0 copy-start
  39.2 0.0 collective-permute-done.kv_ref
  39.3 0.0 copy-done.1
  39.3 2.4 %handed_attention.1 = (f32[8,32,128]{2,1,0:T(8,128)}, bf16[2048,512]{1,0:T(8,128)(2,1)}) custom-call(bf16[2048,256]{1,0:T(8,128)(2,1)S(1)} %collective-permute-done.kv_ref, bf16[64,768]{1,0:T(8,128)(2,1)S(1)} %copy-done.1, bf16[64,768]{1,0:T(8,128)(2,1)S(1)} %bitcast.7, bf16[2048,512]{1,0:T(8,128)(2,1)} %long_prompt.1._), custom_call_target="tpu_custom_call", output_to_operand_aliasing={{1}: (3, {})} | custom-call | flops 402653184 | bytes 2097152 | tf_op jit(solution)/shard_map/handed_attention/pallas_call | solution.py:379
  41.7 5.7 %all-to-all-start.1 = ((f32[8,32,128]{2,1,0:T(8,128)}), f32[8,32,128]{2,1,0:T(8,128)S(1)}, u32[]{:S(2)}, u32[]{:S(2)}) async-start(f32[8,32,128]{2,1,0:T(8,128)} %get-tuple-element.13), calls=%async_computation.1 | async-start | bytes 262144 | tf_op jit(solution)/shard_map/all_to_all | solution.py:534
  47.3 7.0 %short_prompts.1 = bf16[2048,512]{1,0:T(8,128)(2,1)} custom-call(s32[2,3]{1,0:T(2,128)} %refs_0_.3, bf16[2048,512]{1,0:T(8,128)(2,1)} %get-tuple-element.8.q_hbm, bf16[2048,256]{1,0:T(8,128)(2,1)} %get-tuple-element.9.kv_hbm, bf16[2048,512]{1,0:T(8,128)(2,1)} %get-tuple-element.12.refs_0_), custom_call_target="tpu_custom_call", output_to_operand_aliasing={{}: (3, {})} | custom-call | flops 4294967296 | bytes 4194304 | tf_op jit(solution)/shard_map/short_prompts/pallas_call | solution.py:310
  54.4 0.0 copy-done
  54.4 0.3 all-to-all-done.1.refs_7_
  54.7 0.0 copy-start.2
  54.7 0.6 %copy-done.2 = f32[8,32,128]{2,1,0:T(8,128)} copy-done((f32[8,32,128]{2,1,0:T(8,128)}, f32[8,32,128]{2,1,0:T(8,128)S(1)}, u32[]{:S(2)}) %copy-start.2) | copy-done | bytes 131096
  55.3 4.8 %decode_attention.1 = bf16[3,2,4096]{2,1,0:T(2,128)(2,1)} custom-call(s32[2,3]{1,0:T(2,128)} %refs_0_.3, s32[2,3]{1,0:T(2,128)} %refs_1_.3, s32[2,2,16]{2,1,0:T(2,128)} %bitcast.13, s32[2,3]{1,0:T(2,128)} %bitcast.15, s32[3]{0:T(128)} %refs_4_.3, bf16[768,2048]{1,0:T(8,128)(2,1)} %bitcast.9, bf16[64,768]{1,0:T(8,128)(2,1)} %bitcast.8, f32[8,32,128]{2,1,0:T(8,128)} %copy-done.2), custom_call_target="tpu_custom_call" | custom-call | flops 100663296 | bytes 4194304 | tf_op jit(solution)/shard_map/decode_attention/pallas_call | solution.py:487
Async XLA Ops:
  24.7 14.5 %collective-permute-start = (bf16[2048,256]{1,0:T(8,128)(2,1)}, bf16[2048,256]{1,0:T(8,128)(2,1)S(1)}, u32[]{:S(2)}, u32[]{:S(2)}) collective-permute-start(bf16[2048,256]{1,0:T(8,128)(2,1)} %get-tuple-element.9.kv_hbm), channel_id=1, source_target_pairs={{0,8},{8,0},{1,9},{9,1},{2,10},{10,2},{3,11},{11,3},{4,12},{12,4},... | collective-permute-start | bytes 3145736 | tf_op jit(solution)/shard_map/ppermute | solution.py:530
  25.2 14.0 %all-to-all-start = ((bf16[8,8,768]{2,1,0:T(8,128)(2,1)}), bf16[8,8,768]{2,1,0:T(8,128)(2,1)S(1)}, u32[]{:S(2)}, u32[]{:S(2)}) async-start(bf16[8,8,768]{2,1,0:T(8,128)(2,1)} %bitcast.10), calls=%async_computation | async-start | bytes 196608 | tf_op jit(solution)/shard_map/all_to_all | solution.py:531
  32.1 7.2 %copy-start.1 = (bf16[64,768]{1,0:T(8,128)(2,1)S(1)}, bf16[64,768]{1,0:T(8,128)(2,1)}, u32[]{:S(2)}) copy-start(bf16[64,768]{1,0:T(8,128)(2,1)} %get-tuple-element.10.own_ref) | copy-start | bytes 294916
  39.2 15.2 %copy-start = (bf16[8,8,768]{2,1,0:T(8,128)(2,1)}, bf16[8,8,768]{2,1,0:T(8,128)(2,1)S(1)}, u32[]{:S(2)}) copy-start(bf16[8,8,768]{2,1,0:T(8,128)(2,1)S(1)} %all-to-all-done) | copy-start | bytes 294916
  41.7 13.0 %all-to-all-start.1 = ((f32[8,32,128]{2,1,0:T(8,128)}), f32[8,32,128]{2,1,0:T(8,128)S(1)}, u32[]{:S(2)}, u32[]{:S(2)}) async-start(f32[8,32,128]{2,1,0:T(8,128)} %get-tuple-element.13), calls=%async_computation.1 | async-start | bytes 262144 | tf_op jit(solution)/shard_map/all_to_all | solution.py:534
  54.7 0.6 %copy-start.2 = (f32[8,32,128]{2,1,0:T(8,128)}, f32[8,32,128]{2,1,0:T(8,128)S(1)}, u32[]{:S(2)}) copy-start(f32[8,32,128]{2,1,0:T(8,128)S(1)} %all-to-all-done.1.refs_7_) | copy-start | bytes 393220

commit v12 on v11

--- a/solution.py
+++ b/solution.py
@@ -392,10 +392,14 @@
 
 
 def owner_part(n, lq, *refs):
-    cache_hbm, msgs, handed, o_ref, cache, sems, slot_row, slot_limit = refs[5:13]
-    counts, done, placed, table, lens, int_sems = refs[13:]
-    ints = int_copies(refs[:5], refs[13:18], int_sems)
-    for copy in ints:
+    cache_hbm, msgs_hbm, handed_hbm, o_ref, cache, msgs, handed, sems, slot_row, slot_limit = refs[5:15]
+    counts, done, placed, table, lens, int_sems = refs[15:]
+    ints = int_copies(refs[:5], refs[15:20], int_sems)
+    first = [
+        pltpu.make_async_copy(msgs_hbm, msgs, sems.at[DEVICE_SLOTS]),
+        pltpu.make_async_copy(handed_hbm, handed, sems.at[DEVICE_SLOTS + 1]),
+    ]
+    for copy in first:
         copy.start()
     loads = []
     for slot in range(DEVICE_SLOTS):
@@ -403,6 +407,10 @@
         loads.append(pltpu.make_async_copy(cache_hbm.at[part], cache.at[part], sems.at[slot]))
     for load in loads:
         load.start()
+    for copy in ints:
+        copy.start()
+    for copy in first:
+        copy.wait()
     held = msgs[...].astype(jnp.float32)
 
     def tile(t, k):
@@ -486,17 +494,19 @@
     rows = QH * GROUP_ROWS
     return pl.pallas_call(
         functools.partial(owner_part, n, lq),
-        in_specs=[hbm] * 6 + [vmem, vmem],
+        in_specs=[hbm] * 8,
         out_specs=vmem,
         out_shape=jax.ShapeDtypeStruct((ROWS_DEV, STEPS, QH * HD), jnp.bfloat16),
         scratch_shapes=[
             VMEM(cache.shape, jnp.bfloat16),
-            pltpu.SemaphoreType.DMA((DEVICE_SLOTS,)),
+            VMEM(msgs.shape, msgs.dtype),
+            VMEM(parts.shape, parts.dtype),
+            pltpu.SemaphoreType.DMA((DEVICE_SLOTS + 2,)),
             SMEM((DEVICE_SLOTS,), jnp.int32),
             SMEM((DEVICE_SLOTS,), jnp.int32),
         ]
         + int_scratch(ints),
-        compiler_params=pltpu.CompilerParams(vmem_limit_bytes=54 * MIB),
+        compiler_params=pltpu.CompilerParams(vmem_limit_bytes=52 * MIB),
         cost_estimate=pl.CostEstimate(flops=4 * rows * HD * 768, bytes_accessed=4 * MIB, transcendentals=rows * 768),
         name="decode_attention",
     )(*ints, cache, msgs, parts)
@@ -525,7 +535,7 @@
     placement = placement.transpose(0, 2, 1)
     page_table = page_table.transpose(1, 0)
     ints = (prompt_blocks, finished, placement, page_table, row_lens)
-    first, size = 512, 512
+    first, size = 256, 448
     q, kv, own, msgs = project_all(ints, dx, prompt_x, q_weight, kv_weight, n, first, size)
     kv_other = lax.ppermute(kv, "pool", [(0, 1), (1, 0)])
     msgs = lax.all_to_all(msgs, "tp", split_axis=0, concat_axis=0, tiled=True)

time: 60.7 us -> 59.1 us (0.974)
  Pallas kernels: 45.1 us -> 44.3 us
  local copies, waits for them, and re-layouts: 0.65 us -> 0.03 us
    pallas_call x1, Pallas kernels: 4.77 us -> 4.14 us  [decode_attention(): pl.pallas_call(functools.partial(owner_part, n, lq), in_specs=[hbm] * 8,...]
    unnamed x6 -> x12, local copies, waits for them, and re-layouts: 0.65 us -> 0.03 us
  transfers between devices with their start and end apart: 3 -> 3, of which waited for: 2 -> 2; matrix products, arithmetic and copies ran while one was open for 0% -> 0% of each run, Pallas kernels for 23% -> 24%
where the time goes in v12:
time: 59.1 us; the launch traced here: 58.7 us
  Pallas kernels  44.3 us (75%)
  starting transfers between devices  13.1 us (22%)
  between operations  0.88 us (1%)
    pallas_call x1, Pallas kernels, project_all(): pl.pallas_call(functools.partial(project, n, lq, first, size), grid=(1 +...  23.8 us
    pallas_call x2, Pallas kernels, prompt_attention(): pl.pallas_call(functools.partial(attend_prompt, cq // HD, half), in_specs...  14 us
    all_to_all x1, starting transfers between devices, local(): msgs = lax.all_to_all(msgs, 'tp', split_axis=0, concat_axis=0, tiled=True)  6.85 us
    all_to_all x1, starting transfers between devices, local(): lax.all_to_all(handed, 'tp', split_axis=0, concat_axis=0, tiled=True)  5.68 us
    pallas_call x1, Pallas kernels, decode_attention(): pl.pallas_call(functools.partial(owner_part, n, lq), in_specs=[hbm] * 8,...  4.14 us
    pallas_call x1, Pallas kernels, handed_attention(): pl.pallas_call(functools.partial(handed_part, n, lq), in_specs=[vmem] * 3...  2.39 us
  transfers between devices with their start and end apart: 3, of which 2 were waited for; matrix products, arithmetic and copies ran while one was open for 0% of the time, Pallas kernels for 24%

profile of v12, /device:TPU:0, one launch (start us, length us, event | category | flops | bytes accessed | tf_op | source)
XLA Modules:
  0.0 58.7 jit_solution(3005954735121447848)
XLA Ops:
  0.6 23.8 %project.1 = (bf16[2048,512]{1,0:T(8,128)(2,1)}, bf16[2048,256]{1,0:T(8,128)(2,1)}, bf16[64,768]{1,0:T(8,128)(2,1)}, bf16[64,768]{1,0:T(8,128)(2,1)}) custom-call(s32[2,3]{1,0:T(2,128)} %refs_0_.3, s32[2,3]{1,0:T(2,128)} %refs_1_.3, s32[2,2,16]{2,1,0:T(2,128)} %bitcast.9, s32[2,3]{1,0:T(2,128)} %bitcast.11, s32[3]{0:T(128)} %refs_4_.3, ...), custom_call_target="tpu_custom_call" | custom-call | flops 16106127360 | bytes 31981568 | tf_op jit(solution)/shard_map/project/pallas_call | solution.py:206
  24.4 0.5 collective-permute-start
  24.9 6.9 %all-to-all-start = ((bf16[8,8,768]{2,1,0:T(8,128)(2,1)}), bf16[8,8,768]{2,1,0:T(8,128)(2,1)S(1)}, u32[]{:S(2)}, u32[]{:S(2)}) async-start(bf16[8,8,768]{2,1,0:T(8,128)(2,1)} %bitcast.14), calls=%async_computation | async-start | bytes 196608 | tf_op jit(solution)/shard_map/all_to_all | solution.py:541
  31.8 0.0 copy-start
  31.8 6.8 %long_prompt.1._ = bf16[2048,512]{1,0:T(8,128)(2,1)} custom-call(s32[2,3]{1,0:T(2,128)} %refs_0_.3, bf16[2048,512]{1,0:T(8,128)(2,1)} %get-tuple-element.8.q_hbm, bf16[2048,256]{1,0:T(8,128)(2,1)} %get-tuple-element.9.kv_hbm), custom_call_target="tpu_custom_call" | custom-call | flops 4294967296 | bytes 4194304 | tf_op jit(solution)/shard_map/long_prompt/pallas_call | solution.py:310
  38.6 0.3 all-to-all-done
  38.9 0.0 collective-permute-done.kv_ref
  38.9 0.0 copy-done
  38.9 2.4 %handed_attention.1 = (f32[8,32,128]{2,1,0:T(8,128)}, bf16[2048,512]{1,0:T(8,128)(2,1)}) custom-call(bf16[2048,256]{1,0:T(8,128)(2,1)S(1)} %collective-permute-done.kv_ref, bf16[64,768]{1,0:T(8,128)(2,1)S(1)} %copy-done, bf16[64,768]{1,0:T(8,128)(2,1)S(1)} %bitcast.7, bf16[2048,512]{1,0:T(8,128)(2,1)} %long_prompt.1._), custom_call_target="tpu_custom_call", output_to_operand_aliasing={{1}: (3, {})} | custom-call | flops 402653184 | bytes 2097152 | tf_op jit(solution)/shard_map/handed_attention/pallas_call | solution.py:379
  41.3 5.7 %all-to-all-start.1 = ((f32[8,32,128]{2,1,0:T(8,128)}), f32[8,32,128]{2,1,0:T(8,128)S(1)}, u32[]{:S(2)}, u32[]{:S(2)}) async-start(f32[8,32,128]{2,1,0:T(8,128)} %get-tuple-element.13), calls=%async_computation.1 | async-start | bytes 262144 | tf_op jit(solution)/shard_map/all_to_all | solution.py:544
  47.0 0.0 copy-start.1
  47.0 0.0 copy-start.2
  47.0 0.0 copy-start.3
  47.0 0.0 copy-start.4
  47.0 0.0 copy-start.5
  47.1 7.2 %short_prompts.1 = bf16[2048,512]{1,0:T(8,128)(2,1)} custom-call(s32[2,3]{1,0:T(2,128)} %refs_0_.3, bf16[2048,512]{1,0:T(8,128)(2,1)} %get-tuple-element.8.q_hbm, bf16[2048,256]{1,0:T(8,128)(2,1)} %get-tuple-element.9.kv_hbm, bf16[2048,512]{1,0:T(8,128)(2,1)} %get-tuple-element.12.refs_0_), custom_call_target="tpu_custom_call", output_to_operand_aliasing={{}: (3, {})} | custom-call | flops 4294967296 | bytes 4194304 | tf_op jit(solution)/shard_map/short_prompts/pallas_call | solution.py:310
  54.2 0.1 all-to-all-done.1.refs_7_
  54.3 0.0 copy-done.1
  54.3 0.0 copy-done.2
  54.3 0.0 copy-done.3
  54.4 0.0 copy-done.4
  54.4 0.0 copy-done.5
  54.4 4.1 %decode_attention.1 = bf16[3,2,4096]{2,1,0:T(2,128)(2,1)} custom-call(s32[2,3]{1,0:T(2,128)S(1)} %copy-done.2, s32[2,3]{1,0:T(2,128)S(1)} %copy-done.3, s32[2,2,16]{2,1,0:T(2,128)S(1)} %bitcast.10, s32[2,3]{1,0:T(2,128)S(1)} %bitcast.12, s32[3]{0:T(128)S(1)} %copy-done.5, bf16[768,2048]{1,0:T(8,128)(2,1)} %bitcast.13, bf16[64,768]{1,0:T(8,128)(2,1)S(1)} %bitcast.8, ...), custom_call_target="tpu_custom_call" | custom-call | flops 100663296 | bytes 4194304 | tf_op jit(solution)/shard_map/decode_attention/pallas_call | solution.py:495
Async XLA Ops:
  24.4 14.5 %collective-permute-start = (bf16[2048,256]{1,0:T(8,128)(2,1)}, bf16[2048,256]{1,0:T(8,128)(2,1)S(1)}, u32[]{:S(2)}, u32[]{:S(2)}) collective-permute-start(bf16[2048,256]{1,0:T(8,128)(2,1)} %get-tuple-element.9.kv_hbm), channel_id=1, source_target_pairs={{0,8},{8,0},{1,9},{9,1},{2,10},{10,2},{3,11},{11,3},{4,12},{12,4},... | collective-permute-start | bytes 3145736 | tf_op jit(solution)/shard_map/ppermute | solution.py:540
  24.9 14.0 %all-to-all-start = ((bf16[8,8,768]{2,1,0:T(8,128)(2,1)}), bf16[8,8,768]{2,1,0:T(8,128)(2,1)S(1)}, u32[]{:S(2)}, u32[]{:S(2)}) async-start(bf16[8,8,768]{2,1,0:T(8,128)(2,1)} %bitcast.14), calls=%async_computation | async-start | bytes 196608 | tf_op jit(solution)/shard_map/all_to_all | solution.py:541
  31.8 7.2 %copy-start = (bf16[64,768]{1,0:T(8,128)(2,1)S(1)}, bf16[64,768]{1,0:T(8,128)(2,1)}, u32[]{:S(2)}) copy-start(bf16[64,768]{1,0:T(8,128)(2,1)} %get-tuple-element.10.own_ref) | copy-start | bytes 294916
  41.3 13.0 %all-to-all-start.1 = ((f32[8,32,128]{2,1,0:T(8,128)}), f32[8,32,128]{2,1,0:T(8,128)S(1)}, u32[]{:S(2)}, u32[]{:S(2)}) async-start(f32[8,32,128]{2,1,0:T(8,128)} %get-tuple-element.13), calls=%async_computation.1 | async-start | bytes 262144 | tf_op jit(solution)/shard_map/all_to_all | solution.py:544
  47.0 7.3 %copy-start.1 = (s32[2,16,2]{1,2,0:T(2,128)S(1)}, s32[2,16,2]{1,2,0:T(2,128)}, u32[]{:S(2)}) copy-start(s32[2,16,2]{1,2,0:T(2,128)} %param.15) | copy-start | bytes 772
  47.0 7.3 %copy-start.2 = (s32[2,3]{1,0:T(2,128)S(1)}, s32[2,3]{1,0:T(2,128)}, u32[]{:S(2)}) copy-start(s32[2,3]{1,0:T(2,128)} %refs_0_.3) | copy-start | bytes 76
  47.0 7.3 %copy-start.3 = (s32[2,3]{1,0:T(2,128)S(1)}, s32[2,3]{1,0:T(2,128)}, u32[]{:S(2)}) copy-start(s32[2,3]{1,0:T(2,128)} %refs_1_.3) | copy-start | bytes 76
  47.0 7.3 %copy-start.4 = (s32[3,2]{0,1:T(2,128)S(1)}, s32[3,2]{0,1:T(2,128)}, u32[]{:S(2)}) copy-start(s32[3,2]{0,1:T(2,128)} %param.16) | copy-start | bytes 76
  47.0 7.3 %copy-start.5 = (s32[3]{0:T(128)S(1)}, s32[3]{0:T(128)}, u32[]{:S(2)}) copy-start(s32[3]{0:T(128)} %refs_4_.3) | copy-start | bytes 40

commit v13 on v12

--- a/solution.py
+++ b/solution.py
@@ -84,9 +84,9 @@
 def project(n, lq, first, size, *refs):
     dx_hbm, x_hbm, wq_hbm, wkv_hbm = refs[5:9]
     q_hbm, kv_hbm, own_ref, msg_ref = refs[9:13]
-    x0, xs, w, q_out, kv_out, x_sems, w_sems, out_sems = refs[13:21]
-    counts, done, placed, table, lens, int_sems = refs[21:]
-    ints = int_copies(refs[:5], refs[21:26], int_sems)
+    x0, xs, w, flipped, q_out, kv_out, x_sems, w_sems, out_sems = refs[13:22]
+    counts, done, placed, table, lens, int_sems = refs[22:]
+    ints = int_copies(refs[:5], refs[22:27], int_sems)
     depth = w.shape[0]
     count = xs.shape[0]
     cq = lq * HD
@@ -146,6 +146,7 @@
                     copy.start()
             part = slice(c * piece, (c + 1) * piece)
             total += dot(x0[:, part], w[part, :])
+            flipped[:, part] = w[part, cq:].T
         keep(total[:first], pl.ds(0, first))
         for copy in out_copies(0):
             copy.start()
@@ -184,7 +185,9 @@
     def _():
         for copy in x_copies(step - 1):
             copy.wait()
-        keep(dot(xs[step - 1], w[...]), pl.ds(pl.multiple_of(first + (step - 1) * size, 64), size))
+        rows = pl.ds(pl.multiple_of(first + (step - 1) * size, 64), size)
+        q_out[rows, :] = dot(xs[step - 1], w[:, :cq]).astype(jnp.bfloat16)
+        kv_out[rows, :] = dot_t(flipped[...], xs[step - 1]).astype(jnp.bfloat16).T
         for copy in out_copies(step):
             copy.start()
 
@@ -218,6 +221,7 @@
             VMEM((first + dx.shape[0], depth), jnp.bfloat16),
             VMEM((count, size, depth), jnp.bfloat16),
             VMEM((depth, cq + ckv), jnp.bfloat16),
+            VMEM((ckv, depth), jnp.bfloat16),
             VMEM((rows, cq), jnp.bfloat16),
             VMEM((rows, ckv), jnp.bfloat16),
             pltpu.SemaphoreType.DMA((count, STRIPS)),
@@ -535,7 +539,7 @@
     placement = placement.transpose(0, 2, 1)
     page_table = page_table.transpose(1, 0)
     ints = (prompt_blocks, finished, placement, page_table, row_lens)
-    first, size = 256, 448
+    first, size = 512, 512
     q, kv, own, msgs = project_all(ints, dx, prompt_x, q_weight, kv_weight, n, first, size)
     kv_other = lax.ppermute(kv, "pool", [(0, 1), (1, 0)])
     msgs = lax.all_to_all(msgs, "tp", split_axis=0, concat_axis=0, tiled=True)

time: 59.1 us -> 59.5 us (level)
  no operation moved by 1% of the time
where the time goes in v13:
time: 59.5 us; the launch traced here: 59.1 us
  Pallas kernels  44.7 us (75%)
  starting transfers between devices  13.1 us (22%)
  between operations  0.88 us (1%)
    pallas_call x1, Pallas kernels, project_all(): pl.pallas_call(functools.partial(project, n, lq, first, size), grid=(1 +...  24.2 us
    pallas_call x2, Pallas kernels, prompt_attention(): pl.pallas_call(functools.partial(attend_prompt, cq // HD, half), in_specs...  14 us
    all_to_all x1, starting transfers between devices, local(): msgs = lax.all_to_all(msgs, 'tp', split_axis=0, concat_axis=0, tiled=True)  6.85 us
    all_to_all x1, starting transfers between devices, local(): lax.all_to_all(handed, 'tp', split_axis=0, concat_axis=0, tiled=True)  5.68 us
    pallas_call x1, Pallas kernels, decode_attention(): pl.pallas_call(functools.partial(owner_part, n, lq), in_specs=[hbm] * 8,...  4.14 us
    pallas_call x1, Pallas kernels, handed_attention(): pl.pallas_call(functools.partial(handed_part, n, lq), in_specs=[vmem] * 3...  2.39 us
  transfers between devices with their start and end apart: 3, of which 2 were waited for; matrix products, arithmetic and copies ran while one was open for 0% of the time, Pallas kernels for 24%

profile of v13, /device:TPU:0, one launch (start us, length us, event | category | flops | bytes accessed | tf_op | source)
XLA Modules:
  0.0 59.1 jit_solution(4141429629455006743)
XLA Ops:
  0.6 24.2 %project.1 = (bf16[2048,512]{1,0:T(8,128)(2,1)}, bf16[2048,256]{1,0:T(8,128)(2,1)}, bf16[64,768]{1,0:T(8,128)(2,1)}, bf16[64,768]{1,0:T(8,128)(2,1)}) custom-call(s32[2,3]{1,0:T(2,128)} %refs_0_.3, s32[2,3]{1,0:T(2,128)} %refs_1_.3, s32[2,2,16]{2,1,0:T(2,128)} %bitcast.9, s32[2,3]{1,0:T(2,128)} %bitcast.11, s32[3]{0:T(128)} %refs_4_.3, ...), custom_call_target="tpu_custom_call" | custom-call | flops 16106127360 | bytes 31981568 | tf_op jit(solution)/shard_map/project/pallas_call | solution.py:209
  24.8 0.5 collective-permute-start
  25.3 6.9 %all-to-all-start = ((bf16[8,8,768]{2,1,0:T(8,128)(2,1)}), bf16[8,8,768]{2,1,0:T(8,128)(2,1)S(1)}, u32[]{:S(2)}, u32[]{:S(2)}) async-start(bf16[8,8,768]{2,1,0:T(8,128)(2,1)} %bitcast.14), calls=%async_computation | async-start | bytes 196608 | tf_op jit(solution)/shard_map/all_to_all | solution.py:545
  32.2 0.0 copy-start
  32.2 6.8 %long_prompt.1._ = bf16[2048,512]{1,0:T(8,128)(2,1)} custom-call(s32[2,3]{1,0:T(2,128)} %refs_0_.3, bf16[2048,512]{1,0:T(8,128)(2,1)} %get-tuple-element.8.q_hbm, bf16[2048,256]{1,0:T(8,128)(2,1)} %get-tuple-element.9.kv_hbm), custom_call_target="tpu_custom_call" | custom-call | flops 4294967296 | bytes 4194304 | tf_op jit(solution)/shard_map/long_prompt/pallas_call | solution.py:314
  39.0 0.3 all-to-all-done
  39.3 0.0 collective-permute-done.kv_ref
  39.4 0.0 copy-done
  39.4 2.4 %handed_attention.1 = (f32[8,32,128]{2,1,0:T(8,128)}, bf16[2048,512]{1,0:T(8,128)(2,1)}) custom-call(bf16[2048,256]{1,0:T(8,128)(2,1)S(1)} %collective-permute-done.kv_ref, bf16[64,768]{1,0:T(8,128)(2,1)S(1)} %copy-done, bf16[64,768]{1,0:T(8,128)(2,1)S(1)} %bitcast.7, bf16[2048,512]{1,0:T(8,128)(2,1)} %long_prompt.1._), custom_call_target="tpu_custom_call", output_to_operand_aliasing={{1}: (3, {})} | custom-call | flops 402653184 | bytes 2097152 | tf_op jit(solution)/shard_map/handed_attention/pallas_call | solution.py:383
  41.7 5.7 %all-to-all-start.1 = ((f32[8,32,128]{2,1,0:T(8,128)}), f32[8,32,128]{2,1,0:T(8,128)S(1)}, u32[]{:S(2)}, u32[]{:S(2)}) async-start(f32[8,32,128]{2,1,0:T(8,128)} %get-tuple-element.13), calls=%async_computation.1 | async-start | bytes 262144 | tf_op jit(solution)/shard_map/all_to_all | solution.py:548
  47.4 0.0 copy-start.1
  47.4 0.0 copy-start.2
  47.4 0.0 copy-start.3
  47.5 0.0 copy-start.4
  47.5 0.0 copy-start.5
  47.5 7.2 %short_prompts.1 = bf16[2048,512]{1,0:T(8,128)(2,1)} custom-call(s32[2,3]{1,0:T(2,128)} %refs_0_.3, bf16[2048,512]{1,0:T(8,128)(2,1)} %get-tuple-element.8.q_hbm, bf16[2048,256]{1,0:T(8,128)(2,1)} %get-tuple-element.9.kv_hbm, bf16[2048,512]{1,0:T(8,128)(2,1)} %get-tuple-element.12.refs_0_), custom_call_target="tpu_custom_call", output_to_operand_aliasing={{}: (3, {})} | custom-call | flops 4294967296 | bytes 4194304 | tf_op jit(solution)/shard_map/short_prompts/pallas_call | solution.py:314
  54.7 0.1 all-to-all-done.1.refs_7_
  54.8 0.0 copy-done.1
  54.8 0.0 copy-done.2
  54.8 0.0 copy-done.3
  54.8 0.0 copy-done.4
  54.8 0.0 copy-done.5
  54.8 4.1 %decode_attention.1 = bf16[3,2,4096]{2,1,0:T(2,128)(2,1)} custom-call(s32[2,3]{1,0:T(2,128)S(1)} %copy-done.2, s32[2,3]{1,0:T(2,128)S(1)} %copy-done.3, s32[2,2,16]{2,1,0:T(2,128)S(1)} %bitcast.10, s32[2,3]{1,0:T(2,128)S(1)} %bitcast.12, s32[3]{0:T(128)S(1)} %copy-done.5, bf16[768,2048]{1,0:T(8,128)(2,1)} %bitcast.13, bf16[64,768]{1,0:T(8,128)(2,1)S(1)} %bitcast.8, ...), custom_call_target="tpu_custom_call" | custom-call | flops 100663296 | bytes 4194304 | tf_op jit(solution)/shard_map/decode_attention/pallas_call | solution.py:499
Async XLA Ops:
  24.8 14.5 %collective-permute-start = (bf16[2048,256]{1,0:T(8,128)(2,1)}, bf16[2048,256]{1,0:T(8,128)(2,1)S(1)}, u32[]{:S(2)}, u32[]{:S(2)}) collective-permute-start(bf16[2048,256]{1,0:T(8,128)(2,1)} %get-tuple-element.9.kv_hbm), channel_id=1, source_target_pairs={{0,8},{8,0},{1,9},{9,1},{2,10},{10,2},{3,11},{11,3},{4,12},{12,4},... | collective-permute-start | bytes 3145736 | tf_op jit(solution)/shard_map/ppermute | solution.py:544
  25.3 14.0 %all-to-all-start = ((bf16[8,8,768]{2,1,0:T(8,128)(2,1)}), bf16[8,8,768]{2,1,0:T(8,128)(2,1)S(1)}, u32[]{:S(2)}, u32[]{:S(2)}) async-start(bf16[8,8,768]{2,1,0:T(8,128)(2,1)} %bitcast.14), calls=%async_computation | async-start | bytes 196608 | tf_op jit(solution)/shard_map/all_to_all | solution.py:545
  32.2 7.2 %copy-start = (bf16[64,768]{1,0:T(8,128)(2,1)S(1)}, bf16[64,768]{1,0:T(8,128)(2,1)}, u32[]{:S(2)}) copy-start(bf16[64,768]{1,0:T(8,128)(2,1)} %get-tuple-element.10.own_ref) | copy-start | bytes 294916
  41.7 13.0 %all-to-all-start.1 = ((f32[8,32,128]{2,1,0:T(8,128)}), f32[8,32,128]{2,1,0:T(8,128)S(1)}, u32[]{:S(2)}, u32[]{:S(2)}) async-start(f32[8,32,128]{2,1,0:T(8,128)} %get-tuple-element.13), calls=%async_computation.1 | async-start | bytes 262144 | tf_op jit(solution)/shard_map/all_to_all | solution.py:548
  47.4 7.3 %copy-start.1 = (s32[2,16,2]{1,2,0:T(2,128)S(1)}, s32[2,16,2]{1,2,0:T(2,128)}, u32[]{:S(2)}) copy-start(s32[2,16,2]{1,2,0:T(2,128)} %param.15) | copy-start | bytes 772
  47.4 7.3 %copy-start.2 = (s32[2,3]{1,0:T(2,128)S(1)}, s32[2,3]{1,0:T(2,128)}, u32[]{:S(2)}) copy-start(s32[2,3]{1,0:T(2,128)} %refs_0_.3) | copy-start | bytes 76
  47.4 7.3 %copy-start.3 = (s32[2,3]{1,0:T(2,128)S(1)}, s32[2,3]{1,0:T(2,128)}, u32[]{:S(2)}) copy-start(s32[2,3]{1,0:T(2,128)} %refs_1_.3) | copy-start | bytes 76
  47.5 7.3 %copy-start.4 = (s32[3,2]{0,1:T(2,128)S(1)}, s32[3,2]{0,1:T(2,128)}, u32[]{:S(2)}) copy-start(s32[3,2]{0,1:T(2,128)} %param.16) | copy-start | bytes 76
  47.5 7.3 %copy-start.5 = (s32[3]{0:T(128)S(1)}, s32[3]{0:T(128)}, u32[]{:S(2)}) copy-start(s32[3]{0:T(128)} %refs_4_.3) | copy-start | bytes 40

commit v14 on v12

--- a/solution.py
+++ b/solution.py
@@ -81,6 +81,11 @@
     return [pltpu.make_async_copy(a, b, sems.at[i]) for i, (a, b) in enumerate(zip(sources, targets))]
 
 
+def start_all(copies):
+    for i, copy in enumerate(copies):
+        copy.start(priority=i % 2)
+
+
 def project(n, lq, first, size, *refs):
     dx_hbm, x_hbm, wq_hbm, wkv_hbm = refs[5:9]
     q_hbm, kv_hbm, own_ref, msg_ref = refs[9:13]
@@ -98,9 +103,9 @@
         part = pl.ds(c * piece, piece)
         return [
             pltpu.make_async_copy(x_hbm.at[pl.ds(0, first), part], x0.at[pl.ds(0, first), part], w_sems.at[0, c]),
-            pltpu.make_async_copy(dx_hbm.at[:, part], x0.at[pl.ds(first, own_rows), part], w_sems.at[1, c]),
             pltpu.make_async_copy(wq_hbm.at[part], w.at[part, pl.ds(0, cq)], w_sems.at[2, c]),
             pltpu.make_async_copy(wkv_hbm.at[part], w.at[part, pl.ds(cq, 2 * HD)], w_sems.at[3, c]),
+            pltpu.make_async_copy(dx_hbm.at[:, part], x0.at[pl.ds(first, own_rows), part], w_sems.at[1, c]),
         ]
 
     def x_copies(k):
@@ -130,8 +135,7 @@
     @pl.when(step == 0)
     def _():
         for c in range(AHEAD):
-            for copy in piece_copies(c):
-                copy.start()
+            start_all(piece_copies(c))
         for copy in ints:
             copy.start()
         total = 0.0
@@ -139,11 +143,9 @@
             for copy in piece_copies(c):
                 copy.wait()
             if c + AHEAD < PIECES:
-                for copy in piece_copies(c + AHEAD):
-                    copy.start()
+                start_all(piece_copies(c + AHEAD))
             if c + AHEAD >= PIECES:
-                for copy in x_copies(c + AHEAD - PIECES):
-                    copy.start()
+                start_all(x_copies(c + AHEAD - PIECES))
             part = slice(c * piece, (c + 1) * piece)
             total += dot(x0[:, part], w[part, :])
         keep(total[:first], pl.ds(0, first))
@@ -177,8 +179,7 @@
 
     @pl.when((step > 0) & (step + AHEAD <= count))
     def _():
-        for copy in x_copies(step + AHEAD - 1):
-            copy.start()
+        start_all(x_copies(step + AHEAD - 1))
 
     @pl.when(step > 0)
     def _():
@@ -250,8 +251,7 @@
         loads.append(pltpu.make_async_copy(kv_hbm.at[rows], kvs.at[here], sems.at[0, j]))
         loads.append(pltpu.make_async_copy(q_hbm.at[rows], qs.at[here], sems.at[1, j]))
         stores.append(pltpu.make_async_copy(outs.at[here], o_hbm.at[rows], sems.at[2, j]))
-    for copy in loads:
-        copy.start()
+    start_all(loads)
     near = len(loads) // 2
     for copy in loads[:near]:
         copy.wait()
@@ -405,8 +405,7 @@
     for slot in range(DEVICE_SLOTS):
         part = pl.ds(slot * BLOCK_TOKENS, BLOCK_TOKENS)
         loads.append(pltpu.make_async_copy(cache_hbm.at[part], cache.at[part], sems.at[slot]))
-    for load in loads:
-        load.start()
+    start_all(loads)
     for copy in ints:
         copy.start()
     for copy in first:

time: 59.1 us -> 59.4 us (level)
  transfers between devices with their start and end apart: 3 -> 3, of which waited for: 2 -> 1; matrix products, arithmetic and copies ran while one was open for 0% -> 0% of each run, Pallas kernels for 24% -> 24%
where the time goes in v14:
time: 59.4 us; the launch traced here: 58.9 us
  Pallas kernels  44.6 us (75%)
  starting transfers between devices  13.1 us (22%)
  between operations  0.91 us (2%)
    pallas_call x1, Pallas kernels, project_all(): pl.pallas_call(functools.partial(project, n, lq, first, size), grid=(1 +...  23.9 us
    pallas_call x2, Pallas kernels, prompt_attention(): pl.pallas_call(functools.partial(attend_prompt, cq // HD, half), in_specs...  14.2 us
    all_to_all x1, starting transfers between devices, local(): msgs = lax.all_to_all(msgs, 'tp', split_axis=0, concat_axis=0, tiled=True)  6.85 us
    all_to_all x1, starting transfers between devices, local(): lax.all_to_all(handed, 'tp', split_axis=0, concat_axis=0, tiled=True)  5.75 us
    pallas_call x1, Pallas kernels, decode_attention(): pl.pallas_call(functools.partial(owner_part, n, lq), in_specs=[hbm] * 8,...  4.13 us
    pallas_call x1, Pallas kernels, handed_attention(): pl.pallas_call(functools.partial(handed_part, n, lq), in_specs=[vmem] * 3...  2.39 us
  transfers between devices with their start and end apart: 3, of which 1 were waited for; matrix products, arithmetic and copies ran while one was open for 0% of the time, Pallas kernels for 24%

profile of v14, /device:TPU:0, one launch (start us, length us, event | category | flops | bytes accessed | tf_op | source)
XLA Modules:
  0.0 58.9 jit_solution(1775327197269086131)
XLA Ops:
  0.6 23.9 %project.1 = (bf16[2048,512]{1,0:T(8,128)(2,1)}, bf16[2048,256]{1,0:T(8,128)(2,1)}, bf16[64,768]{1,0:T(8,128)(2,1)}, bf16[64,768]{1,0:T(8,128)(2,1)}) custom-call(s32[2,3]{1,0:T(2,128)} %refs_0_.3, s32[2,3]{1,0:T(2,128)} %refs_1_.3, s32[2,2,16]{2,1,0:T(2,128)} %bitcast.9, s32[2,3]{1,0:T(2,128)} %bitcast.11, s32[3]{0:T(128)} %refs_4_.3, ...), custom_call_target="tpu_custom_call" | custom-call | flops 16106127360 | bytes 31981568 | tf_op jit(solution)/shard_map/project/pallas_call | solution.py:207
  24.5 0.5 collective-permute-start
  25.0 6.9 %all-to-all-start = ((bf16[8,8,768]{2,1,0:T(8,128)(2,1)}), bf16[8,8,768]{2,1,0:T(8,128)(2,1)S(1)}, u32[]{:S(2)}, u32[]{:S(2)}) async-start(bf16[8,8,768]{2,1,0:T(8,128)(2,1)} %bitcast.14), calls=%async_computation | async-start | bytes 196608 | tf_op jit(solution)/shard_map/all_to_all | solution.py:540
  31.9 0.0 copy-start
  31.9 6.9 %long_prompt.1._ = bf16[2048,512]{1,0:T(8,128)(2,1)} custom-call(s32[2,3]{1,0:T(2,128)} %refs_0_.3, bf16[2048,512]{1,0:T(8,128)(2,1)} %get-tuple-element.8.q_hbm, bf16[2048,256]{1,0:T(8,128)(2,1)} %get-tuple-element.9.kv_hbm), custom_call_target="tpu_custom_call" | custom-call | flops 4294967296 | bytes 4194304 | tf_op jit(solution)/shard_map/long_prompt/pallas_call | solution.py:310
  38.8 0.3 all-to-all-done
  39.0 0.0 collective-permute-done.kv_ref
  39.0 0.0 copy-done
  39.0 2.4 %handed_attention.1 = (f32[8,32,128]{2,1,0:T(8,128)}, bf16[2048,512]{1,0:T(8,128)(2,1)}) custom-call(bf16[2048,256]{1,0:T(8,128)(2,1)S(1)} %collective-permute-done.kv_ref, bf16[64,768]{1,0:T(8,128)(2,1)S(1)} %copy-done, bf16[64,768]{1,0:T(8,128)(2,1)S(1)} %bitcast.7, bf16[2048,512]{1,0:T(8,128)(2,1)} %long_prompt.1._), custom_call_target="tpu_custom_call", output_to_operand_aliasing={{1}: (3, {})} | custom-call | flops 402653184 | bytes 2097152 | tf_op jit(solution)/shard_map/handed_attention/pallas_call | solution.py:379
  41.4 5.8 %all-to-all-start.1 = ((f32[8,32,128]{2,1,0:T(8,128)}), f32[8,32,128]{2,1,0:T(8,128)S(1)}, u32[]{:S(2)}, u32[]{:S(2)}) async-start(f32[8,32,128]{2,1,0:T(8,128)} %get-tuple-element.13), calls=%async_computation.1 | async-start | bytes 262144 | tf_op jit(solution)/shard_map/all_to_all | solution.py:543
  47.2 0.0 copy-start.1
  47.2 0.0 copy-start.2
  47.2 0.0 copy-start.3
  47.2 0.0 copy-start.4
  47.2 0.0 copy-start.5
  47.2 7.3 %short_prompts.1 = bf16[2048,512]{1,0:T(8,128)(2,1)} custom-call(s32[2,3]{1,0:T(2,128)} %refs_0_.3, bf16[2048,512]{1,0:T(8,128)(2,1)} %get-tuple-element.8.q_hbm, bf16[2048,256]{1,0:T(8,128)(2,1)} %get-tuple-element.9.kv_hbm, bf16[2048,512]{1,0:T(8,128)(2,1)} %get-tuple-element.12.refs_0_), custom_call_target="tpu_custom_call", output_to_operand_aliasing={{}: (3, {})} | custom-call | flops 4294967296 | bytes 4194304 | tf_op jit(solution)/shard_map/short_prompts/pallas_call | solution.py:310
  54.6 0.0 all-to-all-done.1.refs_7_
  54.6 0.0 copy-done.1
  54.6 0.0 copy-done.2
  54.6 0.0 copy-done.3
  54.6 0.0 copy-done.4
  54.6 0.0 copy-done.5
  54.6 4.1 %decode_attention.1 = bf16[3,2,4096]{2,1,0:T(2,128)(2,1)} custom-call(s32[2,3]{1,0:T(2,128)S(1)} %copy-done.2, s32[2,3]{1,0:T(2,128)S(1)} %copy-done.3, s32[2,2,16]{2,1,0:T(2,128)S(1)} %bitcast.10, s32[2,3]{1,0:T(2,128)S(1)} %bitcast.12, s32[3]{0:T(128)S(1)} %copy-done.5, bf16[768,2048]{1,0:T(8,128)(2,1)} %bitcast.13, bf16[64,768]{1,0:T(8,128)(2,1)S(1)} %bitcast.8, ...), custom_call_target="tpu_custom_call" | custom-call | flops 100663296 | bytes 4194304 | tf_op jit(solution)/shard_map/decode_attention/pallas_call | solution.py:494
Async XLA Ops:
  24.5 14.5 %collective-permute-start = (bf16[2048,256]{1,0:T(8,128)(2,1)}, bf16[2048,256]{1,0:T(8,128)(2,1)S(1)}, u32[]{:S(2)}, u32[]{:S(2)}) collective-permute-start(bf16[2048,256]{1,0:T(8,128)(2,1)} %get-tuple-element.9.kv_hbm), channel_id=1, source_target_pairs={{0,8},{8,0},{1,9},{9,1},{2,10},{10,2},{3,11},{11,3},{4,12},{12,4},... | collective-permute-start | bytes 3145736 | tf_op jit(solution)/shard_map/ppermute | solution.py:539
  25.0 14.0 %all-to-all-start = ((bf16[8,8,768]{2,1,0:T(8,128)(2,1)}), bf16[8,8,768]{2,1,0:T(8,128)(2,1)S(1)}, u32[]{:S(2)}, u32[]{:S(2)}) async-start(bf16[8,8,768]{2,1,0:T(8,128)(2,1)} %bitcast.14), calls=%async_computation | async-start | bytes 196608 | tf_op jit(solution)/shard_map/all_to_all | solution.py:540
  31.9 7.2 %copy-start = (bf16[64,768]{1,0:T(8,128)(2,1)S(1)}, bf16[64,768]{1,0:T(8,128)(2,1)}, u32[]{:S(2)}) copy-start(bf16[64,768]{1,0:T(8,128)(2,1)} %get-tuple-element.10.own_ref) | copy-start | bytes 294916
  41.4 13.1 %all-to-all-start.1 = ((f32[8,32,128]{2,1,0:T(8,128)}), f32[8,32,128]{2,1,0:T(8,128)S(1)}, u32[]{:S(2)}, u32[]{:S(2)}) async-start(f32[8,32,128]{2,1,0:T(8,128)} %get-tuple-element.13), calls=%async_computation.1 | async-start | bytes 262144 | tf_op jit(solution)/shard_map/all_to_all | solution.py:543
  47.2 7.4 %copy-start.1 = (s32[2,16,2]{1,2,0:T(2,128)S(1)}, s32[2,16,2]{1,2,0:T(2,128)}, u32[]{:S(2)}) copy-start(s32[2,16,2]{1,2,0:T(2,128)} %param.15) | copy-start | bytes 772
  47.2 7.4 %copy-start.2 = (s32[2,3]{1,0:T(2,128)S(1)}, s32[2,3]{1,0:T(2,128)}, u32[]{:S(2)}) copy-start(s32[2,3]{1,0:T(2,128)} %refs_0_.3) | copy-start | bytes 76
  47.2 7.4 %copy-start.3 = (s32[2,3]{1,0:T(2,128)S(1)}, s32[2,3]{1,0:T(2,128)}, u32[]{:S(2)}) copy-start(s32[2,3]{1,0:T(2,128)} %refs_1_.3) | copy-start | bytes 76
  47.2 7.4 %copy-start.4 = (s32[3,2]{0,1:T(2,128)S(1)}, s32[3,2]{0,1:T(2,128)}, u32[]{:S(2)}) copy-start(s32[3,2]{0,1:T(2,128)} %param.16) | copy-start | bytes 76
  47.2 7.4 %copy-start.5 = (s32[3]{0:T(128)S(1)}, s32[3]{0:T(128)}, u32[]{:S(2)}) copy-start(s32[3]{0:T(128)} %refs_4_.3) | copy-start | bytes 40

commit v15 on v11

--- a/solution.py
+++ b/solution.py
@@ -26,6 +26,7 @@
 MASKED = -1e30
 PIECES = 5
 STRIPS = 4
+WIDE = 2048
 LOG2E = 1.4426950408889634
 AHEAD = 2
 MIB = 1 << 20
@@ -119,8 +120,9 @@
         else:
             rows = pl.ds(pl.multiple_of(first + (k - 1) * size, 64), size)
         return [
-            pltpu.make_async_copy(q_out.at[rows], q_hbm.at[rows], out_sems.at[0, k]),
-            pltpu.make_async_copy(kv_out.at[rows], kv_hbm.at[rows], out_sems.at[1, k]),
+            pltpu.make_async_copy(q_out.at[rows], q_hbm.at[rows, pl.ds(0, cq)], out_sems.at[0, k]),
+            pltpu.make_async_copy(kv_out.at[rows], q_hbm.at[rows, pl.ds(cq, 2 * HD)], out_sems.at[1, k]),
+            pltpu.make_async_copy(kv_out.at[rows], kv_hbm.at[rows], out_sems.at[2, k]),
         ]
 
     def keep(total, rows):
@@ -209,7 +211,7 @@
         in_specs=[hbm] * 9,
         out_specs=[hbm, hbm, vmem, vmem],
         out_shape=[
-            jax.ShapeDtypeStruct((rows, cq), jnp.bfloat16),
+            jax.ShapeDtypeStruct((rows, WIDE), jnp.bfloat16),
             jax.ShapeDtypeStruct((rows, ckv), jnp.bfloat16),
             jax.ShapeDtypeStruct((n * GROUP_ROWS, cq + ckv), jnp.bfloat16),
             jax.ShapeDtypeStruct((n * GROUP_ROWS, cq + ckv), jnp.bfloat16),
@@ -222,7 +224,7 @@
             VMEM((rows, ckv), jnp.bfloat16),
             pltpu.SemaphoreType.DMA((count, STRIPS)),
             pltpu.SemaphoreType.DMA((4, PIECES)),
-            pltpu.SemaphoreType.DMA((2, count + 1)),
+            pltpu.SemaphoreType.DMA((3, count + 1)),
         ]
         + int_scratch(ints),
         compiler_params=pltpu.CompilerParams(vmem_limit_bytes=62 * MIB),
@@ -235,7 +237,7 @@
     )(*ints, dx, x, wq, wkv)
 
 
-def attend_prompt(lq, half, counts, q_hbm, kv_hbm, *refs):
+def attend_prompt(lq, half, counts, q_hbm, *refs):
     o_hbm, qs, kvs, outs, sems = refs[-5:]
     group = lax.axis_index("pool")
     c0, c1 = counts[group, 0], counts[group, 1]
@@ -247,8 +249,10 @@
         block = big + j if half == 0 else j + jnp.where(j >= big, MOST_BLOCKS, 0)
         rows = pl.ds(pl.multiple_of(block * BLOCK_TOKENS, BLOCK_TOKENS), strip * BLOCK_TOKENS)
         here = pl.ds(j * BLOCK_TOKENS, strip * BLOCK_TOKENS)
-        loads.append(pltpu.make_async_copy(kv_hbm.at[rows], kvs.at[here], sems.at[0, j]))
-        loads.append(pltpu.make_async_copy(q_hbm.at[rows], qs.at[here], sems.at[1, j]))
+        cq = lq * HD
+        keys_values, queries = q_hbm.at[rows, pl.ds(cq, 2 * HD)], q_hbm.at[rows, pl.ds(0, cq)]
+        loads.append(pltpu.make_async_copy(keys_values, kvs.at[here], sems.at[0, j]))
+        loads.append(pltpu.make_async_copy(queries, qs.at[here], sems.at[1, j]))
         stores.append(pltpu.make_async_copy(outs.at[here], o_hbm.at[rows], sems.at[2, j]))
     for copy in loads:
         copy.start()
@@ -302,14 +306,14 @@
         copy.wait()
 
 
-def prompt_attention(counts, q, kv, half, so_far=None):
-    rows, cq = q.shape
+def prompt_attention(counts, q, cq, half, so_far=None):
+    rows = q.shape[0]
     hbm = pl.BlockSpec(memory_space=pl.ANY)
     more = () if so_far is None else (so_far,)
     tokens = MOST_BLOCKS * BLOCK_TOKENS
     return pl.pallas_call(
         functools.partial(attend_prompt, cq // HD, half),
-        in_specs=[pl.BlockSpec(memory_space=SMEM), hbm, hbm] + [hbm] * len(more),
+        in_specs=[pl.BlockSpec(memory_space=SMEM), hbm] + [hbm] * len(more),
         out_specs=hbm,
         out_shape=jax.ShapeDtypeStruct((rows, cq), jnp.bfloat16),
         scratch_shapes=[
@@ -318,11 +322,11 @@
             VMEM((tokens, cq), jnp.bfloat16),
             pltpu.SemaphoreType.DMA((3, MOST_BLOCKS)),
         ],
-        input_output_aliases={3: 0} if more else {},
-        compiler_params=pltpu.CompilerParams(vmem_limit_bytes=62 * MIB),
+        input_output_aliases={2: 0} if more else {},
+        compiler_params=pltpu.CompilerParams(vmem_limit_bytes=(62 if half == 0 else 48) * MIB),
         cost_estimate=pl.CostEstimate(flops=2 * rows * rows * cq, bytes_accessed=4 * rows * cq, transcendentals=rows * rows // 2),
         name="long_prompt" if half == 0 else "short_prompts",
-    )(counts, q, kv, *more)
+    )(counts, q, *more)
 
 
 def row_head(n, lq, h, hh):
@@ -392,17 +396,11 @@
 
 
 def owner_part(n, lq, *refs):
-    cache_hbm, msgs, handed, o_ref, cache, sems, slot_row, slot_limit = refs[5:13]
-    counts, done, placed, table, lens, int_sems = refs[13:]
-    ints = int_copies(refs[:5], refs[13:18], int_sems)
+    cache, msgs, handed, o_ref, slot_row, slot_limit = refs[5:11]
+    counts, done, placed, table, lens, int_sems = refs[11:]
+    ints = int_copies(refs[:5], refs[11:16], int_sems)
     for copy in ints:
         copy.start()
-    loads = []
-    for slot in range(DEVICE_SLOTS):
-        part = pl.ds(slot * BLOCK_TOKENS, BLOCK_TOKENS)
-        loads.append(pltpu.make_async_copy(cache_hbm.at[part], cache.at[part], sems.at[slot]))
-    for load in loads:
-        load.start()
     held = msgs[...].astype(jnp.float32)
 
     def tile(t, k):
@@ -445,8 +443,6 @@
         for p in range(PAGES):
             slot_row[table[p, k]] = jnp.int32(k)
             slot_limit[table[p, k]] = jnp.where(found[k][p] < 0, lens[k] - p * BLOCK_TOKENS, 0)
-    for load in loads:
-        load.wait()
     scores = jnp.concatenate(
         [dot_t(rounded[h * span : (h + 1) * span], cache[:, 2 * h * HD : (2 * h + 1) * HD]) for h in range(KVH)],
         axis=0,
@@ -486,17 +482,15 @@
     rows = QH * GROUP_ROWS
     return pl.pallas_call(
         functools.partial(owner_part, n, lq),
-        in_specs=[hbm] * 6 + [vmem, vmem],
+        in_specs=[hbm] * 5 + [vmem] * 3,
         out_specs=vmem,
         out_shape=jax.ShapeDtypeStruct((ROWS_DEV, STEPS, QH * HD), jnp.bfloat16),
         scratch_shapes=[
-            VMEM(cache.shape, jnp.bfloat16),
-            pltpu.SemaphoreType.DMA((DEVICE_SLOTS,)),
             SMEM((DEVICE_SLOTS,), jnp.int32),
             SMEM((DEVICE_SLOTS,), jnp.int32),
         ]
         + int_scratch(ints),
-        compiler_params=pltpu.CompilerParams(vmem_limit_bytes=54 * MIB),
+        compiler_params=pltpu.CompilerParams(vmem_limit_bytes=40 * MIB),
         cost_estimate=pl.CostEstimate(flops=4 * rows * HD * 768, bytes_accessed=4 * MIB, transcendentals=rows * 768),
         name="decode_attention",
     )(*ints, cache, msgs, parts)
@@ -525,14 +519,14 @@
     placement = placement.transpose(0, 2, 1)
     page_table = page_table.transpose(1, 0)
     ints = (prompt_blocks, finished, placement, page_table, row_lens)
-    first, size = 512, 512
+    first, size = 256, 448
     q, kv, own, msgs = project_all(ints, dx, prompt_x, q_weight, kv_weight, n, first, size)
     kv_other = lax.ppermute(kv, "pool", [(0, 1), (1, 0)])
     msgs = lax.all_to_all(msgs, "tp", split_axis=0, concat_axis=0, tiled=True)
-    prompt_attn = prompt_attention(prompt_blocks, q, kv, 0)
+    prompt_attn = prompt_attention(prompt_blocks, q, q_weight.shape[1], 0)
     handed, prompt_attn = handed_attention(kv_other, own, msgs, prompt_attn, n, lq)
     parts = lax.all_to_all(handed, "tp", split_axis=0, concat_axis=0, tiled=True)
-    prompt_attn = prompt_attention(prompt_blocks, q, kv, 1, prompt_attn)
+    prompt_attn = prompt_attention(prompt_blocks, q, q_weight.shape[1], 1, prompt_attn)
     decode_attn = decode_attention(ints, cache, msgs, parts, n, lq)
     return prompt_attn, decode_attn.transpose(1, 0, 2)
 

time: 60.7 us -> 57.7 us (0.951)
  Pallas kernels: 45.1 us -> 43 us
  local copies, waits for them, and re-layouts: 0.65 us -> 0.04 us
    pallas_call x1, Pallas kernels: 4.77 us -> 2.61 us  [decode_attention(): pl.pallas_call(functools.partial(owner_part, n, lq), in_specs=[hbm] * 5 +...]
    unnamed x6 -> x14, local copies, waits for them, and re-layouts: 0.65 us -> 0.04 us
  transfers between devices with their start and end apart: 3 -> 3, of which waited for: 2 -> 2; matrix products, arithmetic and copies ran while one was open for 0% -> 0% of each run, Pallas kernels for 23% -> 24%
where the time goes in v15:
time: 57.7 us; the launch traced here: 57.4 us
  Pallas kernels  43 us (75%)
  starting transfers between devices  13.1 us (23%)
  between operations  0.89 us (2%)
    pallas_call x1, Pallas kernels, project_all(): pl.pallas_call(functools.partial(project, n, lq, first, size), grid=(1 +...  23.9 us
    pallas_call x2, Pallas kernels, prompt_attention(): pl.pallas_call(functools.partial(attend_prompt, cq // HD, half), in_specs...  14 us
    all_to_all x1, starting transfers between devices, local(): msgs = lax.all_to_all(msgs, 'tp', split_axis=0, concat_axis=0, tiled=True)  6.85 us
    all_to_all x1, starting transfers between devices, local(): lax.all_to_all(handed, 'tp', split_axis=0, concat_axis=0, tiled=True)  5.71 us
    pallas_call x1, Pallas kernels, decode_attention(): pl.pallas_call(functools.partial(owner_part, n, lq), in_specs=[hbm] * 5 +...  2.61 us
    pallas_call x1, Pallas kernels, handed_attention(): pl.pallas_call(functools.partial(handed_part, n, lq), in_specs=[vmem] * 3...  2.4 us
  transfers between devices with their start and end apart: 3, of which 2 were waited for; matrix products, arithmetic and copies ran while one was open for 0% of the time, Pallas kernels for 24%

profile of v15, /device:TPU:0, one launch (start us, length us, event | category | flops | bytes accessed | tf_op | source)
XLA Modules:
  0.0 57.4 jit_solution(4056259310786636092)
XLA Ops:
  0.6 23.9 %project.1 = (bf16[2048,2048]{1,0:T(8,128)(2,1)}, bf16[2048,256]{1,0:T(8,128)(2,1)}, bf16[64,768]{1,0:T(8,128)(2,1)}, bf16[64,768]{1,0:T(8,128)(2,1)}) custom-call(s32[2,3]{1,0:T(2,128)} %refs_0_.3, s32[2,3]{1,0:T(2,128)} %refs_1_.3, s32[2,2,16]{2,1,0:T(2,128)} %bitcast.10, s32[2,3]{1,0:T(2,128)} %bitcast.12, s32[3]{0:T(128)} %refs_4_.3, ...), custom_call_target="tpu_custom_call" | custom-call | flops 16106127360 | bytes 31981568 | tf_op jit(solution)/shard_map/project/pallas_call | solution.py:208
  24.6 0.5 collective-permute-start
  25.1 6.9 %all-to-all-start = ((bf16[8,8,768]{2,1,0:T(8,128)(2,1)}), bf16[8,8,768]{2,1,0:T(8,128)(2,1)S(1)}, u32[]{:S(2)}, u32[]{:S(2)}) async-start(bf16[8,8,768]{2,1,0:T(8,128)(2,1)} %bitcast.14), calls=%async_computation | async-start | bytes 196608 | tf_op jit(solution)/shard_map/all_to_all | solution.py:525
  31.9 0.0 copy-start.1
  31.9 6.8 %long_prompt.1._ = bf16[2048,512]{1,0:T(8,128)(2,1)} custom-call(s32[2,3]{1,0:T(2,128)} %refs_0_.3, bf16[2048,2048]{1,0:T(8,128)(2,1)} %get-tuple-element.8.q_hbm), custom_call_target="tpu_custom_call" | custom-call | flops 4294967296 | bytes 4194304 | tf_op jit(solution)/shard_map/long_prompt/pallas_call | solution.py:314
  38.8 0.0 copy-start.3
  38.8 0.3 all-to-all-done
  39.1 0.0 collective-permute-done.kv_ref
  39.1 0.0 copy-done.1
  39.1 2.4 %handed_attention.1 = (f32[8,32,128]{2,1,0:T(8,128)}, bf16[2048,512]{1,0:T(8,128)(2,1)}) custom-call(bf16[2048,256]{1,0:T(8,128)(2,1)S(1)} %collective-permute-done.kv_ref, bf16[64,768]{1,0:T(8,128)(2,1)S(1)} %copy-done.1, bf16[64,768]{1,0:T(8,128)(2,1)S(1)} %bitcast.8, bf16[2048,512]{1,0:T(8,128)(2,1)} %long_prompt.1._), custom_call_target="tpu_custom_call", output_to_operand_aliasing={{1}: (3, {})} | custom-call | flops 402653184 | bytes 2097152 | tf_op jit(solution)/shard_map/handed_attention/pallas_call | solution.py:383
  41.5 5.7 %all-to-all-start.1 = ((f32[8,32,128]{2,1,0:T(8,128)}), f32[8,32,128]{2,1,0:T(8,128)S(1)}, u32[]{:S(2)}, u32[]{:S(2)}) async-start(f32[8,32,128]{2,1,0:T(8,128)} %get-tuple-element.13), calls=%async_computation.1 | async-start | bytes 262144 | tf_op jit(solution)/shard_map/all_to_all | solution.py:528
  47.2 0.0 copy-done.3
  47.2 0.0 copy-start
  47.2 0.0 copy-start.2
  47.2 0.0 copy-start.4
  47.2 0.0 copy-start.5
  47.3 0.0 copy-start.6
  47.3 7.2 %short_prompts.1 = bf16[2048,512]{1,0:T(8,128)(2,1)} custom-call(s32[2,3]{1,0:T(2,128)S(1)} %copy-done.3, bf16[2048,2048]{1,0:T(8,128)(2,1)} %get-tuple-element.8.q_hbm, bf16[2048,512]{1,0:T(8,128)(2,1)} %get-tuple-element.12.refs_0_), custom_call_target="tpu_custom_call", output_to_operand_aliasing={{}: (2, {})} | custom-call | flops 4294967296 | bytes 4194304 | tf_op jit(solution)/shard_map/short_prompts/pallas_call | solution.py:314
  54.5 0.1 all-to-all-done.1.refs_7_
  54.6 0.0 copy-done
  54.6 0.0 copy-done.2
  54.6 0.0 copy-done.4
  54.6 0.0 copy-done.5
  54.6 0.0 copy-done.6
  54.6 2.6 %decode_attention.1 = bf16[3,2,4096]{2,1,0:T(2,128)(2,1)} custom-call(s32[2,3]{1,0:T(2,128)S(1)} %copy-done.3, s32[2,3]{1,0:T(2,128)S(1)} %copy-done.4, s32[2,2,16]{2,1,0:T(2,128)S(1)} %bitcast.11, s32[2,3]{1,0:T(2,128)S(1)} %bitcast.13, s32[3]{0:T(128)S(1)} %copy-done.6, bf16[768,2048]{1,0:T(8,128)(2,1)S(1)} %bitcast.7, bf16[64,768]{1,0:T(8,128)(2,1)S(1)} %bitcast.9, ...), custom_call_target="tpu_custom_call" | custom-call | flops 100663296 | bytes 4194304 | tf_op jit(solution)/shard_map/decode_attention/pallas_call | solution.py:483
Async XLA Ops:
  24.6 14.5 %collective-permute-start = (bf16[2048,256]{1,0:T(8,128)(2,1)}, bf16[2048,256]{1,0:T(8,128)(2,1)S(1)}, u32[]{:S(2)}, u32[]{:S(2)}) collective-permute-start(bf16[2048,256]{1,0:T(8,128)(2,1)} %get-tuple-element.9), channel_id=1, source_target_pairs={{0,8},{8,0},{1,9},{9,1},{2,10},{10,2},{3,11},{11,3},{4,12},{12,4},... | collective-permute-start | bytes 3145736 | tf_op jit(solution)/shard_map/ppermute | solution.py:524
  25.1 14.0 %all-to-all-start = ((bf16[8,8,768]{2,1,0:T(8,128)(2,1)}), bf16[8,8,768]{2,1,0:T(8,128)(2,1)S(1)}, u32[]{:S(2)}, u32[]{:S(2)}) async-start(bf16[8,8,768]{2,1,0:T(8,128)(2,1)} %bitcast.14), calls=%async_computation | async-start | bytes 196608 | tf_op jit(solution)/shard_map/all_to_all | solution.py:525
  31.9 7.2 %copy-start.1 = (bf16[64,768]{1,0:T(8,128)(2,1)S(1)}, bf16[64,768]{1,0:T(8,128)(2,1)}, u32[]{:S(2)}) copy-start(bf16[64,768]{1,0:T(8,128)(2,1)} %get-tuple-element.10.own_ref) | copy-start | bytes 294916
  38.8 8.5 %copy-start.3 = (s32[2,3]{1,0:T(2,128)S(1)}, s32[2,3]{1,0:T(2,128)}, u32[]{:S(2)}) copy-start(s32[2,3]{1,0:T(2,128)} %refs_0_.3) | copy-start | bytes 76
  41.5 13.1 %all-to-all-start.1 = ((f32[8,32,128]{2,1,0:T(8,128)}), f32[8,32,128]{2,1,0:T(8,128)S(1)}, u32[]{:S(2)}, u32[]{:S(2)}) async-start(f32[8,32,128]{2,1,0:T(8,128)} %get-tuple-element.13), calls=%async_computation.1 | async-start | bytes 262144 | tf_op jit(solution)/shard_map/all_to_all | solution.py:528
  47.2 7.3 %copy-start = (bf16[6,128,2048]{2,1,0:T(8,128)(2,1)S(1)}, bf16[6,128,2048]{2,1,0:T(8,128)(2,1)}, u32[]{:S(2)}) copy-start(bf16[6,128,2048]{2,1,0:T(8,128)(2,1)} %param.18) | copy-start | bytes 9437188
  47.2 7.3 %copy-start.2 = (s32[2,16,2]{1,2,0:T(2,128)S(1)}, s32[2,16,2]{1,2,0:T(2,128)}, u32[]{:S(2)}) copy-start(s32[2,16,2]{1,2,0:T(2,128)} %param.15) | copy-start | bytes 772
  47.2 7.3 %copy-start.4 = (s32[2,3]{1,0:T(2,128)S(1)}, s32[2,3]{1,0:T(2,128)}, u32[]{:S(2)}) copy-start(s32[2,3]{1,0:T(2,128)} %refs_1_.3) | copy-start | bytes 76
  47.2 7.3 %copy-start.5 = (s32[3,2]{0,1:T(2,128)S(1)}, s32[3,2]{0,1:T(2,128)}, u32[]{:S(2)}) copy-start(s32[3,2]{0,1:T(2,128)} %param.16) | copy-start | bytes 76
  47.3 7.3 %copy-start.6 = (s32[3]{0:T(128)S(1)}, s32[3]{0:T(128)}, u32[]{:S(2)}) copy-start(s32[3]{0:T(128)} %refs_4_.3) | copy-start | bytes 40

commit v16 on v15

--- a/solution.py
+++ b/solution.py
@@ -365,7 +365,8 @@
     near = raised.astype(jnp.bfloat16)
     rest = (raised - near.astype(jnp.float32)).astype(jnp.bfloat16)
     values = kv_ref[:, HD:]
-    mixed = (dot(near, values) + dot(rest, values)).reshape(lq * n, GROUP_ROWS, HD)
+    mixed = dot(jnp.concatenate([near, rest], axis=0), values)
+    mixed = (mixed[:rows] + mixed[rows:]).reshape(lq * n, GROUP_ROWS, HD)
 
     def line(col):
         spread = jnp.where(lane == rs, col, 0.0).reshape(lq * n, GROUP_ROWS, HD)
@@ -496,6 +497,23 @@
     )(*ints, cache, msgs, parts)
 
 
+def pass_on(*refs):
+    pass
+
+
+def hand_on(kv):
+    hbm = pl.BlockSpec(memory_space=pl.ANY)
+    return pl.pallas_call(
+        pass_on,
+        in_specs=[hbm],
+        out_specs=hbm,
+        out_shape=jax.ShapeDtypeStruct(kv.shape, kv.dtype),
+        input_output_aliases={0: 0},
+        compiler_params=pltpu.CompilerParams(vmem_limit_bytes=62 * MIB),
+        name="hand_on",
+    )(kv)
+
+
 def local(
     prompt_x,
     q_weight,
@@ -521,8 +539,8 @@
     ints = (prompt_blocks, finished, placement, page_table, row_lens)
     first, size = 256, 448
     q, kv, own, msgs = project_all(ints, dx, prompt_x, q_weight, kv_weight, n, first, size)
-    kv_other = lax.ppermute(kv, "pool", [(0, 1), (1, 0)])
     msgs = lax.all_to_all(msgs, "tp", split_axis=0, concat_axis=0, tiled=True)
+    kv_other = lax.ppermute(hand_on(kv), "pool", [(0, 1), (1, 0)])
     prompt_attn = prompt_attention(prompt_blocks, q, q_weight.shape[1], 0)
     handed, prompt_attn = handed_attention(kv_other, own, msgs, prompt_attn, n, lq)
     parts = lax.all_to_all(handed, "tp", split_axis=0, concat_axis=0, tiled=True)

time: 57.7 us -> 57.7 us (level)
  no operation moved by 1% of the time
where the time goes in v16:
time: 57.7 us; the launch traced here: 57.3 us
  Pallas kernels  42.9 us (74%)
  starting transfers between devices  13.1 us (23%)
  between operations  0.9 us (2%)
    pallas_call x1, Pallas kernels, project_all(): pl.pallas_call(functools.partial(project, n, lq, first, size), grid=(1 +...  23.9 us
    pallas_call x2, Pallas kernels, prompt_attention(): pl.pallas_call(functools.partial(attend_prompt, cq // HD, half), in_specs...  14 us
    all_to_all x1, starting transfers between devices, local(): msgs = lax.all_to_all(msgs, 'tp', split_axis=0, concat_axis=0, tiled=True)  6.85 us
    all_to_all x1, starting transfers between devices, local(): lax.all_to_all(handed, 'tp', split_axis=0, concat_axis=0, tiled=True)  5.69 us
    pallas_call x1, Pallas kernels, decode_attention(): pl.pallas_call(functools.partial(owner_part, n, lq), in_specs=[hbm] * 5 +...  2.62 us
    pallas_call x1, Pallas kernels, handed_attention(): pl.pallas_call(functools.partial(handed_part, n, lq), in_specs=[vmem] * 3...  2.36 us
  transfers between devices with their start and end apart: 3, of which 2 were waited for; matrix products, arithmetic and copies ran while one was open for 0% of the time, Pallas kernels for 24%

profile of v16, /device:TPU:0, one launch (start us, length us, event | category | flops | bytes accessed | tf_op | source)
XLA Modules:
  0.0 57.3 jit_solution(1201132022463534214)
XLA Ops:
  0.6 23.9 %project.1 = (bf16[2048,2048]{1,0:T(8,128)(2,1)}, bf16[2048,256]{1,0:T(8,128)(2,1)}, bf16[64,768]{1,0:T(8,128)(2,1)}, bf16[64,768]{1,0:T(8,128)(2,1)}) custom-call(s32[2,3]{1,0:T(2,128)} %refs_0_.3, s32[2,3]{1,0:T(2,128)} %refs_1_.3, s32[2,2,16]{2,1,0:T(2,128)} %bitcast.10, s32[2,3]{1,0:T(2,128)} %bitcast.12, s32[3]{0:T(128)} %refs_4_.3, ...), custom_call_target="tpu_custom_call" | custom-call | flops 16106127360 | bytes 31981568 | tf_op jit(solution)/shard_map/project/pallas_call | solution.py:208
  24.6 0.5 collective-permute-start
  25.1 6.9 %all-to-all-start = ((bf16[8,8,768]{2,1,0:T(8,128)(2,1)}), bf16[8,8,768]{2,1,0:T(8,128)(2,1)S(1)}, u32[]{:S(2)}, u32[]{:S(2)}) async-start(bf16[8,8,768]{2,1,0:T(8,128)(2,1)} %bitcast.14), calls=%async_computation | async-start | bytes 196608 | tf_op jit(solution)/shard_map/all_to_all | solution.py:542
  31.9 0.0 copy-start.1
  32.0 6.8 %long_prompt.1._ = bf16[2048,512]{1,0:T(8,128)(2,1)} custom-call(s32[2,3]{1,0:T(2,128)} %refs_0_.3, bf16[2048,2048]{1,0:T(8,128)(2,1)} %get-tuple-element.8.q_hbm), custom_call_target="tpu_custom_call" | custom-call | flops 4294967296 | bytes 4194304 | tf_op jit(solution)/shard_map/long_prompt/pallas_call | solution.py:314
  38.8 0.0 copy-start.3
  38.8 0.3 all-to-all-done
  39.1 0.0 collective-permute-done.kv_ref
  39.1 0.0 copy-done.1
  39.1 2.4 %handed_attention.1 = (f32[8,32,128]{2,1,0:T(8,128)}, bf16[2048,512]{1,0:T(8,128)(2,1)}) custom-call(bf16[2048,256]{1,0:T(8,128)(2,1)S(1)} %collective-permute-done.kv_ref, bf16[64,768]{1,0:T(8,128)(2,1)S(1)} %copy-done.1, bf16[64,768]{1,0:T(8,128)(2,1)S(1)} %bitcast.8, bf16[2048,512]{1,0:T(8,128)(2,1)} %long_prompt.1._), custom_call_target="tpu_custom_call", output_to_operand_aliasing={{1}: (3, {})} | custom-call | flops 402653184 | bytes 2097152 | tf_op jit(solution)/shard_map/handed_attention/pallas_call | solution.py:384
  41.5 5.7 %all-to-all-start.1 = ((f32[8,32,128]{2,1,0:T(8,128)}), f32[8,32,128]{2,1,0:T(8,128)S(1)}, u32[]{:S(2)}, u32[]{:S(2)}) async-start(f32[8,32,128]{2,1,0:T(8,128)} %get-tuple-element.13), calls=%async_computation.1 | async-start | bytes 262144 | tf_op jit(solution)/shard_map/all_to_all | solution.py:546
  47.2 0.0 copy-done.3
  47.2 0.0 copy-start
  47.2 0.0 copy-start.2
  47.2 0.0 copy-start.4
  47.2 0.0 copy-start.5
  47.2 0.0 copy-start.6
  47.2 7.2 %short_prompts.1 = bf16[2048,512]{1,0:T(8,128)(2,1)} custom-call(s32[2,3]{1,0:T(2,128)S(1)} %copy-done.3, bf16[2048,2048]{1,0:T(8,128)(2,1)} %get-tuple-element.8.q_hbm, bf16[2048,512]{1,0:T(8,128)(2,1)} %get-tuple-element.12.refs_0_), custom_call_target="tpu_custom_call", output_to_operand_aliasing={{}: (2, {})} | custom-call | flops 4294967296 | bytes 4194304 | tf_op jit(solution)/shard_map/short_prompts/pallas_call | solution.py:314
  54.4 0.1 all-to-all-done.1.refs_7_
  54.5 0.0 copy-done
  54.5 0.0 copy-done.2
  54.5 0.0 copy-done.4
  54.5 0.0 copy-done.5
  54.5 0.0 copy-done.6
  54.5 2.6 %decode_attention.1 = bf16[3,2,4096]{2,1,0:T(2,128)(2,1)} custom-call(s32[2,3]{1,0:T(2,128)S(1)} %copy-done.3, s32[2,3]{1,0:T(2,128)S(1)} %copy-done.4, s32[2,2,16]{2,1,0:T(2,128)S(1)} %bitcast.11, s32[2,3]{1,0:T(2,128)S(1)} %bitcast.13, s32[3]{0:T(128)S(1)} %copy-done.6, bf16[768,2048]{1,0:T(8,128)(2,1)S(1)} %bitcast.7, bf16[64,768]{1,0:T(8,128)(2,1)S(1)} %bitcast.9, ...), custom_call_target="tpu_custom_call" | custom-call | flops 100663296 | bytes 4194304 | tf_op jit(solution)/shard_map/decode_attention/pallas_call | solution.py:484
  (1 shorter events, 0.0 us)
Async XLA Ops:
  24.6 14.5 %collective-permute-start = (bf16[2048,256]{1,0:T(8,128)(2,1)}, bf16[2048,256]{1,0:T(8,128)(2,1)S(1)}, u32[]{:S(2)}, u32[]{:S(2)}) collective-permute-start(bf16[2048,256]{1,0:T(8,128)(2,1)} %hand_on.1), channel_id=1, source_target_pairs={{0,8},{8,0},{1,9},{9,1},{2,10},{10,2},{3,11},{11,3},{4,12},{12,4},... | collective-permute-start | bytes 3145736 | tf_op jit(solution)/shard_map/ppermute | solution.py:543
  25.1 14.0 %all-to-all-start = ((bf16[8,8,768]{2,1,0:T(8,128)(2,1)}), bf16[8,8,768]{2,1,0:T(8,128)(2,1)S(1)}, u32[]{:S(2)}, u32[]{:S(2)}) async-start(bf16[8,8,768]{2,1,0:T(8,128)(2,1)} %bitcast.14), calls=%async_computation | async-start | bytes 196608 | tf_op jit(solution)/shard_map/all_to_all | solution.py:542
  31.9 7.2 %copy-start.1 = (bf16[64,768]{1,0:T(8,128)(2,1)S(1)}, bf16[64,768]{1,0:T(8,128)(2,1)}, u32[]{:S(2)}) copy-start(bf16[64,768]{1,0:T(8,128)(2,1)} %get-tuple-element.10.own_ref) | copy-start | bytes 294916
  38.8 8.4 %copy-start.3 = (s32[2,3]{1,0:T(2,128)S(1)}, s32[2,3]{1,0:T(2,128)}, u32[]{:S(2)}) copy-start(s32[2,3]{1,0:T(2,128)} %refs_0_.3) | copy-start | bytes 76
  41.5 13.0 %all-to-all-start.1 = ((f32[8,32,128]{2,1,0:T(8,128)}), f32[8,32,128]{2,1,0:T(8,128)S(1)}, u32[]{:S(2)}, u32[]{:S(2)}) async-start(f32[8,32,128]{2,1,0:T(8,128)} %get-tuple-element.13), calls=%async_computation.1 | async-start | bytes 262144 | tf_op jit(solution)/shard_map/all_to_all | solution.py:546
  47.2 7.3 %copy-start = (bf16[6,128,2048]{2,1,0:T(8,128)(2,1)S(1)}, bf16[6,128,2048]{2,1,0:T(8,128)(2,1)}, u32[]{:S(2)}) copy-start(bf16[6,128,2048]{2,1,0:T(8,128)(2,1)} %param.18) | copy-start | bytes 9437188
  47.2 7.3 %copy-start.2 = (s32[2,16,2]{1,2,0:T(2,128)S(1)}, s32[2,16,2]{1,2,0:T(2,128)}, u32[]{:S(2)}) copy-start(s32[2,16,2]{1,2,0:T(2,128)} %param.15) | copy-start | bytes 772
  47.2 7.3 %copy-start.4 = (s32[2,3]{1,0:T(2,128)S(1)}, s32[2,3]{1,0:T(2,128)}, u32[]{:S(2)}) copy-start(s32[2,3]{1,0:T(2,128)} %refs_1_.3) | copy-start | bytes 76
  47.2 7.3 %copy-start.5 = (s32[3,2]{0,1:T(2,128)S(1)}, s32[3,2]{0,1:T(2,128)}, u32[]{:S(2)}) copy-start(s32[3,2]{0,1:T(2,128)} %param.16) | copy-start | bytes 76
  47.2 7.3 %copy-start.6 = (s32[3]{0:T(128)S(1)}, s32[3]{0:T(128)}, u32[]{:S(2)}) copy-start(s32[3]{0:T(128)} %refs_4_.3) | copy-start | bytes 40

commit v17 on v15

--- a/solution.py
+++ b/solution.py
@@ -24,7 +24,8 @@
 KEY_VALUE_COLUMNS = 2048
 SCALE = HD ** (-0.5)
 MASKED = -1e30
-PIECES = 5
+CUTS = (0, 1, 4, 8, 12, 16, 20)
+PIECES = len(CUTS) - 1
 STRIPS = 4
 WIDE = 2048
 LOG2E = 1.4426950408889634
@@ -91,12 +92,12 @@
     depth = w.shape[0]
     count = xs.shape[0]
     cq = lq * HD
-    piece = depth // PIECES
+    cuts = [cut * depth // CUTS[-1] for cut in CUTS]
     own_rows = dx_hbm.shape[0]
     step = pl.program_id(0)
 
     def piece_copies(c):
-        part = pl.ds(c * piece, piece)
+        part = pl.ds(cuts[c], cuts[c + 1] - cuts[c])
         return [
             pltpu.make_async_copy(x_hbm.at[pl.ds(0, first), part], x0.at[pl.ds(0, first), part], w_sems.at[0, c]),
             pltpu.make_async_copy(dx_hbm.at[:, part], x0.at[pl.ds(first, own_rows), part], w_sems.at[1, c]),
@@ -146,7 +147,7 @@
             if c + AHEAD >= PIECES:
                 for copy in x_copies(c + AHEAD - PIECES):
                     copy.start()
-            part = slice(c * piece, (c + 1) * piece)
+            part = slice(cuts[c], cuts[c + 1])
             total += dot(x0[:, part], w[part, :])
         keep(total[:first], pl.ds(0, first))
         for copy in out_copies(0):

time: 57.7 us -> 58 us (level)
  no operation moved by 1% of the time
where the time goes in v17:
time: 58 us; the launch traced here: 57.6 us
  Pallas kernels  43.2 us (74%)
  starting transfers between devices  13.1 us (23%)
  between operations  0.89 us (2%)
    pallas_call x1, Pallas kernels, project_all(): pl.pallas_call(functools.partial(project, n, lq, first, size), grid=(1 +...  24.2 us
    pallas_call x2, Pallas kernels, prompt_attention(): pl.pallas_call(functools.partial(attend_prompt, cq // HD, half), in_specs...  14 us
    all_to_all x1, starting transfers between devices, local(): msgs = lax.all_to_all(msgs, 'tp', split_axis=0, concat_axis=0, tiled=True)  6.85 us
    all_to_all x1, starting transfers between devices, local(): lax.all_to_all(handed, 'tp', split_axis=0, concat_axis=0, tiled=True)  5.7 us
    pallas_call x1, Pallas kernels, decode_attention(): pl.pallas_call(functools.partial(owner_part, n, lq), in_specs=[hbm] * 5 +...  2.61 us
    pallas_call x1, Pallas kernels, handed_attention(): pl.pallas_call(functools.partial(handed_part, n, lq), in_specs=[vmem] * 3...  2.4 us
  transfers between devices with their start and end apart: 3, of which 2 were waited for; matrix products, arithmetic and copies ran while one was open for 0% of the time, Pallas kernels for 24%

profile of v17, /device:TPU:0, one launch (start us, length us, event | category | flops | bytes accessed | tf_op | source)
XLA Modules:
  0.0 57.6 jit_solution(6250900330838634039)
XLA Ops:
  0.6 24.2 %project.1 = (bf16[2048,2048]{1,0:T(8,128)(2,1)}, bf16[2048,256]{1,0:T(8,128)(2,1)}, bf16[64,768]{1,0:T(8,128)(2,1)}, bf16[64,768]{1,0:T(8,128)(2,1)}) custom-call(s32[2,3]{1,0:T(2,128)} %refs_0_.3, s32[2,3]{1,0:T(2,128)} %refs_1_.3, s32[2,2,16]{2,1,0:T(2,128)} %bitcast.10, s32[2,3]{1,0:T(2,128)} %bitcast.12, s32[3]{0:T(128)} %refs_4_.3, ...), custom_call_target="tpu_custom_call" | custom-call | flops 16106127360 | bytes 31981568 | tf_op jit(solution)/shard_map/project/pallas_call | solution.py:209
  24.8 0.5 collective-permute-start
  25.3 6.9 %all-to-all-start = ((bf16[8,8,768]{2,1,0:T(8,128)(2,1)}), bf16[8,8,768]{2,1,0:T(8,128)(2,1)S(1)}, u32[]{:S(2)}, u32[]{:S(2)}) async-start(bf16[8,8,768]{2,1,0:T(8,128)(2,1)} %bitcast.14), calls=%async_computation | async-start | bytes 196608 | tf_op jit(solution)/shard_map/all_to_all | solution.py:526
  32.2 0.0 copy-start.1
  32.2 6.8 %long_prompt.1._ = bf16[2048,512]{1,0:T(8,128)(2,1)} custom-call(s32[2,3]{1,0:T(2,128)} %refs_0_.3, bf16[2048,2048]{1,0:T(8,128)(2,1)} %get-tuple-element.8.q_hbm), custom_call_target="tpu_custom_call" | custom-call | flops 4294967296 | bytes 4194304 | tf_op jit(solution)/shard_map/long_prompt/pallas_call | solution.py:315
  39.0 0.0 copy-start.3
  39.0 0.3 all-to-all-done
  39.3 0.0 collective-permute-done.kv_ref
  39.3 0.0 copy-done.1
  39.3 2.4 %handed_attention.1 = (f32[8,32,128]{2,1,0:T(8,128)}, bf16[2048,512]{1,0:T(8,128)(2,1)}) custom-call(bf16[2048,256]{1,0:T(8,128)(2,1)S(1)} %collective-permute-done.kv_ref, bf16[64,768]{1,0:T(8,128)(2,1)S(1)} %copy-done.1, bf16[64,768]{1,0:T(8,128)(2,1)S(1)} %bitcast.8, bf16[2048,512]{1,0:T(8,128)(2,1)} %long_prompt.1._), custom_call_target="tpu_custom_call", output_to_operand_aliasing={{1}: (3, {})} | custom-call | flops 402653184 | bytes 2097152 | tf_op jit(solution)/shard_map/handed_attention/pallas_call | solution.py:384
  41.7 5.7 %all-to-all-start.1 = ((f32[8,32,128]{2,1,0:T(8,128)}), f32[8,32,128]{2,1,0:T(8,128)S(1)}, u32[]{:S(2)}, u32[]{:S(2)}) async-start(f32[8,32,128]{2,1,0:T(8,128)} %get-tuple-element.13), calls=%async_computation.1 | async-start | bytes 262144 | tf_op jit(solution)/shard_map/all_to_all | solution.py:529
  47.4 0.0 copy-done.3
  47.4 0.0 copy-start
  47.5 0.0 copy-start.2
  47.5 0.0 copy-start.4
  47.5 0.0 copy-start.5
  47.5 0.0 copy-start.6
  47.5 7.2 %short_prompts.1 = bf16[2048,512]{1,0:T(8,128)(2,1)} custom-call(s32[2,3]{1,0:T(2,128)S(1)} %copy-done.3, bf16[2048,2048]{1,0:T(8,128)(2,1)} %get-tuple-element.8.q_hbm, bf16[2048,512]{1,0:T(8,128)(2,1)} %get-tuple-element.12.refs_0_), custom_call_target="tpu_custom_call", output_to_operand_aliasing={{}: (2, {})} | custom-call | flops 4294967296 | bytes 4194304 | tf_op jit(solution)/shard_map/short_prompts/pallas_call | solution.py:315
  54.7 0.1 all-to-all-done.1.refs_7_
  54.8 0.0 copy-done
  54.8 0.0 copy-done.2
  54.8 0.0 copy-done.4
  54.8 0.0 copy-done.5
  54.8 0.0 copy-done.6
  54.8 2.6 %decode_attention.1 = bf16[3,2,4096]{2,1,0:T(2,128)(2,1)} custom-call(s32[2,3]{1,0:T(2,128)S(1)} %copy-done.3, s32[2,3]{1,0:T(2,128)S(1)} %copy-done.4, s32[2,2,16]{2,1,0:T(2,128)S(1)} %bitcast.11, s32[2,3]{1,0:T(2,128)S(1)} %bitcast.13, s32[3]{0:T(128)S(1)} %copy-done.6, bf16[768,2048]{1,0:T(8,128)(2,1)S(1)} %bitcast.7, bf16[64,768]{1,0:T(8,128)(2,1)S(1)} %bitcast.9, ...), custom_call_target="tpu_custom_call" | custom-call | flops 100663296 | bytes 4194304 | tf_op jit(solution)/shard_map/decode_attention/pallas_call | solution.py:484
Async XLA Ops:
  24.8 14.5 %collective-permute-start = (bf16[2048,256]{1,0:T(8,128)(2,1)}, bf16[2048,256]{1,0:T(8,128)(2,1)S(1)}, u32[]{:S(2)}, u32[]{:S(2)}) collective-permute-start(bf16[2048,256]{1,0:T(8,128)(2,1)} %get-tuple-element.9), channel_id=1, source_target_pairs={{0,8},{8,0},{1,9},{9,1},{2,10},{10,2},{3,11},{11,3},{4,12},{12,4},... | collective-permute-start | bytes 3145736 | tf_op jit(solution)/shard_map/ppermute | solution.py:525
  25.3 14.0 %all-to-all-start = ((bf16[8,8,768]{2,1,0:T(8,128)(2,1)}), bf16[8,8,768]{2,1,0:T(8,128)(2,1)S(1)}, u32[]{:S(2)}, u32[]{:S(2)}) async-start(bf16[8,8,768]{2,1,0:T(8,128)(2,1)} %bitcast.14), calls=%async_computation | async-start | bytes 196608 | tf_op jit(solution)/shard_map/all_to_all | solution.py:526
  32.2 7.2 %copy-start.1 = (bf16[64,768]{1,0:T(8,128)(2,1)S(1)}, bf16[64,768]{1,0:T(8,128)(2,1)}, u32[]{:S(2)}) copy-start(bf16[64,768]{1,0:T(8,128)(2,1)} %get-tuple-element.10.own_ref) | copy-start | bytes 294916
  39.0 8.4 %copy-start.3 = (s32[2,3]{1,0:T(2,128)S(1)}, s32[2,3]{1,0:T(2,128)}, u32[]{:S(2)}) copy-start(s32[2,3]{1,0:T(2,128)} %refs_0_.3) | copy-start | bytes 76
  41.7 13.0 %all-to-all-start.1 = ((f32[8,32,128]{2,1,0:T(8,128)}), f32[8,32,128]{2,1,0:T(8,128)S(1)}, u32[]{:S(2)}, u32[]{:S(2)}) async-start(f32[8,32,128]{2,1,0:T(8,128)} %get-tuple-element.13), calls=%async_computation.1 | async-start | bytes 262144 | tf_op jit(solution)/shard_map/all_to_all | solution.py:529
  47.4 7.3 %copy-start = (bf16[6,128,2048]{2,1,0:T(8,128)(2,1)S(1)}, bf16[6,128,2048]{2,1,0:T(8,128)(2,1)}, u32[]{:S(2)}) copy-start(bf16[6,128,2048]{2,1,0:T(8,128)(2,1)} %param.18) | copy-start | bytes 9437188
  47.5 7.3 %copy-start.2 = (s32[2,16,2]{1,2,0:T(2,128)S(1)}, s32[2,16,2]{1,2,0:T(2,128)}, u32[]{:S(2)}) copy-start(s32[2,16,2]{1,2,0:T(2,128)} %param.15) | copy-start | bytes 772
  47.5 7.3 %copy-start.4 = (s32[2,3]{1,0:T(2,128)S(1)}, s32[2,3]{1,0:T(2,128)}, u32[]{:S(2)}) copy-start(s32[2,3]{1,0:T(2,128)} %refs_1_.3) | copy-start | bytes 76
  47.5 7.3 %copy-start.5 = (s32[3,2]{0,1:T(2,128)S(1)}, s32[3,2]{0,1:T(2,128)}, u32[]{:S(2)}) copy-start(s32[3,2]{0,1:T(2,128)} %param.16) | copy-start | bytes 76
  47.5 7.3 %copy-start.6 = (s32[3]{0:T(128)S(1)}, s32[3]{0:T(128)}, u32[]{:S(2)}) copy-start(s32[3]{0:T(128)} %refs_4_.3) | copy-start | bytes 40

commit v18 on v15

--- a/solution.py
+++ b/solution.py
@@ -28,7 +28,7 @@
 STRIPS = 4
 WIDE = 2048
 LOG2E = 1.4426950408889634
-AHEAD = 2
+AHEAD = 3
 MIB = 1 << 20
 VMEM = pltpu.VMEM
 SMEM = pltpu.SMEM

time: 57.7 us -> 57.1 us (0.990)
  Pallas kernels: 43 us -> 42.4 us
    pallas_call x1, Pallas kernels: 23.9 us -> 23.3 us  [project_all(): pl.pallas_call(functools.partial(project, n, lq, first, size), grid=(1 +...]
  transfers between devices with their start and end apart: 3 -> 3, of which waited for: 2 -> 2; matrix products, arithmetic and copies ran while one was open for 0% -> 0% of each run, Pallas kernels for 24% -> 25%
where the time goes in v18:
time: 57.1 us; the launch traced here: 56.8 us
  Pallas kernels  42.4 us (74%)
  starting transfers between devices  13.1 us (23%)
  between operations  0.89 us (2%)
    pallas_call x1, Pallas kernels, project_all(): pl.pallas_call(functools.partial(project, n, lq, first, size), grid=(1 +...  23.3 us
    pallas_call x2, Pallas kernels, prompt_attention(): pl.pallas_call(functools.partial(attend_prompt, cq // HD, half), in_specs...  14 us
    all_to_all x1, starting transfers between devices, local(): msgs = lax.all_to_all(msgs, 'tp', split_axis=0, concat_axis=0, tiled=True)  6.85 us
    all_to_all x1, starting transfers between devices, local(): lax.all_to_all(handed, 'tp', split_axis=0, concat_axis=0, tiled=True)  5.7 us
    pallas_call x1, Pallas kernels, decode_attention(): pl.pallas_call(functools.partial(owner_part, n, lq), in_specs=[hbm] * 5 +...  2.61 us
    pallas_call x1, Pallas kernels, handed_attention(): pl.pallas_call(functools.partial(handed_part, n, lq), in_specs=[vmem] * 3...  2.4 us
  transfers between devices with their start and end apart: 3, of which 2 were waited for; matrix products, arithmetic and copies ran while one was open for 0% of the time, Pallas kernels for 25%

profile of v18, /device:TPU:0, one launch (start us, length us, event | category | flops | bytes accessed | tf_op | source)
XLA Modules:
  0.0 56.8 jit_solution(14070893036145263309)
XLA Ops:
  0.6 23.3 %project.1 = (bf16[2048,2048]{1,0:T(8,128)(2,1)}, bf16[2048,256]{1,0:T(8,128)(2,1)}, bf16[64,768]{1,0:T(8,128)(2,1)}, bf16[64,768]{1,0:T(8,128)(2,1)}) custom-call(s32[2,3]{1,0:T(2,128)} %refs_0_.3, s32[2,3]{1,0:T(2,128)} %refs_1_.3, s32[2,2,16]{2,1,0:T(2,128)} %bitcast.10, s32[2,3]{1,0:T(2,128)} %bitcast.12, s32[3]{0:T(128)} %refs_4_.3, ...), custom_call_target="tpu_custom_call" | custom-call | flops 16106127360 | bytes 31981568 | tf_op jit(solution)/shard_map/project/pallas_call | solution.py:208
  24.0 0.5 collective-permute-start
  24.5 6.9 %all-to-all-start = ((bf16[8,8,768]{2,1,0:T(8,128)(2,1)}), bf16[8,8,768]{2,1,0:T(8,128)(2,1)S(1)}, u32[]{:S(2)}, u32[]{:S(2)}) async-start(bf16[8,8,768]{2,1,0:T(8,128)(2,1)} %bitcast.14), calls=%async_computation | async-start | bytes 196608 | tf_op jit(solution)/shard_map/all_to_all | solution.py:525
  31.3 0.0 copy-start.1
  31.4 6.8 %long_prompt.1._ = bf16[2048,512]{1,0:T(8,128)(2,1)} custom-call(s32[2,3]{1,0:T(2,128)} %refs_0_.3, bf16[2048,2048]{1,0:T(8,128)(2,1)} %get-tuple-element.8.q_hbm), custom_call_target="tpu_custom_call" | custom-call | flops 4294967296 | bytes 4194304 | tf_op jit(solution)/shard_map/long_prompt/pallas_call | solution.py:314
  38.2 0.0 copy-start.3
  38.2 0.3 all-to-all-done
  38.5 0.0 collective-permute-done.kv_ref
  38.5 0.0 copy-done.1
  38.5 2.4 %handed_attention.1 = (f32[8,32,128]{2,1,0:T(8,128)}, bf16[2048,512]{1,0:T(8,128)(2,1)}) custom-call(bf16[2048,256]{1,0:T(8,128)(2,1)S(1)} %collective-permute-done.kv_ref, bf16[64,768]{1,0:T(8,128)(2,1)S(1)} %copy-done.1, bf16[64,768]{1,0:T(8,128)(2,1)S(1)} %bitcast.8, bf16[2048,512]{1,0:T(8,128)(2,1)} %long_prompt.1._), custom_call_target="tpu_custom_call", output_to_operand_aliasing={{1}: (3, {})} | custom-call | flops 402653184 | bytes 2097152 | tf_op jit(solution)/shard_map/handed_attention/pallas_call | solution.py:383
  40.9 5.7 %all-to-all-start.1 = ((f32[8,32,128]{2,1,0:T(8,128)}), f32[8,32,128]{2,1,0:T(8,128)S(1)}, u32[]{:S(2)}, u32[]{:S(2)}) async-start(f32[8,32,128]{2,1,0:T(8,128)} %get-tuple-element.13), calls=%async_computation.1 | async-start | bytes 262144 | tf_op jit(solution)/shard_map/all_to_all | solution.py:528
  46.6 0.0 copy-done.3
  46.6 0.0 copy-start
  46.6 0.0 copy-start.2
  46.6 0.0 copy-start.4
  46.6 0.0 copy-start.5
  46.7 0.0 copy-start.6
  46.7 7.2 %short_prompts.1 = bf16[2048,512]{1,0:T(8,128)(2,1)} custom-call(s32[2,3]{1,0:T(2,128)S(1)} %copy-done.3, bf16[2048,2048]{1,0:T(8,128)(2,1)} %get-tuple-element.8.q_hbm, bf16[2048,512]{1,0:T(8,128)(2,1)} %get-tuple-element.12.refs_0_), custom_call_target="tpu_custom_call", output_to_operand_aliasing={{}: (2, {})} | custom-call | flops 4294967296 | bytes 4194304 | tf_op jit(solution)/shard_map/short_prompts/pallas_call | solution.py:314
  53.9 0.1 all-to-all-done.1.refs_7_
  53.9 0.0 copy-done
  53.9 0.0 copy-done.2
  53.9 0.0 copy-done.4
  54.0 0.0 copy-done.5
  54.0 0.0 copy-done.6
  54.0 2.6 %decode_attention.1 = bf16[3,2,4096]{2,1,0:T(2,128)(2,1)} custom-call(s32[2,3]{1,0:T(2,128)S(1)} %copy-done.3, s32[2,3]{1,0:T(2,128)S(1)} %copy-done.4, s32[2,2,16]{2,1,0:T(2,128)S(1)} %bitcast.11, s32[2,3]{1,0:T(2,128)S(1)} %bitcast.13, s32[3]{0:T(128)S(1)} %copy-done.6, bf16[768,2048]{1,0:T(8,128)(2,1)S(1)} %bitcast.7, bf16[64,768]{1,0:T(8,128)(2,1)S(1)} %bitcast.9, ...), custom_call_target="tpu_custom_call" | custom-call | flops 100663296 | bytes 4194304 | tf_op jit(solution)/shard_map/decode_attention/pallas_call | solution.py:483
Async XLA Ops:
  24.0 14.5 %collective-permute-start = (bf16[2048,256]{1,0:T(8,128)(2,1)}, bf16[2048,256]{1,0:T(8,128)(2,1)S(1)}, u32[]{:S(2)}, u32[]{:S(2)}) collective-permute-start(bf16[2048,256]{1,0:T(8,128)(2,1)} %get-tuple-element.9), channel_id=1, source_target_pairs={{0,8},{8,0},{1,9},{9,1},{2,10},{10,2},{3,11},{11,3},{4,12},{12,4},... | collective-permute-start | bytes 3145736 | tf_op jit(solution)/shard_map/ppermute | solution.py:524
  24.5 14.0 %all-to-all-start = ((bf16[8,8,768]{2,1,0:T(8,128)(2,1)}), bf16[8,8,768]{2,1,0:T(8,128)(2,1)S(1)}, u32[]{:S(2)}, u32[]{:S(2)}) async-start(bf16[8,8,768]{2,1,0:T(8,128)(2,1)} %bitcast.14), calls=%async_computation | async-start | bytes 196608 | tf_op jit(solution)/shard_map/all_to_all | solution.py:525
  31.3 7.2 %copy-start.1 = (bf16[64,768]{1,0:T(8,128)(2,1)S(1)}, bf16[64,768]{1,0:T(8,128)(2,1)}, u32[]{:S(2)}) copy-start(bf16[64,768]{1,0:T(8,128)(2,1)} %get-tuple-element.10.own_ref) | copy-start | bytes 294916
  38.2 8.4 %copy-start.3 = (s32[2,3]{1,0:T(2,128)S(1)}, s32[2,3]{1,0:T(2,128)}, u32[]{:S(2)}) copy-start(s32[2,3]{1,0:T(2,128)} %refs_0_.3) | copy-start | bytes 76
  40.9 13.0 %all-to-all-start.1 = ((f32[8,32,128]{2,1,0:T(8,128)}), f32[8,32,128]{2,1,0:T(8,128)S(1)}, u32[]{:S(2)}, u32[]{:S(2)}) async-start(f32[8,32,128]{2,1,0:T(8,128)} %get-tuple-element.13), calls=%async_computation.1 | async-start | bytes 262144 | tf_op jit(solution)/shard_map/all_to_all | solution.py:528
  46.6 7.3 %copy-start = (bf16[6,128,2048]{2,1,0:T(8,128)(2,1)S(1)}, bf16[6,128,2048]{2,1,0:T(8,128)(2,1)}, u32[]{:S(2)}) copy-start(bf16[6,128,2048]{2,1,0:T(8,128)(2,1)} %param.18) | copy-start | bytes 9437188
  46.6 7.3 %copy-start.2 = (s32[2,16,2]{1,2,0:T(2,128)S(1)}, s32[2,16,2]{1,2,0:T(2,128)}, u32[]{:S(2)}) copy-start(s32[2,16,2]{1,2,0:T(2,128)} %param.15) | copy-start | bytes 772
  46.6 7.3 %copy-start.4 = (s32[2,3]{1,0:T(2,128)S(1)}, s32[2,3]{1,0:T(2,128)}, u32[]{:S(2)}) copy-start(s32[2,3]{1,0:T(2,128)} %refs_1_.3) | copy-start | bytes 76
  46.6 7.3 %copy-start.5 = (s32[3,2]{0,1:T(2,128)S(1)}, s32[3,2]{0,1:T(2,128)}, u32[]{:S(2)}) copy-start(s32[3,2]{0,1:T(2,128)} %param.16) | copy-start | bytes 76
  46.7 7.3 %copy-start.6 = (s32[3]{0:T(128)S(1)}, s32[3]{0:T(128)}, u32[]{:S(2)}) copy-start(s32[3]{0:T(128)} %refs_4_.3) | copy-start | bytes 40

commit v19 on v18

--- a/solution.py
+++ b/solution.py
@@ -28,7 +28,7 @@
 STRIPS = 4
 WIDE = 2048
 LOG2E = 1.4426950408889634
-AHEAD = 3
+AHEAD = 4
 MIB = 1 << 20
 VMEM = pltpu.VMEM
 SMEM = pltpu.SMEM
@@ -365,7 +365,8 @@
     near = raised.astype(jnp.bfloat16)
     rest = (raised - near.astype(jnp.float32)).astype(jnp.bfloat16)
     values = kv_ref[:, HD:]
-    mixed = (dot(near, values) + dot(rest, values)).reshape(lq * n, GROUP_ROWS, HD)
+    mixed = dot(jnp.concatenate([near, rest], axis=0), values)
+    mixed = (mixed[:rows] + mixed[rows:]).reshape(lq * n, GROUP_ROWS, HD)
 
     def line(col):
         spread = jnp.where(lane == rs, col, 0.0).reshape(lq * n, GROUP_ROWS, HD)

time: 57.1 us -> 57.1 us (level)
  no operation moved by 1% of the time
where the time goes in v19:
time: 57.1 us; the launch traced here: 56.7 us
  Pallas kernels  42.3 us (74%)
  starting transfers between devices  13.1 us (23%)
  between operations  0.89 us (2%)
    pallas_call x1, Pallas kernels, project_all(): pl.pallas_call(functools.partial(project, n, lq, first, size), grid=(1 +...  23.3 us
    pallas_call x2, Pallas kernels, prompt_attention(): pl.pallas_call(functools.partial(attend_prompt, cq // HD, half), in_specs...  14 us
    all_to_all x1, starting transfers between devices, local(): msgs = lax.all_to_all(msgs, 'tp', split_axis=0, concat_axis=0, tiled=True)  6.85 us
    all_to_all x1, starting transfers between devices, local(): lax.all_to_all(handed, 'tp', split_axis=0, concat_axis=0, tiled=True)  5.68 us
    pallas_call x1, Pallas kernels, decode_attention(): pl.pallas_call(functools.partial(owner_part, n, lq), in_specs=[hbm] * 5 +...  2.62 us
    pallas_call x1, Pallas kernels, handed_attention(): pl.pallas_call(functools.partial(handed_part, n, lq), in_specs=[vmem] * 3...  2.37 us
  transfers between devices with their start and end apart: 3, of which 2 were waited for; matrix products, arithmetic and copies ran while one was open for 0% of the time, Pallas kernels for 25%

profile of v19, /device:TPU:0, one launch (start us, length us, event | category | flops | bytes accessed | tf_op | source)
XLA Modules:
  0.0 56.7 jit_solution(3141841861664151842)
XLA Ops:
  0.6 23.3 %project.1 = (bf16[2048,2048]{1,0:T(8,128)(2,1)}, bf16[2048,256]{1,0:T(8,128)(2,1)}, bf16[64,768]{1,0:T(8,128)(2,1)}, bf16[64,768]{1,0:T(8,128)(2,1)}) custom-call(s32[2,3]{1,0:T(2,128)} %refs_0_.3, s32[2,3]{1,0:T(2,128)} %refs_1_.3, s32[2,2,16]{2,1,0:T(2,128)} %bitcast.10, s32[2,3]{1,0:T(2,128)} %bitcast.12, s32[3]{0:T(128)} %refs_4_.3, ...), custom_call_target="tpu_custom_call" | custom-call | flops 16106127360 | bytes 31981568 | tf_op jit(solution)/shard_map/project/pallas_call | solution.py:208
  24.0 0.5 collective-permute-start
  24.5 6.9 %all-to-all-start = ((bf16[8,8,768]{2,1,0:T(8,128)(2,1)}), bf16[8,8,768]{2,1,0:T(8,128)(2,1)S(1)}, u32[]{:S(2)}, u32[]{:S(2)}) async-start(bf16[8,8,768]{2,1,0:T(8,128)(2,1)} %bitcast.14), calls=%async_computation | async-start | bytes 196608 | tf_op jit(solution)/shard_map/all_to_all | solution.py:526
  31.3 0.0 copy-start.1
  31.3 6.8 %long_prompt.1._ = bf16[2048,512]{1,0:T(8,128)(2,1)} custom-call(s32[2,3]{1,0:T(2,128)} %refs_0_.3, bf16[2048,2048]{1,0:T(8,128)(2,1)} %get-tuple-element.8.q_hbm), custom_call_target="tpu_custom_call" | custom-call | flops 4294967296 | bytes 4194304 | tf_op jit(solution)/shard_map/long_prompt/pallas_call | solution.py:314
  38.2 0.0 copy-start.3
  38.2 0.3 all-to-all-done
  38.5 0.0 collective-permute-done.kv_ref
  38.5 0.0 copy-done.1
  38.5 2.4 %handed_attention.1 = (f32[8,32,128]{2,1,0:T(8,128)}, bf16[2048,512]{1,0:T(8,128)(2,1)}) custom-call(bf16[2048,256]{1,0:T(8,128)(2,1)S(1)} %collective-permute-done.kv_ref, bf16[64,768]{1,0:T(8,128)(2,1)S(1)} %copy-done.1, bf16[64,768]{1,0:T(8,128)(2,1)S(1)} %bitcast.8, bf16[2048,512]{1,0:T(8,128)(2,1)} %long_prompt.1._), custom_call_target="tpu_custom_call", output_to_operand_aliasing={{1}: (3, {})} | custom-call | flops 402653184 | bytes 2097152 | tf_op jit(solution)/shard_map/handed_attention/pallas_call | solution.py:384
  40.9 5.7 %all-to-all-start.1 = ((f32[8,32,128]{2,1,0:T(8,128)}), f32[8,32,128]{2,1,0:T(8,128)S(1)}, u32[]{:S(2)}, u32[]{:S(2)}) async-start(f32[8,32,128]{2,1,0:T(8,128)} %get-tuple-element.13), calls=%async_computation.1 | async-start | bytes 262144 | tf_op jit(solution)/shard_map/all_to_all | solution.py:529
  46.5 0.0 copy-done.3
  46.6 0.0 copy-start
  46.6 0.0 copy-start.2
  46.6 0.0 copy-start.4
  46.6 0.0 copy-start.5
  46.6 0.0 copy-start.6
  46.6 7.2 %short_prompts.1 = bf16[2048,512]{1,0:T(8,128)(2,1)} custom-call(s32[2,3]{1,0:T(2,128)S(1)} %copy-done.3, bf16[2048,2048]{1,0:T(8,128)(2,1)} %get-tuple-element.8.q_hbm, bf16[2048,512]{1,0:T(8,128)(2,1)} %get-tuple-element.12.refs_0_), custom_call_target="tpu_custom_call", output_to_operand_aliasing={{}: (2, {})} | custom-call | flops 4294967296 | bytes 4194304 | tf_op jit(solution)/shard_map/short_prompts/pallas_call | solution.py:314
  53.8 0.1 all-to-all-done.1.refs_7_
  53.9 0.0 copy-done
  53.9 0.0 copy-done.2
  53.9 0.0 copy-done.4
  53.9 0.0 copy-done.5
  53.9 0.0 copy-done.6
  53.9 2.6 %decode_attention.1 = bf16[3,2,4096]{2,1,0:T(2,128)(2,1)} custom-call(s32[2,3]{1,0:T(2,128)S(1)} %copy-done.3, s32[2,3]{1,0:T(2,128)S(1)} %copy-done.4, s32[2,2,16]{2,1,0:T(2,128)S(1)} %bitcast.11, s32[2,3]{1,0:T(2,128)S(1)} %bitcast.13, s32[3]{0:T(128)S(1)} %copy-done.6, bf16[768,2048]{1,0:T(8,128)(2,1)S(1)} %bitcast.7, bf16[64,768]{1,0:T(8,128)(2,1)S(1)} %bitcast.9, ...), custom_call_target="tpu_custom_call" | custom-call | flops 100663296 | bytes 4194304 | tf_op jit(solution)/shard_map/decode_attention/pallas_call | solution.py:484
Async XLA Ops:
  24.0 14.5 %collective-permute-start = (bf16[2048,256]{1,0:T(8,128)(2,1)}, bf16[2048,256]{1,0:T(8,128)(2,1)S(1)}, u32[]{:S(2)}, u32[]{:S(2)}) collective-permute-start(bf16[2048,256]{1,0:T(8,128)(2,1)} %get-tuple-element.9), channel_id=1, source_target_pairs={{0,8},{8,0},{1,9},{9,1},{2,10},{10,2},{3,11},{11,3},{4,12},{12,4},... | collective-permute-start | bytes 3145736 | tf_op jit(solution)/shard_map/ppermute | solution.py:525
  24.5 14.0 %all-to-all-start = ((bf16[8,8,768]{2,1,0:T(8,128)(2,1)}), bf16[8,8,768]{2,1,0:T(8,128)(2,1)S(1)}, u32[]{:S(2)}, u32[]{:S(2)}) async-start(bf16[8,8,768]{2,1,0:T(8,128)(2,1)} %bitcast.14), calls=%async_computation | async-start | bytes 196608 | tf_op jit(solution)/shard_map/all_to_all | solution.py:526
  31.3 7.2 %copy-start.1 = (bf16[64,768]{1,0:T(8,128)(2,1)S(1)}, bf16[64,768]{1,0:T(8,128)(2,1)}, u32[]{:S(2)}) copy-start(bf16[64,768]{1,0:T(8,128)(2,1)} %get-tuple-element.10.own_ref) | copy-start | bytes 294916
  38.2 8.4 %copy-start.3 = (s32[2,3]{1,0:T(2,128)S(1)}, s32[2,3]{1,0:T(2,128)}, u32[]{:S(2)}) copy-start(s32[2,3]{1,0:T(2,128)} %refs_0_.3) | copy-start | bytes 76
  40.9 13.0 %all-to-all-start.1 = ((f32[8,32,128]{2,1,0:T(8,128)}), f32[8,32,128]{2,1,0:T(8,128)S(1)}, u32[]{:S(2)}, u32[]{:S(2)}) async-start(f32[8,32,128]{2,1,0:T(8,128)} %get-tuple-element.13), calls=%async_computation.1 | async-start | bytes 262144 | tf_op jit(solution)/shard_map/all_to_all | solution.py:529
  46.6 7.3 %copy-start = (bf16[6,128,2048]{2,1,0:T(8,128)(2,1)S(1)}, bf16[6,128,2048]{2,1,0:T(8,128)(2,1)}, u32[]{:S(2)}) copy-start(bf16[6,128,2048]{2,1,0:T(8,128)(2,1)} %param.18) | copy-start | bytes 9437188
  46.6 7.3 %copy-start.2 = (s32[2,16,2]{1,2,0:T(2,128)S(1)}, s32[2,16,2]{1,2,0:T(2,128)}, u32[]{:S(2)}) copy-start(s32[2,16,2]{1,2,0:T(2,128)} %param.15) | copy-start | bytes 772
  46.6 7.3 %copy-start.4 = (s32[2,3]{1,0:T(2,128)S(1)}, s32[2,3]{1,0:T(2,128)}, u32[]{:S(2)}) copy-start(s32[2,3]{1,0:T(2,128)} %refs_1_.3) | copy-start | bytes 76
  46.6 7.3 %copy-start.5 = (s32[3,2]{0,1:T(2,128)S(1)}, s32[3,2]{0,1:T(2,128)}, u32[]{:S(2)}) copy-start(s32[3,2]{0,1:T(2,128)} %param.16) | copy-start | bytes 76
  46.6 7.3 %copy-start.6 = (s32[3]{0:T(128)S(1)}, s32[3]{0:T(128)}, u32[]{:S(2)}) copy-start(s32[3]{0:T(128)} %refs_4_.3) | copy-start | bytes 40
